TPU v7x, 32 devices: a whole 2x2x4 slice. The times are simulated.
32 devices in a mesh: seq: 4 (over y, x), ctx: 8 (over z, core).
Axes of the slice: x: 2, y: 2, z: 4, core: 2. Of those that a mesh axis runs over, the one named last changes fastest.
Arguments:
- tokens: bfloat16 [4096, 2304], P(('seq', 'ctx')), may hold values from -6 to 6
- w_query: bfloat16 [2304, 2048], P(('seq', 'ctx')), may hold values from -0.125 to 0.125
- w_key: bfloat16 [2304, 1024], P(('seq', 'ctx')), may hold values from -0.125 to 0.125
- w_value: bfloat16 [2304, 1024], P(('seq', 'ctx')), may hold values from -0.125 to 0.125
- w_output: bfloat16 [2048, 2304], P(('seq', 'ctx')), may hold values from -0.125 to 0.125
- w_gate: bfloat16 [2304, 9216], P('seq', 'ctx'), may hold values from -0.125 to 0.125
- w_up: bfloat16 [2304, 9216], P('seq', 'ctx'), may hold values from -0.125 to 0.125
- w_down: bfloat16 [9216, 2304], P('ctx', 'seq'), may hold values from -0.0625 to 0.0625
- first_gain: bfloat16 [2304], P(('seq', 'ctx')), may hold values from 0.25 to 1.75
- second_gain: bfloat16 [2304], P(('seq', 'ctx')), may hold values from 0.25 to 1.75
- third_gain: bfloat16 [2304], P(('seq', 'ctx')), may hold values from 0.25 to 1.75
- fourth_gain: bfloat16 [2304], P(('seq', 'ctx')), may hold values from 0.25 to 1.75
- block_pairs: int32 [8, 2], replicated, may hold values from 0 to 15, as said below
- cotangent: bfloat16 [4096, 2304], P(('seq', 'ctx')), may hold values from -6 to 6
Outputs:
- layer_out: bfloat16 [4096, 2304], P(('seq', 'ctx'))
- grad_tokens: bfloat16 [4096, 2304], P(('seq', 'ctx'))
- grad_query: float32 [2304, 2048], P(('seq', 'ctx'))
- grad_key: float32 [2304, 1024], P(('seq', 'ctx'))
- grad_value: float32 [2304, 1024], P(('seq', 'ctx'))
- grad_output: float32 [2048, 2304], P(('seq', 'ctx'))
- grad_gate: float32 [2304, 9216], P('seq', 'ctx')
- grad_up: float32 [2304, 9216], P('seq', 'ctx')
- grad_down: float32 [9216, 2304], P('ctx', 'seq')
- grad_first: float32 [2304], P(('seq', 'ctx'))
- grad_second: float32 [2304], P(('seq', 'ctx'))
- grad_third: float32 [2304], P(('seq', 'ctx'))
- grad_fourth: float32 [2304], P(('seq', 'ctx'))
Inputs may be any that keep to these rules, and one draw needn't show every extreme that they name: `block_pairs`: row c holds a front block number below 8 and the back block number 2 * 8 - 1 minus it; every block number appears once in the array.
All inputs are finite; a program needn't handle non-finite values.
Results may differ from a plain program's by a relative error of at most 0.023.
Values may be sent and summed in bfloat16 or wider, within the bound.
No kernel may reach another device: no remote copies, remote signals or barrier semaphores. Data moves between devices by JAX's collectives and lax.ppermute only.
A program may use at most 320 MiB of HBM per device.

v0:
```python
import jax
import jax.numpy as jnp
from jax import lax
from jax.sharding import PartitionSpec as P

QUERY_HEAD_COUNT = 8
KV_HEADS = 4
HEAD_FEATURES = 256


epsilon = 1e-06
softcap = 50.0
theta = 10000.0
floor_value = -1e30


def rms_scale(signal, weight):
    return signal * lax.rsqrt(jnp.mean(signal * signal, axis=-1, keepdims=True) + epsilon) * weight


def norm_back(signal, weight, upstream):
    outcome, pullback = jax.vjp(rms_scale, signal, weight)
    return pullback(upstream)


def gate_mix(gate_pre, up_pre):
    return jax.nn.gelu(gate_pre, approximate=True) * up_pre


def rotate(signal, positions, head_width):
    row_count = signal.shape[0]
    head_count = signal.shape[1] // head_width
    half_width = head_width // 2
    frequency = theta ** (-2.0 * jnp.arange(half_width, dtype=jnp.float32) / head_width)
    angles = positions.astype(jnp.float32)[:, None] * frequency[None, :]
    cosine = jnp.cos(angles)[:, None, :]
    sine_wave = jnp.sin(angles)[:, None, :]
    shaped = signal.reshape(row_count, head_count, head_width)
    first_half = shaped[:, :, :half_width]
    second = shaped[:, :, half_width:]
    turned = jnp.concatenate(
        [first_half * cosine - second * sine_wave, second * cosine + first_half * sine_wave], axis=2
    )
    return turned.reshape(row_count, head_count * head_width)


def block_scores(head_queries, key_all, key_pos, query_pos, block_rows, score_scale):
    block_keys = key_all.reshape(block_rows, KV_HEADS, HEAD_FEATURES)
    allowed = key_pos[None, :] <= query_pos[:, None]
    unscaled_score = (
        jnp.einsum("fwvi,hwi->wvfh", head_queries, block_keys, preferred_element_type=jnp.float32)
        * score_scale
    )
    bent_score = jnp.tanh(unscaled_score / softcap)
    capped = jnp.where(allowed, softcap * bent_score, floor_value)
    return (block_keys, allowed, bent_score, capped)


def attend(head_queries, key_all, value_all, query_pos, key_pos, score_scale):
    length_total = key_all.shape[0]
    block_count = max(1, length_total // 2048)
    block_rows = length_total // block_count
    row_count = head_queries.shape[0]
    group_size = head_queries.shape[2]

    def total_step(block_index, carried):
        running_max, running_sum = carried
        block_keys, allowed, bent_score, capped = block_scores(
            head_queries, key_all, key_pos, query_pos, block_rows, score_scale
        )
        new_max = jnp.maximum(running_max, jnp.max(capped, axis=-1))
        added = jnp.sum(jnp.where(allowed, jnp.exp(capped - new_max[..., None]), 0.0), axis=-1)
        return (new_max, running_sum * jnp.exp(running_max - new_max) + added)

    start_max = jnp.full((KV_HEADS, group_size, row_count), floor_value, jnp.float32)
    start_sum = jnp.zeros((KV_HEADS, group_size, row_count), jnp.float32)
    running_max, running_sum = lax.fori_loop(0, block_count, total_step, (start_max, start_sum))
    log_total = running_max + jnp.log(running_sum)

    def mix_step(block_index, carried):
        accum, rest_acc = carried
        block_keys, allowed, bent_score, capped = block_scores(
            head_queries, key_all, key_pos, query_pos, block_rows, score_scale
        )
        block_values = value_all.reshape(block_rows, KV_HEADS, HEAD_FEATURES)
        prob_full = jnp.where(allowed, jnp.exp(capped - log_total[..., None]), 0.0)
        lowered_probs = prob_full.astype(jnp.bfloat16)
        remaining_probs = (prob_full - lowered_probs.astype(jnp.float32)).astype(jnp.bfloat16)
        accum = accum + jnp.einsum(
            "xmbe,exk->bxmk", lowered_probs, block_values, preferred_element_type=jnp.float32
        )
        rest_acc = rest_acc + jnp.einsum(
            "xmbe,exk->bxmk", remaining_probs, block_values, preferred_element_type=jnp.float32
        )
        return (accum, rest_acc)

    start_mix = jnp.zeros((row_count, KV_HEADS, group_size, HEAD_FEATURES), jnp.float32)
    full_mixture, rest_acc = lax.fori_loop(0, block_count, mix_step, (start_mix, start_mix))
    exact_mixture = full_mixture + rest_acc
    return (
        log_total,
        full_mixture.reshape(row_count, QUERY_HEAD_COUNT * HEAD_FEATURES),
        exact_mixture,
    )


def attend_back(
    head_queries,
    key_all,
    value_all,
    query_pos,
    key_pos,
    score_scale,
    log_total,
    exact_mixture,
    mixed_grad,
):
    length_total = key_all.shape[0]
    block_count = max(1, length_total // 2048)
    block_rows = length_total // block_count
    row_count = head_queries.shape[0]
    group_size = head_queries.shape[2]
    head_gradient = mixed_grad.reshape(row_count, KV_HEADS, group_size, HEAD_FEATURES)
    row_difference = jnp.einsum("ozlq,ozlq->zlo", head_gradient.astype(jnp.float32), exact_mixture)

    def grad_step(block_index, carried):
        query_acc, key_acc, value_acc = carried
        block_keys, allowed, bent_score, capped = block_scores(
            head_queries, key_all, key_pos, query_pos, block_rows, score_scale
        )
        block_values = value_all.reshape(block_rows, KV_HEADS, HEAD_FEATURES)
        prob_full = jnp.where(allowed, jnp.exp(capped - log_total[..., None]), 0.0)
        lowered_probs = prob_full.astype(jnp.bfloat16)
        value_part = jnp.einsum(
            "zwcv,czwy->vzy", lowered_probs, head_gradient, preferred_element_type=jnp.float32
        )
        prob_grad = jnp.einsum(
            "fwvi,hwi->wvfh", head_gradient, block_values, preferred_element_type=jnp.float32
        )
        lowered_logits = (
            prob_full * (prob_grad - row_difference[..., None]) * (1.0 - bent_score * bent_score)
        ).astype(jnp.bfloat16)
        query_acc = (
            query_acc
            + jnp.einsum(
                "xmbe,exk->bxmk", lowered_logits, block_keys, preferred_element_type=jnp.float32
            )
            * score_scale
        )
        key_part = (
            jnp.einsum(
                "zwcv,czwy->vzy", lowered_logits, head_queries, preferred_element_type=jnp.float32
            )
            * score_scale
        )
        key_acc = key_part.reshape(block_rows, KV_HEADS * HEAD_FEATURES)
        value_acc = value_part.reshape(block_rows, KV_HEADS * HEAD_FEATURES)
        return (query_acc, key_acc, value_acc)

    start = (
        jnp.zeros((row_count, KV_HEADS, group_size, HEAD_FEATURES), jnp.float32),
        jnp.zeros((length_total, KV_HEADS * HEAD_FEATURES), jnp.float32),
        jnp.zeros((length_total, KV_HEADS * HEAD_FEATURES), jnp.float32),
    )
    query_acc, key_acc, value_acc = lax.fori_loop(0, block_count, grad_step, start)
    return (query_acc.reshape(row_count, QUERY_HEAD_COUNT * HEAD_FEATURES), key_acc, value_acc)


def body(
    tokens,
    w_query,
    w_key,
    w_value,
    w_output,
    w_gate,
    w_up,
    w_down,
    first_gain,
    second_gain,
    third_gain,
    fourth_gain,
    block_pairs,
    cotangent,
):
    query_full, key_full, value_full, output_full, gain_one, gain_two, gain_three, gain_four = (
        lax.all_gather(w_query, ("seq", "ctx"), axis=0, tiled=True),
        lax.all_gather(w_key, ("seq", "ctx"), axis=0, tiled=True),
        lax.all_gather(w_value, ("seq", "ctx"), axis=0, tiled=True),
        lax.all_gather(w_output, ("seq", "ctx"), axis=0, tiled=True),
        lax.all_gather(first_gain, ("seq", "ctx"), axis=0, tiled=True),
        lax.all_gather(second_gain, ("seq", "ctx"), axis=0, tiled=True),
        lax.all_gather(third_gain, ("seq", "ctx"), axis=0, tiled=True),
        lax.all_gather(fourth_gain, ("seq", "ctx"), axis=0, tiled=True),
    )
    gain_one = gain_one.astype(jnp.float32)
    gain_two = gain_two.astype(jnp.float32)
    gain_three = gain_three.astype(jnp.float32)
    gain_four = gain_four.astype(jnp.float32)
    row_count = tokens.shape[0]
    block_size = row_count // 2
    group_size = QUERY_HEAD_COUNT // KV_HEADS
    score_scale = HEAD_FEATURES ** (-0.5)
    own_pair = lax.dynamic_index_in_dim(block_pairs, lax.axis_index("ctx"), 0, keepdims=False)
    offsets = jnp.arange(block_size, dtype=jnp.int32)
    query_pos = jnp.concatenate(
        [own_pair[0] * block_size + offsets, own_pair[1] * block_size + offsets]
    )
    key_pos = (block_pairs[:, :, None] * block_size + offsets[None, None, :]).reshape(-1)
    residual_in = tokens.astype(jnp.float32)
    normed = rms_scale(residual_in, gain_one).astype(jnp.bfloat16)
    query_proj = jnp.dot(normed, query_full, preferred_element_type=jnp.float32)
    key_proj = jnp.dot(normed, key_full, preferred_element_type=jnp.float32)
    value_proj = jnp.dot(normed, value_full, preferred_element_type=jnp.float32)
    query_low = rotate(query_proj, query_pos, HEAD_FEATURES).astype(jnp.bfloat16)
    key_low = rotate(key_proj, query_pos, HEAD_FEATURES).astype(jnp.bfloat16)
    lowered_values = value_proj.astype(jnp.bfloat16)
    key_all, value_all = (
        lax.all_gather(key_low, "ctx", axis=0, tiled=True),
        lax.all_gather(lowered_values, "ctx", axis=0, tiled=True),
    )
    head_queries = query_low.reshape(row_count, KV_HEADS, group_size, HEAD_FEATURES)
    log_total, full_mixture, exact_mixture = attend(
        head_queries, key_all, value_all, query_pos, key_pos, score_scale
    )
    mixed_low = full_mixture.astype(jnp.bfloat16)
    branch = jnp.dot(mixed_low, output_full, preferred_element_type=jnp.float32)
    residual = residual_in + rms_scale(branch, gain_two)
    feed_input = rms_scale(residual, gain_three).astype(jnp.bfloat16)
    part_gate, part_up, part_down = (
        lax.all_gather(w_gate, "seq", axis=0, tiled=True),
        lax.all_gather(w_up, "seq", axis=0, tiled=True),
        lax.all_gather(w_down, "seq", axis=1, tiled=True),
    )
    feed_all = lax.all_gather(feed_input, "ctx", axis=0, tiled=True)
    gate_pre = jnp.dot(feed_all, part_gate, preferred_element_type=jnp.float32)
    up_pre = jnp.dot(feed_all, part_up, preferred_element_type=jnp.float32)
    hidden = gate_mix(gate_pre, up_pre).astype(jnp.bfloat16)
    feed_out = lax.psum_scatter(
        jnp.dot(hidden, part_down, preferred_element_type=jnp.float32).astype(jnp.bfloat16),
        "ctx",
        scatter_dimension=0,
        tiled=True,
    ).astype(jnp.float32)
    layer_out = (residual + rms_scale(feed_out, gain_four)).astype(jnp.bfloat16)
    upstream = cotangent.astype(jnp.float32)
    feed_grad, fourth_term = norm_back(feed_out, gain_four, upstream)
    feed_low = feed_grad.astype(jnp.bfloat16)
    cotangent_all = lax.all_gather(feed_low, "ctx", axis=0, tiled=True)
    hidden_grad = jnp.einsum(
        "td,fd->tf", cotangent_all, part_down, preferred_element_type=jnp.float32
    )
    outcome, mix_pull = jax.vjp(gate_mix, gate_pre, up_pre)
    gate_grad, up_grad = mix_pull(hidden_grad)
    gate_low = gate_grad.astype(jnp.bfloat16)
    up_low = up_grad.astype(jnp.bfloat16)
    input_part = jnp.einsum(
        "tf,df->td", gate_low, part_gate, preferred_element_type=jnp.float32
    ) + jnp.einsum("tf,df->td", up_low, part_up, preferred_element_type=jnp.float32)
    feed_input_grad = lax.psum_scatter(
        input_part.astype(jnp.bfloat16), "ctx", scatter_dimension=0, tiled=True
    ).astype(jnp.float32)
    gate_term = jnp.einsum("tf,td->fd", gate_low, feed_all, preferred_element_type=jnp.float32)
    up_term = jnp.einsum("tf,td->fd", up_low, feed_all, preferred_element_type=jnp.float32)
    down_term = jnp.einsum("tf,td->fd", hidden, cotangent_all, preferred_element_type=jnp.float32)
    gate_sum, up_sum, down_sum = (
        lax.psum_scatter(
            gate_term.astype(jnp.bfloat16), "seq", scatter_dimension=1, tiled=True
        ).astype(jnp.float32),
        lax.psum_scatter(
            up_term.astype(jnp.bfloat16), "seq", scatter_dimension=1, tiled=True
        ).astype(jnp.float32),
        lax.psum_scatter(
            down_term.astype(jnp.bfloat16), "seq", scatter_dimension=1, tiled=True
        ).astype(jnp.float32),
    )
    middle_grad, third_term = norm_back(residual, gain_three, feed_input_grad)
    residual_grad = upstream + middle_grad
    branch_grad, second_term = norm_back(branch, gain_two, residual_grad)
    branch_low = branch_grad.astype(jnp.bfloat16)
    output_term = jnp.einsum("th,td->hd", mixed_low, branch_low, preferred_element_type=jnp.float32)
    mixed_grad = jnp.einsum(
        "td,hd->th", branch_low, output_full, preferred_element_type=jnp.float32
    ).astype(jnp.bfloat16)
    query_sum, key_acc, value_acc = attend_back(
        head_queries,
        key_all,
        value_all,
        query_pos,
        key_pos,
        score_scale,
        log_total,
        exact_mixture,
        mixed_grad,
    )
    key_own, value_own = (
        lax.psum_scatter(
            key_acc.astype(jnp.bfloat16), "ctx", scatter_dimension=0, tiled=True
        ).astype(jnp.float32),
        lax.psum_scatter(
            value_acc.astype(jnp.bfloat16), "ctx", scatter_dimension=0, tiled=True
        ).astype(jnp.float32),
    )
    query_grad = rotate(query_sum, -query_pos, HEAD_FEATURES).astype(jnp.bfloat16)
    key_grad = rotate(key_own, -query_pos, HEAD_FEATURES).astype(jnp.bfloat16)
    value_grad = value_own.astype(jnp.bfloat16)
    normed_grad = jnp.einsum(
        "th,dh->td", query_grad, query_full, preferred_element_type=jnp.float32
    )
    normed_grad = normed_grad + jnp.einsum(
        "th,dh->td", key_grad, key_full, preferred_element_type=jnp.float32
    )
    normed_grad = normed_grad + jnp.einsum(
        "th,dh->td", value_grad, value_full, preferred_element_type=jnp.float32
    )
    query_term = jnp.einsum("td,th->dh", normed, query_grad, preferred_element_type=jnp.float32)
    key_term = jnp.einsum("td,th->dh", normed, key_grad, preferred_element_type=jnp.float32)
    value_term = jnp.einsum("td,th->dh", normed, value_grad, preferred_element_type=jnp.float32)
    input_grad, first_term = norm_back(residual_in, gain_one, normed_grad)
    grad_tokens = (residual_grad + input_grad).astype(jnp.bfloat16)
    grad_sums = (
        lax.psum_scatter(query_term, ("seq", "ctx"), scatter_dimension=0, tiled=True),
        lax.psum_scatter(key_term, ("seq", "ctx"), scatter_dimension=0, tiled=True),
        lax.psum_scatter(value_term, ("seq", "ctx"), scatter_dimension=0, tiled=True),
        lax.psum_scatter(output_term, ("seq", "ctx"), scatter_dimension=0, tiled=True),
        lax.psum_scatter(first_term, ("seq", "ctx"), scatter_dimension=0, tiled=True),
        lax.psum_scatter(second_term, ("seq", "ctx"), scatter_dimension=0, tiled=True),
        lax.psum_scatter(third_term, ("seq", "ctx"), scatter_dimension=0, tiled=True),
        lax.psum_scatter(fourth_term, ("seq", "ctx"), scatter_dimension=0, tiled=True),
    )
    return (
        layer_out,
        grad_tokens,
        grad_sums[0],
        grad_sums[1],
        grad_sums[2],
        grad_sums[3],
        gate_sum.T,
        up_sum.T,
        down_sum,
        grad_sums[4],
        grad_sums[5],
        grad_sums[6],
        grad_sums[7],
    )


def solution(mesh):
    placed = (
        P(("seq", "ctx"), None),
        P(("seq", "ctx"), None),
        P(("seq", "ctx"), None),
        P(("seq", "ctx"), None),
        P(("seq", "ctx"), None),
        P("seq", "ctx"),
        P("seq", "ctx"),
        P("ctx", "seq"),
        P(("seq", "ctx")),
        P(("seq", "ctx")),
        P(("seq", "ctx")),
        P(("seq", "ctx")),
        P(),
        P(("seq", "ctx"), None),
    )
    return jax.shard_map(
        body,
        mesh=mesh,
        in_specs=placed,
        out_specs=(
            P(("seq", "ctx"), None),
            P(("seq", "ctx"), None),
            P(("seq", "ctx"), None),
            P(("seq", "ctx"), None),
            P(("seq", "ctx"), None),
            P(("seq", "ctx"), None),
            P("seq", "ctx"),
            P("seq", "ctx"),
            P("ctx", "seq"),
            P(("seq", "ctx")),
            P(("seq", "ctx")),
            P(("seq", "ctx")),
            P(("seq", "ctx")),
        ),
        check_vma=False,
    )
```

profile of v0, /device:TPU:3, one launch (start us, length us, event | category | flops | bytes accessed | tf_op | source)
XLA Modules:
  0.0 1830.9 jit_solution(15320071579788853866)
XLA Ops:
  12.2 40.4 %all-reduce.9 = (bf16[2304]{0:T(1024)(128)(2,1)S(1)}, bf16[2304]{0:T(1024)(128)(2,1)S(1)}, bf16[2304]{0:T(1024)(128)(2,1)S(1)}, bf16[2304]{0:T(1024)(128)(2,1)}) all-reduce(bf16[2304]{0:T(1024)(128)(2,1)S(1)} %dynamic-update-slice, bf16[2304]{0:T(1024)(128)(2,1)S(1)} %dynamic-update-slice.1, ...), channel_id=1, replica_groups=mesh['seq'=4,'ctx'=8] {'seq','ctx'}, use_global_device_ids=true, to_apply=%add | all-reduce | flops 9216 | bytes 36864
  53.9 22.5 %all-gather.12.cloned.1.call-done = bf16[2304,1024]{1,0:T(8,128)(2,1)} async-done(((bf16[72,1024]{1,0:T(8,128)(2,1)}), bf16[2304,1024]{1,0:T(8,128)(2,1)}) %all-gather.12.cloned.1.call-update) | async-done | bytes 4718608 | tf_op jit(solution)/shard_map/all_gather | solution.py:188
  76.3 4.1 convolution_convert_fusion.5
  84.0 57.8 %all-gather.16.cloned.1.call-done = bf16[2304,1024]{1,0:T(8,128)(2,1)} async-done(((bf16[72,1024]{1,0:T(8,128)(2,1)}), bf16[2304,1024]{1,0:T(8,128)(2,1)}) %all-gather.16.cloned.1.call-update) | async-done | bytes 4718608 | tf_op jit(solution)/shard_map/all_gather | solution.py:187
  141.9 3.2 fusion.70
  148.6 23.5 %all-gather.14.cloned.1.call-done = bf16[1024,1024]{1,0:T(8,128)(2,1)} async-done(((bf16[128,1024]{1,0:T(8,128)(2,1)}), bf16[1024,1024]{1,0:T(8,128)(2,1)}) %all-gather.14.cloned.1.call-update) | async-done | bytes 2097168 | tf_op jit(solution)/shard_map/all_gather | solution.py:219
  172.1 4.5 reshape.316
  176.6 80.0 %all-gather.20.cloned.1.call-done = bf16[2304,2048]{1,0:T(8,128)(2,1)} async-done(((bf16[72,2048]{1,0:T(8,128)(2,1)}), bf16[2304,2048]{1,0:T(8,128)(2,1)}) %all-gather.20.cloned.1.call-update) | async-done | bytes 9437200 | tf_op jit(solution)/shard_map/all_gather | solution.py:186
  256.6 5.1 fusion.68
  262.4 25.4 %all-gather.18.cloned.1.call-done = bf16[1024,1024]{0,1:T(8,128)(2,1)} async-done(((bf16[128,1024]{0,1:T(8,128)(2,1)}), bf16[1024,1024]{0,1:T(8,128)(2,1)}) %all-gather.18.cloned.1.call-update) | async-done | bytes 2097168 | tf_op jit(solution)/shard_map/all_gather | solution.py:218
  287.8 2.9 fusion.11
  290.8 1.3 select_reduce_fusion
  293.9 2.9 fusion.74
  296.7 75.4 %all-gather.22.cloned.1.call-done = bf16[2048,2304]{1,0:T(8,128)(2,1)} async-done(((bf16[64,2304]{1,0:T(8,128)(2,1)}), bf16[2048,2304]{1,0:T(8,128)(2,1)}) %all-gather.22.cloned.1.call-update) | async-done | bytes 9437200 | tf_op jit(solution)/shard_map/all_gather | solution.py:189
  372.1 5.2 multiply_reduce_fusion.3
  380.5 53.7 %all-gather.26.cloned.1.call-done = bf16[2304,1152]{1,0:T(8,128)(2,1)} async-done(((bf16[576,1152]{1,0:T(8,128)(2,1)}), bf16[2304,1152]{1,0:T(8,128)(2,1)}) %all-gather.26.cloned.1.call-update) | async-done | bytes 5308432 | tf_op jit(solution)/shard_map/all_gather | solution.py:230
  434.2 54.4 %all-gather.24.cloned.1.call-done = bf16[1024,2304]{1,0:T(8,128)(2,1)} async-done(((bf16[128,2304]{1,0:T(8,128)(2,1)}), bf16[1024,2304]{1,0:T(8,128)(2,1)}) %all-gather.24.cloned.1.call-update) | async-done | bytes 4718608 | tf_op jit(solution)/shard_map/all_gather | solution.py:234
  488.6 11.1 fusion.75
  499.7 51.2 %all-gather.28.cloned.1.call-done = bf16[2304,1152]{1,0:T(8,128)(2,1)} async-done(((bf16[576,1152]{1,0:T(8,128)(2,1)}), bf16[2304,1152]{1,0:T(8,128)(2,1)}) %all-gather.28.cloned.1.call-update) | async-done | bytes 5308432 | tf_op jit(solution)/shard_map/all_gather | solution.py:231
  550.8 12.5 multiply_convert_fusion.1
  563.3 51.2 %all-gather.30.cloned.1.call-done = bf16[1152,2304]{0,1:T(8,128)(2,1)} async-done(((bf16[1152,576]{0,1:T(8,128)(2,1)}), bf16[1152,2304]{0,1:T(8,128)(2,1)}) %all-gather.30.cloned.1.call-update) | async-done | bytes 5308432 | tf_op jit(solution)/shard_map/all_gather | solution.py:232
  614.5 10.8 convolution_convert_fusion.3
  625.4 1.3 convert_element_type.176
  626.7 51.6 %reduce-scatter.16.cloned.1.call-done = bf16[128,2304]{1,0:T(8,128)(2,1)} async-done(((bf16[1024,2304]{1,0:T(8,128)(2,1)}), bf16[128,2304]{1,0:T(8,128)(2,1)}) %reduce-scatter.16.cloned.1.call-update) | async-done | bytes 589840 | tf_op jit(solution)/shard_map/reduce_scatter | solution.py:238
  679.6 2.3 fusion.42
  681.9 2.2 fusion.43
  684.7 52.2 %all-gather.32.cloned.1.call-done = bf16[1024,2304]{1,0:T(8,128)(2,1)} async-done(((bf16[128,2304]{1,0:T(8,128)(2,1)}), bf16[1024,2304]{1,0:T(8,128)(2,1)}) %all-gather.32.cloned.1.call-update) | async-done | bytes 4718608 | tf_op jit(solution)/shard_map/all_gather | solution.py:248
  736.9 14.3 multiply_convert_fusion
  751.2 10.5 fusion.76
  761.8 10.6 add_convert_fusion
  772.6 51.2 %reduce-scatter.18.cloned.1.call-done = bf16[128,2304]{1,0:T(8,128)(2,1)} async-done(((bf16[1024,2304]{1,0:T(8,128)(2,1)}), bf16[128,2304]{1,0:T(8,128)(2,1)}) %reduce-scatter.18.cloned.1.call-update) | async-done | bytes 589840 | tf_op jit(solution)/shard_map/reduce_scatter | solution.py:259
  823.8 2.1 fusion.41
  826.5 3.6 multiply_reduce_fusion
  832.2 6.8 convolution_convert_fusion.4
  840.0 5.4 bitcast_convert_fusion
  845.4 4.0 copy.110
  849.8 1.3 copy.90
  851.1 5.6 fusion.33
  856.8 2.5 fusion.8
  859.3 2.1 fusion.7
  861.5 4.0 copy.108
  865.7 10.5 convolution_convert_fusion
  876.3 10.6 convolution_convert_fusion.1
  887.0 10.5 convolution_convert_fusion.2
  897.5 6.0 fusion.62
  905.9 13.9 reduce-scatter.34.cloned.1.call-done
  921.9 5.0 fusion.64
  927.0 10.9 fusion.78
  938.0 2.3 convolution_multiply_fusion
  940.5 8.2 fusion.66
  948.8 7.0 fusion.77
  955.8 30.1 %reduce-scatter.32.cloned.1.call-done = bf16[1152,576]{0,1:T(8,128)(2,1)} async-done(((bf16[1152,2304]{0,1:T(8,128)(2,1)}), bf16[1152,576]{0,1:T(8,128)(2,1)}) %reduce-scatter.32.cloned.1.call-update) | async-done | bytes 1327120 | tf_op jit(solution)/shard_map/reduce_scatter | solution.py:272
  985.9 3.0 convert_element_type.202
  988.9 61.9 %reduce-scatter.30.cloned.1.call-done = bf16[1152,576]{0,1:T(8,128)(2,1)} async-done(((bf16[1152,2304]{0,1:T(8,128)(2,1)}), bf16[1152,576]{0,1:T(8,128)(2,1)}) %reduce-scatter.30.cloned.1.call-update) | async-done | bytes 1327120 | tf_op jit(solution)/shard_map/reduce_scatter | solution.py:269
  1050.8 3.0 convert_bitcast_fusion
  1053.8 61.9 %reduce-scatter.28.cloned.1.call-done = bf16[1152,576]{0,1:T(8,128)(2,1)} async-done(((bf16[1152,2304]{0,1:T(8,128)(2,1)}), bf16[1152,576]{0,1:T(8,128)(2,1)}) %reduce-scatter.28.cloned.1.call-update) | async-done | bytes 1327120 | tf_op jit(solution)/shard_map/reduce_scatter | solution.py:266
  1115.7 3.0 convert_bitcast_fusion.1
  1118.7 4.1 convolution_add_fusion.1
  1122.8 4.3 fusion.37
  1127.2 40.3 %all-reduce.8 = (f32[2304]{0:T(1024)S(1)}, f32[2304]{0:T(1024)S(1)}, f32[2304]{0:T(1024)S(1)}, f32[2304]{0:T(1024)S(1)}) all-reduce(f32[2304]{0:T(1024)S(1)} %get-tuple-element.75, f32[2304]{0:T(1024)S(1)} %copy-done.26, f32[2304]{0:T(1024)S(1)} %copy-done.25, ...), channel_id=13, replica_groups=mesh['seq'=4,'ctx'=8] {'seq','ctx'}, use_global_device_ids=true, to_apply=%region_22.23.clone | all-reduce | flops 9216 | bytes 73728
  1171.1 84.9 %reduce-scatter.24.cloned.1.call-done = f32[72,1024]{1,0:T(8,128)} async-done(((f32[2304,1024]{1,0:T(8,128)}), f32[72,1024]{1,0:T(8,128)}) %reduce-scatter.24.cloned.1.call-update) | async-done | bytes 294928 | tf_op jit(solution)/shard_map/reduce_scatter | solution.py:323
  1256.0 141.9 %reduce-scatter.22.cloned.1.call-done = f32[72,1024]{1,0:T(8,128)} async-done(((f32[2304,1024]{1,0:T(8,128)}), f32[72,1024]{1,0:T(8,128)}) %reduce-scatter.22.cloned.1.call-update) | async-done | bytes 294928 | tf_op jit(solution)/shard_map/reduce_scatter | solution.py:322
  1397.9 213.4 %reduce-scatter.26.cloned.1.call-done = f32[64,2304]{1,0:T(8,128)} async-done(((f32[2048,2304]{1,0:T(8,128)}), f32[64,2304]{1,0:T(8,128)}) %reduce-scatter.26.cloned.1.call-update) | async-done | bytes 589840 | tf_op jit(solution)/shard_map/reduce_scatter | solution.py:324
  1611.3 212.7 %reduce-scatter.20.cloned.1.call-done = f32[72,2048]{1,0:T(8,128)} async-done(((f32[2304,2048]{1,0:T(8,128)}), f32[72,2048]{1,0:T(8,128)}) %reduce-scatter.20.cloned.1.call-update) | async-done | bytes 589840 | tf_op jit(solution)/shard_map/reduce_scatter | solution.py:321
  (185 shorter events, 32.4 us)
Async XLA Ops:
  7.2 134.7 %copy-start = (bf16[128,2304]{1,0:T(8,128)(2,1)S(1)}, bf16[128,2304]{1,0:T(8,128)(2,1)}, u32[]{:S(2)}) copy-start(bf16[128,2304]{1,0:T(8,128)(2,1)} %param.14) | copy-start | bytes 1769476
  7.2 73.9 %copy-start.32 = (s32[8,2]{0,1:T(2,128)S(1)}, s32[8,2]{0,1:T(2,128)}, u32[]{:S(2)}) copy-start(s32[8,2]{0,1:T(2,128)} %param.26) | copy-start | bytes 196
  7.2 69.1 %all-gather.12.cloned.1.call-start = ((), (), s32[]{:S(2)}) async-start(), calls=%async_computation.11 | async-start | bytes 4866048 | tf_op jit(solution)/shard_map/all_gather | solution.py:188
  7.9 133.9 %all-gather.16.cloned.1.call-start = ((), (), s32[]{:S(2)}) async-start(), calls=%async_computation.13 | async-start | bytes 4866048 | tf_op jit(solution)/shard_map/all_gather | solution.py:187
  8.7 163.4 %all-gather.14.cloned.1.call-start = ((), (), s32[]{:S(2)}) async-start(), calls=%async_computation.12 | async-start | bytes 2359296 | tf_op jit(solution)/shard_map/all_gather | solution.py:219
  53.9 27.2 %copy-start.34 = (f32[128]{0:T(128)}, f32[128]{0:T(128)S(1)}, u32[]{:S(2)}) copy-start(f32[128]{0:T(128)S(1)} %fusion.49) | copy-start | bytes 1540
  80.4 176.1 %all-gather.20.cloned.1.call-start = ((), (), s32[]{:S(2)}) async-start(), calls=%async_computation.15 | async-start | bytes 9732096 | tf_op jit(solution)/shard_map/all_gather | solution.py:186
  81.0 206.8 %all-gather.18.cloned.1.call-start = ((), (), s32[]{:S(2)}) async-start(), calls=%async_computation.14 | async-start | bytes 2359296 | tf_op jit(solution)/shard_map/all_gather | solution.py:218
  146.5 225.6 %all-gather.22.cloned.1.call-start = ((), (), s32[]{:S(2)}) async-start(), calls=%async_computation.16 | async-start | bytes 9732096 | tf_op jit(solution)/shard_map/all_gather | solution.py:189
  147.1 287.1 %all-gather.26.cloned.1.call-start = ((), (), s32[]{:S(2)}) async-start(), calls=%async_computation.18 | async-start | bytes 6635520 | tf_op jit(solution)/shard_map/all_gather | solution.py:230
  147.8 340.7 %all-gather.24.cloned.1.call-start = ((), (), s32[]{:S(2)}) async-start(), calls=%async_computation.17 | async-start | bytes 5308416 | tf_op jit(solution)/shard_map/all_gather | solution.py:234
  148.4 229.0 %copy-start.21 = (f32[2304]{0:T(1024)}, f32[2304]{0:T(1024)S(1)}, u32[]{:S(2)}) copy-start(f32[2304]{0:T(1024)S(1)} %convert_element_type.170) | copy-start | bytes 27652
  148.4 229.4 %copy-start.23 = (f32[2304]{0:T(1024)}, f32[2304]{0:T(1024)S(1)}, u32[]{:S(2)}) copy-start(f32[2304]{0:T(1024)S(1)} %convert_element_type.171) | copy-start | bytes 27652
  148.6 143.5 %copy-start.15 = (pred[128,1024]{0,1:T(8,128)(4,1)}, pred[128,1024]{0,1:T(8,128)(4,1)S(1)}, u32[]{:S(2)}) copy-start(pred[128,1024]{0,1:T(8,128)(4,1)S(1)} %broadcast_compare_fusion) | copy-start | bytes 393220
  262.4 28.4 %copy-start.8 = (bf16[128,8,256]{2,0,1:T(8,128)(2,1)}, bf16[128,8,256]{2,0,1:T(8,128)(2,1)S(1)}, u32[]{:S(2)}) copy-start(bf16[128,8,256]{2,0,1:T(8,128)(2,1)S(1)} %copy.62) | copy-start | bytes 1572868
  290.8 2.1 copy-start.5
  290.8 3.1 copy-start.10
  292.1 4.6 copy-start.30
  296.7 80.6 %copy-start.7 = (bf16[4,256,2,128]{3,1,2,0:T(8,128)(2,1)}, bf16[4,256,2,128]{3,1,2,0:T(8,128)(2,1)S(1)}, u32[]{:S(2)}) copy-start(bf16[4,256,2,128]{3,1,2,0:T(8,128)(2,1)S(1)} %get-tuple-element.137) | copy-start | bytes 1572868
  377.3 122.3 %copy-start.33 = (f32[128]{0:T(128)}, f32[128]{0:T(128)S(1)}, u32[]{:S(2)}) copy-start(f32[128]{0:T(128)S(1)} %get-tuple-element.139) | copy-start | bytes 1540
  377.4 122.3 %copy-start.29 = (f32[128]{0:T(128)}, f32[128]{0:T(128)S(1)}, u32[]{:S(2)}) copy-start(f32[128]{0:T(128)S(1)} %fusion.52) | copy-start | bytes 1540
  377.8 121.9 %copy-start.36 = (f32[128]{0:T(128)}, f32[128]{0:T(128)S(1)}, u32[]{:S(2)}) copy-start(f32[128]{0:T(128)S(1)} %get-tuple-element.114) | copy-start | bytes 1540
  377.8 121.9 %copy-start.28 = (f32[128]{0:T(128)}, f32[128]{0:T(128)S(1)}, u32[]{:S(2)}) copy-start(f32[128]{0:T(128)S(1)} %fusion.53) | copy-start | bytes 1540
  378.8 172.0 %all-gather.28.cloned.1.call-start = ((), (), s32[]{:S(2)}) async-start(), calls=%async_computation.19 | async-start | bytes 6635520 | tf_op jit(solution)/shard_map/all_gather | solution.py:231
  379.5 235.0 %all-gather.30.cloned.1.call-start = ((), (), s32[]{:S(2)}) async-start(), calls=%async_computation.20 | async-start | bytes 6635520 | tf_op jit(solution)/shard_map/all_gather | solution.py:232
  380.1 298.1 %reduce-scatter.16.cloned.1.call-start = ((), (), s32[]{:S(2)}) async-start(), calls=%async_computation.21 | async-start | bytes 5308416 | tf_op jit(solution)/shard_map/reduce_scatter | solution.py:238
  625.3 54.3 %copy-start.4 = (bf16[128,2304]{1,0:T(8,128)(2,1)S(1)}, bf16[128,2304]{1,0:T(8,128)(2,1)}, u32[]{:S(2)}) copy-start(bf16[128,2304]{1,0:T(8,128)(2,1)} %param.27) | copy-start | bytes 1769476
  625.3 111.6 %all-gather.32.cloned.1.call-start = ((), (), s32[]{:S(2)}) async-start(), calls=%async_computation.22 | async-start | bytes 5308416 | tf_op jit(solution)/shard_map/all_gather | solution.py:248
  679.6 2.3 copy-start.27
  684.1 139.6 %reduce-scatter.18.cloned.1.call-start = ((), (), s32[]{:S(2)}) async-start(), calls=%async_computation.23 | async-start | bytes 5308416 | tf_op jit(solution)/shard_map/reduce_scatter | solution.py:259
  751.2 10.5 copy-start.38
  751.2 10.5 copy-start.37
  772.4 54.2 %copy-start.3 = (bf16[128,2304]{1,0:T(8,128)(2,1)S(1)}, bf16[128,2304]{1,0:T(8,128)(2,1)}, u32[]{:S(2)}) copy-start(bf16[128,2304]{1,0:T(8,128)(2,1)} %reduce-scatter.16.cloned.1.call-done) | copy-start | bytes 1769476
  772.4 125.2 %reduce-scatter.36.cloned.1.call-start = ((), (), s32[]{:S(2)}) async-start(), calls=%async_computation.32 | async-start | bytes 2359296
  823.8 7.5 copy-start.22
  830.1 1.1 copy-start.1
  832.2 7.8 copy-start.16
  832.2 7.8 copy-start.31
  840.0 5.4 copy-start.17
  849.4 70.4 %reduce-scatter.34.cloned.1.call-start = ((), (), s32[]{:S(2)}) async-start(), calls=%async_computation.31 | async-start | bytes 2359296
  851.1 5.7 copy-start.6
  851.1 5.7 copy-start.11
  851.1 5.7 copy-start.18
  856.8 2.6 copy-start.9
  865.5 120.5 %reduce-scatter.32.cloned.1.call-start = ((), (), s32[]{:S(2)}) async-start(), calls=%async_computation.30 | async-start | bytes 6635520 | tf_op jit(solution)/shard_map/reduce_scatter | solution.py:272
  876.3 174.5 %reduce-scatter.30.cloned.1.call-start = ((), (), s32[]{:S(2)}) async-start(), calls=%async_computation.29 | async-start | bytes 6635520 | tf_op jit(solution)/shard_map/reduce_scatter | solution.py:269
  886.9 228.8 %reduce-scatter.28.cloned.1.call-start = ((), (), s32[]{:S(2)}) async-start(), calls=%async_computation.28 | async-start | bytes 6635520 | tf_op jit(solution)/shard_map/reduce_scatter | solution.py:266
  897.5 358.5 %reduce-scatter.24.cloned.1.call-start = ((), (), s32[]{:S(2)}) async-start(), calls=%async_computation.26 | async-start | bytes 9732096 | tf_op jit(solution)/shard_map/reduce_scatter | solution.py:323
  903.6 0.8 copy-start.20
  903.6 1.6 copy-start.19
  903.6 494.3 %reduce-scatter.22.cloned.1.call-start = ((), (), s32[]{:S(2)}) async-start(), calls=%async_computation.25 | async-start | bytes 9732096 | tf_op jit(solution)/shard_map/reduce_scatter | solution.py:322
  927.0 684.4 %reduce-scatter.26.cloned.1.call-start = ((), (), s32[]{:S(2)}) async-start(), calls=%async_computation.27 | async-start | bytes 19464192 | tf_op jit(solution)/shard_map/reduce_scatter | solution.py:324
  937.9 2.4 copy-start.13
  938.0 2.4 copy-start.14
  938.0 886.0 %reduce-scatter.20.cloned.1.call-start = ((), (), s32[]{:S(2)}) async-start(), calls=%async_computation.24 | async-start | bytes 19464192 | tf_op jit(solution)/shard_map/reduce_scatter | solution.py:321
  1118.7 4.1 copy-start.12
  1122.8 4.4 copy-start.24
  1122.8 4.4 copy-start.25
  1122.8 4.4 copy-start.26
  1122.8 47.0 %copy-start.35 = (f32[128]{0:T(128)S(1)}, f32[128]{0:T(128)}, u32[]{:S(2)}) copy-start(f32[128]{0:T(128)} %copy-done.34) | copy-start | bytes 1540
  1122.8 47.0 %copy-start.2 = (f32[128,2304]{1,0:T(8,128)S(1)}, f32[128,2304]{1,0:T(8,128)}, u32[]{:S(2)}) copy-start(f32[128,2304]{1,0:T(8,128)} %copy-done.1) | copy-start | bytes 3538948
Sparse Core Ops, SparseCore 0:
  11.1 65.2 all-gather.11
  79.4 62.4 all-gather.15
  144.1 27.9 all-gather.13
  175.0 81.5 all-gather.19
  258.6 29.1 all-gather.17
  290.7 81.4 all-gather.21
  374.0 60.1 all-gather.25
  436.4 52.1 all-gather.23
  490.4 60.3 all-gather.27
  552.5 61.9 all-gather.29
  625.4 52.8 reduce-scatter.15
  684.3 52.5 all-gather.31
  772.5 51.2 reduce-scatter.17
  849.5 33.5 reduce-scatter.35
  885.2 34.5 reduce-scatter.33
  922.6 63.2 reduce-scatter.31
  988.8 61.9 reduce-scatter.29
  1053.7 61.9 reduce-scatter.27
  1122.2 133.7 reduce-scatter.23
  1263.3 134.5 reduce-scatter.21
  1404.9 206.3 reduce-scatter.25
  1618.3 205.6 reduce-scatter.19
where the time goes:
time: 1840 us; the launch traced here: 1830 us
  waiting for transfers between devices  1480 us (80%)
  matrix products  195 us (11%)
  blocking collectives  80.7 us (4%)
  other arithmetic  32.7 us (2%)
  local copies, waits for them, and re-layouts  28 us (2%)
    reduce_scatter x1, waiting for transfers between devices, body(): lax.psum_scatter(output_term, ('seq', 'ctx'), scatter_dimension=0, tiled=...  213 us
    reduce_scatter x1, waiting for transfers between devices, body(): lax.psum_scatter(query_term, ('seq', 'ctx'), scatter_dimension=0, tiled=T...  213 us
    reduce_scatter x1, waiting for transfers between devices, body(): lax.psum_scatter(key_term, ('seq', 'ctx'), scatter_dimension=0, tiled=True)  142 us
    reduce_scatter x1, waiting for transfers between devices, body(): lax.psum_scatter(value_term, ('seq', 'ctx'), scatter_dimension=0, tiled=T...  84.9 us
    unnamed x2, blocking collectives  80.7 us
    all_gather x1, waiting for transfers between devices, body(): lax.all_gather(w_query, ('seq', 'ctx'), axis=0, tiled=True)  80 us
    all_gather x1, waiting for transfers between devices, body(): lax.all_gather(w_output, ('seq', 'ctx'), axis=0, tiled=True)  75.4 us
    reduce_scatter x1, waiting for transfers between devices, body(): lax.psum_scatter(gate_term.astype(jnp.bfloat16), 'seq', scatter_dimension...  61.9 us
  transfers between devices with their start and end apart: 22, of which 21 were waited for; matrix products, arithmetic and copies ran while one was open for 10% of the time, Pallas kernels for 0%

commit v1 on v0

--- a/solution.py
+++ b/solution.py
@@ -1,3 +1,5 @@
+from functools import partial
+
 import jax
 import jax.numpy as jnp
 from jax import lax
@@ -166,7 +168,7 @@
     return (query_acc.reshape(row_count, QUERY_HEAD_COUNT * HEAD_FEATURES), key_acc, value_acc)
 
 
-def body(
+def context_body(
     tokens,
     w_query,
     w_key,
@@ -344,6 +346,296 @@
     )
 
 
+CORES = 2
+GELU_IN = 0.7978845608
+GELU_CUBE = 0.044715
+
+
+def rms_parts(signal):
+    scale = lax.rsqrt(jnp.mean(signal * signal, axis=-1, keepdims=True) + epsilon)
+    return scale, signal * scale
+
+
+def rms_back(scale, unit, weight, upstream):
+    weighted = upstream * weight
+    mean = jnp.mean(weighted * unit, axis=-1, keepdims=True)
+    return scale * (weighted - unit * mean), jnp.sum(upstream * unit, axis=0)
+
+
+def dot_nn(left, right):
+    return jnp.dot(left, right, preferred_element_type=jnp.float32)
+
+
+def dot_nt(left, right):
+    return jnp.einsum("ab,cb->ac", left, right, preferred_element_type=jnp.float32)
+
+
+def dot_tn(left, right):
+    return jnp.einsum("ab,ac->bc", left, right, preferred_element_type=jnp.float32)
+
+
+class Moves:
+    def __init__(self, n_seq, n_ctx):
+        self.n_seq, self.n_ctx = n_seq, n_ctx
+        self.line = n_ctx // CORES
+        self.seq = lax.axis_index("seq")
+        ctx = lax.axis_index("ctx")
+        self.plane = ctx // CORES
+        self.core = ctx % CORES
+
+    def _send(self, value, move):
+        pairs = []
+        for s in range(self.n_seq):
+            for c in range(self.n_ctx):
+                t = move(s, c // CORES, c % CORES)
+                pairs.append((s * self.n_ctx + c, t[0] * self.n_ctx + t[1] * CORES + t[2]))
+        return lax.ppermute(value, ("seq", "ctx"), pairs)
+
+    def across(self, value, mask):
+        return self._send(value, lambda s, z, k: (s ^ mask, z, k))
+
+    def along(self, value, step):
+        return self._send(value, lambda s, z, k: (s, (z + step) % self.line, k))
+
+    def swap(self, value):
+        return self._send(value, lambda s, z, k: (s, z, k ^ 1))
+
+    def gather_seq(self, block):
+        half = block.shape[0] // 2
+        by_x = self.across(block, 1)
+        by_y = self.across(block, 2)
+        far_low = self.across(by_x[:half], 2)
+        far_high = self.across(by_y[half:], 1)
+        out = jnp.zeros((self.n_seq,) + block.shape, block.dtype)
+        out = lax.dynamic_update_index_in_dim(out, block, self.seq, 0)
+        out = lax.dynamic_update_index_in_dim(out, by_x, self.seq ^ 1, 0)
+        out = lax.dynamic_update_index_in_dim(out, by_y, self.seq ^ 2, 0)
+        far = jnp.concatenate([far_low, far_high], axis=0)
+        return lax.dynamic_update_index_in_dim(out, far, self.seq ^ 3, 0)
+
+    def scatter_seq(self, parts):
+        half = parts.shape[1] // 2
+        take = lambda mask, low: lax.dynamic_index_in_dim(parts, self.seq ^ mask, 0, False)[
+            slice(0, half) if low else slice(half, None)
+        ]
+        low_in = self.across(jnp.stack([take(1, True), take(3, True)]), 1)
+        high_in = self.across(jnp.stack([take(2, False), take(3, False)]), 2)
+        wide = lambda v: v.astype(jnp.float32)
+        low_on = (wide(take(2, True)) + wide(low_in[1])).astype(jnp.bfloat16)
+        high_on = (wide(take(1, False)) + wide(high_in[1])).astype(jnp.bfloat16)
+        low_far = self.across(low_on, 2)
+        high_far = self.across(high_on, 1)
+        low = wide(take(0, True)) + wide(low_in[0]) + wide(low_far)
+        high = wide(take(0, False)) + wide(high_in[0]) + wide(high_far)
+        return jnp.concatenate([low, high], axis=0)
+
+    def exchange_line(self, blocks):
+        out = jnp.zeros_like(blocks)
+        own = lax.dynamic_index_in_dim(blocks, self.plane, 0, False)
+        out = lax.dynamic_update_index_in_dim(out, own, self.plane, 0)
+        for step in range(1, self.line):
+            sent = lax.dynamic_index_in_dim(blocks, (self.plane + step) % self.line, 0, False)
+            got = self.along(sent, step)
+            out = lax.dynamic_update_index_in_dim(out, got, (self.plane - step) % self.line, 0)
+        return out
+
+    def exchange_cores(self, blocks):
+        own = lax.dynamic_index_in_dim(blocks, self.core, 0, False)
+        got = self.swap(lax.dynamic_index_in_dim(blocks, 1 - self.core, 0, False))
+        first = self.core == 0
+        return jnp.stack([jnp.where(first, own, got), jnp.where(first, got, own)])
+
+
+def head_body(
+    tokens,
+    w_query,
+    w_key,
+    w_value,
+    w_output,
+    w_gate,
+    w_up,
+    w_down,
+    first_gain,
+    second_gain,
+    third_gain,
+    fourth_gain,
+    block_pairs,
+    cotangent,
+    n_seq,
+    n_ctx,
+):
+    moves = Moves(n_seq, n_ctx)
+    line = moves.line
+    core_zero = moves.core == 0
+    width = tokens.shape[1]
+    row_count = tokens.shape[0]
+    length_total = row_count * n_ctx
+    feat_rows = w_query.shape[0]
+    out_rows = w_output.shape[0]
+    feats = HEAD_FEATURES
+    score_scale = feats ** (-0.5)
+    pad = 128
+    block_size = row_count // 2
+    offsets = jnp.arange(block_size, dtype=jnp.int32)
+    pos = (block_pairs[:, :, None] * block_size + offsets[None, None, :]).reshape(-1)
+
+    tokens_all = lax.all_gather(tokens, "ctx", axis=0, tiled=True)
+    gains_in = jnp.stack([first_gain, second_gain, third_gain, fourth_gain], axis=1)
+    gains_in = jnp.pad(gains_in, ((0, 0), (0, pad - 4)))
+    by_head = jnp.concatenate(
+        [
+            w_query.reshape(feat_rows, line, CORES, feats),
+            jnp.stack(
+                [
+                    w_key.reshape(feat_rows, line, feats),
+                    w_value.reshape(feat_rows, line, feats),
+                ],
+                axis=2,
+            ),
+            jnp.broadcast_to(gains_in[:, None, None, :], (feat_rows, line, CORES, pad)),
+        ],
+        axis=3,
+    ).transpose(2, 1, 0, 3)
+    by_plane = moves.exchange_cores(by_head).transpose(1, 0, 2, 3)
+    own_columns = moves.exchange_line(by_plane).reshape(n_ctx * feat_rows, 2 * feats + pad)
+    columns = moves.gather_seq(own_columns).reshape(width, 2 * feats + pad)
+    w_qkv = columns[:, : 2 * feats]
+    gains = columns[:, 2 * feats : 2 * feats + 8].astype(jnp.float32).T
+    gain_one, gain_two, gain_three, gain_four = gains[0], gains[1], gains[2], gains[3]
+
+    out_seq = jnp.zeros((n_seq,) + w_output.shape, w_output.dtype)
+    out_seq = lax.dynamic_update_index_in_dim(out_seq, w_output, moves.seq, 0)
+    for mask in (1, 2, 3):
+        out_seq = lax.dynamic_update_index_in_dim(
+            out_seq, moves.across(w_output, mask), moves.seq ^ mask, 0
+        )
+    out_line = moves.exchange_line(out_seq).reshape(CORES, CORES, out_rows, width)
+    w_out = moves.exchange_cores(out_line).transpose(1, 0, 2, 3).reshape(feats, width)
+
+    gate_w = moves.gather_seq(w_gate).reshape(width, -1)
+    up_w = moves.gather_seq(w_up).reshape(width, -1)
+    down_w = moves.gather_seq(w_down.T).reshape(width, -1)
+
+    wide_all = tokens_all.astype(jnp.float32)
+    normed = (rms_parts(wide_all)[1] * gain_one).astype(jnp.bfloat16)
+    qkv = dot_nn(normed, w_qkv)
+    query_low = rotate(qkv[:, :feats], pos, feats).astype(jnp.bfloat16)
+    pair = qkv[:, feats:]
+    pair_low = jnp.where(core_zero, rotate(pair, pos, feats), pair).astype(jnp.bfloat16)
+    pair_other = moves.swap(pair_low)
+    key_low = jnp.where(core_zero, pair_low, pair_other)
+    value_low = jnp.where(core_zero, pair_other, pair_low)
+    allowed = pos[None, :] <= pos[:, None]
+    bent = jnp.tanh(dot_nt(query_low, key_low) * (score_scale / softcap))
+    weight = jnp.where(allowed, jnp.exp(softcap * bent), 0.0)
+    probs = weight / jnp.sum(weight, axis=-1, keepdims=True)
+    prob_low = probs.astype(jnp.bfloat16)
+    mixed_low = dot_nn(prob_low, value_low).astype(jnp.bfloat16)
+    branch = lax.psum_scatter(
+        dot_nn(mixed_low, w_out).astype(jnp.bfloat16), "ctx", scatter_dimension=0, tiled=True
+    ).astype(jnp.float32)
+
+    residual_in = tokens.astype(jnp.float32)
+    scale_two, unit_two = rms_parts(branch)
+    residual = residual_in + unit_two * gain_two
+    scale_three, unit_three = rms_parts(residual)
+    feed_input = (unit_three * gain_three).astype(jnp.bfloat16)
+    feed_all = lax.all_gather(feed_input, "ctx", axis=0, tiled=True)
+    gate_pre = dot_nn(feed_all, gate_w)
+    up_pre = dot_nn(feed_all, up_w)
+    bend = jnp.tanh(GELU_IN * (gate_pre + GELU_CUBE * gate_pre * gate_pre * gate_pre))
+    gelu = 0.5 * gate_pre * (1.0 + bend)
+    hidden = (gelu * up_pre).astype(jnp.bfloat16)
+    feed_out = lax.psum_scatter(
+        dot_nt(hidden, down_w).astype(jnp.bfloat16), "ctx", scatter_dimension=0, tiled=True
+    ).astype(jnp.float32)
+    scale_four, unit_four = rms_parts(feed_out)
+    layer_out = (residual + unit_four * gain_four).astype(jnp.bfloat16)
+
+    upstream = cotangent.astype(jnp.float32)
+    feed_grad, fourth_term = rms_back(scale_four, unit_four, gain_four, upstream)
+    feed_low = feed_grad.astype(jnp.bfloat16)
+    grad_all = lax.all_gather(feed_low, "ctx", axis=0, tiled=True)
+    hidden_grad = dot_nn(grad_all, down_w)
+    slope = 0.5 * (1.0 + bend) + 0.5 * gate_pre * (1.0 - bend * bend) * GELU_IN * (
+        1.0 + 3.0 * GELU_CUBE * gate_pre * gate_pre
+    )
+    gate_low = (hidden_grad * up_pre * slope).astype(jnp.bfloat16)
+    up_low = (hidden_grad * gelu).astype(jnp.bfloat16)
+    input_part = dot_nt(gate_low, gate_w) + dot_nt(up_low, up_w)
+    feed_input_grad = lax.psum_scatter(
+        input_part.astype(jnp.bfloat16), "ctx", scatter_dimension=0, tiled=True
+    ).astype(jnp.float32)
+    shape = (n_seq, width // n_seq, gate_low.shape[1])
+    down_sum = moves.scatter_seq(dot_tn(grad_all, hidden).astype(jnp.bfloat16).reshape(shape)).T
+    gate_sum = moves.scatter_seq(dot_tn(feed_all, gate_low).astype(jnp.bfloat16).reshape(shape))
+    up_sum = moves.scatter_seq(dot_tn(feed_all, up_low).astype(jnp.bfloat16).reshape(shape))
+
+    middle_grad, third_term = rms_back(scale_three, unit_three, gain_three, feed_input_grad)
+    residual_grad = upstream + middle_grad
+    branch_grad, second_term = rms_back(scale_two, unit_two, gain_two, residual_grad)
+    branch_low = branch_grad.astype(jnp.bfloat16)
+
+    branch_all = lax.all_gather(branch_low, "ctx", axis=0, tiled=True)
+    output_term = dot_tn(mixed_low, branch_all).astype(jnp.bfloat16)
+    mixed_grad = dot_nt(branch_all, w_out).astype(jnp.bfloat16)
+    value_part = dot_tn(prob_low, mixed_grad)
+    prob_grad = dot_nt(mixed_grad, value_low)
+    delta = jnp.sum(probs * prob_grad, axis=-1, keepdims=True)
+    raw_low = (probs * (prob_grad - delta) * (1.0 - bent * bent)).astype(jnp.bfloat16)
+    query_sum = dot_nn(raw_low, key_low) * score_scale
+    key_part = dot_tn(raw_low, query_low) * score_scale
+    pair_sum = jnp.where(core_zero, key_part, value_part) + moves.swap(
+        jnp.where(core_zero, value_part, key_part)
+    )
+    query_grad = rotate(query_sum, -pos, feats)
+    pair_grad = jnp.where(core_zero, rotate(pair_sum, -pos, feats), pair_sum)
+    qkv_grad = jnp.concatenate([query_grad, pair_grad], axis=1).astype(jnp.bfloat16)
+    normed_grad = lax.psum_scatter(
+        dot_nt(qkv_grad, w_qkv).astype(jnp.bfloat16), "ctx", scatter_dimension=0, tiled=True
+    ).astype(jnp.float32)
+    scale_one, unit_one = rms_parts(residual_in)
+    input_grad, _ = rms_back(scale_one, unit_one, gain_one, normed_grad)
+    grad_tokens = (residual_grad + input_grad).astype(jnp.bfloat16)
+
+    terms = jnp.stack([second_term, third_term, fourth_term])
+    terms = jnp.pad(terms, ((0, pad - 3), (0, 0))).T
+    qkv_term = jnp.concatenate([dot_tn(normed, qkv_grad), terms], axis=1).astype(jnp.bfloat16)
+    own_term = moves.scatter_seq(qkv_term.reshape(n_seq, width // n_seq, -1)).astype(jnp.bfloat16)
+    own_term = own_term.reshape(line, CORES, feat_rows, 2 * feats + pad)
+    own_term = moves.exchange_line(own_term).transpose(1, 0, 2, 3)
+    own_term = moves.exchange_cores(own_term).transpose(2, 1, 0, 3).astype(jnp.float32)
+    grad_query = own_term[..., :feats].reshape(feat_rows, -1)
+    grad_key = own_term[:, :, 0, feats : 2 * feats].reshape(feat_rows, -1)
+    grad_value = own_term[:, :, 1, feats : 2 * feats].reshape(feat_rows, -1)
+    grad_gains = jnp.sum(own_term[..., 2 * feats : 2 * feats + 3], axis=(1, 2))
+    grad_first = (
+        jnp.sum(w_query.astype(jnp.float32) * grad_query, axis=1)
+        + jnp.sum(w_key.astype(jnp.float32) * grad_key, axis=1)
+        + jnp.sum(w_value.astype(jnp.float32) * grad_value, axis=1)
+    ) / first_gain.astype(jnp.float32)
+
+    out_term = output_term.reshape(CORES, CORES, out_rows, width).transpose(1, 0, 2, 3)
+    out_term = moves.exchange_cores(out_term).reshape(line, out_rows, width)
+    out_term = moves.exchange_line(out_term)
+    grad_output = moves.scatter_seq(out_term)
+    return (
+        layer_out,
+        grad_tokens,
+        grad_query,
+        grad_key,
+        grad_value,
+        grad_output,
+        gate_sum,
+        up_sum,
+        down_sum,
+        grad_first,
+        grad_gains[:, 0],
+        grad_gains[:, 1],
+        grad_gains[:, 2],
+    )
+
+
 def solution(mesh):
     placed = (
         P(("seq", "ctx"), None),
@@ -361,6 +653,11 @@
         P(),
         P(("seq", "ctx"), None),
     )
+    n_seq, n_ctx = mesh.shape["seq"], mesh.shape["ctx"]
+    if n_ctx == QUERY_HEAD_COUNT and n_seq == 4:
+        body = partial(head_body, n_seq=n_seq, n_ctx=n_ctx)
+    else:
+        body = context_body
     return jax.shard_map(
         body,
         mesh=mesh,

time: 1840 us -> 835 us (0.45)
  waiting for transfers between devices: 1480 us -> 471 us
  starting transfers between devices: 2.75 us -> 87.5 us
  blocking collectives: 80.7 us -> 0 us
  matrix products: 195 us -> 124 us
  other arithmetic: 32.7 us -> 74.9 us
  local copies, waits for them, and re-layouts: 28 us -> 55.8 us
    reduce_scatter x9 -> x4, waiting for transfers between devices: 910 us -> 136 us  [the longest x1 56.8 us: head_body(): lax.psum_scatter(dot_nt(hidden, down_w).astype(jnp.bfloat16), 'ctx', scat...]
    all_gather x11 -> x4, waiting for transfers between devices: 547 us -> 52.7 us  [the longest x1 52.7 us: head_body(): grad_all = lax.all_gather(feed_low, 'ctx', axis=0, tiled=True)]
    ppermute x0 -> x57, waiting for transfers between devices: none -> 282 us  [_send(): return lax.ppermute(value, ('seq', 'ctx'), pairs)]
    ppermute x0 -> x57, starting transfers between devices: none -> 87.2 us  [_send(): return lax.ppermute(value, ('seq', 'ctx'), pairs)]
    unnamed x2 -> x0, blocking collectives: 80.7 us -> none
    dot_general x28 -> x21, matrix products: 195 us -> 124 us  [the longest x7 45.7 us: dot_nn(): return jnp.dot(left, right, preferred_element_type=jnp.float32)]
  transfers between devices with their start and end apart: 22 -> 65, of which waited for: 21 -> 30; matrix products, arithmetic and copies ran while one was open for 10% -> 17% of each run, Pallas kernels for 0% -> 0%
where the time goes in v1:
time: 835 us; the launch traced here: 829 us
  waiting for transfers between devices  471 us (56%)
  matrix products  124 us (15%)
  starting transfers between devices  87.5 us (10%)
  other arithmetic  74.9 us (9%)
  local copies, waits for them, and re-layouts  55.8 us (7%)
  between operations  16 us (2%)
    ppermute x57, waiting for transfers between devices, _send(): return lax.ppermute(value, ('seq', 'ctx'), pairs)  282 us
    ppermute x57, starting transfers between devices, _send(): return lax.ppermute(value, ('seq', 'ctx'), pairs)  87.2 us
    reduce_scatter x1, waiting for transfers between devices, head_body(): lax.psum_scatter(dot_nt(hidden, down_w).astype(jnp.bfloat16), 'ctx', scat...  56.8 us
    reduce_scatter x1, waiting for transfers between devices, head_body(): lax.psum_scatter(dot_nn(mixed_low, w_out).astype(jnp.bfloat16), 'ctx', sc...  56.2 us
    all_gather x1, waiting for transfers between devices, head_body(): grad_all = lax.all_gather(feed_low, 'ctx', axis=0, tiled=True)  52.7 us
    dot_general x7, matrix products, dot_nn(): return jnp.dot(left, right, preferred_element_type=jnp.float32)  45.7 us
    dot_general x7, matrix products, dot_nt(): jnp.einsum('ab,cb->ac', left, right, preferred_element_type=jnp.float32)  42.9 us
    dot_general x7, matrix products, dot_tn(): jnp.einsum('ab,ac->bc', left, right, preferred_element_type=jnp.float32)  35.5 us
  transfers between devices with their start and end apart: 65, of which 30 were waited for; matrix products, arithmetic and copies ran while one was open for 17% of the time, Pallas kernels for 0%

profile of v1, /device:TPU:3, one launch (start us, length us, event | category | flops | bytes accessed | tf_op | source)
XLA Modules:
  0.0 829.1 jit_solution(14581186103495987552)
XLA Ops:
  27.2 2.3 collective-permute-start.14
  31.9 8.2 collective-permute-done.12
  40.1 24.9 %collective-permute-done.13 = bf16[64,2304]{1,0:T(8,128)(2,1)S(1)} collective-permute-done((bf16[64,2304]{1,0:T(8,128)(2,1)S(1)}, bf16[64,2304]{1,0:T(8,128)(2,1)S(1)}, u32[]{:S(2)}, u32[]{:S(2)}) %collective-permute-start.13) | collective-permute-done | bytes 294944 | tf_op jit(solution)/shard_map/ppermute | solution.py:392
  65.2 5.8 collective-permute-start.15
  71.0 29.4 %collective-permute-done.2 = bf16[2,72,640]{2,1,0:T(8,128)(2,1)S(1)} collective-permute-done((bf16[2,72,640]{2,1,0:T(8,128)(2,1)S(1)}, bf16[2,72,640]{2,1,0:T(8,128)(2,1)S(1)}, u32[]{:S(2)}, u32[]{:S(2)}) %collective-permute-start.2) | collective-permute-done | bytes 184352 | tf_op jit(solution)/shard_map/ppermute | solution.py:392
  103.2 14.6 %collective-permute-done.4 = bf16[576,640]{1,0:T(8,128)(2,1)S(1)} collective-permute-done((bf16[576,640]{1,0:T(8,128)(2,1)S(1)}, bf16[576,640]{1,0:T(8,128)(2,1)S(1)}, u32[]{:S(2)}, u32[]{:S(2)}) %collective-permute-start.4) | collective-permute-done | bytes 737312 | tf_op jit(solution)/shard_map/ppermute | solution.py:392
  119.8 6.7 collective-permute-done.6
  127.8 2.8 slice_reduce_fusion
  130.6 3.5 fusion
  134.3 2.9 fusion.13
  137.9 2.4 fusion.105
  140.5 2.8 collective-permute-start.8
  143.5 2.3 fusion.102
  149.3 3.6 convolution_convert_fusion.5
  152.9 56.2 %reduce-scatter.5.cloned.1.call-done = bf16[128,2304]{1,0:T(8,128)(2,1)} async-done(((bf16[1024,2304]{1,0:T(8,128)(2,1)}), bf16[128,2304]{1,0:T(8,128)(2,1)}) %reduce-scatter.5.cloned.1.call-update) | async-done | bytes 589840 | tf_op jit(solution)/shard_map/reduce_scatter | solution.py:534
  216.6 2.8 broadcast.274.clone
  220.5 2.8 broadcast.274.clone.1
  224.6 2.7 broadcast.274.clone.2
  228.5 13.0 %collective-permute-done.16 = bf16[576,1152]{1,0:T(8,128)(2,1)S(1)} collective-permute-done((bf16[576,1152]{1,0:T(8,128)(2,1)}, bf16[576,1152]{1,0:T(8,128)(2,1)S(1)}, u32[]{:S(2)}, u32[]{:S(2)}) %collective-permute-start.16) | collective-permute-done | bytes 1327136 | tf_op jit(solution)/shard_map/ppermute | solution.py:392
  245.5 24.3 %collective-permute-done.20 = bf16[576,1152]{1,0:T(8,128)(2,1)S(1)} collective-permute-done((bf16[576,1152]{1,0:T(8,128)(2,1)}, bf16[576,1152]{1,0:T(8,128)(2,1)S(1)}, u32[]{:S(2)}, u32[]{:S(2)}) %collective-permute-start.20) | collective-permute-done | bytes 1327136 | tf_op jit(solution)/shard_map/ppermute | solution.py:392
  273.8 24.4 %collective-permute-done.24 = bf16[576,1152]{1,0:T(8,128)(2,1)S(1)} collective-permute-done((bf16[576,1152]{1,0:T(8,128)(2,1)}, bf16[576,1152]{1,0:T(8,128)(2,1)S(1)}, u32[]{:S(2)}, u32[]{:S(2)}) %collective-permute-start.24) | collective-permute-done | bytes 1327136 | tf_op jit(solution)/shard_map/ppermute | solution.py:392
  301.1 11.4 %collective-permute-done.18 = bf16[288,1152]{1,0:T(8,128)(2,1)S(1)} collective-permute-done((bf16[288,1152]{1,0:T(8,128)(2,1)S(1)}, bf16[288,1152]{1,0:T(8,128)(2,1)S(1)}, u32[]{:S(2)}, u32[]{:S(2)}) %collective-permute-start.18) | collective-permute-done | bytes 663584 | tf_op jit(solution)/shard_map/ppermute | solution.py:392
  316.0 10.7 %collective-permute-done.22 = bf16[288,1152]{1,0:T(8,128)(2,1)S(1)} collective-permute-done((bf16[288,1152]{1,0:T(8,128)(2,1)S(1)}, bf16[288,1152]{1,0:T(8,128)(2,1)S(1)}, u32[]{:S(2)}, u32[]{:S(2)}) %collective-permute-start.22) | collective-permute-done | bytes 663584 | tf_op jit(solution)/shard_map/ppermute | solution.py:392
  327.9 13.0 %collective-permute-done.26 = bf16[288,1152]{1,0:T(8,128)(2,1)S(1)} collective-permute-done((bf16[288,1152]{1,0:T(8,128)(2,1)S(1)}, bf16[288,1152]{1,0:T(8,128)(2,1)S(1)}, u32[]{:S(2)}, u32[]{:S(2)}) %collective-permute-start.26) | collective-permute-done | bytes 663584 | tf_op jit(solution)/shard_map/ppermute | solution.py:392
  342.1 10.0 %fusion.141 = f32[1024,1152]{1,0:T(8,128)S(1)} fusion(bf16[1024,2304]{1,0:T(8,128)(2,1)} %all-gather.7.cloned.1.call-done, bf16[2304,1152]{1,0:T(8,128)(2,1)} %bitcast.50), kind=kOutput, calls=%fused_computation.348 | convolution fusion | flops 5435817984 | bytes 14745600 | tf_op jit(solution)/shard_map/dot_general | solution.py:366
  352.2 12.5 %multiply_convert_fusion.1 = (bf16[1024,1152]{1,0:T(8,128)(2,1)S(1)}, f32[1024,1152]{1,0:T(8,128)}) fusion(f32[1024,1152]{1,0:T(8,128)S(1)} %fusion.141, bf16[1024,2304]{1,0:T(8,128)(2,1)S(1)} %copy-done.60, bf16[2304,1152]{1,0:T(8,128)(2,1)} %bitcast.55), kind=kOutput, calls=%fused_computation.26 | convolution fusion | flops 5447614464 | bytes 21823488 | tf_op jit(solution)/shard_map/dot_general | solution.py:366
  366.1 10.4 %convolution_convert_fusion.4 = bf16[1024,2304]{1,0:T(8,128)(2,1)} fusion(bf16[1024,1152]{1,0:T(8,128)(2,1)S(1)} %get-tuple-element.112, bf16[2304,1152]{1,0:T(8,128)(2,1)} %bitcast.61), kind=kOutput, calls=%fused_computation.12 | convolution fusion | flops 5438177280 | bytes 12386304 | tf_op jit(solution)/shard_map/ab,cb->ac/dot_general | solution.py:370
  376.6 56.8 %reduce-scatter.7.cloned.1.call-done = bf16[128,2304]{1,0:T(8,128)(2,1)} async-done(((bf16[1024,2304]{1,0:T(8,128)(2,1)}), bf16[128,2304]{1,0:T(8,128)(2,1)}) %reduce-scatter.7.cloned.1.call-update) | async-done | bytes 589840 | tf_op jit(solution)/shard_map/reduce_scatter | solution.py:549
  438.2 52.7 %all-gather.9.cloned.1.call-done = bf16[1024,2304]{1,0:T(8,128)(2,1)} async-done(((bf16[128,2304]{1,0:T(8,128)(2,1)}), bf16[1024,2304]{1,0:T(8,128)(2,1)}) %all-gather.9.cloned.1.call-update) | async-done | bytes 4718608 | tf_op jit(solution)/shard_map/all_gather | solution.py:558
  490.9 14.3 %fusion.9 = (bf16[1024,1152]{1,0:T(8,128)(2,1)S(1)}, bf16[1024,1152]{1,0:T(8,128)(2,1)S(1)}) fusion(f32[1024,1152]{1,0:T(8,128)} %copy-done.61, f32[1024,1152]{1,0:T(8,128)} %get-tuple-element.113, bf16[1024,2304]{1,0:T(8,128)(2,1)} %all-gather.9.cloned.1.call-done, bf16[2304,1152]{1,0:T(8,128)(2,1)} %bitcast.61), kind=kOutput, calls=%fused_computation.24 | convolution fusion | flops 5462949888 | bytes 24182784 | tf_op jit(solution)/shard_map/dot_general | solution.py:366
  505.3 10.5 %fusion.142 = f32[1024,2304]{1,0:T(8,128)S(1)} fusion(bf16[1024,1152]{1,0:T(8,128)(2,1)S(1)} %get-tuple-element.29, bf16[2304,1152]{1,0:T(8,128)(2,1)} %bitcast.55), kind=kOutput, calls=%fused_computation.349 | convolution fusion | flops 5435817984 | bytes 17104896 | tf_op jit(solution)/shard_map/ab,cb->ac/dot_general | solution.py:370
  515.8 10.6 %add_convert_fusion = bf16[1024,2304]{1,0:T(8,128)(2,1)} fusion(f32[1024,2304]{1,0:T(8,128)S(1)} %fusion.142, bf16[1024,1152]{1,0:T(8,128)(2,1)S(1)} %get-tuple-element.28, bf16[2304,1152]{1,0:T(8,128)(2,1)} %bitcast.50), kind=kOutput, calls=%fused_computation.8 | convolution fusion | flops 5440536576 | bytes 21823488 | tf_op jit(solution)/shard_map/ab,cb->ac/dot_general | solution.py:370
  526.5 9.1 %convolution_convert_fusion.1 = bf16[2304,1152]{1,0:T(8,128)(2,1)S(1)} fusion(bf16[1024,2304]{1,0:T(8,128)(2,1)} %all-gather.7.cloned.1.call-done, bf16[1024,1152]{1,0:T(8,128)(2,1)} %copy-done.64), kind=kOutput, calls=%fused_computation.3 | convolution fusion | flops 5438472192 | bytes 12386304 | tf_op jit(solution)/shard_map/ab,ac->bc/dot_general | solution.py:374
  541.9 8.2 convolution_convert_fusion
  554.4 23.4 %reduce-scatter.9.cloned.1.call-done = bf16[128,2304]{1,0:T(8,128)(2,1)} async-done(((bf16[1024,2304]{1,0:T(8,128)(2,1)}), bf16[128,2304]{1,0:T(8,128)(2,1)}) %reduce-scatter.9.cloned.1.call-update) | async-done | bytes 589840 | tf_op jit(solution)/shard_map/reduce_scatter | solution.py:566
  577.8 2.5 fusion.52
  580.3 3.3 fusion.46
  586.7 8.6 %convolution_convert_fusion.2 = bf16[2304,1152]{1,0:T(8,128)(2,1)S(1)} fusion(bf16[1024,2304]{1,0:T(8,128)(2,1)} %all-gather.7.cloned.1.call-done, bf16[1024,1152]{1,0:T(8,128)(2,1)S(1)} %copy-done.63), kind=kOutput, calls=%fused_computation.4 | convolution fusion | flops 5438472192 | bytes 12386304 | tf_op jit(solution)/shard_map/ab,ac->bc/dot_general | solution.py:374
  600.3 3.1 fusion.90
  604.1 10.2 %collective-permute-done.53 = bf16[2,288,1152]{2,1,0:T(8,128)(2,1)S(1)} collective-permute-done((bf16[2,288,1152]{2,1,0:T(8,128)(2,1)S(1)}, bf16[2,288,1152]{2,1,0:T(8,128)(2,1)S(1)}, u32[]{:S(2)}, u32[]{:S(2)}) %collective-permute-start.53) | collective-permute-done | bytes 1327136 | tf_op jit(solution)/shard_map/ppermute | solution.py:392
  614.2 3.3 fusion.92
  618.8 6.8 collective-permute-done.47
  627.6 15.1 %collective-permute-done.45 = bf16[2,288,1152]{2,1,0:T(8,128)(2,1)} collective-permute-done((bf16[2,288,1152]{2,1,0:T(8,128)(2,1)S(1)}, bf16[2,288,1152]{2,1,0:T(8,128)(2,1)}, u32[]{:S(2)}, u32[]{:S(2)}) %collective-permute-start.45) | collective-permute-done | bytes 1327136 | tf_op jit(solution)/shard_map/ppermute | solution.py:392
  646.2 10.7 %collective-permute-done.52 = bf16[288,1152]{1,0:T(8,128)(2,1)} collective-permute-done((bf16[288,1152]{1,0:T(8,128)(2,1)}, bf16[288,1152]{1,0:T(8,128)(2,1)}, u32[]{:S(2)}, u32[]{:S(2)}) %collective-permute-start.52) | collective-permute-done | bytes 663584 | tf_op jit(solution)/shard_map/ppermute | solution.py:392
  656.9 14.2 %collective-permute-done.56 = bf16[288,1152]{1,0:T(8,128)(2,1)} collective-permute-done((bf16[288,1152]{1,0:T(8,128)(2,1)}, bf16[288,1152]{1,0:T(8,128)(2,1)}, u32[]{:S(2)}, u32[]{:S(2)}) %collective-permute-start.56) | collective-permute-done | bytes 663584 | tf_op jit(solution)/shard_map/ppermute | solution.py:392
  671.1 4.1 bitcast_add_fusion.1
  678.6 6.6 collective-permute-done.48
  690.7 3.9 convolution_convert_fusion.8
  696.4 2.6 multiply_convert_fusion.2
  701.5 3.8 collective-permute-start.28
  707.8 2.3 fusion.108
  716.7 2.3 fusion.111
  720.9 4.3 convolution_convert_fusion.3
  726.2 10.1 %collective-permute-done.39 = bf16[64,2304]{1,0:T(8,128)(2,1)} collective-permute-done((bf16[64,2304]{1,0:T(8,128)(2,1)}, bf16[64,2304]{1,0:T(8,128)(2,1)}, u32[]{:S(2)}, u32[]{:S(2)}) %collective-permute-start.39) | collective-permute-done | bytes 294944 | tf_op jit(solution)/shard_map/ppermute | solution.py:392
  737.4 5.7 convolution_convert_fusion.6
  746.4 14.5 %collective-permute-done.31 = bf16[2,288,640]{2,1,0:T(8,128)(2,1)S(1)} collective-permute-done((bf16[2,288,640]{2,1,0:T(8,128)(2,1)S(1)}, bf16[2,288,640]{2,1,0:T(8,128)(2,1)S(1)}, u32[]{:S(2)}, u32[]{:S(2)}) %collective-permute-start.31) | collective-permute-done | bytes 737312 | tf_op jit(solution)/shard_map/ppermute | solution.py:392
  764.4 5.2 collective-permute-done.32
  770.8 12.9 %collective-permute-start.33 = (bf16[2,72,640]{2,1,0:T(8,128)(2,1)S(1)}, bf16[2,72,640]{2,1,0:T(8,128)(2,1)S(1)}, u32[]{:S(2)}, u32[]{:S(2)}) collective-permute-start(bf16[2,72,640]{2,1,0:T(8,128)(2,1)S(1)} %get-tuple-element.97), channel_id=1, source_target_pairs={{0,2},{1,3},{2,4},{3,5},{4,6},{5,7},{6,0},{7,1},{8,10},{9,11},{10,... | collective-permute-start | bytes 552968 | tf_op jit(solution)/shard_map/ppermute | solution.py:392
  787.5 4.2 collective-permute-start.34
  791.7 5.4 collective-permute-start.35
  797.2 4.0 collective-permute-done.35
  801.3 6.1 collective-permute-start.36
  812.1 2.3 reshape.534
  819.7 2.3 fusion.39
  (398 shorter events, 140.4 us)
Async XLA Ops:
  7.2 123.4 %all-gather.5.cloned.1.call-start = ((), (), s32[]{:S(2)}) async-start(), calls=%async_computation.4 | async-start | bytes 5308416 | tf_op jit(solution)/shard_map/all_gather | solution.py:482
  7.2 13.7 %collective-permute-start.9 = (bf16[64,2304]{1,0:T(8,128)(2,1)}, bf16[64,2304]{1,0:T(8,128)(2,1)}, u32[]{:S(2)}, u32[]{:S(2)}) collective-permute-start(bf16[64,2304]{1,0:T(8,128)(2,1)} %param.18), channel_id=1, source_target_pairs={{0,8},{1,9},{2,10},{3,11},{4,12},{5,13},{6,14},{7,15},{8,0},{9,1},... | collective-permute-start | bytes 884744 | tf_op jit(solution)/shard_map/ppermute | solution.py:392
  7.3 14.6 %collective-permute-start.10 = (bf16[64,2304]{1,0:T(8,128)(2,1)}, bf16[64,2304]{1,0:T(8,128)(2,1)}, u32[]{:S(2)}, u32[]{:S(2)}) collective-permute-start(bf16[64,2304]{1,0:T(8,128)(2,1)} %param.18), channel_id=1, source_target_pairs={{0,16},{1,17},{2,18},{3,19},{4,20},{5,21},{6,22},{7,23},{8,24},{9,... | collective-permute-start | bytes 884744 | tf_op jit(solution)/shard_map/ppermute | solution.py:392
  8.8 14.2 %collective-permute-start.11 = (bf16[64,2304]{1,0:T(8,128)(2,1)}, bf16[64,2304]{1,0:T(8,128)(2,1)S(1)}, u32[]{:S(2)}, u32[]{:S(2)}) collective-permute-start(bf16[64,2304]{1,0:T(8,128)(2,1)} %param.18), channel_id=1, source_target_pairs={{0,24},{1,25},{2,26},{3,27},{4,28},{5,29},{6,30},{7,31},{8,16},{9,... | collective-permute-start | bytes 884744 | tf_op jit(solution)/shard_map/ppermute | solution.py:392
  17.6 5.4 collective-permute-start
  19.2 189.9 %reduce-scatter.5.cloned.1.call-start = ((), (), s32[]{:S(2)}) async-start(), calls=%async_computation.5 | async-start | bytes 5308416 | tf_op jit(solution)/shard_map/reduce_scatter | solution.py:534
  23.2 6.9 collective-permute-start.1
  24.7 15.4 %collective-permute-start.12 = (bf16[64,2304]{1,0:T(8,128)(2,1)S(1)}, bf16[64,2304]{1,0:T(8,128)(2,1)S(1)}, u32[]{:S(2)}, u32[]{:S(2)}) collective-permute-start(bf16[64,2304]{1,0:T(8,128)(2,1)S(1)} %get-tuple-element.81), channel_id=1, source_target_pairs={{0,2},{1,3},{2,4},{3,5},{4,6},{5,7},{6,0},{7,1},{8,10},{9,11},{10,... | collective-permute-start | bytes 884744 | tf_op jit(solution)/shard_map/ppermute | solution.py:392
  26.1 39.0 %collective-permute-start.13 = (bf16[64,2304]{1,0:T(8,128)(2,1)S(1)}, bf16[64,2304]{1,0:T(8,128)(2,1)S(1)}, u32[]{:S(2)}, u32[]{:S(2)}) collective-permute-start(bf16[64,2304]{1,0:T(8,128)(2,1)S(1)} %get-tuple-element.80), channel_id=1, source_target_pairs={{0,4},{1,5},{2,6},{3,7},{4,0},{5,1},{6,2},{7,3},{8,12},{9,13},{10,... | collective-permute-start | bytes 884744 | tf_op jit(solution)/shard_map/ppermute | solution.py:392
  27.2 37.9 %collective-permute-start.14 = (bf16[64,2304]{1,0:T(8,128)(2,1)S(1)}, bf16[64,2304]{1,0:T(8,128)(2,1)S(1)}, u32[]{:S(2)}, u32[]{:S(2)}) collective-permute-start(bf16[64,2304]{1,0:T(8,128)(2,1)S(1)} %get-tuple-element.79), channel_id=1, source_target_pairs={{0,6},{1,7},{2,0},{3,1},{4,2},{5,3},{6,4},{7,5},{8,14},{9,15},{10,... | collective-permute-start | bytes 884744 | tf_op jit(solution)/shard_map/ppermute | solution.py:392
  29.4 70.9 %collective-permute-start.2 = (bf16[2,72,640]{2,1,0:T(8,128)(2,1)S(1)}, bf16[2,72,640]{2,1,0:T(8,128)(2,1)S(1)}, u32[]{:S(2)}, u32[]{:S(2)}) collective-permute-start(bf16[2,72,640]{2,1,0:T(8,128)(2,1)S(1)} %get-tuple-element.105), channel_id=1, source_target_pairs={{0,4},{1,5},{2,6},{3,7},{4,0},{5,1},{6,2},{7,3},{8,12},{9,13},{10,... | collective-permute-start | bytes 552968 | tf_op jit(solution)/shard_map/ppermute | solution.py:392
  30.1 70.3 %collective-permute-start.3 = (bf16[2,72,640]{2,1,0:T(8,128)(2,1)S(1)}, bf16[2,72,640]{2,1,0:T(8,128)(2,1)S(1)}, u32[]{:S(2)}, u32[]{:S(2)}) collective-permute-start(bf16[2,72,640]{2,1,0:T(8,128)(2,1)S(1)} %get-tuple-element.103), channel_id=1, source_target_pairs={{0,6},{1,7},{2,0},{3,1},{4,2},{5,3},{6,4},{7,5},{8,14},{9,15},{10,... | collective-permute-start | bytes 552968 | tf_op jit(solution)/shard_map/ppermute | solution.py:392
  65.2 37.1 %collective-permute-start.15 = (bf16[2,64,2304]{2,1,0:T(8,128)(2,1)S(1)}, bf16[2,64,2304]{2,1,0:T(8,128)(2,1)S(1)}, u32[]{:S(2)}, u32[]{:S(2)}) collective-permute-start(bf16[2,64,2304]{2,1,0:T(8,128)(2,1)S(1)} %dynamic-slice_bitcast_fusion.3), channel_id=1, source_target_pairs={{0,1},{1,0},{2,3},{3,2},{4,5},{5,4},{6,7},{7,6},{8,9},{9,8},{10,11... | collective-permute-start | bytes 1769480 | tf_op jit(solution)/shard_map/ppermute | solution.py:392
  100.4 17.4 %collective-permute-start.4 = (bf16[576,640]{1,0:T(8,128)(2,1)S(1)}, bf16[576,640]{1,0:T(8,128)(2,1)S(1)}, u32[]{:S(2)}, u32[]{:S(2)}) collective-permute-start(bf16[576,640]{1,0:T(8,128)(2,1)S(1)} %bitcast.315), channel_id=1, source_target_pairs={{0,8},{1,9},{2,10},{3,11},{4,12},{5,13},{6,14},{7,15},{8,0},{9,1},... | collective-permute-start | bytes 2211848 | tf_op jit(solution)/shard_map/ppermute | solution.py:392
  100.7 18.5 %collective-permute-start.5 = (bf16[576,640]{1,0:T(8,128)(2,1)S(1)}, bf16[576,640]{1,0:T(8,128)(2,1)S(1)}, u32[]{:S(2)}, u32[]{:S(2)}) collective-permute-start(bf16[576,640]{1,0:T(8,128)(2,1)S(1)} %bitcast.316), channel_id=1, source_target_pairs={{0,16},{1,17},{2,18},{3,19},{4,20},{5,21},{6,22},{7,23},{8,24},{9,... | collective-permute-start | bytes 2211848 | tf_op jit(solution)/shard_map/ppermute | solution.py:392
  117.9 8.6 %collective-permute-start.6 = (bf16[288,640]{1,0:T(8,128)(2,1)S(1)}, bf16[288,640]{1,0:T(8,128)(2,1)S(1)}, u32[]{:S(2)}, u32[]{:S(2)}) collective-permute-start(bf16[288,640]{1,0:T(8,128)(2,1)S(1)} %slice.404), channel_id=1, source_target_pairs={{0,16},{1,17},{2,18},{3,19},{4,20},{5,21},{6,22},{7,23},{8,24},{9,... | collective-permute-start | bytes 1105928 | tf_op jit(solution)/shard_map/ppermute | solution.py:392
  119.2 8.3 %collective-permute-start.7 = (bf16[288,640]{1,0:T(8,128)(2,1)S(1)}, bf16[288,640]{1,0:T(8,128)(2,1)S(1)}, u32[]{:S(2)}, u32[]{:S(2)}) collective-permute-start(bf16[288,640]{1,0:T(8,128)(2,1)S(1)} %slice.405), channel_id=1, source_target_pairs={{0,8},{1,9},{2,10},{3,11},{4,12},{5,13},{6,14},{7,15},{8,0},{9,1},... | collective-permute-start | bytes 1105928 | tf_op jit(solution)/shard_map/ppermute | solution.py:392
  140.5 5.3 collective-permute-start.8
  152.9 189.3 %all-gather.7.cloned.1.call-start = ((), (), s32[]{:S(2)}) async-start(), calls=%async_computation.6 | async-start | bytes 5308416 | tf_op jit(solution)/shard_map/all_gather | solution.py:543
  213.2 220.2 %reduce-scatter.7.cloned.1.call-start = ((), (), s32[]{:S(2)}) async-start(), calls=%async_computation.7 | async-start | bytes 5308416 | tf_op jit(solution)/shard_map/reduce_scatter | solution.py:549
  213.3 28.2 %collective-permute-start.16 = (bf16[576,1152]{1,0:T(8,128)(2,1)}, bf16[576,1152]{1,0:T(8,128)(2,1)S(1)}, u32[]{:S(2)}, u32[]{:S(2)}) collective-permute-start(bf16[576,1152]{1,0:T(8,128)(2,1)} %param.19), channel_id=1, source_target_pairs={{0,8},{1,9},{2,10},{3,11},{4,12},{5,13},{6,14},{7,15},{8,0},{9,1},... | collective-permute-start | bytes 3981320 | tf_op jit(solution)/shard_map/ppermute | solution.py:392
  213.6 30.2 %collective-permute-start.17 = (bf16[576,1152]{1,0:T(8,128)(2,1)}, bf16[576,1152]{1,0:T(8,128)(2,1)S(1)}, u32[]{:S(2)}, u32[]{:S(2)}) collective-permute-start(bf16[576,1152]{1,0:T(8,128)(2,1)} %param.19), channel_id=1, source_target_pairs={{0,16},{1,17},{2,18},{3,19},{4,20},{5,21},{6,22},{7,23},{8,24},{9,... | collective-permute-start | bytes 3981320 | tf_op jit(solution)/shard_map/ppermute | solution.py:392
  214.8 55.0 %collective-permute-start.20 = (bf16[576,1152]{1,0:T(8,128)(2,1)}, bf16[576,1152]{1,0:T(8,128)(2,1)S(1)}, u32[]{:S(2)}, u32[]{:S(2)}) collective-permute-start(bf16[576,1152]{1,0:T(8,128)(2,1)} %param.20), channel_id=1, source_target_pairs={{0,8},{1,9},{2,10},{3,11},{4,12},{5,13},{6,14},{7,15},{8,0},{9,1},... | collective-permute-start | bytes 3981320 | tf_op jit(solution)/shard_map/ppermute | solution.py:392
  216.0 55.3 %collective-permute-start.21 = (bf16[576,1152]{1,0:T(8,128)(2,1)}, bf16[576,1152]{1,0:T(8,128)(2,1)S(1)}, u32[]{:S(2)}, u32[]{:S(2)}) collective-permute-start(bf16[576,1152]{1,0:T(8,128)(2,1)} %param.20), channel_id=1, source_target_pairs={{0,16},{1,17},{2,18},{3,19},{4,20},{5,21},{6,22},{7,23},{8,24},{9,... | collective-permute-start | bytes 3981320 | tf_op jit(solution)/shard_map/ppermute | solution.py:392
  216.3 82.0 %collective-permute-start.24 = (bf16[576,1152]{1,0:T(8,128)(2,1)}, bf16[576,1152]{1,0:T(8,128)(2,1)S(1)}, u32[]{:S(2)}, u32[]{:S(2)}) collective-permute-start(bf16[576,1152]{1,0:T(8,128)(2,1)} %bitcast.320), channel_id=1, source_target_pairs={{0,8},{1,9},{2,10},{3,11},{4,12},{5,13},{6,14},{7,15},{8,0},{9,1},... | collective-permute-start | bytes 3981320 | tf_op jit(solution)/shard_map/ppermute | solution.py:392
  241.4 58.4 %collective-permute-start.25 = (bf16[576,1152]{1,0:T(8,128)(2,1)S(1)}, bf16[576,1152]{1,0:T(8,128)(2,1)S(1)}, u32[]{:S(2)}, u32[]{:S(2)}) collective-permute-start(bf16[576,1152]{1,0:T(8,128)(2,1)S(1)} %bitcast.321), channel_id=1, source_target_pairs={{0,16},{1,17},{2,18},{3,19},{4,20},{5,21},{6,22},{7,23},{8,24},{9,... | collective-permute-start | bytes 3981320 | tf_op jit(solution)/shard_map/ppermute | solution.py:392
  243.9 68.6 %collective-permute-start.18 = (bf16[288,1152]{1,0:T(8,128)(2,1)S(1)}, bf16[288,1152]{1,0:T(8,128)(2,1)S(1)}, u32[]{:S(2)}, u32[]{:S(2)}) collective-permute-start(bf16[288,1152]{1,0:T(8,128)(2,1)S(1)} %slice.417), channel_id=1, source_target_pairs={{0,16},{1,17},{2,18},{3,19},{4,20},{5,21},{6,22},{7,23},{8,24},{9,... | collective-permute-start | bytes 1990664 | tf_op jit(solution)/shard_map/ppermute | solution.py:392
  269.8 45.0 %collective-permute-start.19 = (bf16[288,1152]{1,0:T(8,128)(2,1)S(1)}, bf16[288,1152]{1,0:T(8,128)(2,1)S(1)}, u32[]{:S(2)}, u32[]{:S(2)}) collective-permute-start(bf16[288,1152]{1,0:T(8,128)(2,1)S(1)} %slice.418), channel_id=1, source_target_pairs={{0,8},{1,9},{2,10},{3,11},{4,12},{5,13},{6,14},{7,15},{8,0},{9,1},... | collective-permute-start | bytes 1990664 | tf_op jit(solution)/shard_map/ppermute | solution.py:392
  271.3 55.4 %collective-permute-start.22 = (bf16[288,1152]{1,0:T(8,128)(2,1)S(1)}, bf16[288,1152]{1,0:T(8,128)(2,1)S(1)}, u32[]{:S(2)}, u32[]{:S(2)}) collective-permute-start(bf16[288,1152]{1,0:T(8,128)(2,1)S(1)} %slice.419), channel_id=1, source_target_pairs={{0,16},{1,17},{2,18},{3,19},{4,20},{5,21},{6,22},{7,23},{8,24},{9,... | collective-permute-start | bytes 1990664 | tf_op jit(solution)/shard_map/ppermute | solution.py:392
  298.2 28.5 %collective-permute-start.23 = (bf16[288,1152]{1,0:T(8,128)(2,1)S(1)}, bf16[288,1152]{1,0:T(8,128)(2,1)S(1)}, u32[]{:S(2)}, u32[]{:S(2)}) collective-permute-start(bf16[288,1152]{1,0:T(8,128)(2,1)S(1)} %slice.420), channel_id=1, source_target_pairs={{0,8},{1,9},{2,10},{3,11},{4,12},{5,13},{6,14},{7,15},{8,0},{9,1},... | collective-permute-start | bytes 1990664 | tf_op jit(solution)/shard_map/ppermute | solution.py:392
  299.9 41.1 %collective-permute-start.26 = (bf16[288,1152]{1,0:T(8,128)(2,1)S(1)}, bf16[288,1152]{1,0:T(8,128)(2,1)S(1)}, u32[]{:S(2)}, u32[]{:S(2)}) collective-permute-start(bf16[288,1152]{1,0:T(8,128)(2,1)S(1)} %slice.421), channel_id=1, source_target_pairs={{0,16},{1,17},{2,18},{3,19},{4,20},{5,21},{6,22},{7,23},{8,24},{9,... | collective-permute-start | bytes 1990664 | tf_op jit(solution)/shard_map/ppermute | solution.py:392
  312.5 28.4 %collective-permute-start.27 = (bf16[288,1152]{1,0:T(8,128)(2,1)S(1)}, bf16[288,1152]{1,0:T(8,128)(2,1)S(1)}, u32[]{:S(2)}, u32[]{:S(2)}) collective-permute-start(bf16[288,1152]{1,0:T(8,128)(2,1)S(1)} %slice.422), channel_id=1, source_target_pairs={{0,8},{1,9},{2,10},{3,11},{4,12},{5,13},{6,14},{7,15},{8,0},{9,1},... | collective-permute-start | bytes 1990664 | tf_op jit(solution)/shard_map/ppermute | solution.py:392
  376.6 114.3 %all-gather.9.cloned.1.call-start = ((), (), s32[]{:S(2)}) async-start(), calls=%async_computation.8 | async-start | bytes 5308416 | tf_op jit(solution)/shard_map/all_gather | solution.py:558
  438.1 139.7 %reduce-scatter.9.cloned.1.call-start = ((), (), s32[]{:S(2)}) async-start(), calls=%async_computation.9 | async-start | bytes 5308416 | tf_op jit(solution)/shard_map/reduce_scatter | solution.py:566
  526.4 164.3 %all-gather.11.cloned.1.call-start = ((), (), s32[]{:S(2)}) async-start(), calls=%async_computation.10 | async-start | bytes 5308416 | tf_op jit(solution)/shard_map/all_gather | solution.py:579
  539.2 60.0 %collective-permute-start.51 = (bf16[2,288,1152]{2,1,0:T(8,128)(2,1)}, bf16[2,288,1152]{2,1,0:T(8,128)(2,1)}, u32[]{:S(2)}, u32[]{:S(2)}) collective-permute-start(bf16[2,288,1152]{2,1,0:T(8,128)(2,1)} %pad_maximum_fusion.5), channel_id=1, source_target_pairs={{0,16},{1,17},{2,18},{3,19},{4,20},{5,21},{6,22},{7,23},{8,24},{9,... | collective-permute-start | bytes 3981320 | tf_op jit(solution)/shard_map/ppermute | solution.py:392
  541.6 58.7 %collective-permute-start.49 = (bf16[2,288,1152]{2,1,0:T(8,128)(2,1)}, bf16[2,288,1152]{2,1,0:T(8,128)(2,1)}, u32[]{:S(2)}, u32[]{:S(2)}) collective-permute-start(bf16[2,288,1152]{2,1,0:T(8,128)(2,1)} %pad_maximum_fusion.4), channel_id=1, source_target_pairs={{0,8},{1,9},{2,10},{3,11},{4,12},{5,13},{6,14},{7,15},{8,0},{9,1},... | collective-permute-start | bytes 3981320 | tf_op jit(solution)/shard_map/ppermute | solution.py:392
  554.1 49.6 %collective-permute-start.55 = (bf16[2,288,1152]{2,1,0:T(8,128)(2,1)}, bf16[2,288,1152]{2,1,0:T(8,128)(2,1)}, u32[]{:S(2)}, u32[]{:S(2)}) collective-permute-start(bf16[2,288,1152]{2,1,0:T(8,128)(2,1)} %pad_maximum_fusion.7), channel_id=1, source_target_pairs={{0,16},{1,17},{2,18},{3,19},{4,20},{5,21},{6,22},{7,23},{8,24},{9,... | collective-permute-start | bytes 3981320 | tf_op jit(solution)/shard_map/ppermute | solution.py:392
  584.8 233.5 %reduce-scatter.11.cloned.1.call-start = ((), (), s32[]{:S(2)}) async-start(), calls=%async_computation.11 | async-start | bytes 5308416 | tf_op jit(solution)/shard_map/reduce_scatter | solution.py:594
  586.3 28.0 %collective-permute-start.53 = (bf16[2,288,1152]{2,1,0:T(8,128)(2,1)S(1)}, bf16[2,288,1152]{2,1,0:T(8,128)(2,1)S(1)}, u32[]{:S(2)}, u32[]{:S(2)}) collective-permute-start(bf16[2,288,1152]{2,1,0:T(8,128)(2,1)S(1)} %pad_maximum_fusion.6), channel_id=1, source_target_pairs={{0,8},{1,9},{2,10},{3,11},{4,12},{5,13},{6,14},{7,15},{8,0},{9,1},... | collective-permute-start | bytes 3981320 | tf_op jit(solution)/shard_map/ppermute | solution.py:392
  597.8 27.8 %collective-permute-start.47 = (bf16[2,288,1152]{2,1,0:T(8,128)(2,1)S(1)}, bf16[2,288,1152]{2,1,0:T(8,128)(2,1)S(1)}, u32[]{:S(2)}, u32[]{:S(2)}) collective-permute-start(bf16[2,288,1152]{2,1,0:T(8,128)(2,1)S(1)} %pad_maximum_fusion.3), channel_id=1, source_target_pairs={{0,16},{1,17},{2,18},{3,19},{4,20},{5,21},{6,22},{7,23},{8,24},{9,... | collective-permute-start | bytes 3981320 | tf_op jit(solution)/shard_map/ppermute | solution.py:392
  599.2 43.5 %collective-permute-start.45 = (bf16[2,288,1152]{2,1,0:T(8,128)(2,1)S(1)}, bf16[2,288,1152]{2,1,0:T(8,128)(2,1)}, u32[]{:S(2)}, u32[]{:S(2)}) collective-permute-start(bf16[2,288,1152]{2,1,0:T(8,128)(2,1)S(1)} %pad_maximum_fusion.2), channel_id=1, source_target_pairs={{0,8},{1,9},{2,10},{3,11},{4,12},{5,13},{6,14},{7,15},{8,0},{9,1},... | collective-permute-start | bytes 3981320 | tf_op jit(solution)/shard_map/ppermute | solution.py:392
  603.5 42.5 %collective-permute-start.50 = (bf16[288,1152]{1,0:T(8,128)(2,1)}, bf16[288,1152]{1,0:T(8,128)(2,1)}, u32[]{:S(2)}, u32[]{:S(2)}) collective-permute-start(bf16[288,1152]{1,0:T(8,128)(2,1)} %get-tuple-element.40), channel_id=1, source_target_pairs={{0,16},{1,17},{2,18},{3,19},{4,20},{5,21},{6,22},{7,23},{8,24},{9,... | collective-permute-start | bytes 1990664 | tf_op jit(solution)/shard_map/ppermute | solution.py:392
  603.7 53.2 %collective-permute-start.52 = (bf16[288,1152]{1,0:T(8,128)(2,1)}, bf16[288,1152]{1,0:T(8,128)(2,1)}, u32[]{:S(2)}, u32[]{:S(2)}) collective-permute-start(bf16[288,1152]{1,0:T(8,128)(2,1)} %get-tuple-element.41), channel_id=1, source_target_pairs={{0,8},{1,9},{2,10},{3,11},{4,12},{5,13},{6,14},{7,15},{8,0},{9,1},... | collective-permute-start | bytes 1990664 | tf_op jit(solution)/shard_map/ppermute | solution.py:392
  617.6 39.3 %collective-permute-start.54 = (bf16[288,1152]{1,0:T(8,128)(2,1)}, bf16[288,1152]{1,0:T(8,128)(2,1)}, u32[]{:S(2)}, u32[]{:S(2)}) collective-permute-start(bf16[288,1152]{1,0:T(8,128)(2,1)} %get-tuple-element.32), channel_id=1, source_target_pairs={{0,16},{1,17},{2,18},{3,19},{4,20},{5,21},{6,22},{7,23},{8,24},{9,... | collective-permute-start | bytes 1990664 | tf_op jit(solution)/shard_map/ppermute | solution.py:392
  626.7 44.5 %collective-permute-start.56 = (bf16[288,1152]{1,0:T(8,128)(2,1)}, bf16[288,1152]{1,0:T(8,128)(2,1)}, u32[]{:S(2)}, u32[]{:S(2)}) collective-permute-start(bf16[288,1152]{1,0:T(8,128)(2,1)} %get-tuple-element.33), channel_id=1, source_target_pairs={{0,8},{1,9},{2,10},{3,11},{4,12},{5,13},{6,14},{7,15},{8,0},{9,1},... | collective-permute-start | bytes 1990664 | tf_op jit(solution)/shard_map/ppermute | solution.py:392
  644.7 33.9 %collective-permute-start.46 = (bf16[288,1152]{1,0:T(8,128)(2,1)S(1)}, bf16[288,1152]{1,0:T(8,128)(2,1)S(1)}, u32[]{:S(2)}, u32[]{:S(2)}) collective-permute-start(bf16[288,1152]{1,0:T(8,128)(2,1)S(1)} %get-tuple-element.48), channel_id=1, source_target_pairs={{0,16},{1,17},{2,18},{3,19},{4,20},{5,21},{6,22},{7,23},{8,24},{9,... | collective-permute-start | bytes 1990664 | tf_op jit(solution)/shard_map/ppermute | solution.py:392
  645.9 39.3 %collective-permute-start.48 = (bf16[288,1152]{1,0:T(8,128)(2,1)S(1)}, bf16[288,1152]{1,0:T(8,128)(2,1)S(1)}, u32[]{:S(2)}, u32[]{:S(2)}) collective-permute-start(bf16[288,1152]{1,0:T(8,128)(2,1)S(1)} %get-tuple-element.49), channel_id=1, source_target_pairs={{0,8},{1,9},{2,10},{3,11},{4,12},{5,13},{6,14},{7,15},{8,0},{9,1},... | collective-permute-start | bytes 1990664 | tf_op jit(solution)/shard_map/ppermute | solution.py:392
  701.5 15.0 %collective-permute-start.28 = (f32[1024,256]{0,1:T(8,128)S(1)}, f32[1024,256]{0,1:T(8,128)S(1)}, u32[]{:S(2)}, u32[]{:S(2)}) collective-permute-start(f32[1024,256]{0,1:T(8,128)S(1)} %get-tuple-element.116), channel_id=1, source_target_pairs={{0,1},{1,0},{2,3},{3,2},{4,5},{5,4},{6,7},{7,6},{8,9},{9,8},{10,11... | collective-permute-start | bytes 3145736 | tf_op jit(solution)/shard_map/ppermute | solution.py:392
  711.4 13.8 %collective-permute-start.38 = (bf16[64,2304]{1,0:T(8,128)(2,1)}, bf16[64,2304]{1,0:T(8,128)(2,1)}, u32[]{:S(2)}, u32[]{:S(2)}) collective-permute-start(bf16[64,2304]{1,0:T(8,128)(2,1)} %get-tuple-element.77), channel_id=1, source_target_pairs={{0,2},{1,3},{2,4},{3,5},{4,6},{5,7},{6,0},{7,1},{8,10},{9,11},{10,... | collective-permute-start | bytes 884744 | tf_op jit(solution)/shard_map/ppermute | solution.py:392
  712.8 23.6 %collective-permute-start.39 = (bf16[64,2304]{1,0:T(8,128)(2,1)}, bf16[64,2304]{1,0:T(8,128)(2,1)}, u32[]{:S(2)}, u32[]{:S(2)}) collective-permute-start(bf16[64,2304]{1,0:T(8,128)(2,1)} %get-tuple-element.76), channel_id=1, source_target_pairs={{0,4},{1,5},{2,6},{3,7},{4,0},{5,1},{6,2},{7,3},{8,12},{9,13},{10,... | collective-permute-start | bytes 884744 | tf_op jit(solution)/shard_map/ppermute | solution.py:392
  714.3 31.1 %collective-permute-start.40 = (bf16[64,2304]{1,0:T(8,128)(2,1)}, bf16[64,2304]{1,0:T(8,128)(2,1)}, u32[]{:S(2)}, u32[]{:S(2)}) collective-permute-start(bf16[64,2304]{1,0:T(8,128)(2,1)} %get-tuple-element.75), channel_id=1, source_target_pairs={{0,6},{1,7},{2,0},{3,1},{4,2},{5,3},{6,4},{7,5},{8,14},{9,15},{10,... | collective-permute-start | bytes 884744 | tf_op jit(solution)/shard_map/ppermute | solution.py:392
  743.6 17.2 %collective-permute-start.31 = (bf16[2,288,640]{2,1,0:T(8,128)(2,1)S(1)}, bf16[2,288,640]{2,1,0:T(8,128)(2,1)S(1)}, u32[]{:S(2)}, u32[]{:S(2)}) collective-permute-start(bf16[2,288,640]{2,1,0:T(8,128)(2,1)S(1)} %pad_maximum_fusion.13), channel_id=1, source_target_pairs={{0,16},{1,17},{2,18},{3,19},{4,20},{5,21},{6,22},{7,23},{8,24},{9,... | collective-permute-start | bytes 2211848 | tf_op jit(solution)/shard_map/ppermute | solution.py:392
  745.0 16.9 %collective-permute-start.29 = (bf16[2,288,640]{2,1,0:T(8,128)(2,1)S(1)}, bf16[2,288,640]{2,1,0:T(8,128)(2,1)S(1)}, u32[]{:S(2)}, u32[]{:S(2)}) collective-permute-start(bf16[2,288,640]{2,1,0:T(8,128)(2,1)S(1)} %pad_maximum_fusion.12), channel_id=1, source_target_pairs={{0,8},{1,9},{2,10},{3,11},{4,12},{5,13},{6,14},{7,15},{8,0},{9,1},... | collective-permute-start | bytes 2211848 | tf_op jit(solution)/shard_map/ppermute | solution.py:392
  761.0 8.5 %collective-permute-start.32 = (bf16[288,640]{1,0:T(8,128)(2,1)S(1)}, bf16[288,640]{1,0:T(8,128)(2,1)S(1)}, u32[]{:S(2)}, u32[]{:S(2)}) collective-permute-start(bf16[288,640]{1,0:T(8,128)(2,1)S(1)} %fusion.114), channel_id=1, source_target_pairs={{0,8},{1,9},{2,10},{3,11},{4,12},{5,13},{6,14},{7,15},{8,0},{9,1},... | collective-permute-start | bytes 1105928 | tf_op jit(solution)/shard_map/ppermute | solution.py:392
  762.1 8.2 collective-permute-start.30
  762.7 21.0 %collective-permute-start.43 = (bf16[2,32,2304]{2,1,0:T(8,128)(2,1)S(1)}, bf16[2,32,2304]{2,1,0:T(8,128)(2,1)S(1)}, u32[]{:S(2)}, u32[]{:S(2)}) collective-permute-start(bf16[2,32,2304]{2,1,0:T(8,128)(2,1)S(1)} %pad_maximum_fusion.19), channel_id=1, source_target_pairs={{0,16},{1,17},{2,18},{3,19},{4,20},{5,21},{6,22},{7,23},{8,24},{9,... | collective-permute-start | bytes 884744 | tf_op jit(solution)/shard_map/ppermute | solution.py:392
  763.7 20.0 %collective-permute-start.41 = (bf16[2,32,2304]{2,1,0:T(8,128)(2,1)S(1)}, bf16[2,32,2304]{2,1,0:T(8,128)(2,1)S(1)}, u32[]{:S(2)}, u32[]{:S(2)}) collective-permute-start(bf16[2,32,2304]{2,1,0:T(8,128)(2,1)S(1)} %pad_maximum_fusion.18), channel_id=1, source_target_pairs={{0,8},{1,9},{2,10},{3,11},{4,12},{5,13},{6,14},{7,15},{8,0},{9,1},... | collective-permute-start | bytes 884744 | tf_op jit(solution)/shard_map/ppermute | solution.py:392
  770.8 26.3 %collective-permute-start.33 = (bf16[2,72,640]{2,1,0:T(8,128)(2,1)S(1)}, bf16[2,72,640]{2,1,0:T(8,128)(2,1)S(1)}, u32[]{:S(2)}, u32[]{:S(2)}) collective-permute-start(bf16[2,72,640]{2,1,0:T(8,128)(2,1)S(1)} %get-tuple-element.97), channel_id=1, source_target_pairs={{0,2},{1,3},{2,4},{3,5},{4,6},{5,7},{6,0},{7,1},{8,10},{9,11},{10,... | collective-permute-start | bytes 552968 | tf_op jit(solution)/shard_map/ppermute | solution.py:392
  783.8 23.6 %collective-permute-start.42 = (bf16[32,2304]{1,0:T(8,128)(2,1)S(1)}, bf16[32,2304]{1,0:T(8,128)(2,1)S(1)}, u32[]{:S(2)}, u32[]{:S(2)}) collective-permute-start(bf16[32,2304]{1,0:T(8,128)(2,1)S(1)} %get-tuple-element.69), channel_id=1, source_target_pairs={{0,16},{1,17},{2,18},{3,19},{4,20},{5,21},{6,22},{7,23},{8,24},{9,... | collective-permute-start | bytes 442376 | tf_op jit(solution)/shard_map/ppermute | solution.py:392
  785.8 21.6 %collective-permute-start.44 = (bf16[32,2304]{1,0:T(8,128)(2,1)S(1)}, bf16[32,2304]{1,0:T(8,128)(2,1)S(1)}, u32[]{:S(2)}, u32[]{:S(2)}) collective-permute-start(bf16[32,2304]{1,0:T(8,128)(2,1)S(1)} %get-tuple-element.70), channel_id=1, source_target_pairs={{0,8},{1,9},{2,10},{3,11},{4,12},{5,13},{6,14},{7,15},{8,0},{9,1},... | collective-permute-start | bytes 442376 | tf_op jit(solution)/shard_map/ppermute | solution.py:392
  787.5 9.6 %collective-permute-start.34 = (bf16[2,72,640]{2,1,0:T(8,128)(2,1)S(1)}, bf16[2,72,640]{2,1,0:T(8,128)(2,1)S(1)}, u32[]{:S(2)}, u32[]{:S(2)}) collective-permute-start(bf16[2,72,640]{2,1,0:T(8,128)(2,1)S(1)} %get-tuple-element.96), channel_id=1, source_target_pairs={{0,4},{1,5},{2,6},{3,7},{4,0},{5,1},{6,2},{7,3},{8,12},{9,13},{10,... | collective-permute-start | bytes 552968 | tf_op jit(solution)/shard_map/ppermute | solution.py:392
  791.7 9.5 %collective-permute-start.35 = (bf16[2,72,640]{2,1,0:T(8,128)(2,1)S(1)}, bf16[2,72,640]{2,1,0:T(8,128)(2,1)S(1)}, u32[]{:S(2)}, u32[]{:S(2)}) collective-permute-start(bf16[2,72,640]{2,1,0:T(8,128)(2,1)S(1)} %get-tuple-element.95), channel_id=1, source_target_pairs={{0,6},{1,7},{2,0},{3,1},{4,2},{5,3},{6,4},{7,5},{8,14},{9,15},{10,... | collective-permute-start | bytes 552968 | tf_op jit(solution)/shard_map/ppermute | solution.py:392
  801.3 7.5 collective-permute-start.36
  (70 other events, 1128.8 us)
Sparse Core Ops, SparseCore 0:
  19.3 87.6 all-gather.4
  153.0 56.0 reduce-scatter.4
  213.3 52.6 all-gather.6
  376.7 56.6 reduce-scatter.6
  438.2 52.6 all-gather.8
  526.5 51.2 reduce-scatter.8
  584.9 52.6 all-gather.10
  725.4 59.3 reduce-scatter.10

commit v2 on v0

--- a/solution.py
+++ b/solution.py
@@ -1,6 +1,10 @@
+from functools import partial
+
 import jax
 import jax.numpy as jnp
 from jax import lax
+from jax.experimental import pallas as pl
+from jax.experimental.pallas import tpu as pltpu
 from jax.sharding import PartitionSpec as P
 
 QUERY_HEAD_COUNT = 8
@@ -166,7 +170,7 @@
     return (query_acc.reshape(row_count, QUERY_HEAD_COUNT * HEAD_FEATURES), key_acc, value_acc)
 
 
-def body(
+def context_body(
     tokens,
     w_query,
     w_key,
@@ -344,6 +348,898 @@
     )
 
 
+CORES = 2
+GELU_IN = 0.7978845608
+GELU_CUBE = 0.044715
+VMEM_LIMIT = 56 * 2**20
+
+
+def wide(value):
+    return value.astype(jnp.float32)
+
+
+def narrow(value):
+    return value.astype(jnp.bfloat16)
+
+
+def rms_parts(signal):
+    scale = lax.rsqrt(jnp.mean(signal * signal, axis=-1, keepdims=True) + epsilon)
+    return scale, signal * scale
+
+
+def rms_back(scale, unit, weight, upstream):
+    weighted = upstream * weight
+    mean = jnp.mean(weighted * unit, axis=-1, keepdims=True)
+    return scale * (weighted - unit * mean), jnp.sum(upstream * unit, axis=0)
+
+
+def dot_nn(left, right):
+    return jnp.dot(left, right, preferred_element_type=jnp.float32)
+
+
+def dot_nt(left, right):
+    return jnp.einsum("ab,cb->ac", left, right, preferred_element_type=jnp.float32)
+
+
+def dot_tn(left, right):
+    return jnp.einsum("ab,ac->bc", left, right, preferred_element_type=jnp.float32)
+
+
+def after(value, *others):
+    anywhere = pl.BlockSpec(memory_space=pl.ANY)
+    return pl.pallas_call(
+        lambda *refs: None,
+        in_specs=[anywhere] * (1 + len(others)),
+        out_specs=anywhere,
+        out_shape=jax.ShapeDtypeStruct(value.shape, value.dtype),
+        input_output_aliases={0: 0},
+    )(value, *others)
+
+
+def fresh(shape, dtype, *others):
+    anywhere = pl.BlockSpec(memory_space=pl.ANY)
+    return pl.pallas_call(
+        lambda *refs: None,
+        in_specs=[anywhere] * len(others),
+        out_specs=anywhere,
+        out_shape=jax.ShapeDtypeStruct(shape, dtype),
+    )(*others)
+
+
+def lull(*others):
+    anywhere = pl.BlockSpec(memory_space=pl.ANY)
+    return pl.pallas_call(
+        lambda *refs: None,
+        in_specs=[anywhere] * len(others),
+        out_specs=anywhere,
+        out_shape=jax.ShapeDtypeStruct((8, 128), jnp.float32),
+        cost_estimate=pl.CostEstimate(flops=10**12, bytes_accessed=0, transcendentals=0),
+    )(*others)
+
+
+class Order:
+    def __init__(self):
+        self.last = ()
+
+    def pin(self, value, sent=None):
+        extra = () if sent is None else (lull(sent),)
+        value = after(value, *self.last, *extra)
+        self.last = (value,)
+        return value
+
+    def mark(self, value):
+        self.last = (value,)
+
+    def hold(self, value):
+        return after(value, *self.last)
+
+
+class Moves:
+    def __init__(self, n_seq, n_ctx):
+        self.n_seq, self.n_ctx = n_seq, n_ctx
+        self.line = n_ctx // CORES
+        self.seq = lax.axis_index("seq")
+        self.ctx = lax.axis_index("ctx")
+        self.plane = self.ctx // CORES
+        self.core = self.ctx % CORES
+
+    def _send(self, value, move):
+        pairs = []
+        for s in range(self.n_seq):
+            for c in range(self.n_ctx):
+                t = move(s, c // CORES, c % CORES)
+                pairs.append((s * self.n_ctx + c, t[0] * self.n_ctx + t[1] * CORES + t[2]))
+        return lax.ppermute(value, ("seq", "ctx"), pairs)
+
+    def across(self, value, mask):
+        return self._send(value, lambda s, z, k: (s ^ mask, z, k))
+
+    def along(self, value, step):
+        return self._send(value, lambda s, z, k: (s, (z + step) % self.line, k))
+
+    def plane_swap(self, value, mask):
+        return self._send(value, lambda s, z, k: (s, z ^ mask, k))
+
+    def swap(self, value):
+        return self._send(value, lambda s, z, k: (s, z, k ^ 1))
+
+    def gather_halves(self, block, gate):
+        half = block.shape[0] // 2
+        low, high = block[:half], block[half:]
+        low_near = self.across(low, 2)
+        high_near = self.across(high, 1)
+        yield None
+        low_near, high_near = gate(low_near, block), gate(high_near)
+        low_two, high_two = jnp.stack([low, low_near]), jnp.stack([high, high_near])
+        low_far = self.across(low_two, 1)
+        high_far = self.across(high_two, 2)
+        yield None
+        yield block, low_near, high_near, gate(low_far, low_two), gate(high_far)
+
+    def place_halves(self, pieces):
+        block, low_near, high_near, low_far, high_far = pieces
+        half = block.shape[0] // 2
+        out = fresh((self.n_seq,) + block.shape, block.dtype, low_near)
+        put = lambda out, piece, mask, at: lax.dynamic_update_slice(
+            out, piece[None], (self.seq ^ mask, at) + (0,) * (block.ndim - 1)
+        )
+        out = lax.dynamic_update_index_in_dim(out, block, self.seq, 0)
+        out = put(out, low_near, 2, 0)
+        out = put(out, high_near, 1, half)
+        out = put(out, low_far[0], 1, 0)
+        out = put(out, low_far[1], 3, 0)
+        out = put(out, high_far[0], 2, half)
+        return put(out, high_far[1], 3, half).reshape((-1,) + block.shape[1:])
+
+    def scatter_whole(self, terms, mask, gate):
+        other = 3 - mask
+        pick = lambda m: lax.dynamic_index_in_dim(terms, self.seq ^ m, 0, False)
+        sent = jnp.stack([pick(mask), pick(3)])
+        near = self.across(sent, mask)
+        yield None
+        near = gate(near, sent)
+        onward = narrow(wide(pick(other)) + wide(near[1]))
+        far = self.across(onward, other)
+        yield None
+        yield wide(pick(0)) + wide(near[0]) + wide(gate(far, onward))
+
+    def scatter_halves(self, terms, gate):
+        half = terms.shape[1] // 2
+        low = self.scatter_whole(terms[:, :half], 1, gate)
+        high = self.scatter_whole(terms[:, half:], 2, gate)
+        for _ in range(2):
+            next(low), next(high)
+            yield None
+        yield jnp.concatenate([next(low), next(high)], axis=0)
+
+    def exchange_line(self, blocks):
+        out = fresh(blocks.shape, blocks.dtype, blocks)
+        own = lax.dynamic_index_in_dim(blocks, self.plane, 0, False)
+        out = lax.dynamic_update_index_in_dim(out, own, self.plane, 0)
+        for step in range(1, self.line):
+            sent = lax.dynamic_index_in_dim(blocks, (self.plane + step) % self.line, 0, False)
+            got = self.along(sent, step)
+            out = lax.dynamic_update_index_in_dim(out, got, (self.plane - step) % self.line, 0)
+        return out
+
+    def exchange_planes(self, blocks, pin):
+        pick = lambda mask: lax.dynamic_index_in_dim(blocks, self.plane ^ mask, 0, False)
+        sent = jnp.stack([pick(2), pick(3)])
+        near = self.plane_swap(sent, 2)
+        yield None
+        near = pin(near, sent)
+        sent = jnp.stack([pick(1), near[1]])
+        far = self.plane_swap(sent, 1)
+        yield None
+        far = pin(far, sent)
+        out = fresh(blocks.shape, blocks.dtype, far)
+        for mask, block in ((0, pick(0)), (2, near[0]), (1, far[0]), (3, far[1])):
+            out = lax.dynamic_update_index_in_dim(out, block, self.plane ^ mask, 0)
+        yield out
+
+    def exchange_cores(self, blocks):
+        own = lax.dynamic_index_in_dim(blocks, self.core, 0, False)
+        got = self.swap(lax.dynamic_index_in_dim(blocks, 1 - self.core, 0, False))
+        first = self.core == 0
+        return jnp.stack([jnp.where(first, own, got), jnp.where(first, got, own)])
+
+
+ANYWHERE = pl.BlockSpec(memory_space=pl.ANY)
+
+
+def tile(rows, columns):
+    return pl.BlockSpec((rows, columns), lambda i: (i, 0))
+
+
+def whole(*shape):
+    return pl.BlockSpec(shape, lambda i: (0,) * len(shape))
+
+
+def call(kernel, steps, in_specs, out_specs, out_shape, flops, args, scratch=(), others=()):
+    count = len(args)
+
+    def body(*refs):
+        kernel(*refs[:count], *refs[count + len(others) :])
+
+    return pl.pallas_call(
+        body,
+        grid=(steps,),
+        in_specs=in_specs + [ANYWHERE] * len(others),
+        out_specs=out_specs,
+        out_shape=out_shape,
+        scratch_shapes=list(scratch),
+        compiler_params=pltpu.CompilerParams(vmem_limit_bytes=VMEM_LIMIT),
+        cost_estimate=pl.CostEstimate(flops=flops, bytes_accessed=0, transcendentals=0),
+    )(*args, *others)
+
+
+def array(dtype, *shape):
+    return jax.ShapeDtypeStruct(shape, dtype)
+
+
+def mul_nt(left, right):
+    return lax.dot_general(
+        left, right, (((1,), (1,)), ((), ())), preferred_element_type=jnp.float32
+    )
+
+
+def mul_tn(left, right):
+    return lax.dot_general(
+        left, right, (((0,), (0,)), ((), ())), preferred_element_type=jnp.float32
+    )
+
+
+def turn_pair(value, cosine, sine):
+    half = value.shape[1] // 2
+    first, second = value[:, :half], value[:, half:]
+    return jnp.concatenate(
+        [first * cosine - second * sine, second * cosine + first * sine], axis=1
+    )
+
+
+BF16, F32 = jnp.bfloat16, jnp.float32
+TILE = 256
+
+
+def load(copies, sems):
+    started = [pltpu.make_async_copy(a, b, sems.at[i]) for i, (a, b) in enumerate(copies)]
+    for copy in started:
+        copy.start()
+    return started
+
+
+def whole_copies(seq, pieces, target):
+    mask, own, near, far = pieces
+    rows = own.shape[0]
+    at = lambda m: target.at[pl.ds(pl.multiple_of((seq ^ m) * rows, 64), rows)]
+    other = 3 - mask
+    first, second = far.at[pl.ds(0, rows)], far.at[pl.ds(rows, rows)]
+    return [(own, at(0)), (near, at(mask)), (first, at(other)), (second, at(3))]
+
+
+def half_copies(seq, pieces, target):
+    own, low_near, high_near, low_far, high_far = pieces
+    rows = own.shape[0]
+    half = rows // 2
+    at = lambda m, h: target.at[pl.ds(pl.multiple_of((seq ^ m) * rows + h * half, 32), half)]
+    return [
+        (own, target.at[pl.ds(pl.multiple_of(seq * rows, 64), rows)]),
+        (low_near, at(2, 0)),
+        (high_near, at(1, 1)),
+        (low_far.at[0], at(1, 0)),
+        (low_far.at[1], at(3, 0)),
+        (high_far.at[0], at(2, 1)),
+        (high_far.at[1], at(3, 1)),
+    ]
+
+
+SCALARS = pl.BlockSpec(memory_space=pltpu.SMEM)
+
+
+def project_rows(place, tokens, pieces, feats, tables):
+    rows, width = tokens.shape
+    wide_columns = pieces[0].shape[1]
+
+    def kernel(place_ref, x_ref, own, near_a, near_b, far_a, far_b, cq, sq, cp, sp, *refs):
+        normed_ref, query_ref, pair_ref, gains_ref, w_ref, sems = refs
+
+        @pl.when(pl.program_id(0) == 0)
+        def _():
+            copies = half_copies(place_ref[2], (own, near_a, near_b, far_a, far_b), w_ref)
+            for copy in load(copies, sems):
+                copy.wait()
+            gains_ref[...] = w_ref[:, 2 * feats :].astype(F32).T[:8]
+
+        x = x_ref[...].astype(F32)
+        scale = lax.rsqrt(jnp.mean(x * x, axis=-1, keepdims=True) + epsilon)
+        normed = (x * scale * gains_ref[0:1]).astype(BF16)
+        normed_ref[...] = normed
+        both = dot_nn(normed, w_ref[:, : 2 * feats])
+        query_ref[...] = turn_pair(both[:, :feats], cq[...], sq[...]).astype(BF16)
+        pair_ref[...] = turn_pair(both[:, feats:], cp[...], sp[...]).astype(BF16)
+
+    half = feats // 2
+    return call(
+        kernel,
+        rows // TILE,
+        [SCALARS, tile(TILE, width)] + [ANYWHERE] * 5 + [tile(TILE, half)] * 4,
+        [tile(TILE, width), tile(TILE, feats), tile(TILE, feats), whole(8, width)],
+        [
+            array(BF16, rows, width),
+            array(BF16, rows, feats),
+            array(BF16, rows, feats),
+            array(F32, 8, width),
+        ],
+        4 * rows * width * feats,
+        (place, tokens) + pieces + tables,
+        [pltpu.VMEM((width, wide_columns), BF16), pltpu.SemaphoreType.DMA((7,))],
+    )
+
+
+def soft_rows(query, keys, place, places):
+    bent = jnp.tanh(mul_nt(query, keys) * (HEAD_FEATURES ** (-0.5) / softcap))
+    weight = jnp.where(places <= place, jnp.exp(softcap * bent), 0.0)
+    return bent, weight / jnp.sum(weight, axis=-1, keepdims=True)
+
+
+def attend_head(query, key, value, place, places, others):
+    rows, feats = query.shape
+
+    def kernel(q_ref, k_ref, v_ref, place_ref, places_ref, out_ref):
+        _, probs = soft_rows(q_ref[...], k_ref[...], place_ref[...], places_ref[...])
+        out_ref[...] = dot_nn(probs.astype(BF16), v_ref[...]).astype(BF16)
+
+    return call(
+        kernel,
+        rows // TILE,
+        [tile(TILE, feats), whole(rows, feats), whole(rows, feats), tile(TILE, 1), whole(1, rows)],
+        [tile(TILE, feats)],
+        [array(BF16, rows, feats)],
+        4 * rows * rows * feats,
+        (query, key, value, place, places),
+        (),
+        others,
+    )[0]
+
+
+def attend_head_back(place, query, key, value, mixed_grad, spot, spots, cosine, sine, others):
+    rows, feats = query.shape
+    score_scale = HEAD_FEATURES ** (-0.5)
+    steps = rows // TILE
+
+    def kernel(place_ref, q_ref, k_ref, v_ref, g_ref, spot_ref, spots_ref, c_ref, s_ref, *refs):
+        dq, own_ref, send_ref, dk, dv = refs
+        step = pl.program_id(0)
+
+        @pl.when(step == 0)
+        def _():
+            dk[...] = jnp.zeros_like(dk)
+            dv[...] = jnp.zeros_like(dv)
+
+        query, keys, grad = q_ref[...], k_ref[...], g_ref[...]
+        bent, probs = soft_rows(query, keys, spot_ref[...], spots_ref[...])
+        prob_grad = mul_nt(grad, v_ref[...])
+        delta = jnp.sum(probs * prob_grad, axis=-1, keepdims=True)
+        raw = (probs * (prob_grad - delta) * (1.0 - bent * bent)).astype(BF16)
+        total = dot_nn(raw, keys) * score_scale
+        dq[...] = turn_pair(total, c_ref[...], -s_ref[...]).astype(BF16)
+        dk[...] += mul_tn(raw, query) * score_scale
+        dv[...] += mul_tn(probs.astype(BF16), grad)
+
+        @pl.when(step == steps - 1)
+        def _():
+            first = place_ref[1] == 0
+            own_ref[...] = jnp.where(first, dk[...], dv[...])
+            send_ref[...] = jnp.where(first, dv[...], dk[...])
+
+    return call(
+        kernel,
+        steps,
+        [SCALARS, tile(TILE, feats), whole(rows, feats), whole(rows, feats), tile(TILE, feats)]
+        + [tile(TILE, 1), whole(1, rows)]
+        + [tile(TILE, feats // 2), tile(TILE, feats // 2)],
+        [tile(TILE, feats), whole(rows, feats), whole(rows, feats)],
+        [array(BF16, rows, feats), array(F32, rows, feats), array(F32, rows, feats)],
+        10 * rows * rows * feats,
+        (place, query, key, value, mixed_grad, spot, spots, cosine, sine),
+        [pltpu.VMEM((rows, feats), F32)] * 2,
+        others,
+    )
+
+
+def branch_rows(place, mixed, own, other, tokens, gain_two, gain_three):
+    heads, rows, feats = mixed.shape
+    blocks, out_rows, width = own.shape
+    per_head = feats // (CORES * out_rows)
+    own_rows = TILE // CORES
+
+    def kernel(
+        place_ref, m_ref, own_ref, other_ref, x_ref, two_ref, three_ref, out_ref, mine_ref, w_ref, sems
+    ):
+        step = pl.program_id(0)
+        core = place_ref[1]
+
+        @pl.when(step == 0)
+        def _():
+            copies = [(own_ref, w_ref.at[:, core]), (other_ref, w_ref.at[:, 1 - core])]
+            for copy in load(copies, sems):
+                copy.wait()
+
+        branch = 0.0
+        for h in range(heads):
+            head = w_ref[h * per_head : (h + 1) * per_head].reshape(feats, width)
+            branch += dot_nn(m_ref[h], head)
+
+        @pl.when(step == place_ref[0])
+        def _():
+            mine_ref[...] = jnp.where(core == 0, branch[:own_rows], branch[own_rows:])
+
+        scale = lax.rsqrt(jnp.mean(branch * branch, axis=-1, keepdims=True) + epsilon)
+        residual = x_ref[...].astype(F32) + branch * scale * two_ref[...]
+        scale = lax.rsqrt(jnp.mean(residual * residual, axis=-1, keepdims=True) + epsilon)
+        out_ref[...] = (residual * scale * three_ref[...]).astype(BF16)
+
+    return call(
+        kernel,
+        rows // TILE,
+        [
+            pl.BlockSpec(memory_space=pltpu.SMEM),
+            pl.BlockSpec((heads, TILE, feats), lambda i: (0, i, 0)),
+            ANYWHERE,
+            ANYWHERE,
+            tile(TILE, width),
+            whole(1, width),
+            whole(1, width),
+        ],
+        [tile(TILE, width), whole(own_rows, width)],
+        [array(BF16, rows, width), array(F32, own_rows, width)],
+        2 * heads * rows * feats * width,
+        (place, mixed, own, other, tokens, gain_two, gain_three),
+        [
+            pltpu.VMEM((blocks, CORES, out_rows, width), BF16),
+            pltpu.SemaphoreType.DMA((2,)),
+        ],
+    )
+
+
+def feed_open(place, feed, gate_pieces, up_pieces):
+    rows, width = feed.shape
+    units = gate_pieces[0].shape[1]
+
+    def kernel(place_ref, x_ref, *refs):
+        gates, ups = refs[:3], refs[3:6]
+        hidden_ref, gate_ref, up_ref, gw_ref, uw_ref, gate_sems, up_sems = refs[6:]
+        seq = place_ref[2]
+        gate_copies = whole_copies(seq, (1,) + gates, gw_ref)
+        up_copies = whole_copies(seq, (2,) + ups, uw_ref)
+        first = pl.program_id(0) == 0
+
+        @pl.when(first)
+        def _():
+            started = load(gate_copies, gate_sems)
+            load(up_copies, up_sems)
+            for copy in started:
+                copy.wait()
+
+        x = x_ref[...]
+        gate = dot_nn(x, gw_ref[...])
+
+        @pl.when(first)
+        def _():
+            for i, (a, b) in enumerate(up_copies):
+                pltpu.make_async_copy(a, b, up_sems.at[i]).wait()
+
+        up = dot_nn(x, uw_ref[...])
+        square = gate * gate
+        bend = jnp.tanh(GELU_IN * (gate + GELU_CUBE * square * gate))
+        half = 0.5 * (1.0 + bend)
+        gelu = half * gate
+        slope = half + 0.5 * gate * (1.0 - bend * bend) * (
+            GELU_IN + 3.0 * GELU_IN * GELU_CUBE * square
+        )
+        hidden_ref[...] = (gelu * up).astype(BF16)
+        gate_ref[...] = (up * slope).astype(BF16)
+        up_ref[...] = gelu.astype(BF16)
+
+    return call(
+        kernel,
+        rows // TILE,
+        [SCALARS, tile(TILE, width)] + [ANYWHERE] * 6,
+        [tile(TILE, units)] * 3,
+        [array(BF16, rows, units)] * 3,
+        4 * rows * width * units,
+        (place, feed) + gate_pieces + up_pieces,
+        [pltpu.VMEM((width, units), BF16)] * 2 + [pltpu.SemaphoreType.DMA((4,))] * 2,
+    )
+
+
+def feed_close(place, hidden, down_pieces):
+    rows, units = hidden.shape
+    width = down_pieces[0].shape[0] * 4
+
+    def kernel(place_ref, x_ref, *refs):
+        out_ref, dw_ref, sems = refs[5:]
+
+        @pl.when(pl.program_id(0) == 0)
+        def _():
+            for copy in load(half_copies(place_ref[2], refs[:5], dw_ref), sems):
+                copy.wait()
+
+        out_ref[...] = mul_nt(x_ref[...], dw_ref[...]).astype(BF16)
+
+    return call(
+        kernel,
+        rows // TILE,
+        [SCALARS, tile(TILE, units)] + [ANYWHERE] * 5,
+        [tile(TILE, width)],
+        [array(BF16, rows, width)],
+        2 * rows * width * units,
+        (place, hidden) + down_pieces,
+        [pltpu.VMEM((width, units), BF16), pltpu.SemaphoreType.DMA((7,))],
+    )[0]
+
+
+def mixed_back(place, branch, own, other):
+    rows, width = branch.shape
+    blocks, out_rows, _ = own.shape
+    heads = QUERY_HEAD_COUNT
+    per_head = blocks // heads
+    feats = per_head * CORES * out_rows
+
+    def kernel(place_ref, b_ref, own_ref, other_ref, out_ref, w_ref):
+        core = place_ref[1]
+        w_ref[:, pl.ds(core, 1)] = own_ref[...][:, None]
+        w_ref[:, pl.ds(1 - core, 1)] = other_ref[...][:, None]
+        out_ref[0] = mul_nt(b_ref[...], w_ref[...].reshape(feats, width)).astype(BF16)
+
+    blocks_of = pl.BlockSpec((per_head, out_rows, width), lambda i: (i, 0, 0))
+    return call(
+        kernel,
+        heads,
+        [SCALARS, whole(rows, width), blocks_of, blocks_of],
+        [pl.BlockSpec((1, rows, feats), lambda i: (i, 0, 0))],
+        [array(BF16, heads, rows, feats)],
+        2 * rows * width * heads * feats,
+        (place, branch, own, other),
+        [pltpu.VMEM((per_head, CORES, out_rows, width), BF16)],
+    )[0]
+
+
+def feed_back(place, grad, gate_factor, up_factor, gate_pieces, up_pieces, down_pieces):
+    rows, width = grad.shape
+    units = gate_factor.shape[1]
+
+    def kernel(place_ref, g_ref, gf_ref, uf_ref, *refs):
+        gates, ups, downs = refs[:3], refs[3:6], refs[6:11]
+        gate_ref, up_ref, out_ref, gw_ref, uw_ref, dw_ref, gate_sems, up_sems, down_sems = refs[11:]
+        seq = place_ref[2]
+        gate_copies = whole_copies(seq, (1,) + gates, gw_ref)
+        up_copies = whole_copies(seq, (2,) + ups, uw_ref)
+        first = pl.program_id(0) == 0
+
+        @pl.when(first)
+        def _():
+            started = load(half_copies(seq, downs, dw_ref), down_sems)
+            load(gate_copies, gate_sems)
+            load(up_copies, up_sems)
+            for copy in started:
+                copy.wait()
+
+        hidden_grad = dot_nn(g_ref[...], dw_ref[...])
+        gate_low = (hidden_grad * gf_ref[...].astype(F32)).astype(BF16)
+        up_low = (hidden_grad * uf_ref[...].astype(F32)).astype(BF16)
+        gate_ref[...] = gate_low
+        up_ref[...] = up_low
+
+        @pl.when(first)
+        def _():
+            for copies, sems in ((gate_copies, gate_sems), (up_copies, up_sems)):
+                for i, (a, b) in enumerate(copies):
+                    pltpu.make_async_copy(a, b, sems.at[i]).wait()
+
+        out_ref[...] = (mul_nt(gate_low, gw_ref[...]) + mul_nt(up_low, uw_ref[...])).astype(BF16)
+
+    return call(
+        kernel,
+        rows // TILE,
+        [SCALARS, tile(TILE, width), tile(TILE, units), tile(TILE, units)] + [ANYWHERE] * 11,
+        [tile(TILE, units), tile(TILE, units), tile(TILE, width)],
+        [array(BF16, rows, units), array(BF16, rows, units), array(BF16, rows, width)],
+        6 * rows * width * units,
+        (place, grad, gate_factor, up_factor) + gate_pieces + up_pieces + down_pieces,
+        [pltpu.VMEM((width, units), BF16)] * 3
+        + [pltpu.SemaphoreType.DMA((4,))] * 2
+        + [pltpu.SemaphoreType.DMA((7,))],
+    )
+
+
+def normed_back(place, query_grad, own, other, cosine, sine, pieces):
+    rows, feats = query_grad.shape
+    width, wide_columns = pieces[0].shape[0] * 4, pieces[0].shape[1]
+
+    def kernel(place_ref, q_ref, own_ref, other_ref, c_ref, s_ref, *refs):
+        both_ref, out_ref, w_ref, sems = refs[5:]
+
+        @pl.when(pl.program_id(0) == 0)
+        def _():
+            for copy in load(half_copies(place_ref[2], refs[:5], w_ref), sems):
+                copy.wait()
+
+        pair = turn_pair(own_ref[...] + other_ref[...], c_ref[...], -s_ref[...]).astype(BF16)
+        both_ref[:, :feats] = q_ref[...]
+        both_ref[:, feats:] = pair
+        out_ref[...] = mul_nt(both_ref[...], w_ref[:, : 2 * feats]).astype(BF16)
+
+    return call(
+        kernel,
+        rows // TILE,
+        [SCALARS] + [tile(TILE, feats)] * 3 + [tile(TILE, feats // 2)] * 2 + [ANYWHERE] * 5,
+        [tile(TILE, 2 * feats), tile(TILE, width)],
+        [array(BF16, rows, 2 * feats), array(BF16, rows, width)],
+        4 * rows * feats * width,
+        (place, query_grad, own, other, cosine, sine) + pieces,
+        [pltpu.VMEM((width, wide_columns), BF16), pltpu.SemaphoreType.DMA((7,))],
+    )
+
+
+def weight_grad(left, right, block, others, more=None):
+    rows, width = left.shape
+    columns = right.shape[1]
+    total = columns + (0 if more is None else more.shape[1])
+
+    def kernel(left_ref, right_ref, *refs):
+        refs[-1][:, :columns] = mul_tn(left_ref[...], right_ref[...]).astype(BF16)
+        if more is not None:
+            refs[-1][:, columns:] = refs[0][...]
+
+    extra = () if more is None else (more,)
+    return call(
+        kernel,
+        width // block,
+        [pl.BlockSpec((rows, block), lambda i: (0, i)), whole(rows, columns)]
+        + [tile(block, v.shape[1]) for v in extra],
+        [tile(block, total)],
+        [array(BF16, width, total)],
+        2 * rows * width * columns,
+        (left, right) + extra,
+        (),
+        others,
+    )[0]
+
+
+def head_body(
+    tokens,
+    w_query,
+    w_key,
+    w_value,
+    w_output,
+    w_gate,
+    w_up,
+    w_down,
+    first_gain,
+    second_gain,
+    third_gain,
+    fourth_gain,
+    block_pairs,
+    cotangent,
+    n_seq,
+    n_ctx,
+):
+    moves = Moves(n_seq, n_ctx)
+    order = Order()
+    pin, hold = order.pin, order.hold
+    free = lambda v: v
+    line = moves.line
+    core_zero = moves.core == 0
+    rows, width = tokens.shape
+    feat_rows = w_query.shape[0]
+    out_rows = w_output.shape[0]
+    feats = HEAD_FEATURES
+    pad = 128
+    gather = lambda v: lax.all_gather(v, "ctx", axis=0, tiled=True)
+    scatter = lambda v: lax.psum_scatter(v, "ctx", scatter_dimension=0, tiled=True)
+
+    place = jnp.stack([moves.plane, moves.core, moves.seq]).astype(jnp.int32)
+    block = w_gate.shape[0]
+    half = block // 2
+
+    gate_near = moves.across(w_gate, 1)
+    up_near = moves.across(w_up, 2)
+    gains_in = jnp.stack([first_gain, second_gain, third_gain, fourth_gain], axis=1)
+    gains_in = jnp.pad(gains_in, ((0, 0), (0, pad - 4)))
+    by_head = jnp.concatenate(
+        [
+            w_query.reshape(feat_rows, line, CORES, feats),
+            jnp.stack(
+                [
+                    w_key.reshape(feat_rows, line, feats),
+                    w_value.reshape(feat_rows, line, feats),
+                ],
+                axis=2,
+            ),
+            jnp.broadcast_to(gains_in[:, None, None, :], (feat_rows, line, CORES, pad)),
+        ],
+        axis=3,
+    ).transpose(2, 1, 0, 3)
+    by_plane = moves.exchange_cores(by_head).transpose(1, 0, 2, 3)
+    own_columns = moves.exchange_line(by_plane).reshape(n_ctx * feat_rows, 2 * feats + pad)
+    own_columns = pin(own_columns, by_plane)
+    tokens_in = hold(tokens)
+    tokens_all = gather(tokens_in)
+    columns_move = moves.gather_halves(own_columns, pin)
+    next(columns_move)
+    gate_near, up_near = pin(gate_near), pin(up_near)
+    over_y = pin(jnp.stack([w_gate, gate_near]))
+    over_x = pin(jnp.stack([w_up, up_near]))
+    next(columns_move)
+
+    block_size = rows // 2
+    offsets = jnp.arange(block_size, dtype=jnp.int32)
+    pos = (hold(block_pairs)[:, :, None] * block_size + offsets[None, None, :]).reshape(-1)
+    spot, spots = pos[:, None], pos[None, :]
+    frequency = theta ** (-2.0 * jnp.arange(feats // 2, dtype=jnp.float32) / feats)
+    angles = wide(pos)[:, None] * frequency[None, :]
+    cosine, sine = pin(jnp.cos(angles)), pin(jnp.sin(angles))
+    pair_cosine = pin(jnp.where(core_zero, cosine, 1.0))
+    pair_sine = pin(jnp.where(core_zero, sine, 0.0))
+    tables = (cosine, sine, pair_cosine, pair_sine)
+
+    columns = next(columns_move)
+    over_y = moves.across(hold(over_y), 2)
+    over_x = moves.across(hold(over_x), 1)
+    down_own = pin(hold(w_down).T)
+    tokens_all = pin(tokens_all, tokens_in)
+    out_near = moves.plane_swap(hold(w_output), 2)
+
+    normed, query, pair, gains = project_rows(place, tokens_all, columns, feats, tables)
+    gain_one, gain_two, gain_three, gain_four = (gains[i : i + 1] for i in range(4))
+    pair_other = moves.swap(pair)
+    order.mark(pair)
+    out_near = pin(out_near)
+    out_two = pin(jnp.stack([w_output, out_near]))
+    out_far = moves.plane_swap(out_two, 1)
+    pair_other = pin(pair_other, pair)
+    key = jnp.where(core_zero, pair, pair_other)
+    value = jnp.where(core_zero, pair_other, pair)
+    mixed = pin(attend_head(query, key, value, spot, spots, order.last))
+    mixed_all = lax.all_gather(mixed, "ctx", axis=0)
+
+    out_far = pin(out_far, out_two)
+    out_line = fresh((line,) + w_output.shape, w_output.dtype, out_far)
+    for mask, piece in ((0, w_output), (2, out_near), (1, out_far[0]), (3, out_far[1])):
+        out_line = lax.dynamic_update_index_in_dim(out_line, piece, moves.plane ^ mask, 0)
+    out_move = moves.gather_halves(pin(out_line), pin)
+    next(out_move), next(out_move)
+    down_move = moves.gather_halves(hold(down_own), pin)
+    next(down_move)
+    out_own = pin(moves.place_halves(next(out_move)))
+    out_other = moves.swap(out_own)
+    next(down_move)
+    out_other = pin(out_other, out_own)
+    mixed_all = pin(mixed_all, mixed)
+    feed_all, branch = branch_rows(
+        place, mixed_all, out_own, out_other, tokens_all, gain_two, gain_three
+    )
+    order.mark(branch)
+    over_x, over_y = pin(over_x), pin(over_y)
+    gate_pieces = (w_gate, gate_near, over_y.reshape(-1, over_y.shape[2]))
+    up_pieces = (w_up, up_near, over_x.reshape(-1, over_x.shape[2]))
+    hidden, gate_factor, up_factor = feed_open(place, feed_all, gate_pieces, up_pieces)
+    order.mark(hidden)
+    down_pieces = next(down_move)
+    feed_part = feed_close(place, hidden, down_pieces)
+    order.mark(feed_part)
+    feed_out = scatter(feed_part)
+
+    scale_two, unit_two = rms_parts(hold(branch))
+    residual = wide(tokens) + unit_two * gain_two
+    scale_three, unit_three = rms_parts(residual)
+    unit_two, unit_three, residual = pin(unit_two), pin(unit_three), pin(residual)
+
+    upstream = wide(cotangent)
+    feed_out = pin(feed_out, feed_part)
+    scale_four, unit_four = rms_parts(wide(feed_out))
+    layer_out = narrow(residual + unit_four * gain_four)
+    feed_grad, fourth_term = rms_back(scale_four, unit_four, gain_four, upstream)
+    feed_low = pin(narrow(feed_grad))
+    grad_all = pin(gather(feed_low), feed_low)
+    gate_low, up_low, input_part = feed_back(
+        place, grad_all, gate_factor, up_factor, gate_pieces, up_pieces, down_pieces
+    )
+    order.mark(input_part)
+    feed_input_grad = scatter(input_part)
+    shape = (n_seq, block, gate_low.shape[1])
+    down_term = weight_grad(grad_all, hidden, 384, order.last).reshape(shape)
+    order.mark(down_term)
+    down_move = moves.scatter_halves(down_term, pin)
+    next(down_move)
+    gate_term = weight_grad(feed_all, gate_low, 384, order.last).reshape(shape)
+    order.mark(gate_term)
+    gate_move = moves.scatter_whole(gate_term, 1, pin)
+    next(gate_move)
+    up_term = weight_grad(feed_all, up_low, 384, order.last).reshape(shape)
+    order.mark(up_term)
+    up_move = moves.scatter_whole(up_term, 2, pin)
+    next(up_move)
+    next(down_move)
+    feed_input_grad = wide(pin(feed_input_grad, input_part))
+    middle_grad, third_term = rms_back(scale_three, unit_three, gain_three, feed_input_grad)
+    residual_grad = upstream + middle_grad
+    branch_grad, second_term = rms_back(scale_two, unit_two, gain_two, residual_grad)
+    branch_low = pin(narrow(branch_grad))
+    branch_all = gather(branch_low)
+
+    mixed_own = pin(mixed_back(place, branch_low, out_own, out_other))
+    mixed_grad = lax.all_to_all(mixed_own, "ctx", split_axis=0, concat_axis=0, tiled=True)
+    mixed_grad = pin(mixed_grad.reshape(-1, feats), mixed_own)
+    query_grad, pair_own, pair_send = attend_head_back(
+        place, query, key, value, mixed_grad, spot, spots, cosine, sine, order.last
+    )
+    order.mark(query_grad)
+    pair_other = moves.swap(pair_send)
+    down_sum = pin(next(down_move)).T
+    pair_other = pin(pair_other, pair_send)
+    qkv_grad, normed_part = normed_back(
+        place, query_grad, pair_own, pair_other, pair_cosine, pair_sine, columns
+    )
+    order.mark(normed_part)
+    normed_grad = scatter(normed_part)
+
+    next(gate_move), next(up_move)
+    branch_all = pin(branch_all)
+    output_term = weight_grad(mixed, branch_all, feats, order.last)
+    order.mark(output_term)
+    out_term = output_term.reshape(CORES, CORES, out_rows, width).transpose(1, 0, 2, 3)
+    out_term = moves.exchange_cores(out_term).reshape(line, out_rows, width)
+    terms = jnp.stack([second_term, third_term, fourth_term])
+    terms = narrow(jnp.pad(terms, ((0, pad - 3), (0, 0))).T)
+    qkv_term = weight_grad(normed, qkv_grad, 384, order.last, terms)
+    order.mark(qkv_term)
+    qkv_move = moves.scatter_halves(qkv_term.reshape(n_seq, width // n_seq, -1), pin)
+    next(qkv_move)
+    out_move = moves.exchange_planes(pin(out_term), pin)
+    next(out_move)
+    next(qkv_move)
+    next(out_move)
+    gate_sum, up_sum = next(gate_move), next(up_move)
+    own_term = pin(narrow(next(qkv_move))).reshape(line, CORES, feat_rows, 2 * feats + pad)
+    own_term = moves.exchange_line(own_term).transpose(1, 0, 2, 3)
+    out_term = next(out_move)
+    out_move = moves.scatter_whole(out_term, 1, pin)
+    next(out_move)
+    next(out_move)
+    own_term = wide(pin(moves.exchange_cores(own_term)).transpose(2, 1, 0, 3))
+    grad_query = own_term[..., :feats].reshape(feat_rows, -1)
+    grad_key = own_term[:, :, 0, feats : 2 * feats].reshape(feat_rows, -1)
+    grad_value = own_term[:, :, 1, feats : 2 * feats].reshape(feat_rows, -1)
+    grad_gains = jnp.sum(own_term[..., 2 * feats : 2 * feats + 3], axis=(1, 2))
+    grad_first = (
+        jnp.sum(wide(w_query) * grad_query, axis=1)
+        + jnp.sum(wide(w_key) * grad_key, axis=1)
+        + jnp.sum(wide(w_value) * grad_value, axis=1)
+    ) / wide(first_gain)
+    grad_output = next(out_move)
+
+    scale_one, unit_one = rms_parts(wide(tokens))
+    input_grad, _ = rms_back(scale_one, unit_one, gain_one, wide(normed_grad))
+    grad_tokens = narrow(residual_grad + input_grad)
+    return (
+        layer_out,
+        grad_tokens,
+        grad_query,
+        grad_key,
+        grad_value,
+        grad_output,
+        gate_sum,
+        up_sum,
+        down_sum,
+        grad_first,
+        grad_gains[:, 0],
+        grad_gains[:, 1],
+        grad_gains[:, 2],
+    )
+
+
 def solution(mesh):
     placed = (
         P(("seq", "ctx"), None),
@@ -361,6 +1257,11 @@
         P(),
         P(("seq", "ctx"), None),
     )
+    n_seq, n_ctx = mesh.shape["seq"], mesh.shape["ctx"]
+    if n_ctx == QUERY_HEAD_COUNT and n_seq == 4:
+        body = partial(head_body, n_seq=n_seq, n_ctx=n_ctx)
+    else:
+        body = context_body
     return jax.shard_map(
         body,
         mesh=mesh,

time: 1840 us -> 724 us (0.39)
  waiting for transfers between devices: 1480 us -> 281 us
  matrix products: 195 us -> 0 us
  Pallas kernels: 0 us -> 171 us
  blocking collectives: 80.7 us -> 0 us
  local copies, waits for them, and re-layouts: 28 us -> 92.9 us
  other arithmetic: 32.7 us -> 97 us
  starting transfers between devices: 2.75 us -> 54.8 us
    reduce_scatter x9 -> x3, waiting for transfers between devices: 910 us -> 47.7 us  [head_body(): lax.psum_scatter(v, 'ctx', scatter_dimension=0, tiled=True)]
    all_gather x11 -> x4, waiting for transfers between devices: 547 us -> 66.7 us  [the longest x3 66.7 us: head_body(): gather = lambda v: lax.all_gather(v, 'ctx', axis=0, tiled=True)]
    dot_general x28 -> x0, matrix products: 195 us -> none  [the longest x1 14.3 us: body(): jnp.einsum('td,fd->tf', cotangent_all, part_down, preferred_element_type=...]
    pallas_call x0 -> x126, Pallas kernels: none -> 171 us  [the longest x14 171 us: call(): pl.pallas_call(body, grid=(steps,), in_specs=in_specs + [ANYWHERE] * len(...]
    ppermute x0 -> x46, waiting for transfers between devices: none -> 153 us  [_send(): return lax.ppermute(value, ('seq', 'ctx'), pairs)]
    unnamed x2 -> x0, blocking collectives: 80.7 us -> none
    ppermute x0 -> x46, starting transfers between devices: none -> 47.7 us  [_send(): return lax.ppermute(value, ('seq', 'ctx'), pairs)]
    another operation x4 -> x28, other arithmetic: 1.38 us -> 36.2 us  [the longest x7 8.84 us: scatter_whole(): sent = jnp.stack([pick(mask), pick(3)])]
  transfers between devices with their start and end apart: 22 -> 54, of which waited for: 21 -> 24; matrix products, arithmetic and copies ran while one was open for 10% -> 22% of each run, Pallas kernels for 0% -> 18%
where the time goes in v2:
time: 724 us; the launch traced here: 712 us
  waiting for transfers between devices  281 us (39%)
  Pallas kernels  171 us (24%)
  other arithmetic  97 us (13%)
  local copies, waits for them, and re-layouts  92.9 us (13%)
  starting transfers between devices  54.8 us (8%)
  between operations  15.4 us (2%)
    pallas_call x14, Pallas kernels, call(): pl.pallas_call(body, grid=(steps,), in_specs=in_specs + [ANYWHERE] * len(...  171 us
    ppermute x46, waiting for transfers between devices, _send(): return lax.ppermute(value, ('seq', 'ctx'), pairs)  153 us
    all_gather x3, waiting for transfers between devices, head_body(): gather = lambda v: lax.all_gather(v, 'ctx', axis=0, tiled=True)  66.7 us
    ppermute x46, starting transfers between devices, _send(): return lax.ppermute(value, ('seq', 'ctx'), pairs)  47.7 us
    reduce_scatter x3, waiting for transfers between devices, head_body(): lax.psum_scatter(v, 'ctx', scatter_dimension=0, tiled=True)  47.7 us
    unnamed x157, local copies, waits for them, and re-layouts  28.1 us
    convert_element_type x10, other arithmetic, narrow(): return value.astype(jnp.bfloat16)  20.3 us
  transfers between devices with their start and end apart: 54, of which 24 were waited for; matrix products, arithmetic and copies ran while one was open for 22% of the time, Pallas kernels for 18%

profile of v2, /device:TPU:3, one launch (start us, length us, event | category | flops | bytes accessed | tf_op | source)
XLA Modules:
  0.0 712.0 jit_solution(2617152700773649053)
XLA Ops:
  22.2 2.3 collective-permute-start.2
  29.4 7.1 collective-permute-done.2
  43.4 3.1 pad_maximum_fusion.1.refs_0_
  47.9 3.2 pad_maximum_fusion.refs_0_
  59.0 3.0 multiply_cosine_fusion
  64.2 6.0 collective-permute-done.9.refs_0_
  70.2 2.4 collective-permute-done.8.refs_0_
  73.4 2.6 copy.147
  76.7 15.5 %all-gather.6.cloned.1.call-done.refs_0_ = bf16[1024,2304]{1,0:T(8,128)(2,1)} async-done(((bf16[128,2304]{1,0:T(8,128)(2,1)}), bf16[1024,2304]{1,0:T(8,128)(2,1)}) %all-gather.6.cloned.1.call-update) | async-done | bytes 4718608 | tf_op jit(solution)/shard_map/all_gather | solution.py:1039
  92.2 9.2 %shard_map.260 = (bf16[1024,2304]{1,0:T(8,128)(2,1)}, bf16[1024,256]{1,0:T(8,128)(2,1)}, bf16[1024,256]{1,0:T(8,128)(2,1)}, f32[8,2304]{1,0:T(8,128)}) custom-call(s32[3]{0:T(128)} %pad_add_fusion.refs_0_, bf16[1024,2304]{1,0:T(8,128)(2,1)} %shard_map.259.refs_1_.refs_4_, bf16[576,640]{1,0:T(8,128)(2,1)} %shard_map.239.refs_1_.refs_0_.refs_2_.refs_6_, ...), custom_call_target="tpu_custom_call" | custom-call | flops 2415919104 | tf_op jit(solution)/shard_map/pallas_call | solution.py:564
  104.8 12.8 %collective-permute-done.11.refs_0_ = bf16[64,2304]{1,0:T(8,128)(2,1)} collective-permute-done((bf16[64,2304]{1,0:T(8,128)(2,1)}, bf16[64,2304]{1,0:T(8,128)(2,1)}, u32[]{:S(2)}, u32[]{:S(2)}) %collective-permute-start.11) | collective-permute-done | bytes 294944 | tf_op jit(solution)/shard_map/ppermute | solution.py:452
  120.5 2.1 broadcast_select_fusion
  122.6 5.9 shard_map.266.refs_0_
  128.8 5.4 collective-permute-done.12.refs_0_
  140.1 2.7 slice_bitcast_fusion.2
  144.3 12.3 %collective-permute-done.13.refs_0_ = bf16[2,64,2304]{2,1,0:T(8,128)(2,1)} collective-permute-done((bf16[2,64,2304]{2,1,0:T(8,128)(2,1)}, bf16[2,64,2304]{2,1,0:T(8,128)(2,1)}, u32[]{:S(2)}, u32[]{:S(2)}) %collective-permute-start.13) | collective-permute-done | bytes 589856 | tf_op jit(solution)/shard_map/ppermute | solution.py:452
  156.6 2.2 pad_maximum_fusion.9.refs_0_
  159.3 2.9 slice_bitcast_fusion.5
  171.8 12.5 %collective-permute-done.15.refs_0_ = bf16[2,2,64,2304]{3,2,1,0:T(8,128)(2,1)} collective-permute-done((bf16[2,2,64,2304]{3,2,1,0:T(8,128)(2,1)}, bf16[2,2,64,2304]{3,2,1,0:T(8,128)(2,1)}, u32[]{:S(2)}, u32[]{:S(2)}) %collective-permute-start.15) | collective-permute-done | bytes 1179680 | tf_op jit(solution)/shard_map/ppermute | solution.py:452
  190.7 2.0 slice_dynamic-update-slice_fusion.1
  193.6 6.3 collective-permute-start.17
  199.9 4.0 collective-permute-done.19.refs_0_
  203.9 2.3 pad_maximum_fusion.5.refs_0_
  210.9 20.9 %shard_map.288 = (bf16[1024,2304]{1,0:T(8,128)(2,1)}, f32[128,2304]{1,0:T(8,128)}) custom-call(s32[3]{0:T(128)} %pad_add_fusion.refs_0_, bf16[8,1024,256]{2,1,0:T(8,128)(2,1)} %shard_map.287.refs_1_, bf16[16,64,2304]{2,1,0:T(8,128)(2,1)} %shard_map.279.refs_1_.refs_0_.refs_2_, bf16[16,64,2304]{2,1,0:T(8,128)(2,1)} %shard_map.285.refs_1_.refs_3_, ...), custom_call_target="tpu_custom_call" | custom-call | flops 9663676416 | tf_op jit(solution)/shard_map/pallas_call | solution.py:564
  231.8 21.7 %shard_map.293 = (bf16[1024,1152]{1,0:T(8,128)(2,1)}, bf16[1024,1152]{1,0:T(8,128)(2,1)}, bf16[1024,1152]{1,0:T(8,128)(2,1)}) custom-call(s32[3]{0:T(128)} %pad_add_fusion.refs_0_, bf16[1024,2304]{1,0:T(8,128)(2,1)} %get-tuple-element.34.refs_1_.refs_0_, bf16[576,1152]{1,0:T(8,128)(2,1)} %refs_4_.1, bf16[576,1152]{1,0:T(8,128)(2,1)} %shard_map.241.refs_1_.refs_3_.refs_5_, ...), custom_call_target="tpu_custom_call" | custom-call | flops 10871635968 | tf_op jit(solution)/shard_map/pallas_call | solution.py:564
  254.5 11.8 %shard_map.297.refs_1_.refs_0_ = bf16[1024,2304]{1,0:T(8,128)(2,1)} custom-call(s32[3]{0:T(128)} %pad_add_fusion.refs_0_, bf16[1024,1152]{1,0:T(8,128)(2,1)} %get-tuple-element.35.refs_1_, bf16[576,1152]{1,0:T(8,128)(2,1)} %shard_map.280.refs_0_.refs_2_.refs_10_, bf16[288,1152]{1,0:T(8,128)(2,1)} %shard_map.282.refs_1_.refs_3_.refs_11_, ...), custom_call_target="tpu_custom_call" | custom-call | flops 5435817984 | tf_op jit(solution)/shard_map/pallas_call | solution.py:564
  272.5 47.7 %reduce-scatter.4.cloned.1.call-done.refs_0_ = bf16[128,2304]{1,0:T(8,128)(2,1)} async-done(((bf16[1024,2304]{1,0:T(8,128)(2,1)}), bf16[128,2304]{1,0:T(8,128)(2,1)}) %reduce-scatter.4.cloned.1.call-update) | async-done | bytes 589840 | tf_op jit(solution)/shard_map/reduce_scatter | solution.py:1040
  321.6 2.1 fusion.25
  326.8 51.2 %all-gather.8.cloned.1.call-done.refs_0_ = bf16[1024,2304]{1,0:T(8,128)(2,1)} async-done(((bf16[128,2304]{1,0:T(8,128)(2,1)}), bf16[1024,2304]{1,0:T(8,128)(2,1)}) %all-gather.8.cloned.1.call-update) | async-done | bytes 4718608 | tf_op jit(solution)/shard_map/all_gather | solution.py:1039
  378.0 30.0 %shard_map.307 = (bf16[1024,1152]{1,0:T(8,128)(2,1)}, bf16[1024,1152]{1,0:T(8,128)(2,1)}, bf16[1024,2304]{1,0:T(8,128)(2,1)}) custom-call(s32[3]{0:T(128)} %pad_add_fusion.refs_0_, bf16[1024,2304]{1,0:T(8,128)(2,1)} %shard_map.306.refs_1_.refs_0_, bf16[1024,1152]{1,0:T(8,128)(2,1)} %get-tuple-element.36.refs_2_, ...), custom_call_target="tpu_custom_call" | custom-call | flops 16307453952 | tf_op jit(solution)/shard_map/pallas_call | solution.py:564
  408.0 10.9 %shard_map.308 = bf16[2304,1152]{1,0:T(8,128)(2,1)} custom-call(bf16[1024,2304]{1,0:T(8,128)(2,1)} %shard_map.306.refs_1_.refs_0_, bf16[1024,1152]{1,0:T(8,128)(2,1)} %get-tuple-element.35.refs_1_, bf16[1024,2304]{1,0:T(8,128)(2,1)} %get-tuple-element.38.refs_2_.refs_0_), custom_call_target="tpu_custom_call" | custom-call | flops 5435817984 | tf_op jit(solution)/shard_map/pallas_call | solution.py:564
  418.9 4.5 fusion.50
  430.6 10.8 %shard_map.309 = bf16[2304,1152]{1,0:T(8,128)(2,1)} custom-call(bf16[1024,2304]{1,0:T(8,128)(2,1)} %get-tuple-element.34.refs_1_.refs_0_, bf16[1024,1152]{1,0:T(8,128)(2,1)} %get-tuple-element.40.refs_1_, bf16[4,576,1152]{2,1,0:T(8,128)(2,1)} %bitcast.185), custom_call_target="tpu_custom_call" | custom-call | flops 5435817984 | tf_op jit(solution)/shard_map/pallas_call | solution.py:564
  441.5 2.0 constant_dynamic-slice_fusion.10
  446.4 10.8 %shard_map.310 = bf16[2304,1152]{1,0:T(8,128)(2,1)} custom-call(bf16[1024,2304]{1,0:T(8,128)(2,1)} %get-tuple-element.34.refs_1_.refs_0_, bf16[1024,1152]{1,0:T(8,128)(2,1)} %get-tuple-element.39.refs_1_, bf16[4,576,1152]{2,1,0:T(8,128)(2,1)} %bitcast.187), custom_call_target="tpu_custom_call" | custom-call | flops 5435817984 | tf_op jit(solution)/shard_map/pallas_call | solution.py:564
  457.2 2.0 constant_dynamic-slice_fusion.12
  461.1 2.3 fusion.29.refs_0_
  464.7 2.3 fusion.30.refs_0_
  468.5 2.0 fusion.23
  473.8 9.3 %shard_map.318.refs_0_ = bf16[8,128,256]{2,1,0:T(8,128)(2,1)} custom-call(s32[3]{0:T(128)} %pad_add_fusion.refs_0_, bf16[128,2304]{1,0:T(8,128)(2,1)} %shard_map.317.refs_1_, bf16[16,64,2304]{2,1,0:T(8,128)(2,1)} %shard_map.279.refs_1_.refs_0_.refs_2_, bf16[16,64,2304]{2,1,0:T(8,128)(2,1)} %shard_map.285.refs_1_.refs_3_), custom_call_target="tpu_custom_call" | custom-call | flops 1207959552 | tf_op jit(solution)/shard_map/pallas_call | solution.py:564
  483.2 6.0 all-to-all-start
  491.6 12.2 %all-to-all-done = bf16[8,128,256]{2,1,0:T(8,128)(2,1)} async-done(((bf16[8,128,256]{2,1,0:T(8,128)(2,1)}), bf16[8,128,256]{2,1,0:T(8,128)(2,1)}, u32[]{:S(2)}, u32[]{:S(2)}) %all-to-all-start) | async-done | bytes 524320 | tf_op jit(solution)/shard_map/all_to_all | solution.py:1173
  503.8 9.0 %shard_map.322 = (bf16[1024,256]{1,0:T(8,128)(2,1)}, f32[1024,256]{1,0:T(8,128)}, f32[1024,256]{1,0:T(8,128)}) custom-call(s32[3]{0:T(128)} %pad_add_fusion.refs_0_, bf16[1024,256]{1,0:T(8,128)(2,1)} %get-tuple-element.30.refs_0_.refs_1_, bf16[1024,256]{1,0:T(8,128)(2,1)} %get-tuple-element.102.refs_1_.refs_2_, ...), custom_call_target="tpu_custom_call" | custom-call | flops 2684354560 | tf_op jit(solution)/shard_map/pallas_call | solution.py:564
  512.8 3.2 collective-permute-start.26
  516.1 17.4 %collective-permute-done.27.refs_0_ = bf16[288,1152]{1,0:T(8,128)(2,1)} collective-permute-done((bf16[288,1152]{1,0:T(8,128)(2,1)}, bf16[288,1152]{1,0:T(8,128)(2,1)}, u32[]{:S(2)}, u32[]{:S(2)}) %collective-permute-start.27) | collective-permute-done | bytes 663584 | tf_op jit(solution)/shard_map/ppermute | solution.py:452
  538.5 8.4 %shard_map.330 = (bf16[1024,512]{1,0:T(8,128)(2,1)}, bf16[1024,2304]{1,0:T(8,128)(2,1)}) custom-call(s32[3]{0:T(128)} %pad_add_fusion.refs_0_, bf16[1024,256]{1,0:T(8,128)(2,1)} %get-tuple-element.41.refs_1_, f32[1024,256]{1,0:T(8,128)} %get-tuple-element.42.refs_2_, f32[1024,256]{1,0:T(8,128)} %shard_map.329.refs_3_, ...), custom_call_target="tpu_custom_call" | custom-call | flops 2415919104 | tf_op jit(solution)/shard_map/pallas_call | solution.py:564
  547.0 3.1 fusion.9.refs_0_
  550.3 3.1 fusion.8.refs_0_
  553.6 5.0 shard_map.336.refs_3_
  558.5 7.5 %shard_map.337.refs_1_ = bf16[2304,640]{1,0:T(8,128)(2,1)} custom-call(bf16[1024,2304]{1,0:T(8,128)(2,1)} %get-tuple-element.45.refs_0_, bf16[1024,512]{1,0:T(8,128)(2,1)} %get-tuple-element.46.refs_1_, bf16[2304,128]{1,0:T(8,128)(2,1)} %pad_bitcast_fusion.refs_2_, bf16[256,2304]{1,0:T(8,128)(2,1)} %shard_map.336.refs_3_), custom_call_target="tpu_custom_call" | custom-call | flops 2415919104 | tf_op jit(solution)/shard_map/pallas_call | solution.py:564
  566.1 3.2 fusion.51
  576.6 3.0 collective-permute-start.32
  579.7 2.0 collective-permute-done.32
  587.9 10.0 %collective-permute-done.31.refs_0_ = bf16[2,288,640]{2,1,0:T(8,128)(2,1)} collective-permute-done((bf16[2,288,640]{2,1,0:T(8,128)(2,1)}, bf16[2,288,640]{2,1,0:T(8,128)(2,1)}, u32[]{:S(2)}, u32[]{:S(2)}) %collective-permute-start.31) | collective-permute-done | bytes 737312 | tf_op jit(solution)/shard_map/ppermute | solution.py:452
  603.1 28.2 %collective-permute-done.36.refs_0_ = bf16[2,64,2304]{2,1,0:T(8,128)(2,1)} collective-permute-done((bf16[2,64,2304]{2,1,0:T(8,128)(2,1)}, bf16[2,64,2304]{2,1,0:T(8,128)(2,1)}, u32[]{:S(2)}, u32[]{:S(2)}) %collective-permute-start.36) | collective-permute-done | bytes 589856 | tf_op jit(solution)/shard_map/ppermute | solution.py:452
  640.2 4.1 bitcast_add_fusion.1
  644.3 2.3 collective-permute-start.41
  646.6 4.5 collective-permute-done.39
  651.2 7.6 %collective-permute-done.40 = bf16[2,72,640]{2,1,0:T(8,128)(2,1)S(1)} collective-permute-done((bf16[2,72,640]{2,1,0:T(8,128)(2,1)S(1)}, bf16[2,72,640]{2,1,0:T(8,128)(2,1)S(1)}, u32[]{:S(2)}, u32[]{:S(2)}) %collective-permute-start.40) | collective-permute-done | bytes 184352 | tf_op jit(solution)/shard_map/ppermute | solution.py:452
  659.1 2.0 collective-permute-start.42
  661.1 4.1 bitcast_add_fusion
  675.2 15.0 %collective-permute-done.44.refs_0_ = bf16[2,64,2304]{2,1,0:T(8,128)(2,1)} collective-permute-done((bf16[2,64,2304]{2,1,0:T(8,128)(2,1)}, bf16[2,64,2304]{2,1,0:T(8,128)(2,1)}, u32[]{:S(2)}, u32[]{:S(2)}) %collective-permute-start.44) | collective-permute-done | bytes 589856 | tf_op jit(solution)/shard_map/ppermute | solution.py:452
  698.0 2.1 collective-permute-done.45.refs_0_
  700.0 2.1 bitcast_add_fusion.6
  (476 shorter events, 161.3 us)
Async XLA Ops:
  7.2 85.1 %all-gather.6.cloned.1.call-start = ((), (), s32[]{:S(2)}) async-start(), calls=%async_computation.4 | async-start | bytes 5308416 | tf_op jit(solution)/shard_map/all_gather | solution.py:1039
  10.7 7.3 %collective-permute-start = (bf16[4,72,640]{2,1,0:T(8,128)(2,1)S(1)}, bf16[4,72,640]{2,1,0:T(8,128)(2,1)S(1)}, u32[]{:S(2)}, u32[]{:S(2)}) collective-permute-start(bf16[4,72,640]{2,1,0:T(8,128)(2,1)S(1)} %dynamic-slice_bitcast_fusion.2), channel_id=1, source_target_pairs={{0,1},{1,0},{2,3},{3,2},{4,5},{5,4},{6,7},{7,6},{8,9},{9,8},{10,11... | collective-permute-start | bytes 1105928 | tf_op jit(solution)/shard_map/ppermute | solution.py:452
  11.4 35.0 %collective-permute-start.6 = (bf16[576,1152]{1,0:T(8,128)(2,1)}, bf16[576,1152]{1,0:T(8,128)(2,1)}, u32[]{:S(2)}, u32[]{:S(2)}) collective-permute-start(bf16[576,1152]{1,0:T(8,128)(2,1)} %refs_7_.1), channel_id=1, source_target_pairs={{0,16},{1,17},{2,18},{3,19},{4,20},{5,21},{6,22},{7,23},{8,24},{9,... | collective-permute-start | bytes 3981320 | tf_op jit(solution)/shard_map/ppermute | solution.py:452
  12.7 30.7 %collective-permute-start.7 = (bf16[576,1152]{1,0:T(8,128)(2,1)}, bf16[576,1152]{1,0:T(8,128)(2,1)}, u32[]{:S(2)}, u32[]{:S(2)}) collective-permute-start(bf16[576,1152]{1,0:T(8,128)(2,1)} %refs_4_.1), channel_id=1, source_target_pairs={{0,8},{1,9},{2,10},{3,11},{4,12},{5,13},{6,14},{7,15},{8,0},{9,1},... | collective-permute-start | bytes 3981320 | tf_op jit(solution)/shard_map/ppermute | solution.py:452
  20.0 7.8 %collective-permute-start.1 = (bf16[2,72,640]{2,1,0:T(8,128)(2,1)}, bf16[2,72,640]{2,1,0:T(8,128)(2,1)}, u32[]{:S(2)}, u32[]{:S(2)}) collective-permute-start(bf16[2,72,640]{2,1,0:T(8,128)(2,1)} %get-tuple-element.112), channel_id=1, source_target_pairs={{0,2},{1,3},{2,4},{3,5},{4,6},{5,7},{6,0},{7,1},{8,10},{9,11},{10,... | collective-permute-start | bytes 552968 | tf_op jit(solution)/shard_map/ppermute | solution.py:452
  22.2 14.3 %collective-permute-start.2 = (bf16[2,72,640]{2,1,0:T(8,128)(2,1)S(1)}, bf16[2,72,640]{2,1,0:T(8,128)(2,1)S(1)}, u32[]{:S(2)}, u32[]{:S(2)}) collective-permute-start(bf16[2,72,640]{2,1,0:T(8,128)(2,1)S(1)} %copy-done.58), channel_id=1, source_target_pairs={{0,4},{1,5},{2,6},{3,7},{4,0},{5,1},{6,2},{7,3},{8,12},{9,13},{10,... | collective-permute-start | bytes 552968 | tf_op jit(solution)/shard_map/ppermute | solution.py:452
  24.5 12.7 %collective-permute-start.3 = (bf16[2,72,640]{2,1,0:T(8,128)(2,1)S(1)}, bf16[2,72,640]{2,1,0:T(8,128)(2,1)S(1)}, u32[]{:S(2)}, u32[]{:S(2)}) collective-permute-start(bf16[2,72,640]{2,1,0:T(8,128)(2,1)S(1)} %copy-done.57), channel_id=1, source_target_pairs={{0,6},{1,7},{2,0},{3,1},{4,2},{5,3},{6,4},{7,5},{8,14},{9,15},{10,... | collective-permute-start | bytes 552968 | tf_op jit(solution)/shard_map/ppermute | solution.py:452
  37.9 173.0 %all-gather.12.cloned.1.call-start = ((), (), s32[]{:S(2)}) async-start(), calls=%async_computation.10 | async-start | bytes 4718592 | tf_op jit(solution)/shard_map/all_gather | solution.py:1105
  40.0 14.0 %collective-permute-start.4 = (bf16[288,640]{1,0:T(8,128)(2,1)}, bf16[288,640]{1,0:T(8,128)(2,1)}, u32[]{:S(2)}, u32[]{:S(2)}) collective-permute-start(bf16[288,640]{1,0:T(8,128)(2,1)} %get-tuple-element.110), channel_id=1, source_target_pairs={{0,8},{1,9},{2,10},{3,11},{4,12},{5,13},{6,14},{7,15},{8,0},{9,1},... | collective-permute-start | bytes 1105928 | tf_op jit(solution)/shard_map/ppermute | solution.py:452
  41.2 9.8 %collective-permute-start.5 = (bf16[288,640]{1,0:T(8,128)(2,1)S(1)}, bf16[288,640]{1,0:T(8,128)(2,1)S(1)}, u32[]{:S(2)}, u32[]{:S(2)}) collective-permute-start(bf16[288,640]{1,0:T(8,128)(2,1)S(1)} %get-tuple-element.109), channel_id=1, source_target_pairs={{0,16},{1,17},{2,18},{3,19},{4,20},{5,21},{6,22},{7,23},{8,24},{9,... | collective-permute-start | bytes 1105928 | tf_op jit(solution)/shard_map/ppermute | solution.py:452
  53.7 16.4 %collective-permute-start.9 = (bf16[2,288,640]{2,1,0:T(8,128)(2,1)}, bf16[2,288,640]{2,1,0:T(8,128)(2,1)}, u32[]{:S(2)}, u32[]{:S(2)}) collective-permute-start(bf16[2,288,640]{2,1,0:T(8,128)(2,1)} %pad_maximum_fusion.15.refs_0_), channel_id=1, source_target_pairs={{0,8},{1,9},{2,10},{3,11},{4,12},{5,13},{6,14},{7,15},{8,0},{9,1},... | collective-permute-start | bytes 2211848 | tf_op jit(solution)/shard_map/ppermute | solution.py:452
  54.0 5.1 copy-start.74
  56.0 16.5 %collective-permute-start.8 = (bf16[2,288,640]{2,1,0:T(8,128)(2,1)S(1)}, bf16[2,288,640]{2,1,0:T(8,128)(2,1)S(1)}, u32[]{:S(2)}, u32[]{:S(2)}) collective-permute-start(bf16[2,288,640]{2,1,0:T(8,128)(2,1)S(1)} %pad_maximum_fusion.14), channel_id=1, source_target_pairs={{0,16},{1,17},{2,18},{3,19},{4,20},{5,21},{6,22},{7,23},{8,24},{9,... | collective-permute-start | bytes 2211848 | tf_op jit(solution)/shard_map/ppermute | solution.py:452
  76.0 155.8 %collective-permute-start.20 = (bf16[2,576,1152]{2,1,0:T(8,128)(2,1)}, bf16[2,576,1152]{2,1,0:T(8,128)(2,1)}, u32[]{:S(2)}, u32[]{:S(2)}) collective-permute-start(bf16[2,576,1152]{2,1,0:T(8,128)(2,1)} %shard_map.289), channel_id=1, source_target_pairs={{0,16},{1,17},{2,18},{3,19},{4,20},{5,21},{6,22},{7,23},{8,24},{9,... | collective-permute-start | bytes 7962632 | tf_op jit(solution)/shard_map/ppermute | solution.py:452
  76.0 155.8 %collective-permute-start.21 = (bf16[2,576,1152]{2,1,0:T(8,128)(2,1)}, bf16[2,576,1152]{2,1,0:T(8,128)(2,1)}, u32[]{:S(2)}, u32[]{:S(2)}) collective-permute-start(bf16[2,576,1152]{2,1,0:T(8,128)(2,1)} %shard_map.290), channel_id=1, source_target_pairs={{0,8},{1,9},{2,10},{3,11},{4,12},{5,13},{6,14},{7,15},{8,0},{9,1},... | collective-permute-start | bytes 7962632 | tf_op jit(solution)/shard_map/ppermute | solution.py:452
  101.4 18.1 %collective-permute-start.10 = (bf16[1024,256]{1,0:T(8,128)(2,1)}, bf16[1024,256]{1,0:T(8,128)(2,1)}, u32[]{:S(2)}, u32[]{:S(2)}) collective-permute-start(bf16[1024,256]{1,0:T(8,128)(2,1)} %get-tuple-element.31.refs_1_.refs_0_), channel_id=1, source_target_pairs={{0,1},{1,0},{2,3},{3,2},{4,5},{5,4},{6,7},{7,6},{8,9},{9,8},{10,11... | collective-permute-start | bytes 1572872 | tf_op jit(solution)/shard_map/ppermute | solution.py:452
  101.8 15.9 %collective-permute-start.11 = (bf16[64,2304]{1,0:T(8,128)(2,1)}, bf16[64,2304]{1,0:T(8,128)(2,1)}, u32[]{:S(2)}, u32[]{:S(2)}) collective-permute-start(bf16[64,2304]{1,0:T(8,128)(2,1)} %shard_map.261), channel_id=1, source_target_pairs={{0,4},{1,5},{2,6},{3,7},{4,0},{5,1},{6,2},{7,3},{8,12},{9,13},{10,... | collective-permute-start | bytes 884744 | tf_op jit(solution)/shard_map/ppermute | solution.py:452
  102.7 14.9 %copy-start.34 = (bf16[64,2304]{1,0:T(8,128)(2,1)S(1)}, bf16[64,2304]{1,0:T(8,128)(2,1)}, u32[]{:S(2)}) copy-start(bf16[64,2304]{1,0:T(8,128)(2,1)} %param.18) | copy-start | bytes 884740
  119.5 14.8 %collective-permute-start.12 = (bf16[2,64,2304]{2,1,0:T(8,128)(2,1)}, bf16[2,64,2304]{2,1,0:T(8,128)(2,1)}, u32[]{:S(2)}, u32[]{:S(2)}) collective-permute-start(bf16[2,64,2304]{2,1,0:T(8,128)(2,1)} %shard_map.263.refs_1_.refs_0_), channel_id=1, source_target_pairs={{0,2},{1,3},{2,0},{3,1},{4,6},{5,7},{6,4},{7,5},{8,10},{9,11},{10,... | collective-permute-start | bytes 1769480 | tf_op jit(solution)/shard_map/ppermute | solution.py:452
  128.6 191.6 %reduce-scatter.4.cloned.1.call-start = ((), (), s32[]{:S(2)}) async-start(), calls=%async_computation.5 | async-start | bytes 5308416 | tf_op jit(solution)/shard_map/reduce_scatter | solution.py:1040
  128.8 5.4 copy-start.35
  142.8 13.8 %collective-permute-start.13 = (bf16[2,64,2304]{2,1,0:T(8,128)(2,1)}, bf16[2,64,2304]{2,1,0:T(8,128)(2,1)}, u32[]{:S(2)}, u32[]{:S(2)}) collective-permute-start(bf16[2,64,2304]{2,1,0:T(8,128)(2,1)} %get-tuple-element.96), channel_id=1, source_target_pairs={{0,16},{1,17},{2,18},{3,19},{4,20},{5,21},{6,22},{7,23},{8,24},{9,... | collective-permute-start | bytes 1769480 | tf_op jit(solution)/shard_map/ppermute | solution.py:452
  144.0 12.6 %copy-start.40 = (bf16[1,2,64,2304]{3,2,1,0:T(8,128)(2,1)S(1)}, bf16[1,2,64,2304]{3,2,1,0:T(8,128)(2,1)}, u32[]{:S(2)}) copy-start(bf16[1,2,64,2304]{3,2,1,0:T(8,128)(2,1)} %get-tuple-element.94) | copy-start | bytes 1769476
  144.0 15.3 %collective-permute-start.14 = (bf16[2,64,2304]{2,1,0:T(8,128)(2,1)}, bf16[2,64,2304]{2,1,0:T(8,128)(2,1)}, u32[]{:S(2)}, u32[]{:S(2)}) collective-permute-start(bf16[2,64,2304]{2,1,0:T(8,128)(2,1)} %get-tuple-element.95), channel_id=1, source_target_pairs={{0,8},{1,9},{2,10},{3,11},{4,12},{5,13},{6,14},{7,15},{8,0},{9,1},... | collective-permute-start | bytes 1769480 | tf_op jit(solution)/shard_map/ppermute | solution.py:452
  158.8 25.5 %collective-permute-start.15 = (bf16[2,2,64,2304]{3,2,1,0:T(8,128)(2,1)}, bf16[2,2,64,2304]{3,2,1,0:T(8,128)(2,1)}, u32[]{:S(2)}, u32[]{:S(2)}) collective-permute-start(bf16[2,2,64,2304]{3,2,1,0:T(8,128)(2,1)} %pad_maximum_fusion.9.refs_0_), channel_id=1, source_target_pairs={{0,8},{1,9},{2,10},{3,11},{4,12},{5,13},{6,14},{7,15},{8,0},{9,1},... | collective-permute-start | bytes 3538952 | tf_op jit(solution)/shard_map/ppermute | solution.py:452
  164.5 25.2 %collective-permute-start.16 = (bf16[2,2,64,2304]{3,2,1,0:T(8,128)(2,1)S(1)}, bf16[2,2,64,2304]{3,2,1,0:T(8,128)(2,1)S(1)}, u32[]{:S(2)}, u32[]{:S(2)}) collective-permute-start(bf16[2,2,64,2304]{3,2,1,0:T(8,128)(2,1)S(1)} %pad_maximum_fusion.10), channel_id=1, source_target_pairs={{0,16},{1,17},{2,18},{3,19},{4,20},{5,21},{6,22},{7,23},{8,24},{9,... | collective-permute-start | bytes 3538952 | tf_op jit(solution)/shard_map/ppermute | solution.py:452
  165.6 41.6 %collective-permute-start.18 = (bf16[288,1152]{1,0:T(8,128)(2,1)}, bf16[288,1152]{1,0:T(8,128)(2,1)}, u32[]{:S(2)}, u32[]{:S(2)}) collective-permute-start(bf16[288,1152]{1,0:T(8,128)(2,1)} %get-tuple-element.87), channel_id=1, source_target_pairs={{0,8},{1,9},{2,10},{3,11},{4,12},{5,13},{6,14},{7,15},{8,0},{9,1},... | collective-permute-start | bytes 1990664 | tf_op jit(solution)/shard_map/ppermute | solution.py:452
  184.3 19.6 %collective-permute-start.19 = (bf16[288,1152]{1,0:T(8,128)(2,1)}, bf16[288,1152]{1,0:T(8,128)(2,1)}, u32[]{:S(2)}, u32[]{:S(2)}) collective-permute-start(bf16[288,1152]{1,0:T(8,128)(2,1)} %get-tuple-element.86), channel_id=1, source_target_pairs={{0,16},{1,17},{2,18},{3,19},{4,20},{5,21},{6,22},{7,23},{8,24},{9,... | collective-permute-start | bytes 1990664 | tf_op jit(solution)/shard_map/ppermute | solution.py:452
  193.6 17.2 %collective-permute-start.17 = (bf16[16,64,2304]{2,1,0:T(8,128)(2,1)}, bf16[16,64,2304]{2,1,0:T(8,128)(2,1)}, u32[]{:S(2)}, u32[]{:S(2)}) collective-permute-start(bf16[16,64,2304]{2,1,0:T(8,128)(2,1)} %shard_map.279.refs_1_.refs_0_.refs_2_), channel_id=1, source_target_pairs={{0,1},{1,0},{2,3},{3,2},{4,5},{5,4},{6,7},{7,6},{8,9},{9,8},{10,11... | collective-permute-start | bytes 14155784 | tf_op jit(solution)/shard_map/ppermute | solution.py:452
  206.2 47.3 %collective-permute-start.22 = (bf16[2,288,1152]{2,1,0:T(8,128)(2,1)}, bf16[2,288,1152]{2,1,0:T(8,128)(2,1)}, u32[]{:S(2)}, u32[]{:S(2)}) collective-permute-start(bf16[2,288,1152]{2,1,0:T(8,128)(2,1)} %pad_maximum_fusion.5.refs_0_), channel_id=1, source_target_pairs={{0,8},{1,9},{2,10},{3,11},{4,12},{5,13},{6,14},{7,15},{8,0},{9,1},... | collective-permute-start | bytes 3981320 | tf_op jit(solution)/shard_map/ppermute | solution.py:452
  209.6 43.9 %collective-permute-start.23 = (bf16[2,288,1152]{2,1,0:T(8,128)(2,1)S(1)}, bf16[2,288,1152]{2,1,0:T(8,128)(2,1)S(1)}, u32[]{:S(2)}, u32[]{:S(2)}) collective-permute-start(bf16[2,288,1152]{2,1,0:T(8,128)(2,1)S(1)} %pad_maximum_fusion.6), channel_id=1, source_target_pairs={{0,16},{1,17},{2,18},{3,19},{4,20},{5,21},{6,22},{7,23},{8,24},{9,... | collective-permute-start | bytes 3981320 | tf_op jit(solution)/shard_map/ppermute | solution.py:452
  266.4 111.6 %all-gather.8.cloned.1.call-start = ((), (), s32[]{:S(2)}) async-start(), calls=%async_computation.6 | async-start | bytes 5308416 | tf_op jit(solution)/shard_map/all_gather | solution.py:1039
  272.5 49.1 %copy-start.30 = (bf16[128,2304]{1,0:T(8,128)(2,1)S(1)}, bf16[128,2304]{1,0:T(8,128)(2,1)}, u32[]{:S(2)}) copy-start(bf16[128,2304]{1,0:T(8,128)(2,1)} %param.27) | copy-start | bytes 1769476
  272.5 49.1 %copy-start.60 = (f32[2304]{0:T(1024)S(1)}, f32[2304]{0:T(1024)}, u32[]{:S(2)}) copy-start(f32[2304]{0:T(1024)} %get-tuple-element.56) | copy-start | bytes 27652
  325.2 142.0 %reduce-scatter.6.cloned.1.call-start = ((), (), s32[]{:S(2)}) async-start(), calls=%async_computation.7 | async-start | bytes 5308416 | tf_op jit(solution)/shard_map/reduce_scatter | solution.py:1040
  426.1 35.0 %collective-permute-start.25 = (bf16[2,288,1152]{2,1,0:T(8,128)(2,1)}, bf16[2,288,1152]{2,1,0:T(8,128)(2,1)}, u32[]{:S(2)}, u32[]{:S(2)}) collective-permute-start(bf16[2,288,1152]{2,1,0:T(8,128)(2,1)} %pad_maximum_fusion.8.refs_0_), channel_id=1, source_target_pairs={{0,8},{1,9},{2,10},{3,11},{4,12},{5,13},{6,14},{7,15},{8,0},{9,1},... | collective-permute-start | bytes 3981320 | tf_op jit(solution)/shard_map/ppermute | solution.py:452
  429.4 35.3 %collective-permute-start.24 = (bf16[2,288,1152]{2,1,0:T(8,128)(2,1)}, bf16[2,288,1152]{2,1,0:T(8,128)(2,1)}, u32[]{:S(2)}, u32[]{:S(2)}) collective-permute-start(bf16[2,288,1152]{2,1,0:T(8,128)(2,1)} %pad_maximum_fusion.7.refs_0_), channel_id=1, source_target_pairs={{0,16},{1,17},{2,18},{3,19},{4,20},{5,21},{6,22},{7,23},{8,24},{9,... | collective-permute-start | bytes 3981320 | tf_op jit(solution)/shard_map/ppermute | solution.py:452
  445.2 101.8 %collective-permute-start.30 = (bf16[2,576,1152]{2,1,0:T(8,128)(2,1)}, bf16[2,576,1152]{2,1,0:T(8,128)(2,1)}, u32[]{:S(2)}, u32[]{:S(2)}) collective-permute-start(bf16[2,576,1152]{2,1,0:T(8,128)(2,1)} %pad_maximum_fusion.4.refs_0_), channel_id=1, source_target_pairs={{0,8},{1,9},{2,10},{3,11},{4,12},{5,13},{6,14},{7,15},{8,0},{9,1},... | collective-permute-start | bytes 7962632 | tf_op jit(solution)/shard_map/ppermute | solution.py:452
  460.9 89.4 %collective-permute-start.29 = (bf16[2,576,1152]{2,1,0:T(8,128)(2,1)}, bf16[2,576,1152]{2,1,0:T(8,128)(2,1)}, u32[]{:S(2)}, u32[]{:S(2)}) collective-permute-start(bf16[2,576,1152]{2,1,0:T(8,128)(2,1)} %pad_maximum_fusion.3.refs_0_), channel_id=1, source_target_pairs={{0,16},{1,17},{2,18},{3,19},{4,20},{5,21},{6,22},{7,23},{8,24},{9,... | collective-permute-start | bytes 7962632 | tf_op jit(solution)/shard_map/ppermute | solution.py:452
  463.4 70.0 %collective-permute-start.27 = (bf16[288,1152]{1,0:T(8,128)(2,1)}, bf16[288,1152]{1,0:T(8,128)(2,1)}, u32[]{:S(2)}, u32[]{:S(2)}) collective-permute-start(bf16[288,1152]{1,0:T(8,128)(2,1)} %fusion.29.refs_0_), channel_id=1, source_target_pairs={{0,16},{1,17},{2,18},{3,19},{4,20},{5,21},{6,22},{7,23},{8,24},{9,... | collective-permute-start | bytes 1990664 | tf_op jit(solution)/shard_map/ppermute | solution.py:452
  467.0 68.2 %collective-permute-start.28 = (bf16[288,1152]{1,0:T(8,128)(2,1)}, bf16[288,1152]{1,0:T(8,128)(2,1)}, u32[]{:S(2)}, u32[]{:S(2)}) collective-permute-start(bf16[288,1152]{1,0:T(8,128)(2,1)} %fusion.30.refs_0_), channel_id=1, source_target_pairs={{0,8},{1,9},{2,10},{3,11},{4,12},{5,13},{6,14},{7,15},{8,0},{9,1},... | collective-permute-start | bytes 1990664 | tf_op jit(solution)/shard_map/ppermute | solution.py:452
  483.2 20.6 %all-to-all-start = ((bf16[8,128,256]{2,1,0:T(8,128)(2,1)}), bf16[8,128,256]{2,1,0:T(8,128)(2,1)}, u32[]{:S(2)}, u32[]{:S(2)}) async-start(bf16[8,128,256]{2,1,0:T(8,128)(2,1)} %shard_map.319.refs_0_.refs_1_), calls=%async_computation.2 | async-start | bytes 1048576 | tf_op jit(solution)/shard_map/all_to_all | solution.py:1173
  489.2 64.4 %all-gather.10.cloned.1.call-start = ((), (), s32[]{:S(2)}) async-start(), calls=%async_computation.9 | async-start | bytes 5308416 | tf_op jit(solution)/shard_map/all_gather | solution.py:1039
  489.7 212.5 %reduce-scatter.8.cloned.1.call-start = ((), (), s32[]{:S(2)}) async-start(), calls=%async_computation.8 | async-start | bytes 5308416 | tf_op jit(solution)/shard_map/reduce_scatter | solution.py:1040
  512.8 25.7 %collective-permute-start.26 = (f32[1024,256]{1,0:T(8,128)}, f32[1024,256]{1,0:T(8,128)}, u32[]{:S(2)}, u32[]{:S(2)}) collective-permute-start(f32[1024,256]{1,0:T(8,128)} %get-tuple-element.43.refs_0_), channel_id=1, source_target_pairs={{0,1},{1,0},{2,3},{3,2},{4,5},{5,4},{6,7},{7,6},{8,9},{9,8},{10,11... | collective-permute-start | bytes 3145736 | tf_op jit(solution)/shard_map/ppermute | solution.py:452
  550.1 83.1 %collective-permute-start.35 = (bf16[576,1152]{1,0:T(8,128)(2,1)}, bf16[576,1152]{1,0:T(8,128)(2,1)}, u32[]{:S(2)}, u32[]{:S(2)}) collective-permute-start(bf16[576,1152]{1,0:T(8,128)(2,1)} %fusion.9.refs_0_), channel_id=1, source_target_pairs={{0,16},{1,17},{2,18},{3,19},{4,20},{5,21},{6,22},{7,23},{8,24},{9,... | collective-permute-start | bytes 3981320 | tf_op jit(solution)/shard_map/ppermute | solution.py:452
  553.4 79.8 %collective-permute-start.34 = (bf16[576,1152]{1,0:T(8,128)(2,1)}, bf16[576,1152]{1,0:T(8,128)(2,1)}, u32[]{:S(2)}, u32[]{:S(2)}) collective-permute-start(bf16[576,1152]{1,0:T(8,128)(2,1)} %fusion.8.refs_0_), channel_id=1, source_target_pairs={{0,8},{1,9},{2,10},{3,11},{4,12},{5,13},{6,14},{7,15},{8,0},{9,1},... | collective-permute-start | bytes 3981320 | tf_op jit(solution)/shard_map/ppermute | solution.py:452
  570.6 27.3 %collective-permute-start.31 = (bf16[2,288,640]{2,1,0:T(8,128)(2,1)}, bf16[2,288,640]{2,1,0:T(8,128)(2,1)}, u32[]{:S(2)}, u32[]{:S(2)}) collective-permute-start(bf16[2,288,640]{2,1,0:T(8,128)(2,1)} %pad_maximum_fusion.16.refs_0_), channel_id=1, source_target_pairs={{0,8},{1,9},{2,10},{3,11},{4,12},{5,13},{6,14},{7,15},{8,0},{9,1},... | collective-permute-start | bytes 2211848 | tf_op jit(solution)/shard_map/ppermute | solution.py:452
  574.7 26.4 %collective-permute-start.37 = (bf16[2,288,640]{2,1,0:T(8,128)(2,1)}, bf16[2,288,640]{2,1,0:T(8,128)(2,1)}, u32[]{:S(2)}, u32[]{:S(2)}) collective-permute-start(bf16[2,288,640]{2,1,0:T(8,128)(2,1)} %pad_maximum_fusion.17.refs_0_), channel_id=1, source_target_pairs={{0,16},{1,17},{2,18},{3,19},{4,20},{5,21},{6,22},{7,23},{8,24},{9,... | collective-permute-start | bytes 2211848 | tf_op jit(solution)/shard_map/ppermute | solution.py:452
  576.6 5.1 collective-permute-start.32
  586.9 44.5 %collective-permute-start.36 = (bf16[2,64,2304]{2,1,0:T(8,128)(2,1)}, bf16[2,64,2304]{2,1,0:T(8,128)(2,1)}, u32[]{:S(2)}, u32[]{:S(2)}) collective-permute-start(bf16[2,64,2304]{2,1,0:T(8,128)(2,1)} %pad_maximum_fusion.21.refs_0_), channel_id=1, source_target_pairs={{0,4},{1,5},{2,6},{3,7},{4,0},{5,1},{6,2},{7,3},{8,12},{9,13},{10,... | collective-permute-start | bytes 1769480 | tf_op jit(solution)/shard_map/ppermute | solution.py:452
  599.8 33.4 %collective-permute-start.33 = (bf16[288,640]{1,0:T(8,128)(2,1)}, bf16[288,640]{1,0:T(8,128)(2,1)}, u32[]{:S(2)}, u32[]{:S(2)}) collective-permute-start(bf16[288,640]{1,0:T(8,128)(2,1)} %fusion.33.refs_0_), channel_id=1, source_target_pairs={{0,16},{1,17},{2,18},{3,19},{4,20},{5,21},{6,22},{7,23},{8,24},{9,... | collective-permute-start | bytes 1105928 | tf_op jit(solution)/shard_map/ppermute | solution.py:452
  603.0 31.6 %collective-permute-start.38 = (bf16[288,640]{1,0:T(8,128)(2,1)}, bf16[288,640]{1,0:T(8,128)(2,1)}, u32[]{:S(2)}, u32[]{:S(2)}) collective-permute-start(bf16[288,640]{1,0:T(8,128)(2,1)} %fusion.34.refs_0_), channel_id=1, source_target_pairs={{0,8},{1,9},{2,10},{3,11},{4,12},{5,13},{6,14},{7,15},{8,0},{9,1},... | collective-permute-start | bytes 1105928 | tf_op jit(solution)/shard_map/ppermute | solution.py:452
  603.1 29.2 %copy-start.52 = (bf16[1,64,2304]{2,1,0:T(8,128)(2,1)S(1)}, bf16[1,64,2304]{2,1,0:T(8,128)(2,1)}, u32[]{:S(2)}) copy-start(bf16[1,64,2304]{2,1,0:T(8,128)(2,1)} %get-tuple-element.90) | copy-start | bytes 884740
  633.2 33.1 %collective-permute-start.43 = (bf16[2,64,2304]{2,1,0:T(8,128)(2,1)}, bf16[2,64,2304]{2,1,0:T(8,128)(2,1)}, u32[]{:S(2)}, u32[]{:S(2)}) collective-permute-start(bf16[2,64,2304]{2,1,0:T(8,128)(2,1)} %pad_maximum_fusion.22.refs_0_), channel_id=1, source_target_pairs={{0,2},{1,3},{2,0},{3,1},{4,6},{5,7},{6,4},{7,5},{8,10},{9,11},{10,... | collective-permute-start | bytes 1769480 | tf_op jit(solution)/shard_map/ppermute | solution.py:452
  638.8 12.4 %copy-start.32 = (bf16[4,2,72,640]{3,2,1,0:T(8,128)(2,1)S(1)}, bf16[4,2,72,640]{3,2,1,0:T(8,128)(2,1)}, u32[]{:S(2)}) copy-start(bf16[4,2,72,640]{3,2,1,0:T(8,128)(2,1)} %get-tuple-element.106) | copy-start | bytes 2211844
  638.8 12.4 %collective-permute-start.39 = (bf16[2,72,640]{2,1,0:T(8,128)(2,1)S(1)}, bf16[2,72,640]{2,1,0:T(8,128)(2,1)S(1)}, u32[]{:S(2)}, u32[]{:S(2)}) collective-permute-start(bf16[2,72,640]{2,1,0:T(8,128)(2,1)S(1)} %get-tuple-element.105), channel_id=1, source_target_pairs={{0,2},{1,3},{2,4},{3,5},{4,6},{5,7},{6,0},{7,1},{8,10},{9,11},{10,... | collective-permute-start | bytes 552968 | tf_op jit(solution)/shard_map/ppermute | solution.py:452
  644.3 14.5 %collective-permute-start.40 = (bf16[2,72,640]{2,1,0:T(8,128)(2,1)S(1)}, bf16[2,72,640]{2,1,0:T(8,128)(2,1)S(1)}, u32[]{:S(2)}, u32[]{:S(2)}) collective-permute-start(bf16[2,72,640]{2,1,0:T(8,128)(2,1)S(1)} %get-tuple-element.104), channel_id=1, source_target_pairs={{0,4},{1,5},{2,6},{3,7},{4,0},{5,1},{6,2},{7,3},{8,12},{9,13},{10,... | collective-permute-start | bytes 552968 | tf_op jit(solution)/shard_map/ppermute | solution.py:452
  644.3 14.8 %collective-permute-start.41 = (bf16[2,72,640]{2,1,0:T(8,128)(2,1)S(1)}, bf16[2,72,640]{2,1,0:T(8,128)(2,1)S(1)}, u32[]{:S(2)}, u32[]{:S(2)}) collective-permute-start(bf16[2,72,640]{2,1,0:T(8,128)(2,1)S(1)} %get-tuple-element.103), channel_id=1, source_target_pairs={{0,6},{1,7},{2,0},{3,1},{4,2},{5,3},{6,4},{7,5},{8,14},{9,15},{10,... | collective-permute-start | bytes 552968 | tf_op jit(solution)/shard_map/ppermute | solution.py:452
  659.1 6.1 collective-permute-start.42
  675.0 15.2 %collective-permute-start.44 = (bf16[2,64,2304]{2,1,0:T(8,128)(2,1)}, bf16[2,64,2304]{2,1,0:T(8,128)(2,1)}, u32[]{:S(2)}, u32[]{:S(2)}) collective-permute-start(bf16[2,64,2304]{2,1,0:T(8,128)(2,1)} %pad_maximum_fusion.23.refs_0_), channel_id=1, source_target_pairs={{0,8},{1,9},{2,10},{3,11},{4,12},{5,13},{6,14},{7,15},{8,0},{9,1},... | collective-permute-start | bytes 1769480 | tf_op jit(solution)/shard_map/ppermute | solution.py:452
  692.0 8.0 %collective-permute-start.45 = (bf16[64,2304]{1,0:T(8,128)(2,1)}, bf16[64,2304]{1,0:T(8,128)(2,1)}, u32[]{:S(2)}, u32[]{:S(2)}) collective-permute-start(bf16[64,2304]{1,0:T(8,128)(2,1)} %fusion.39.refs_0_), channel_id=1, source_target_pairs={{0,16},{1,17},{2,18},{3,19},{4,20},{5,21},{6,22},{7,23},{8,24},{9,... | collective-permute-start | bytes 884744 | tf_op jit(solution)/shard_map/ppermute | solution.py:452
  697.4 4.8 copy-start.59
  697.4 4.8 copy-start.70
  (65 other events, 129.9 us)
Sparse Core Ops, SparseCore 0:
  38.0 54.2 all-gather.5
  128.7 47.2 all-gather.11
  266.5 53.6 reduce-scatter.3
  325.3 52.6 all-gather.7
  408.1 51.2 reduce-scatter.5
  491.9 52.3 all-gather.9
  553.6 70.7 reduce-scatter.7

commit v3 on v2

--- a/solution.py
+++ b/solution.py
@@ -463,33 +463,16 @@
     def swap(self, value):
         return self._send(value, lambda s, z, k: (s, z, k ^ 1))
 
-    def gather_halves(self, block, gate):
-        half = block.shape[0] // 2
-        low, high = block[:half], block[half:]
+    def gather_halves(self, low, high, gate):
         low_near = self.across(low, 2)
         high_near = self.across(high, 1)
         yield None
-        low_near, high_near = gate(low_near, block), gate(high_near)
+        low_near, high_near = gate(low_near, low), gate(high_near)
         low_two, high_two = jnp.stack([low, low_near]), jnp.stack([high, high_near])
         low_far = self.across(low_two, 1)
         high_far = self.across(high_two, 2)
         yield None
-        yield block, low_near, high_near, gate(low_far, low_two), gate(high_far)
-
-    def place_halves(self, pieces):
-        block, low_near, high_near, low_far, high_far = pieces
-        half = block.shape[0] // 2
-        out = fresh((self.n_seq,) + block.shape, block.dtype, low_near)
-        put = lambda out, piece, mask, at: lax.dynamic_update_slice(
-            out, piece[None], (self.seq ^ mask, at) + (0,) * (block.ndim - 1)
-        )
-        out = lax.dynamic_update_index_in_dim(out, block, self.seq, 0)
-        out = put(out, low_near, 2, 0)
-        out = put(out, high_near, 1, half)
-        out = put(out, low_far[0], 1, 0)
-        out = put(out, low_far[1], 3, 0)
-        out = put(out, high_far[0], 2, half)
-        return put(out, high_far[1], 3, half).reshape((-1,) + block.shape[1:])
+        yield low_near, high_near, gate(low_far, low_two), gate(high_far)
 
     def scatter_whole(self, terms, mask, gate):
         other = 3 - mask
@@ -522,20 +505,12 @@
             out = lax.dynamic_update_index_in_dim(out, got, (self.plane - step) % self.line, 0)
         return out
 
-    def exchange_planes(self, blocks, pin):
-        pick = lambda mask: lax.dynamic_index_in_dim(blocks, self.plane ^ mask, 0, False)
-        sent = jnp.stack([pick(2), pick(3)])
-        near = self.plane_swap(sent, 2)
-        yield None
-        near = pin(near, sent)
-        sent = jnp.stack([pick(1), near[1]])
-        far = self.plane_swap(sent, 1)
-        yield None
-        far = pin(far, sent)
-        out = fresh(blocks.shape, blocks.dtype, far)
-        for mask, block in ((0, pick(0)), (2, near[0]), (1, far[0]), (3, far[1])):
-            out = lax.dynamic_update_index_in_dim(out, block, self.plane ^ mask, 0)
-        yield out
+    def exchange_steps(self, blocks):
+        pick = lambda step: lax.dynamic_index_in_dim(blocks, (self.plane + step) % self.line, 0, False)
+        return jnp.stack([pick(0)] + [self.along(pick(step), step) for step in range(1, self.line)])
+
+    def transpose_chips(self, value):
+        return self._send(value, lambda s, z, k: (z, s, k))
 
     def exchange_cores(self, blocks):
         own = lax.dynamic_index_in_dim(blocks, self.core, 0, False)
@@ -609,18 +584,20 @@
 
 
 def whole_copies(seq, pieces, target):
-    mask, own, near, far = pieces
+    mask, own, near, far, last = pieces
     rows = own.shape[0]
+    near = near.at[pl.ds(0, rows)]
     at = lambda m: target.at[pl.ds(pl.multiple_of((seq ^ m) * rows, 64), rows)]
     other = 3 - mask
-    first, second = far.at[pl.ds(0, rows)], far.at[pl.ds(rows, rows)]
-    return [(own, at(0)), (near, at(mask)), (first, at(other)), (second, at(3))]
+    return [(own, at(0)), (near, at(mask)), (far, at(other)), (last, at(3))]
 
 
 def half_copies(seq, pieces, target):
     own, low_near, high_near, low_far, high_far = pieces
     rows = own.shape[0]
     half = rows // 2
+    last = pl.ds(low_near.shape[0] - half, half)
+    low_near, high_near = low_near.at[last], high_near.at[last]
     at = lambda m, h: target.at[pl.ds(pl.multiple_of((seq ^ m) * rows + h * half, 32), half)]
     return [
         (own, target.at[pl.ds(pl.multiple_of(seq * rows, 64), rows)]),
@@ -747,30 +724,54 @@
     )
 
 
+OUT_ORDER = ((0, 0), (0, 2), (0, 1), (0, 3), (2, 0), (2, 2), (1, 1), (1, 3)) + (
+    ((1, 0), (1, 2), (3, 0), (3, 2), (2, 1), (2, 3), (3, 1), (3, 3))
+)
+
+
 def branch_rows(place, mixed, own, other, tokens, gain_two, gain_three):
     heads, rows, feats = mixed.shape
     blocks, out_rows, width = own.shape
     per_head = feats // (CORES * out_rows)
     own_rows = TILE // CORES
+    planes = 4
 
     def kernel(
-        place_ref, m_ref, own_ref, other_ref, x_ref, two_ref, three_ref, out_ref, mine_ref, w_ref, sems
+        place_ref,
+        m_ref,
+        own_ref,
+        other_ref,
+        x_ref,
+        two_ref,
+        three_ref,
+        out_ref,
+        mine_ref,
+        full_ref,
+        w_ref,
+        sems,
+        full_sem,
     ):
         step = pl.program_id(0)
-        core = place_ref[1]
+        plane, core, seq = place_ref[0], place_ref[1], place_ref[2]
+        keep = pltpu.make_async_copy(w_ref, full_ref, full_sem)
 
         @pl.when(step == 0)
         def _():
-            copies = [(own_ref, w_ref.at[:, core]), (other_ref, w_ref.at[:, 1 - core])]
+            copies = []
+            for i, (m, x) in enumerate(OUT_ORDER):
+                at = (seq ^ m) * planes + (plane ^ x)
+                copies.append((own_ref.at[i], w_ref.at[at, core]))
+                copies.append((other_ref.at[i], w_ref.at[at, 1 - core]))
             for copy in load(copies, sems):
                 copy.wait()
+            keep.start()
 
         branch = 0.0
         for h in range(heads):
             head = w_ref[h * per_head : (h + 1) * per_head].reshape(feats, width)
             branch += dot_nn(m_ref[h], head)
 
-        @pl.when(step == place_ref[0])
+        @pl.when(step == plane)
         def _():
             mine_ref[...] = jnp.where(core == 0, branch[:own_rows], branch[own_rows:])
 
@@ -779,11 +780,15 @@
         scale = lax.rsqrt(jnp.mean(residual * residual, axis=-1, keepdims=True) + epsilon)
         out_ref[...] = (residual * scale * three_ref[...]).astype(BF16)
 
+        @pl.when(step == rows // TILE - 1)
+        def _():
+            keep.wait()
+
     return call(
         kernel,
         rows // TILE,
         [
-            pl.BlockSpec(memory_space=pltpu.SMEM),
+            SCALARS,
             pl.BlockSpec((heads, TILE, feats), lambda i: (0, i, 0)),
             ANYWHERE,
             ANYWHERE,
@@ -791,13 +796,18 @@
             whole(1, width),
             whole(1, width),
         ],
-        [tile(TILE, width), whole(own_rows, width)],
-        [array(BF16, rows, width), array(F32, own_rows, width)],
+        [tile(TILE, width), whole(own_rows, width), ANYWHERE],
+        [
+            array(BF16, rows, width),
+            array(F32, own_rows, width),
+            array(BF16, blocks, CORES, out_rows, width),
+        ],
         2 * heads * rows * feats * width,
         (place, mixed, own, other, tokens, gain_two, gain_three),
         [
             pltpu.VMEM((blocks, CORES, out_rows, width), BF16),
-            pltpu.SemaphoreType.DMA((2,)),
+            pltpu.SemaphoreType.DMA((2 * blocks,)),
+            pltpu.SemaphoreType.DMA,
         ],
     )
 
@@ -807,8 +817,8 @@
     units = gate_pieces[0].shape[1]
 
     def kernel(place_ref, x_ref, *refs):
-        gates, ups = refs[:3], refs[3:6]
-        hidden_ref, gate_ref, up_ref, gw_ref, uw_ref, gate_sems, up_sems = refs[6:]
+        gates, ups = refs[:4], refs[4:8]
+        hidden_ref, gate_ref, up_ref, gw_ref, uw_ref, gate_sems, up_sems = refs[8:]
         seq = place_ref[2]
         gate_copies = whole_copies(seq, (1,) + gates, gw_ref)
         up_copies = whole_copies(seq, (2,) + ups, uw_ref)
@@ -844,7 +854,7 @@
     return call(
         kernel,
         rows // TILE,
-        [SCALARS, tile(TILE, width)] + [ANYWHERE] * 6,
+        [SCALARS, tile(TILE, width)] + [ANYWHERE] * 8,
         [tile(TILE, units)] * 3,
         [array(BF16, rows, units)] * 3,
         4 * rows * width * units,
@@ -879,29 +889,22 @@
     )[0]
 
 
-def mixed_back(place, branch, own, other):
+def mixed_back(branch, w_full):
     rows, width = branch.shape
-    blocks, out_rows, _ = own.shape
     heads = QUERY_HEAD_COUNT
-    per_head = blocks // heads
-    feats = per_head * CORES * out_rows
-
-    def kernel(place_ref, b_ref, own_ref, other_ref, out_ref, w_ref):
-        core = place_ref[1]
-        w_ref[:, pl.ds(core, 1)] = own_ref[...][:, None]
-        w_ref[:, pl.ds(1 - core, 1)] = other_ref[...][:, None]
-        out_ref[0] = mul_nt(b_ref[...], w_ref[...].reshape(feats, width)).astype(BF16)
-
-    blocks_of = pl.BlockSpec((per_head, out_rows, width), lambda i: (i, 0, 0))
+    feats = w_full.shape[0] // heads
+
+    def kernel(b_ref, w_ref, out_ref):
+        out_ref[0] = mul_nt(b_ref[...], w_ref[...]).astype(BF16)
+
     return call(
         kernel,
         heads,
-        [SCALARS, whole(rows, width), blocks_of, blocks_of],
+        [whole(rows, width), tile(feats, width)],
         [pl.BlockSpec((1, rows, feats), lambda i: (i, 0, 0))],
         [array(BF16, heads, rows, feats)],
         2 * rows * width * heads * feats,
-        (place, branch, own, other),
-        [pltpu.VMEM((per_head, CORES, out_rows, width), BF16)],
+        (branch, w_full),
     )[0]
 
 
@@ -910,8 +913,8 @@
     units = gate_factor.shape[1]
 
     def kernel(place_ref, g_ref, gf_ref, uf_ref, *refs):
-        gates, ups, downs = refs[:3], refs[3:6], refs[6:11]
-        gate_ref, up_ref, out_ref, gw_ref, uw_ref, dw_ref, gate_sems, up_sems, down_sems = refs[11:]
+        gates, ups, downs = refs[:4], refs[4:8], refs[8:13]
+        gate_ref, up_ref, out_ref, gw_ref, uw_ref, dw_ref, gate_sems, up_sems, down_sems = refs[13:]
         seq = place_ref[2]
         gate_copies = whole_copies(seq, (1,) + gates, gw_ref)
         up_copies = whole_copies(seq, (2,) + ups, uw_ref)
@@ -942,7 +945,7 @@
     return call(
         kernel,
         rows // TILE,
-        [SCALARS, tile(TILE, width), tile(TILE, units), tile(TILE, units)] + [ANYWHERE] * 11,
+        [SCALARS, tile(TILE, width), tile(TILE, units), tile(TILE, units)] + [ANYWHERE] * 13,
         [tile(TILE, units), tile(TILE, units), tile(TILE, width)],
         [array(BF16, rows, units), array(BF16, rows, units), array(BF16, rows, width)],
         6 * rows * width * units,
@@ -979,6 +982,42 @@
         4 * rows * feats * width,
         (place, query_grad, own, other, cosine, sine) + pieces,
         [pltpu.VMEM((width, wide_columns), BF16), pltpu.SemaphoreType.DMA((7,))],
+    )
+
+
+def own_grads(place, own, other, weights, gain):
+    line, rows, columns = own.shape
+    feats = HEAD_FEATURES
+
+    def kernel(place_ref, own_ref, other_ref, wq, wk, wv, g_ref, dq, dk, dv, gains_ref, first_ref):
+        front = place_ref[1] == 0
+        total, first = 0.0, 0.0
+        for step in range(line):
+            plane = (place_ref[0] + (line - step)) % line
+            a, b = own_ref[step].astype(F32), other_ref[step].astype(F32)
+            pair = jnp.where(front, a, b), jnp.where(front, b, a)
+            total += a[:, 2 * feats :] + b[:, 2 * feats :]
+            at = pl.ds(pl.multiple_of(plane * feats, feats), feats)
+            for core, (out, w) in enumerate(((dk, wk), (dv, wv))):
+                value = pair[core][:, feats : 2 * feats]
+                out[:, at] = value
+                first += jnp.sum(w[:, at].astype(F32) * value, axis=1, keepdims=True)
+                spot = pl.ds(pl.multiple_of((plane * CORES + core) * feats, feats), feats)
+                value = pair[core][:, :feats]
+                dq[:, spot] = value
+                first += jnp.sum(wq[:, spot].astype(F32) * value, axis=1, keepdims=True)
+        gains_ref[...] = total
+        first_ref[...] = first / g_ref[...].astype(F32)
+
+    shapes = [w.shape for w in weights] + [(rows, columns - 2 * feats), (rows, 1)]
+    return call(
+        kernel,
+        1,
+        [SCALARS, whole(*own.shape), whole(*own.shape)] + [whole(*w.shape) for w in weights] + [whole(rows, 1)],
+        [whole(*s) for s in shapes],
+        [array(F32, *s) for s in shapes],
+        0,
+        (place, own, other) + weights + (gain,),
     )
 
 
@@ -1028,7 +1067,6 @@
     moves = Moves(n_seq, n_ctx)
     order = Order()
     pin, hold = order.pin, order.hold
-    free = lambda v: v
     line = moves.line
     core_zero = moves.core == 0
     rows, width = tokens.shape
@@ -1043,8 +1081,7 @@
     block = w_gate.shape[0]
     half = block // 2
 
-    gate_near = moves.across(w_gate, 1)
-    up_near = moves.across(w_up, 2)
+    out_near = moves.plane_swap(w_output, 2)
     gains_in = jnp.stack([first_gain, second_gain, third_gain, fourth_gain], axis=1)
     gains_in = jnp.pad(gains_in, ((0, 0), (0, pad - 4)))
     by_head = jnp.concatenate(
@@ -1062,15 +1099,17 @@
         axis=3,
     ).transpose(2, 1, 0, 3)
     by_plane = moves.exchange_cores(by_head).transpose(1, 0, 2, 3)
+    down_own = w_down.T
+    near_x = moves.across(jnp.concatenate([w_gate, down_own[half:]]), 1)
+    near_y = moves.across(jnp.concatenate([w_up, down_own[:half]]), 2)
     own_columns = moves.exchange_line(by_plane).reshape(n_ctx * feat_rows, 2 * feats + pad)
     own_columns = pin(own_columns, by_plane)
     tokens_in = hold(tokens)
     tokens_all = gather(tokens_in)
-    columns_move = moves.gather_halves(own_columns, pin)
+    columns_move = moves.gather_halves(own_columns[:half], own_columns[half:], pin)
     next(columns_move)
-    gate_near, up_near = pin(gate_near), pin(up_near)
-    over_y = pin(jnp.stack([w_gate, gate_near]))
-    over_x = pin(jnp.stack([w_up, up_near]))
+    near_x, near_y = pin(near_x), pin(near_y)
+    out_two = pin(jnp.stack([w_output, pin(out_near)]))
     next(columns_move)
 
     block_size = rows // 2
@@ -1084,20 +1123,17 @@
     pair_sine = pin(jnp.where(core_zero, sine, 0.0))
     tables = (cosine, sine, pair_cosine, pair_sine)
 
-    columns = next(columns_move)
-    over_y = moves.across(hold(over_y), 2)
-    over_x = moves.across(hold(over_x), 1)
-    down_own = pin(hold(w_down).T)
+    columns = (own_columns,) + next(columns_move)
+    gate_far = moves.across(hold(w_gate), 2)
+    up_far = moves.across(hold(w_up), 1)
     tokens_all = pin(tokens_all, tokens_in)
-    out_near = moves.plane_swap(hold(w_output), 2)
+    out_two = hold(out_two)
+    out_far = moves.plane_swap(out_two, 1)
 
     normed, query, pair, gains = project_rows(place, tokens_all, columns, feats, tables)
     gain_one, gain_two, gain_three, gain_four = (gains[i : i + 1] for i in range(4))
     pair_other = moves.swap(pair)
     order.mark(pair)
-    out_near = pin(out_near)
-    out_two = pin(jnp.stack([w_output, out_near]))
-    out_far = moves.plane_swap(out_two, 1)
     pair_other = pin(pair_other, pair)
     key = jnp.where(core_zero, pair, pair_other)
     value = jnp.where(core_zero, pair_other, pair)
@@ -1105,28 +1141,32 @@
     mixed_all = lax.all_gather(mixed, "ctx", axis=0)
 
     out_far = pin(out_far, out_two)
-    out_line = fresh((line,) + w_output.shape, w_output.dtype, out_far)
-    for mask, piece in ((0, w_output), (2, out_near), (1, out_far[0]), (3, out_far[1])):
-        out_line = lax.dynamic_update_index_in_dim(out_line, piece, moves.plane ^ mask, 0)
-    out_move = moves.gather_halves(pin(out_line), pin)
-    next(out_move), next(out_move)
-    down_move = moves.gather_halves(hold(down_own), pin)
-    next(down_move)
-    out_own = pin(moves.place_halves(next(out_move)))
+    out_move = moves.gather_halves(out_two, out_far, pin)
+    next(out_move)
+    next(out_move)
+    gate_far, up_far = pin(gate_far), pin(up_far)
+    low_near, high_near, low_far, high_far = next(out_move)
+    gate_last = moves.across(hold(near_x[:block]), 2)
+    up_last = moves.across(hold(near_y[:block]), 1)
+    out_own = jnp.concatenate(
+        [out_two, out_far, low_near, high_near, *(v.reshape(4, *v.shape[2:]) for v in (low_far, high_far))]
+    )
+    out_own = pin(out_own)
     out_other = moves.swap(out_own)
-    next(down_move)
+    low_two = pin(jnp.stack([down_own[:half], near_y[block:]]))
+    high_two = pin(jnp.stack([down_own[half:], near_x[block:]]))
     out_other = pin(out_other, out_own)
     mixed_all = pin(mixed_all, mixed)
-    feed_all, branch = branch_rows(
+    feed_all, branch, w_full = branch_rows(
         place, mixed_all, out_own, out_other, tokens_all, gain_two, gain_three
     )
     order.mark(branch)
-    over_x, over_y = pin(over_x), pin(over_y)
-    gate_pieces = (w_gate, gate_near, over_y.reshape(-1, over_y.shape[2]))
-    up_pieces = (w_up, up_near, over_x.reshape(-1, over_x.shape[2]))
+    gate_pieces = (w_gate, near_x, gate_far, pin(gate_last))
+    up_pieces = (w_up, near_y, up_far, pin(up_last))
+    down_low, down_high = moves.across(hold(low_two), 1), moves.across(hold(high_two), 2)
     hidden, gate_factor, up_factor = feed_open(place, feed_all, gate_pieces, up_pieces)
     order.mark(hidden)
-    down_pieces = next(down_move)
+    down_pieces = (down_own, near_y, near_x, pin(down_low), pin(down_high))
     feed_part = feed_close(place, hidden, down_pieces)
     order.mark(feed_part)
     feed_out = scatter(feed_part)
@@ -1161,7 +1201,6 @@
     order.mark(up_term)
     up_move = moves.scatter_whole(up_term, 2, pin)
     next(up_move)
-    next(down_move)
     feed_input_grad = wide(pin(feed_input_grad, input_part))
     middle_grad, third_term = rms_back(scale_three, unit_three, gain_three, feed_input_grad)
     residual_grad = upstream + middle_grad
@@ -1169,60 +1208,53 @@
     branch_low = pin(narrow(branch_grad))
     branch_all = gather(branch_low)
 
-    mixed_own = pin(mixed_back(place, branch_low, out_own, out_other))
+    mixed_own = pin(mixed_back(branch_low, w_full.reshape(-1, width)))
     mixed_grad = lax.all_to_all(mixed_own, "ctx", split_axis=0, concat_axis=0, tiled=True)
-    mixed_grad = pin(mixed_grad.reshape(-1, feats), mixed_own)
+    next(down_move)
+    mixed_grad = pin(mixed_grad.reshape(-1, feats))
     query_grad, pair_own, pair_send = attend_head_back(
         place, query, key, value, mixed_grad, spot, spots, cosine, sine, order.last
     )
     order.mark(query_grad)
     pair_other = moves.swap(pair_send)
-    down_sum = pin(next(down_move)).T
-    pair_other = pin(pair_other, pair_send)
+    pair_other = pin(pair_other)
     qkv_grad, normed_part = normed_back(
         place, query_grad, pair_own, pair_other, pair_cosine, pair_sine, columns
     )
     order.mark(normed_part)
     normed_grad = scatter(normed_part)
 
-    next(gate_move), next(up_move)
-    branch_all = pin(branch_all)
+    terms = jnp.stack([second_term, third_term, fourth_term])
+    terms = narrow(jnp.pad(terms, ((0, pad - 3), (0, 0))).T)
+    qkv_term = weight_grad(normed, qkv_grad, 384, order.last, terms)
+    order.mark(qkv_term)
+    down_sum = next(down_move).T
+    qkv_move = moves.scatter_halves(qkv_term.reshape(n_seq, width // n_seq, -1), pin)
+    next(qkv_move)
+    branch_all = pin(branch_all, branch_low)
     output_term = weight_grad(mixed, branch_all, feats, order.last)
     order.mark(output_term)
     out_term = output_term.reshape(CORES, CORES, out_rows, width).transpose(1, 0, 2, 3)
     out_term = moves.exchange_cores(out_term).reshape(line, out_rows, width)
-    terms = jnp.stack([second_term, third_term, fourth_term])
-    terms = narrow(jnp.pad(terms, ((0, pad - 3), (0, 0))).T)
-    qkv_term = weight_grad(normed, qkv_grad, 384, order.last, terms)
-    order.mark(qkv_term)
-    qkv_move = moves.scatter_halves(qkv_term.reshape(n_seq, width // n_seq, -1), pin)
     next(qkv_move)
-    out_move = moves.exchange_planes(pin(out_term), pin)
+    next(gate_move), next(up_move)
+    out_move = moves.scatter_whole(pin(out_term), 2, pin)
     next(out_move)
-    next(qkv_move)
+    own_term = pin(narrow(next(qkv_move))).reshape(line, CORES, feat_rows, 2 * feats + pad)
+    own_term = pin(moves.exchange_steps(own_term))
+    own_other = moves.swap(lax.dynamic_index_in_dim(own_term, 1 - moves.core, 1, False))
+    own_term = lax.dynamic_index_in_dim(own_term, moves.core, 1, False)
     next(out_move)
-    gate_sum, up_sum = next(gate_move), next(up_move)
-    own_term = pin(narrow(next(qkv_move))).reshape(line, CORES, feat_rows, 2 * feats + pad)
-    own_term = moves.exchange_line(own_term).transpose(1, 0, 2, 3)
-    out_term = next(out_move)
-    out_move = moves.scatter_whole(out_term, 1, pin)
-    next(out_move)
-    next(out_move)
-    own_term = wide(pin(moves.exchange_cores(own_term)).transpose(2, 1, 0, 3))
-    grad_query = own_term[..., :feats].reshape(feat_rows, -1)
-    grad_key = own_term[:, :, 0, feats : 2 * feats].reshape(feat_rows, -1)
-    grad_value = own_term[:, :, 1, feats : 2 * feats].reshape(feat_rows, -1)
-    grad_gains = jnp.sum(own_term[..., 2 * feats : 2 * feats + 3], axis=(1, 2))
-    grad_first = (
-        jnp.sum(wide(w_query) * grad_query, axis=1)
-        + jnp.sum(wide(w_key) * grad_key, axis=1)
-        + jnp.sum(wide(w_value) * grad_value, axis=1)
-    ) / wide(first_gain)
-    grad_output = next(out_move)
-
+    normed_grad = pin(normed_grad)
     scale_one, unit_one = rms_parts(wide(tokens))
     input_grad, _ = rms_back(scale_one, unit_one, gain_one, wide(normed_grad))
-    grad_tokens = narrow(residual_grad + input_grad)
+    grad_tokens = pin(narrow(residual_grad + input_grad))
+    grad_output = moves.transpose_chips(narrow(next(out_move)))
+    gate_sum, up_sum = next(gate_move), next(up_move)
+    grad_query, grad_key, grad_value, grad_gains, grad_first = own_grads(
+        place, own_term, pin(own_other), (w_query, w_key, w_value), first_gain[:, None]
+    )
+    grad_output = wide(pin(grad_output))
     return (
         layer_out,
         grad_tokens,
@@ -1233,7 +1265,7 @@
         gate_sum,
         up_sum,
         down_sum,
-        grad_first,
+        grad_first[:, 0],
         grad_gains[:, 0],
         grad_gains[:, 1],
         grad_gains[:, 2],

time: 724 us -> 661 us (0.913)
  waiting for transfers between devices: 281 us -> 236 us
  local copies, waits for them, and re-layouts: 92.9 us -> 81.3 us
    ppermute x46 -> x45, waiting for transfers between devices: 153 us -> 114 us  [_send(): return lax.ppermute(value, ('seq', 'ctx'), pairs)]
    dynamic_update_slice x15 -> x0, local copies, waits for them, and re-layouts: 24.3 us -> none  [the longest x6 10.6 us: place_halves(): lax.dynamic_update_slice(out, piece[None], (self.seq ^ mask, at) + (0,) *...]
    all_gather x3, waiting for transfers between devices: 66.7 us -> 53 us  [head_body(): gather = lambda v: lax.all_gather(v, 'ctx', axis=0, tiled=True)]
    all_to_all x1, waiting for transfers between devices: 12.2 us -> 22.3 us  [head_body(): lax.all_to_all(mixed_own, 'ctx', split_axis=0, concat_axis=0, tiled=True)]
    unnamed x157 -> x138, local copies, waits for them, and re-layouts: 28.1 us -> 36.4 us
    ppermute x46 -> x45, starting transfers between devices: 47.7 us -> 43 us  [_send(): return lax.ppermute(value, ('seq', 'ctx'), pairs)]
    pallas_call x14 -> x15, Pallas kernels: 171 us -> 174 us  [call(): pl.pallas_call(body, grid=(steps,), in_specs=in_specs + [ANYWHERE] * len(...]
    convert_element_type x10 -> x11, other arithmetic: 20.3 us -> 21.8 us  [narrow(): return value.astype(jnp.bfloat16)]
  transfers between devices with their start and end apart: 54 -> 53, of which waited for: 24 -> 25; matrix products, arithmetic and copies ran while one was open for 22% -> 22% of each run, Pallas kernels for 18% -> 20%
where the time goes in v3:
time: 661 us; the launch traced here: 651 us
  waiting for transfers between devices  236 us (36%)
  Pallas kernels  174 us (26%)
  other arithmetic  94.4 us (14%)
  local copies, waits for them, and re-layouts  81.3 us (12%)
  starting transfers between devices  49.3 us (7%)
  between operations  15.4 us (2%)
    pallas_call x15, Pallas kernels, call(): pl.pallas_call(body, grid=(steps,), in_specs=in_specs + [ANYWHERE] * len(...  174 us
    ppermute x45, waiting for transfers between devices, _send(): return lax.ppermute(value, ('seq', 'ctx'), pairs)  114 us
    all_gather x3, waiting for transfers between devices, head_body(): gather = lambda v: lax.all_gather(v, 'ctx', axis=0, tiled=True)  53 us
    reduce_scatter x3, waiting for transfers between devices, head_body(): lax.psum_scatter(v, 'ctx', scatter_dimension=0, tiled=True)  46.8 us
    ppermute x45, starting transfers between devices, _send(): return lax.ppermute(value, ('seq', 'ctx'), pairs)  43 us
    unnamed x138, local copies, waits for them, and re-layouts  36.4 us
    all_to_all x1, waiting for transfers between devices, head_body(): lax.all_to_all(mixed_own, 'ctx', split_axis=0, concat_axis=0, tiled=True)  22.3 us
    convert_element_type x11, other arithmetic, narrow(): return value.astype(jnp.bfloat16)  21.8 us
  transfers between devices with their start and end apart: 53, of which 25 were waited for; matrix products, arithmetic and copies ran while one was open for 22% of the time, Pallas kernels for 20%

profile of v3, /device:TPU:3, one launch (start us, length us, event | category | flops | bytes accessed | tf_op | source)
XLA Modules:
  0.0 650.9 jit_solution(17585311184084160953)
XLA Ops:
  12.1 2.3 collective-permute-start.6
  31.9 4.3 collective-permute-done.1
  37.7 7.5 %collective-permute-done.2 = bf16[2,72,640]{2,1,0:T(8,128)(2,1)S(1)} collective-permute-done((bf16[2,72,640]{2,1,0:T(8,128)(2,1)S(1)}, bf16[2,72,640]{2,1,0:T(8,128)(2,1)S(1)}, u32[]{:S(2)}, u32[]{:S(2)}) %collective-permute-start.2) | collective-permute-done | bytes 184352 | tf_op jit(solution)/shard_map/ppermute | solution.py:452
  46.5 2.3 slice_bitcast_fusion.2
  50.6 14.3 %collective-permute-done.8.refs_0_ = bf16[864,1152]{1,0:T(8,128)(2,1)} collective-permute-done((bf16[864,1152]{1,0:T(8,128)(2,1)}, bf16[864,1152]{1,0:T(8,128)(2,1)}, u32[]{:S(2)}, u32[]{:S(2)}) %collective-permute-start.8) | collective-permute-done | bytes 1990688 | tf_op jit(solution)/shard_map/ppermute | solution.py:452
  66.9 3.6 collective-permute-done.5.refs_0_
  70.5 2.0 pad_maximum_fusion.14.refs_0_
  75.6 2.5 slice.140.refs_0_
  78.0 2.5 slice.141.refs_0_
  82.9 3.0 multiply_cosine_fusion
  93.0 5.3 collective-permute-done.9.refs_0_
  103.4 9.2 %shard_map.258 = (bf16[1024,2304]{1,0:T(8,128)(2,1)}, bf16[1024,256]{1,0:T(8,128)(2,1)}, bf16[1024,256]{1,0:T(8,128)(2,1)}, f32[8,2304]{1,0:T(8,128)}) custom-call(s32[3]{0:T(128)} %pad_add_fusion.refs_0_, bf16[1024,2304]{1,0:T(8,128)(2,1)} %shard_map.257.refs_1_.refs_4_, bf16[576,640]{1,0:T(8,128)(2,1)} %shard_map.239.refs_1_.refs_2_.refs_6_, ...), custom_call_target="tpu_custom_call" | custom-call | flops 2415919104 | tf_op jit(solution)/shard_map/pallas_call | solution.py:539
  117.1 2.0 constant_dynamic-update-slice_fusion.5
  119.1 2.1 broadcast_select_fusion
  121.2 5.9 shard_map.261.refs_0_
  129.2 12.3 %collective-permute-done.13.refs_0_ = bf16[2,64,2304]{2,1,0:T(8,128)(2,1)} collective-permute-done((bf16[2,64,2304]{2,1,0:T(8,128)(2,1)}, bf16[2,64,2304]{2,1,0:T(8,128)(2,1)}, u32[]{:S(2)}, u32[]{:S(2)}) %collective-permute-start.13) | collective-permute-done | bytes 589856 | tf_op jit(solution)/shard_map/ppermute | solution.py:452
  141.4 2.4 pad_maximum_fusion.8.refs_0_
  152.6 15.5 %collective-permute-done.15.refs_0_ = bf16[2,2,64,2304]{3,2,1,0:T(8,128)(2,1)} collective-permute-done((bf16[2,2,64,2304]{3,2,1,0:T(8,128)(2,1)}, bf16[2,2,64,2304]{3,2,1,0:T(8,128)(2,1)}, u32[]{:S(2)}, u32[]{:S(2)}) %collective-permute-start.15) | collective-permute-done | bytes 1179680 | tf_op jit(solution)/shard_map/ppermute | solution.py:452
  168.1 2.4 constant_dynamic-update-slice_fusion.1
  171.5 2.4 constant_dynamic-update-slice_fusion.refs_0_
  173.9 4.4 collective-permute-start.19
  179.8 6.3 collective-permute-done.19.refs_0_
  186.1 21.3 %shard_map.282 = (bf16[1024,2304]{1,0:T(8,128)(2,1)}, f32[128,2304]{1,0:T(8,128)}, bf16[16,2,64,2304]{3,2,1,0:T(8,128)(2,1)}) custom-call(s32[3]{0:T(128)} %pad_add_fusion.refs_0_, bf16[8,1024,256]{2,1,0:T(8,128)(2,1)} %shard_map.281.refs_1_, bf16[16,64,2304]{2,1,0:T(8,128)(2,1)} %shard_map.275.refs_1_.refs_0_.refs_2_, ...), custom_call_target="tpu_custom_call" | custom-call | flops 9663676416 | tf_op jit(solution)/shard_map/pallas_call | solution.py:539
  211.6 21.7 %shard_map.287 = (bf16[1024,1152]{1,0:T(8,128)(2,1)}, bf16[1024,1152]{1,0:T(8,128)(2,1)}, bf16[1024,1152]{1,0:T(8,128)(2,1)}) custom-call(s32[3]{0:T(128)} %pad_add_fusion.refs_0_, bf16[1024,2304]{1,0:T(8,128)(2,1)} %get-tuple-element.40.refs_1_.refs_0_, bf16[576,1152]{1,0:T(8,128)(2,1)} %refs_4_.2, ...), custom_call_target="tpu_custom_call" | custom-call | flops 10871635968 | tf_op jit(solution)/shard_map/pallas_call | solution.py:539
  233.3 6.7 %collective-permute-done.22.refs_0_ = bf16[2,288,1152]{2,1,0:T(8,128)(2,1)S(1)} collective-permute-done((bf16[2,288,1152]{2,1,0:T(8,128)(2,1)}, bf16[2,288,1152]{2,1,0:T(8,128)(2,1)S(1)}, u32[]{:S(2)}, u32[]{:S(2)}) %collective-permute-start.22) | collective-permute-done | bytes 1327136 | tf_op jit(solution)/shard_map/ppermute | solution.py:452
  242.1 11.8 %shard_map.292.refs_1_.refs_0_ = bf16[1024,2304]{1,0:T(8,128)(2,1)} custom-call(s32[3]{0:T(128)} %pad_add_fusion.refs_0_, bf16[1024,1152]{1,0:T(8,128)(2,1)} %get-tuple-element.41.refs_1_, bf16[576,1152]{1,0:T(8,128)(2,1)} %bitcast.161, bf16[864,1152]{1,0:T(8,128)(2,1)} %shard_map.242.refs_1_.refs_7_.refs_3_.refs_9_.refs_13_, ...), custom_call_target="tpu_custom_call" | custom-call | flops 5435817984 | tf_op jit(solution)/shard_map/pallas_call | solution.py:539
  259.9 46.8 %reduce-scatter.4.cloned.1.call-done.refs_0_ = bf16[128,2304]{1,0:T(8,128)(2,1)} async-done(((bf16[1024,2304]{1,0:T(8,128)(2,1)}), bf16[128,2304]{1,0:T(8,128)(2,1)}) %reduce-scatter.4.cloned.1.call-update) | async-done | bytes 589840 | tf_op jit(solution)/shard_map/reduce_scatter | solution.py:1078
  308.2 2.1 fusion.25
  313.3 51.2 %all-gather.8.cloned.1.call-done.refs_0_ = bf16[1024,2304]{1,0:T(8,128)(2,1)} async-done(((bf16[128,2304]{1,0:T(8,128)(2,1)}), bf16[1024,2304]{1,0:T(8,128)(2,1)}) %all-gather.8.cloned.1.call-update) | async-done | bytes 4718608 | tf_op jit(solution)/shard_map/all_gather | solution.py:1077
  364.5 30.4 %shard_map.302 = (bf16[1024,1152]{1,0:T(8,128)(2,1)}, bf16[1024,1152]{1,0:T(8,128)(2,1)}, bf16[1024,2304]{1,0:T(8,128)(2,1)}) custom-call(s32[3]{0:T(128)} %pad_add_fusion.refs_0_, bf16[1024,2304]{1,0:T(8,128)(2,1)} %shard_map.301.refs_1_.refs_0_, bf16[1024,1152]{1,0:T(8,128)(2,1)} %get-tuple-element.42.refs_2_, ...), custom_call_target="tpu_custom_call" | custom-call | flops 16307453952 | tf_op jit(solution)/shard_map/pallas_call | solution.py:539
  395.0 10.9 %shard_map.303 = bf16[2304,1152]{1,0:T(8,128)(2,1)} custom-call(bf16[1024,2304]{1,0:T(8,128)(2,1)} %shard_map.301.refs_1_.refs_0_, bf16[1024,1152]{1,0:T(8,128)(2,1)} %get-tuple-element.41.refs_1_, bf16[1024,2304]{1,0:T(8,128)(2,1)} %get-tuple-element.44.refs_2_.refs_0_), custom_call_target="tpu_custom_call" | custom-call | flops 5435817984 | tf_op jit(solution)/shard_map/pallas_call | solution.py:539
  405.8 4.5 fusion.49
  417.6 10.8 %shard_map.304 = bf16[2304,1152]{1,0:T(8,128)(2,1)} custom-call(bf16[1024,2304]{1,0:T(8,128)(2,1)} %get-tuple-element.40.refs_1_.refs_0_, bf16[1024,1152]{1,0:T(8,128)(2,1)} %get-tuple-element.46.refs_1_, bf16[4,576,1152]{2,1,0:T(8,128)(2,1)} %bitcast.155), custom_call_target="tpu_custom_call" | custom-call | flops 5435817984 | tf_op jit(solution)/shard_map/pallas_call | solution.py:539
  428.4 2.0 constant_dynamic-slice_fusion.8
  433.4 10.8 %shard_map.305 = bf16[2304,1152]{1,0:T(8,128)(2,1)} custom-call(bf16[1024,2304]{1,0:T(8,128)(2,1)} %get-tuple-element.40.refs_1_.refs_0_, bf16[1024,1152]{1,0:T(8,128)(2,1)} %get-tuple-element.45.refs_1_, bf16[4,576,1152]{2,1,0:T(8,128)(2,1)} %bitcast.157), custom_call_target="tpu_custom_call" | custom-call | flops 5435817984 | tf_op jit(solution)/shard_map/pallas_call | solution.py:539
  444.2 2.0 constant_dynamic-slice_fusion.10
  449.4 2.0 fusion.23
  454.8 9.1 %shard_map.309.refs_0_ = bf16[8,128,256]{2,1,0:T(8,128)(2,1)} custom-call(bf16[128,2304]{1,0:T(8,128)(2,1)} %shard_map.308.refs_0_.refs_1_, bf16[2048,2304]{1,0:T(8,128)(2,1)} %bitcast.153), custom_call_target="tpu_custom_call" | custom-call | flops 1207959552 | tf_op jit(solution)/shard_map/pallas_call | solution.py:539
  463.9 5.4 all-to-all-start
  469.6 2.4 fusion.30.refs_0_
  473.2 2.3 fusion.29.refs_0_
  475.8 22.3 %all-to-all-done = bf16[8,128,256]{2,1,0:T(8,128)(2,1)} async-done(((bf16[8,128,256]{2,1,0:T(8,128)(2,1)}), bf16[8,128,256]{2,1,0:T(8,128)(2,1)}, u32[]{:S(2)}, u32[]{:S(2)}) %all-to-all-start) | async-done | bytes 524320 | tf_op jit(solution)/shard_map/all_to_all | solution.py:1212
  498.1 9.0 %shard_map.316 = (bf16[1024,256]{1,0:T(8,128)(2,1)}, f32[1024,256]{1,0:T(8,128)}, f32[1024,256]{1,0:T(8,128)}) custom-call(s32[3]{0:T(128)} %pad_add_fusion.refs_0_, bf16[1024,256]{1,0:T(8,128)(2,1)} %get-tuple-element.36.refs_0_.refs_1_, bf16[1024,256]{1,0:T(8,128)(2,1)} %get-tuple-element.103.refs_1_.refs_2_, ...), custom_call_target="tpu_custom_call" | custom-call | flops 2684354560 | tf_op jit(solution)/shard_map/pallas_call | solution.py:539
  507.1 2.2 collective-permute-start.26
  512.0 8.4 %shard_map.318 = (bf16[1024,512]{1,0:T(8,128)(2,1)}, bf16[1024,2304]{1,0:T(8,128)(2,1)}) custom-call(s32[3]{0:T(128)} %pad_add_fusion.refs_0_, bf16[1024,256]{1,0:T(8,128)(2,1)} %get-tuple-element.48.refs_1_, f32[1024,256]{1,0:T(8,128)} %get-tuple-element.49.refs_2_, f32[1024,256]{1,0:T(8,128)} %shard_map.317.refs_3_, ...), custom_call_target="tpu_custom_call" | custom-call | flops 2415919104 | tf_op jit(solution)/shard_map/pallas_call | solution.py:539
  520.4 7.6 %shard_map.319.refs_1_ = bf16[2304,640]{1,0:T(8,128)(2,1)} custom-call(bf16[1024,2304]{1,0:T(8,128)(2,1)} %get-tuple-element.52.refs_0_, bf16[1024,512]{1,0:T(8,128)(2,1)} %get-tuple-element.53.refs_1_, bf16[2304,128]{1,0:T(8,128)(2,1)} %pad_bitcast_fusion.refs_2_, bf16[1024,2304]{1,0:T(8,128)(2,1)} %get-tuple-element.51.refs_3_), custom_call_target="tpu_custom_call" | custom-call | flops 2415919104 | tf_op jit(solution)/shard_map/pallas_call | solution.py:539
  528.0 3.2 fusion.50
  542.8 5.1 shard_map.326.refs_1_
  547.8 6.8 %collective-permute-done.33.refs_0_ = bf16[2,288,640]{2,1,0:T(8,128)(2,1)S(1)} collective-permute-done((bf16[2,288,640]{2,1,0:T(8,128)(2,1)S(1)}, bf16[2,288,640]{2,1,0:T(8,128)(2,1)S(1)}, u32[]{:S(2)}, u32[]{:S(2)}) %collective-permute-start.33) | collective-permute-done | bytes 737312 | tf_op jit(solution)/shard_map/ppermute | solution.py:452
  560.0 3.2 fusion.9.refs_0_
  563.2 3.1 fusion.8.refs_0_
  569.6 2.3 collective-permute-start.29
  571.9 2.0 collective-permute-done.29
  582.9 2.1 constant_dynamic-slice_fusion
  586.5 6.1 collective-permute-done.39
  592.8 7.4 %collective-permute-done.38 = bf16[2,72,640]{2,1,0:T(8,128)(2,1)} collective-permute-done((bf16[2,72,640]{2,1,0:T(8,128)(2,1)}, bf16[2,72,640]{2,1,0:T(8,128)(2,1)}, u32[]{:S(2)}, u32[]{:S(2)}) %collective-permute-start.38) | collective-permute-done | bytes 184352 | tf_op jit(solution)/shard_map/ppermute | solution.py:452
  600.2 2.1 pad_maximum_fusion.18.refs_0_
  602.3 2.0 dynamic-slice_bitcast_fusion.1
  611.7 4.9 collective-permute-done.43.refs_0_
  617.9 3.7 collective-permute-start.44
  621.9 4.1 bitcast_add_fusion.1
  626.0 4.1 bitcast_add_fusion
  630.0 2.5 shard_map.353
  635.6 5.5 collective-permute-done.44.refs_0_
  (417 shorter events, 147.5 us)
Async XLA Ops:
  7.2 96.2 %all-gather.6.cloned.1.call-start = ((), (), s32[]{:S(2)}) async-start(), calls=%async_computation.4 | async-start | bytes 5308416 | tf_op jit(solution)/shard_map/all_gather | solution.py:1077
  10.5 3.9 copy-start.38
  11.4 14.3 %collective-permute-start = (bf16[4,72,640]{2,1,0:T(8,128)(2,1)}, bf16[4,72,640]{2,1,0:T(8,128)(2,1)}, u32[]{:S(2)}, u32[]{:S(2)}) collective-permute-start(bf16[4,72,640]{2,1,0:T(8,128)(2,1)} %dynamic-slice_bitcast_fusion.3), channel_id=1, source_target_pairs={{0,1},{1,0},{2,3},{3,2},{4,5},{5,4},{6,7},{7,6},{8,9},{9,8},{10,11... | collective-permute-start | bytes 1105928 | tf_op jit(solution)/shard_map/ppermute | solution.py:452
  12.1 52.9 %collective-permute-start.6 = (bf16[64,2304]{1,0:T(8,128)(2,1)}, bf16[64,2304]{1,0:T(8,128)(2,1)}, u32[]{:S(2)}, u32[]{:S(2)}) collective-permute-start(bf16[64,2304]{1,0:T(8,128)(2,1)} %param.18), channel_id=1, source_target_pairs={{0,4},{1,5},{2,6},{3,7},{4,0},{5,1},{6,2},{7,3},{8,12},{9,13},{10,... | collective-permute-start | bytes 884744 | tf_op jit(solution)/shard_map/ppermute | solution.py:452
  17.6 47.3 %collective-permute-start.7 = (bf16[864,1152]{1,0:T(8,128)(2,1)}, bf16[864,1152]{1,0:T(8,128)(2,1)}, u32[]{:S(2)}, u32[]{:S(2)}) collective-permute-start(bf16[864,1152]{1,0:T(8,128)(2,1)} %pad_maximum_fusion.2), channel_id=1, source_target_pairs={{0,16},{1,17},{2,18},{3,19},{4,20},{5,21},{6,22},{7,23},{8,24},{9,... | collective-permute-start | bytes 5971976 | tf_op jit(solution)/shard_map/ppermute | solution.py:452
  20.3 44.7 %collective-permute-start.8 = (bf16[864,1152]{1,0:T(8,128)(2,1)}, bf16[864,1152]{1,0:T(8,128)(2,1)}, u32[]{:S(2)}, u32[]{:S(2)}) collective-permute-start(bf16[864,1152]{1,0:T(8,128)(2,1)} %pad_maximum_fusion.3), channel_id=1, source_target_pairs={{0,8},{1,9},{2,10},{3,11},{4,12},{5,13},{6,14},{7,15},{8,0},{9,1},... | collective-permute-start | bytes 5971976 | tf_op jit(solution)/shard_map/ppermute | solution.py:452
  28.7 7.4 %collective-permute-start.1 = (bf16[2,72,640]{2,1,0:T(8,128)(2,1)}, bf16[2,72,640]{2,1,0:T(8,128)(2,1)}, u32[]{:S(2)}, u32[]{:S(2)}) collective-permute-start(bf16[2,72,640]{2,1,0:T(8,128)(2,1)} %get-tuple-element.115), channel_id=1, source_target_pairs={{0,2},{1,3},{2,4},{3,5},{4,6},{5,7},{6,0},{7,1},{8,10},{9,11},{10,... | collective-permute-start | bytes 552968 | tf_op jit(solution)/shard_map/ppermute | solution.py:452
  30.0 6.1 copy-start.46
  30.9 14.3 %collective-permute-start.2 = (bf16[2,72,640]{2,1,0:T(8,128)(2,1)S(1)}, bf16[2,72,640]{2,1,0:T(8,128)(2,1)S(1)}, u32[]{:S(2)}, u32[]{:S(2)}) collective-permute-start(bf16[2,72,640]{2,1,0:T(8,128)(2,1)S(1)} %copy-done.47), channel_id=1, source_target_pairs={{0,4},{1,5},{2,6},{3,7},{4,0},{5,1},{6,2},{7,3},{8,12},{9,13},{10,... | collective-permute-start | bytes 552968 | tf_op jit(solution)/shard_map/ppermute | solution.py:452
  36.1 9.7 %collective-permute-start.3 = (bf16[2,72,640]{2,1,0:T(8,128)(2,1)S(1)}, bf16[2,72,640]{2,1,0:T(8,128)(2,1)S(1)}, u32[]{:S(2)}, u32[]{:S(2)}) collective-permute-start(bf16[2,72,640]{2,1,0:T(8,128)(2,1)S(1)} %copy-done.46), channel_id=1, source_target_pairs={{0,6},{1,7},{2,0},{3,1},{4,2},{5,3},{6,4},{7,5},{8,14},{9,15},{10,... | collective-permute-start | bytes 552968 | tf_op jit(solution)/shard_map/ppermute | solution.py:452
  48.8 21.7 %collective-permute-start.5 = (bf16[288,640]{1,0:T(8,128)(2,1)}, bf16[288,640]{1,0:T(8,128)(2,1)}, u32[]{:S(2)}, u32[]{:S(2)}) collective-permute-start(bf16[288,640]{1,0:T(8,128)(2,1)} %get-tuple-element.112.refs_0_), channel_id=1, source_target_pairs={{0,16},{1,17},{2,18},{3,19},{4,20},{5,21},{6,22},{7,23},{8,24},{9,... | collective-permute-start | bytes 1105928 | tf_op jit(solution)/shard_map/ppermute | solution.py:452
  49.3 136.9 %all-gather.12.cloned.1.call-start = ((), (), s32[]{:S(2)}) async-start(), calls=%async_computation.10 | async-start | bytes 4718592 | tf_op jit(solution)/shard_map/all_gather | solution.py:1141
  49.3 23.5 %collective-permute-start.4 = (bf16[288,640]{1,0:T(8,128)(2,1)}, bf16[288,640]{1,0:T(8,128)(2,1)}, u32[]{:S(2)}, u32[]{:S(2)}) collective-permute-start(bf16[288,640]{1,0:T(8,128)(2,1)} %get-tuple-element.113), channel_id=1, source_target_pairs={{0,8},{1,9},{2,10},{3,11},{4,12},{5,13},{6,14},{7,15},{8,0},{9,1},... | collective-permute-start | bytes 1105928 | tf_op jit(solution)/shard_map/ppermute | solution.py:452
  66.9 3.6 copy-start.37
  72.5 20.6 %collective-permute-start.10 = (bf16[2,288,640]{2,1,0:T(8,128)(2,1)}, bf16[2,288,640]{2,1,0:T(8,128)(2,1)}, u32[]{:S(2)}, u32[]{:S(2)}) collective-permute-start(bf16[2,288,640]{2,1,0:T(8,128)(2,1)} %pad_maximum_fusion.14.refs_0_), channel_id=1, source_target_pairs={{0,8},{1,9},{2,10},{3,11},{4,12},{5,13},{6,14},{7,15},{8,0},{9,1},... | collective-permute-start | bytes 2211848 | tf_op jit(solution)/shard_map/ppermute | solution.py:452
  81.7 16.7 %collective-permute-start.9 = (bf16[2,288,640]{2,1,0:T(8,128)(2,1)S(1)}, bf16[2,288,640]{2,1,0:T(8,128)(2,1)S(1)}, u32[]{:S(2)}, u32[]{:S(2)}) collective-permute-start(bf16[2,288,640]{2,1,0:T(8,128)(2,1)S(1)} %pad_maximum_fusion.13), channel_id=1, source_target_pairs={{0,16},{1,17},{2,18},{3,19},{4,20},{5,21},{6,22},{7,23},{8,24},{9,... | collective-permute-start | bytes 2211848 | tf_op jit(solution)/shard_map/ppermute | solution.py:452
  99.3 51.4 %collective-permute-start.16 = (bf16[576,1152]{1,0:T(8,128)(2,1)}, bf16[576,1152]{1,0:T(8,128)(2,1)}, u32[]{:S(2)}, u32[]{:S(2)}) collective-permute-start(bf16[576,1152]{1,0:T(8,128)(2,1)} %shard_map.268), channel_id=1, source_target_pairs={{0,8},{1,9},{2,10},{3,11},{4,12},{5,13},{6,14},{7,15},{8,0},{9,1},... | collective-permute-start | bytes 3981320 | tf_op jit(solution)/shard_map/ppermute | solution.py:452
  100.4 50.2 %collective-permute-start.17 = (bf16[576,1152]{1,0:T(8,128)(2,1)}, bf16[576,1152]{1,0:T(8,128)(2,1)}, u32[]{:S(2)}, u32[]{:S(2)}) collective-permute-start(bf16[576,1152]{1,0:T(8,128)(2,1)} %shard_map.269), channel_id=1, source_target_pairs={{0,16},{1,17},{2,18},{3,19},{4,20},{5,21},{6,22},{7,23},{8,24},{9,... | collective-permute-start | bytes 3981320 | tf_op jit(solution)/shard_map/ppermute | solution.py:452
  112.6 6.5 %collective-permute-start.11 = (bf16[1024,256]{1,0:T(8,128)(2,1)}, bf16[1024,256]{1,0:T(8,128)(2,1)}, u32[]{:S(2)}, u32[]{:S(2)}) collective-permute-start(bf16[1024,256]{1,0:T(8,128)(2,1)} %get-tuple-element.37.refs_0_.refs_1_), channel_id=1, source_target_pairs={{0,1},{1,0},{2,3},{3,2},{4,5},{5,4},{6,7},{7,6},{8,9},{9,8},{10,11... | collective-permute-start | bytes 1572872 | tf_op jit(solution)/shard_map/ppermute | solution.py:452
  113.7 15.2 %collective-permute-start.12 = (bf16[2,64,2304]{2,1,0:T(8,128)(2,1)}, bf16[2,64,2304]{2,1,0:T(8,128)(2,1)}, u32[]{:S(2)}, u32[]{:S(2)}) collective-permute-start(bf16[2,64,2304]{2,1,0:T(8,128)(2,1)} %shard_map.263.refs_0_), channel_id=1, source_target_pairs={{0,2},{1,3},{2,0},{3,1},{4,6},{5,7},{6,4},{7,5},{8,10},{9,11},{10,... | collective-permute-start | bytes 1769480 | tf_op jit(solution)/shard_map/ppermute | solution.py:452
  115.0 26.4 %collective-permute-start.13 = (bf16[2,64,2304]{2,1,0:T(8,128)(2,1)}, bf16[2,64,2304]{2,1,0:T(8,128)(2,1)}, u32[]{:S(2)}, u32[]{:S(2)}) collective-permute-start(bf16[2,64,2304]{2,1,0:T(8,128)(2,1)} %shard_map.263.refs_0_), channel_id=1, source_target_pairs={{0,16},{1,17},{2,18},{3,19},{4,20},{5,21},{6,22},{7,23},{8,24},{9,... | collective-permute-start | bytes 1769480 | tf_op jit(solution)/shard_map/ppermute | solution.py:452
  127.2 179.6 %reduce-scatter.4.cloned.1.call-start = ((), (), s32[]{:S(2)}) async-start(), calls=%async_computation.5 | async-start | bytes 5308416 | tf_op jit(solution)/shard_map/reduce_scatter | solution.py:1078
  128.9 15.2 %collective-permute-start.14 = (bf16[2,64,2304]{2,1,0:T(8,128)(2,1)}, bf16[2,64,2304]{2,1,0:T(8,128)(2,1)}, u32[]{:S(2)}, u32[]{:S(2)}) collective-permute-start(bf16[2,64,2304]{2,1,0:T(8,128)(2,1)} %shard_map.265.refs_1_), channel_id=1, source_target_pairs={{0,8},{1,9},{2,10},{3,11},{4,12},{5,13},{6,14},{7,15},{8,0},{9,1},... | collective-permute-start | bytes 1769480 | tf_op jit(solution)/shard_map/ppermute | solution.py:452
  143.8 24.3 %collective-permute-start.15 = (bf16[2,2,64,2304]{3,2,1,0:T(8,128)(2,1)}, bf16[2,2,64,2304]{3,2,1,0:T(8,128)(2,1)}, u32[]{:S(2)}, u32[]{:S(2)}) collective-permute-start(bf16[2,2,64,2304]{3,2,1,0:T(8,128)(2,1)} %pad_maximum_fusion.8.refs_0_), channel_id=1, source_target_pairs={{0,8},{1,9},{2,10},{3,11},{4,12},{5,13},{6,14},{7,15},{8,0},{9,1},... | collective-permute-start | bytes 3538952 | tf_op jit(solution)/shard_map/ppermute | solution.py:452
  145.5 25.0 %collective-permute-start.18 = (bf16[2,2,64,2304]{3,2,1,0:T(8,128)(2,1)S(1)}, bf16[2,2,64,2304]{3,2,1,0:T(8,128)(2,1)S(1)}, u32[]{:S(2)}, u32[]{:S(2)}) collective-permute-start(bf16[2,2,64,2304]{3,2,1,0:T(8,128)(2,1)S(1)} %pad_maximum_fusion.9), channel_id=1, source_target_pairs={{0,16},{1,17},{2,18},{3,19},{4,20},{5,21},{6,22},{7,23},{8,24},{9,... | collective-permute-start | bytes 3538952 | tf_op jit(solution)/shard_map/ppermute | solution.py:452
  173.9 12.2 %collective-permute-start.19 = (bf16[16,64,2304]{2,1,0:T(8,128)(2,1)}, bf16[16,64,2304]{2,1,0:T(8,128)(2,1)}, u32[]{:S(2)}, u32[]{:S(2)}) collective-permute-start(bf16[16,64,2304]{2,1,0:T(8,128)(2,1)} %shard_map.275.refs_1_.refs_0_.refs_2_), channel_id=1, source_target_pairs={{0,1},{1,0},{2,3},{3,2},{4,5},{5,4},{6,7},{7,6},{8,9},{9,8},{10,11... | collective-permute-start | bytes 14155784 | tf_op jit(solution)/shard_map/ppermute | solution.py:452
  178.3 31.1 %collective-permute-start.20 = (bf16[576,1152]{1,0:T(8,128)(2,1)}, bf16[576,1152]{1,0:T(8,128)(2,1)}, u32[]{:S(2)}, u32[]{:S(2)}) collective-permute-start(bf16[576,1152]{1,0:T(8,128)(2,1)} %shard_map.283), channel_id=1, source_target_pairs={{0,16},{1,17},{2,18},{3,19},{4,20},{5,21},{6,22},{7,23},{8,24},{9,... | collective-permute-start | bytes 3981320 | tf_op jit(solution)/shard_map/ppermute | solution.py:452
  179.5 30.8 %collective-permute-start.21 = (bf16[576,1152]{1,0:T(8,128)(2,1)}, bf16[576,1152]{1,0:T(8,128)(2,1)}, u32[]{:S(2)}, u32[]{:S(2)}) collective-permute-start(bf16[576,1152]{1,0:T(8,128)(2,1)} %shard_map.285), channel_id=1, source_target_pairs={{0,8},{1,9},{2,10},{3,11},{4,12},{5,13},{6,14},{7,15},{8,0},{9,1},... | collective-permute-start | bytes 3981320 | tf_op jit(solution)/shard_map/ppermute | solution.py:452
  210.2 29.7 %collective-permute-start.22 = (bf16[2,288,1152]{2,1,0:T(8,128)(2,1)}, bf16[2,288,1152]{2,1,0:T(8,128)(2,1)S(1)}, u32[]{:S(2)}, u32[]{:S(2)}) collective-permute-start(bf16[2,288,1152]{2,1,0:T(8,128)(2,1)} %shard_map.288), channel_id=1, source_target_pairs={{0,8},{1,9},{2,10},{3,11},{4,12},{5,13},{6,14},{7,15},{8,0},{9,1},... | collective-permute-start | bytes 3981320 | tf_op jit(solution)/shard_map/ppermute | solution.py:452
  210.6 30.5 %collective-permute-start.23 = (bf16[2,288,1152]{2,1,0:T(8,128)(2,1)}, bf16[2,288,1152]{2,1,0:T(8,128)(2,1)S(1)}, u32[]{:S(2)}, u32[]{:S(2)}) collective-permute-start(bf16[2,288,1152]{2,1,0:T(8,128)(2,1)} %shard_map.290), channel_id=1, source_target_pairs={{0,16},{1,17},{2,18},{3,19},{4,20},{5,21},{6,22},{7,23},{8,24},{9,... | collective-permute-start | bytes 3981320 | tf_op jit(solution)/shard_map/ppermute | solution.py:452
  253.9 110.6 %all-gather.8.cloned.1.call-start = ((), (), s32[]{:S(2)}) async-start(), calls=%async_computation.6 | async-start | bytes 5308416 | tf_op jit(solution)/shard_map/all_gather | solution.py:1077
  259.9 48.2 %copy-start.28 = (bf16[128,2304]{1,0:T(8,128)(2,1)S(1)}, bf16[128,2304]{1,0:T(8,128)(2,1)}, u32[]{:S(2)}) copy-start(bf16[128,2304]{1,0:T(8,128)(2,1)} %param.27) | copy-start | bytes 1769476
  259.9 48.2 %copy-start.49 = (f32[2304]{0:T(1024)S(1)}, f32[2304]{0:T(1024)}, u32[]{:S(2)}) copy-start(f32[2304]{0:T(1024)} %get-tuple-element.68) | copy-start | bytes 27652
  306.8 3.5 copy-start.1
  306.8 3.5 copy-start.7
  311.8 136.4 %reduce-scatter.6.cloned.1.call-start = ((), (), s32[]{:S(2)}) async-start(), calls=%async_computation.7 | async-start | bytes 5308416 | tf_op jit(solution)/shard_map/reduce_scatter | solution.py:1078
  394.9 147.8 %all-gather.10.cloned.1.call-start = ((), (), s32[]{:S(2)}) async-start(), calls=%async_computation.9 | async-start | bytes 5308416 | tf_op jit(solution)/shard_map/all_gather | solution.py:1077
  413.0 56.5 %collective-permute-start.25 = (bf16[2,288,1152]{2,1,0:T(8,128)(2,1)}, bf16[2,288,1152]{2,1,0:T(8,128)(2,1)}, u32[]{:S(2)}, u32[]{:S(2)}) collective-permute-start(bf16[2,288,1152]{2,1,0:T(8,128)(2,1)} %pad_maximum_fusion.7.refs_0_), channel_id=1, source_target_pairs={{0,8},{1,9},{2,10},{3,11},{4,12},{5,13},{6,14},{7,15},{8,0},{9,1},... | collective-permute-start | bytes 3981320 | tf_op jit(solution)/shard_map/ppermute | solution.py:452
  416.4 56.8 %collective-permute-start.24 = (bf16[2,288,1152]{2,1,0:T(8,128)(2,1)}, bf16[2,288,1152]{2,1,0:T(8,128)(2,1)}, u32[]{:S(2)}, u32[]{:S(2)}) collective-permute-start(bf16[2,288,1152]{2,1,0:T(8,128)(2,1)} %pad_maximum_fusion.6.refs_0_), channel_id=1, source_target_pairs={{0,16},{1,17},{2,18},{3,19},{4,20},{5,21},{6,22},{7,23},{8,24},{9,... | collective-permute-start | bytes 3981320 | tf_op jit(solution)/shard_map/ppermute | solution.py:452
  432.2 127.8 %collective-permute-start.31 = (bf16[2,576,1152]{2,1,0:T(8,128)(2,1)}, bf16[2,576,1152]{2,1,0:T(8,128)(2,1)}, u32[]{:S(2)}, u32[]{:S(2)}) collective-permute-start(bf16[2,576,1152]{2,1,0:T(8,128)(2,1)} %pad_maximum_fusion.1.refs_0_), channel_id=1, source_target_pairs={{0,8},{1,9},{2,10},{3,11},{4,12},{5,13},{6,14},{7,15},{8,0},{9,1},... | collective-permute-start | bytes 7962632 | tf_op jit(solution)/shard_map/ppermute | solution.py:452
  447.9 115.3 %collective-permute-start.30 = (bf16[2,576,1152]{2,1,0:T(8,128)(2,1)}, bf16[2,576,1152]{2,1,0:T(8,128)(2,1)}, u32[]{:S(2)}, u32[]{:S(2)}) collective-permute-start(bf16[2,576,1152]{2,1,0:T(8,128)(2,1)} %pad_maximum_fusion.refs_0_), channel_id=1, source_target_pairs={{0,16},{1,17},{2,18},{3,19},{4,20},{5,21},{6,22},{7,23},{8,24},{9,... | collective-permute-start | bytes 7962632 | tf_op jit(solution)/shard_map/ppermute | solution.py:452
  448.2 3.3 copy-start.29
  448.2 3.2 copy-start.4
  448.2 3.2 copy-start.15
  463.9 34.2 %all-to-all-start = ((bf16[8,128,256]{2,1,0:T(8,128)(2,1)}), bf16[8,128,256]{2,1,0:T(8,128)(2,1)}, u32[]{:S(2)}, u32[]{:S(2)}) async-start(bf16[8,128,256]{2,1,0:T(8,128)(2,1)} %shard_map.310.refs_1_), calls=%async_computation.2 | async-start | bytes 1048576 | tf_op jit(solution)/shard_map/all_to_all | solution.py:1212
  469.3 138.7 %reduce-scatter.8.cloned.1.call-start = ((), (), s32[]{:S(2)}) async-start(), calls=%async_computation.8 | async-start | bytes 5308416 | tf_op jit(solution)/shard_map/reduce_scatter | solution.py:1078
  471.9 64.2 %collective-permute-start.28 = (bf16[288,1152]{1,0:T(8,128)(2,1)}, bf16[288,1152]{1,0:T(8,128)(2,1)}, u32[]{:S(2)}, u32[]{:S(2)}) collective-permute-start(bf16[288,1152]{1,0:T(8,128)(2,1)} %fusion.30.refs_0_), channel_id=1, source_target_pairs={{0,16},{1,17},{2,18},{3,19},{4,20},{5,21},{6,22},{7,23},{8,24},{9,... | collective-permute-start | bytes 1990664 | tf_op jit(solution)/shard_map/ppermute | solution.py:452
  475.5 63.9 %collective-permute-start.27 = (bf16[288,1152]{1,0:T(8,128)(2,1)}, bf16[288,1152]{1,0:T(8,128)(2,1)}, u32[]{:S(2)}, u32[]{:S(2)}) collective-permute-start(bf16[288,1152]{1,0:T(8,128)(2,1)} %fusion.29.refs_0_), channel_id=1, source_target_pairs={{0,8},{1,9},{2,10},{3,11},{4,12},{5,13},{6,14},{7,15},{8,0},{9,1},... | collective-permute-start | bytes 1990664 | tf_op jit(solution)/shard_map/ppermute | solution.py:452
  507.1 4.9 collective-permute-start.26
  532.5 25.2 %collective-permute-start.32 = (bf16[2,288,640]{2,1,0:T(8,128)(2,1)}, bf16[2,288,640]{2,1,0:T(8,128)(2,1)}, u32[]{:S(2)}, u32[]{:S(2)}) collective-permute-start(bf16[2,288,640]{2,1,0:T(8,128)(2,1)} %pad_maximum_fusion.15.refs_0_), channel_id=1, source_target_pairs={{0,16},{1,17},{2,18},{3,19},{4,20},{5,21},{6,22},{7,23},{8,24},{9,... | collective-permute-start | bytes 2211848 | tf_op jit(solution)/shard_map/ppermute | solution.py:452
  537.2 17.4 %collective-permute-start.33 = (bf16[2,288,640]{2,1,0:T(8,128)(2,1)S(1)}, bf16[2,288,640]{2,1,0:T(8,128)(2,1)S(1)}, u32[]{:S(2)}, u32[]{:S(2)}) collective-permute-start(bf16[2,288,640]{2,1,0:T(8,128)(2,1)S(1)} %copy-done.42), channel_id=1, source_target_pairs={{0,8},{1,9},{2,10},{3,11},{4,12},{5,13},{6,14},{7,15},{8,0},{9,1},... | collective-permute-start | bytes 2211848 | tf_op jit(solution)/shard_map/ppermute | solution.py:452
  557.4 21.9 %collective-permute-start.35 = (bf16[288,640]{1,0:T(8,128)(2,1)}, bf16[288,640]{1,0:T(8,128)(2,1)}, u32[]{:S(2)}, u32[]{:S(2)}) collective-permute-start(bf16[288,640]{1,0:T(8,128)(2,1)} %fusion.34.refs_0_), channel_id=1, source_target_pairs={{0,16},{1,17},{2,18},{3,19},{4,20},{5,21},{6,22},{7,23},{8,24},{9,... | collective-permute-start | bytes 1105928 | tf_op jit(solution)/shard_map/ppermute | solution.py:452
  559.6 21.0 %collective-permute-start.36 = (bf16[288,640]{1,0:T(8,128)(2,1)}, bf16[288,640]{1,0:T(8,128)(2,1)}, u32[]{:S(2)}, u32[]{:S(2)}) collective-permute-start(bf16[288,640]{1,0:T(8,128)(2,1)} %fusion.35.refs_0_), channel_id=1, source_target_pairs={{0,8},{1,9},{2,10},{3,11},{4,12},{5,13},{6,14},{7,15},{8,0},{9,1},... | collective-permute-start | bytes 1105928 | tf_op jit(solution)/shard_map/ppermute | solution.py:452
  566.4 59.6 %collective-permute-start.41 = (bf16[576,1152]{1,0:T(8,128)(2,1)}, bf16[576,1152]{1,0:T(8,128)(2,1)}, u32[]{:S(2)}, u32[]{:S(2)}) collective-permute-start(bf16[576,1152]{1,0:T(8,128)(2,1)} %fusion.8.refs_0_), channel_id=1, source_target_pairs={{0,8},{1,9},{2,10},{3,11},{4,12},{5,13},{6,14},{7,15},{8,0},{9,1},... | collective-permute-start | bytes 3981320 | tf_op jit(solution)/shard_map/ppermute | solution.py:452
  569.6 4.3 collective-permute-start.29
  578.1 27.7 %collective-permute-start.34 = (bf16[2,64,2304]{2,1,0:T(8,128)(2,1)}, bf16[2,64,2304]{2,1,0:T(8,128)(2,1)}, u32[]{:S(2)}, u32[]{:S(2)}) collective-permute-start(bf16[2,64,2304]{2,1,0:T(8,128)(2,1)} %pad_maximum_fusion.20.refs_0_), channel_id=1, source_target_pairs={{0,16},{1,17},{2,18},{3,19},{4,20},{5,21},{6,22},{7,23},{8,24},{9,... | collective-permute-start | bytes 1769480 | tf_op jit(solution)/shard_map/ppermute | solution.py:452
  585.0 7.5 %collective-permute-start.39 = (bf16[2,72,640]{2,1,0:T(8,128)(2,1)}, bf16[2,72,640]{2,1,0:T(8,128)(2,1)}, u32[]{:S(2)}, u32[]{:S(2)}) collective-permute-start(bf16[2,72,640]{2,1,0:T(8,128)(2,1)} %get-tuple-element.107), channel_id=1, source_target_pairs={{0,6},{1,7},{2,0},{3,1},{4,2},{5,3},{6,4},{7,5},{8,14},{9,15},{10,... | collective-permute-start | bytes 552968 | tf_op jit(solution)/shard_map/ppermute | solution.py:452
  585.5 14.6 %collective-permute-start.38 = (bf16[2,72,640]{2,1,0:T(8,128)(2,1)}, bf16[2,72,640]{2,1,0:T(8,128)(2,1)}, u32[]{:S(2)}, u32[]{:S(2)}) collective-permute-start(bf16[2,72,640]{2,1,0:T(8,128)(2,1)} %get-tuple-element.108), channel_id=1, source_target_pairs={{0,4},{1,5},{2,6},{3,7},{4,0},{5,1},{6,2},{7,3},{8,12},{9,13},{10,... | collective-permute-start | bytes 552968 | tf_op jit(solution)/shard_map/ppermute | solution.py:452
  585.5 14.6 %collective-permute-start.37 = (bf16[2,72,640]{2,1,0:T(8,128)(2,1)}, bf16[2,72,640]{2,1,0:T(8,128)(2,1)}, u32[]{:S(2)}, u32[]{:S(2)}) collective-permute-start(bf16[2,72,640]{2,1,0:T(8,128)(2,1)} %get-tuple-element.109), channel_id=1, source_target_pairs={{0,2},{1,3},{2,4},{3,5},{4,6},{5,7},{6,0},{7,1},{8,10},{9,11},{10,... | collective-permute-start | bytes 552968 | tf_op jit(solution)/shard_map/ppermute | solution.py:452
  586.5 13.7 %copy-start.43 = (bf16[1,2,72,640]{3,2,1,0:T(8,128)(2,1)S(1)}, bf16[1,2,72,640]{3,2,1,0:T(8,128)(2,1)}, u32[]{:S(2)}) copy-start(bf16[1,2,72,640]{3,2,1,0:T(8,128)(2,1)} %get-tuple-element.106) | copy-start | bytes 552964
  592.5 29.4 %collective-permute-start.42 = (bf16[576,1152]{1,0:T(8,128)(2,1)}, bf16[576,1152]{1,0:T(8,128)(2,1)}, u32[]{:S(2)}, u32[]{:S(2)}) collective-permute-start(bf16[576,1152]{1,0:T(8,128)(2,1)} %fusion.9.refs_0_), channel_id=1, source_target_pairs={{0,16},{1,17},{2,18},{3,19},{4,20},{5,21},{6,22},{7,23},{8,24},{9,... | collective-permute-start | bytes 3981320 | tf_op jit(solution)/shard_map/ppermute | solution.py:452
  604.3 25.7 %collective-permute-start.40 = (bf16[4,72,640]{2,1,0:T(8,128)(2,1)}, bf16[4,72,640]{2,1,0:T(8,128)(2,1)}, u32[]{:S(2)}, u32[]{:S(2)}) collective-permute-start(bf16[4,72,640]{2,1,0:T(8,128)(2,1)} %get-tuple-element.104), channel_id=1, source_target_pairs={{0,1},{1,0},{2,3},{3,2},{4,5},{5,4},{6,7},{7,6},{8,9},{9,8},{10,11... | collective-permute-start | bytes 1105928 | tf_op jit(solution)/shard_map/ppermute | solution.py:452
  607.7 8.9 %collective-permute-start.43 = (bf16[64,2304]{1,0:T(8,128)(2,1)}, bf16[64,2304]{1,0:T(8,128)(2,1)}, u32[]{:S(2)}, u32[]{:S(2)}) collective-permute-start(bf16[64,2304]{1,0:T(8,128)(2,1)} %fusion.38.refs_0_), channel_id=1, source_target_pairs={{0,8},{1,9},{2,10},{3,11},{4,12},{5,13},{6,14},{7,15},{8,0},{9,1},... | collective-permute-start | bytes 884744 | tf_op jit(solution)/shard_map/ppermute | solution.py:452
  617.9 23.2 %collective-permute-start.44 = (bf16[64,2304]{1,0:T(8,128)(2,1)S(1)}, bf16[64,2304]{1,0:T(8,128)(2,1)S(1)}, u32[]{:S(2)}, u32[]{:S(2)}) collective-permute-start(bf16[64,2304]{1,0:T(8,128)(2,1)S(1)} %fusion.31), channel_id=1, source_target_pairs={{0,0},{1,1},{2,8},{3,9},{4,16},{5,17},{6,24},{7,25},{8,2},{9,3},{1... | collective-permute-start | bytes 884744 | tf_op jit(solution)/shard_map/ppermute | solution.py:452
  (53 other events, 83.2 us)
Sparse Core Ops, SparseCore 0:
  49.4 53.9 all-gather.5
  127.3 45.2 all-gather.11
  254.1 52.6 reduce-scatter.3
  311.9 52.5 all-gather.7
  395.1 51.2 reduce-scatter.5
  454.9 62.6 all-gather.9
  533.9 50.2 reduce-scatter.7

commit v4 on v3

--- a/solution.py
+++ b/solution.py
@@ -396,6 +396,22 @@
     )(value, *others)
 
 
+def copied(value, rows, *others):
+    columns = value.shape[1]
+    part = pl.BlockSpec((rows // 4, columns), lambda i: (i, 0))
+
+    def kernel(*refs):
+        refs[-1][...] = refs[0][...]
+
+    return pl.pallas_call(
+        kernel,
+        grid=(4,),
+        in_specs=[part] + [pl.BlockSpec(memory_space=pl.ANY)] * len(others),
+        out_specs=part,
+        out_shape=jax.ShapeDtypeStruct((rows, columns), value.dtype),
+    )(value, *others)
+
+
 def fresh(shape, dtype, *others):
     anywhere = pl.BlockSpec(memory_space=pl.ANY)
     return pl.pallas_call(
@@ -429,6 +445,9 @@
 
     def mark(self, value):
         self.last = (value,)
+
+    def late(self, value, rows):
+        return copied(value, rows, *self.last)
 
     def hold(self, value):
         return after(value, *self.last)
@@ -474,10 +493,10 @@
         yield None
         yield low_near, high_near, gate(low_far, low_two), gate(high_far)
 
-    def scatter_whole(self, terms, mask, gate):
+    def scatter_whole(self, terms, mask, gate, ready=lambda v: v):
         other = 3 - mask
         pick = lambda m: lax.dynamic_index_in_dim(terms, self.seq ^ m, 0, False)
-        sent = jnp.stack([pick(mask), pick(3)])
+        sent = ready(jnp.stack([pick(mask), pick(3)]))
         near = self.across(sent, mask)
         yield None
         near = gate(near, sent)
@@ -486,10 +505,10 @@
         yield None
         yield wide(pick(0)) + wide(near[0]) + wide(gate(far, onward))
 
-    def scatter_halves(self, terms, gate):
+    def scatter_halves(self, terms, gate, ready=lambda v: v):
         half = terms.shape[1] // 2
-        low = self.scatter_whole(terms[:, :half], 1, gate)
-        high = self.scatter_whole(terms[:, half:], 2, gate)
+        low = self.scatter_whole(terms[:, :half], 1, gate, ready)
+        high = self.scatter_whole(terms[:, half:], 2, gate, ready)
         for _ in range(2):
             next(low), next(high)
             yield None
@@ -504,10 +523,6 @@
             got = self.along(sent, step)
             out = lax.dynamic_update_index_in_dim(out, got, (self.plane - step) % self.line, 0)
         return out
-
-    def exchange_steps(self, blocks):
-        pick = lambda step: lax.dynamic_index_in_dim(blocks, (self.plane + step) % self.line, 0, False)
-        return jnp.stack([pick(0)] + [self.along(pick(step), step) for step in range(1, self.line)])
 
     def transpose_chips(self, value):
         return self._send(value, lambda s, z, k: (z, s, k))
@@ -583,11 +598,12 @@
     return started
 
 
-def whole_copies(seq, pieces, target):
+def whole_copies(seq, pieces, target, left):
     mask, own, near, far, last = pieces
     rows = own.shape[0]
     near = near.at[pl.ds(0, rows)]
-    at = lambda m: target.at[pl.ds(pl.multiple_of((seq ^ m) * rows, 64), rows)]
+    columns = pl.ds(left, own.shape[1])
+    at = lambda m: target.at[pl.ds(pl.multiple_of((seq ^ m) * rows, 64), rows), columns]
     other = 3 - mask
     return [(own, at(0)), (near, at(mask)), (far, at(other)), (last, at(3))]
 
@@ -625,7 +641,11 @@
             copies = half_copies(place_ref[2], (own, near_a, near_b, far_a, far_b), w_ref)
             for copy in load(copies, sems):
                 copy.wait()
-            gains_ref[...] = w_ref[:, 2 * feats :].astype(F32).T[:8]
+            pad = wide_columns - 2 * feats
+            rows8 = lax.broadcasted_iota(jnp.int32, (8, pad), 0)
+            columns8 = lax.broadcasted_iota(jnp.int32, (8, pad), 1)
+            picks = (rows8 == columns8).astype(BF16)
+            gains_ref[...] = mul_nt(picks, w_ref[:, 2 * feats :])
 
         x = x_ref[...].astype(F32)
         scale = lax.rsqrt(jnp.mean(x * x, axis=-1, keepdims=True) + epsilon)
@@ -679,12 +699,15 @@
     )[0]
 
 
-def attend_head_back(place, query, key, value, mixed_grad, spot, spots, cosine, sine, others):
+def attend_head_back(
+    place, query, key, value, branch, w_out, spot, spots, cosine, sine, others
+):
     rows, feats = query.shape
+    width = branch.shape[1]
     score_scale = HEAD_FEATURES ** (-0.5)
     steps = rows // TILE
 
-    def kernel(place_ref, q_ref, k_ref, v_ref, g_ref, spot_ref, spots_ref, c_ref, s_ref, *refs):
+    def kernel(place_ref, q_ref, k_ref, v_ref, b_ref, w_ref, spot_ref, spots_ref, c_ref, s_ref, *refs):
         dq, own_ref, send_ref, dk, dv = refs
         step = pl.program_id(0)
 
@@ -693,7 +716,8 @@
             dk[...] = jnp.zeros_like(dk)
             dv[...] = jnp.zeros_like(dv)
 
-        query, keys, grad = q_ref[...], k_ref[...], g_ref[...]
+        query, keys = q_ref[...], k_ref[...]
+        grad = mul_nt(b_ref[...], w_ref[...]).astype(BF16)
         bent, probs = soft_rows(query, keys, spot_ref[...], spots_ref[...])
         prob_grad = mul_nt(grad, v_ref[...])
         delta = jnp.sum(probs * prob_grad, axis=-1, keepdims=True)
@@ -712,13 +736,13 @@
     return call(
         kernel,
         steps,
-        [SCALARS, tile(TILE, feats), whole(rows, feats), whole(rows, feats), tile(TILE, feats)]
-        + [tile(TILE, 1), whole(1, rows)]
+        [SCALARS, tile(TILE, feats), whole(rows, feats), whole(rows, feats), tile(TILE, width)]
+        + [whole(feats, width), tile(TILE, 1), whole(1, rows)]
         + [tile(TILE, feats // 2), tile(TILE, feats // 2)],
         [tile(TILE, feats), whole(rows, feats), whole(rows, feats)],
         [array(BF16, rows, feats), array(F32, rows, feats), array(F32, rows, feats)],
-        10 * rows * rows * feats,
-        (place, query, key, value, mixed_grad, spot, spots, cosine, sine),
+        10 * rows * rows * feats + 2 * rows * width * feats,
+        (place, query, key, value, branch, w_out, spot, spots, cosine, sine),
         [pltpu.VMEM((rows, feats), F32)] * 2,
         others,
     )
@@ -732,7 +756,6 @@
 def branch_rows(place, mixed, own, other, tokens, gain_two, gain_three):
     heads, rows, feats = mixed.shape
     blocks, out_rows, width = own.shape
-    per_head = feats // (CORES * out_rows)
     own_rows = TILE // CORES
     planes = 4
 
@@ -766,10 +789,8 @@
                 copy.wait()
             keep.start()
 
-        branch = 0.0
-        for h in range(heads):
-            head = w_ref[h * per_head : (h + 1) * per_head].reshape(feats, width)
-            branch += dot_nn(m_ref[h], head)
+        rows_in = jnp.concatenate([m_ref[h] for h in range(heads)], axis=1)
+        branch = dot_nn(rows_in, w_ref[...].reshape(heads * feats, width))
 
         @pl.when(step == plane)
         def _():
@@ -818,28 +839,17 @@
 
     def kernel(place_ref, x_ref, *refs):
         gates, ups = refs[:4], refs[4:8]
-        hidden_ref, gate_ref, up_ref, gw_ref, uw_ref, gate_sems, up_sems = refs[8:]
-        seq = place_ref[2]
-        gate_copies = whole_copies(seq, (1,) + gates, gw_ref)
-        up_copies = whole_copies(seq, (2,) + ups, uw_ref)
-        first = pl.program_id(0) == 0
-
-        @pl.when(first)
+        hidden_ref, gate_ref, up_ref, w_ref, sems = refs[8:]
+
+        @pl.when(pl.program_id(0) == 0)
         def _():
-            started = load(gate_copies, gate_sems)
-            load(up_copies, up_sems)
-            for copy in started:
+            copies = whole_copies(place_ref[2], (1,) + gates, w_ref, 0)
+            copies += whole_copies(place_ref[2], (2,) + ups, w_ref, units)
+            for copy in load(copies, sems):
                 copy.wait()
 
-        x = x_ref[...]
-        gate = dot_nn(x, gw_ref[...])
-
-        @pl.when(first)
-        def _():
-            for i, (a, b) in enumerate(up_copies):
-                pltpu.make_async_copy(a, b, up_sems.at[i]).wait()
-
-        up = dot_nn(x, uw_ref[...])
+        both = dot_nn(x_ref[...], w_ref[...])
+        gate, up = both[:, :units], both[:, units:]
         square = gate * gate
         bend = jnp.tanh(GELU_IN * (gate + GELU_CUBE * square * gate))
         half = 0.5 * (1.0 + bend)
@@ -859,7 +869,7 @@
         [array(BF16, rows, units)] * 3,
         4 * rows * width * units,
         (place, feed) + gate_pieces + up_pieces,
-        [pltpu.VMEM((width, units), BF16)] * 2 + [pltpu.SemaphoreType.DMA((4,))] * 2,
+        [pltpu.VMEM((width, 2 * units), BF16), pltpu.SemaphoreType.DMA((8,))],
     )
 
 
@@ -889,42 +899,24 @@
     )[0]
 
 
-def mixed_back(branch, w_full):
-    rows, width = branch.shape
-    heads = QUERY_HEAD_COUNT
-    feats = w_full.shape[0] // heads
-
-    def kernel(b_ref, w_ref, out_ref):
-        out_ref[0] = mul_nt(b_ref[...], w_ref[...]).astype(BF16)
-
-    return call(
-        kernel,
-        heads,
-        [whole(rows, width), tile(feats, width)],
-        [pl.BlockSpec((1, rows, feats), lambda i: (i, 0, 0))],
-        [array(BF16, heads, rows, feats)],
-        2 * rows * width * heads * feats,
-        (branch, w_full),
-    )[0]
-
-
-def feed_back(place, grad, gate_factor, up_factor, gate_pieces, up_pieces, down_pieces):
+def feed_back(
+    place, grad, gate_factor, up_factor, gate_pieces, up_pieces, down_pieces, others
+):
     rows, width = grad.shape
     units = gate_factor.shape[1]
 
     def kernel(place_ref, g_ref, gf_ref, uf_ref, *refs):
         gates, ups, downs = refs[:4], refs[4:8], refs[8:13]
-        gate_ref, up_ref, out_ref, gw_ref, uw_ref, dw_ref, gate_sems, up_sems, down_sems = refs[13:]
+        gate_ref, up_ref, out_ref, w_ref, dw_ref, both_ref, sems, down_sems = refs[13:]
         seq = place_ref[2]
-        gate_copies = whole_copies(seq, (1,) + gates, gw_ref)
-        up_copies = whole_copies(seq, (2,) + ups, uw_ref)
+        copies = whole_copies(seq, (1,) + gates, w_ref, 0)
+        copies += whole_copies(seq, (2,) + ups, w_ref, units)
         first = pl.program_id(0) == 0
 
         @pl.when(first)
         def _():
             started = load(half_copies(seq, downs, dw_ref), down_sems)
-            load(gate_copies, gate_sems)
-            load(up_copies, up_sems)
+            load(copies, sems)
             for copy in started:
                 copy.wait()
 
@@ -933,14 +925,15 @@
         up_low = (hidden_grad * uf_ref[...].astype(F32)).astype(BF16)
         gate_ref[...] = gate_low
         up_ref[...] = up_low
+        both_ref[:, :units] = gate_low
+        both_ref[:, units:] = up_low
 
         @pl.when(first)
         def _():
-            for copies, sems in ((gate_copies, gate_sems), (up_copies, up_sems)):
-                for i, (a, b) in enumerate(copies):
-                    pltpu.make_async_copy(a, b, sems.at[i]).wait()
-
-        out_ref[...] = (mul_nt(gate_low, gw_ref[...]) + mul_nt(up_low, uw_ref[...])).astype(BF16)
+            for i, (a, b) in enumerate(copies):
+                pltpu.make_async_copy(a, b, sems.at[i]).wait()
+
+        out_ref[...] = mul_nt(both_ref[...], w_ref[...]).astype(BF16)
 
     return call(
         kernel,
@@ -950,62 +943,114 @@
         [array(BF16, rows, units), array(BF16, rows, units), array(BF16, rows, width)],
         6 * rows * width * units,
         (place, grad, gate_factor, up_factor) + gate_pieces + up_pieces + down_pieces,
-        [pltpu.VMEM((width, units), BF16)] * 3
-        + [pltpu.SemaphoreType.DMA((4,))] * 2
-        + [pltpu.SemaphoreType.DMA((7,))],
-    )
-
-
-def normed_back(place, query_grad, own, other, cosine, sine, pieces):
+        [
+            pltpu.VMEM((width, 2 * units), BF16),
+            pltpu.VMEM((width, units), BF16),
+            pltpu.VMEM((TILE, 2 * units), BF16),
+            pltpu.SemaphoreType.DMA((8,)),
+            pltpu.SemaphoreType.DMA((7,)),
+        ],
+        others,
+    )
+
+
+def qkv_back(normed, query_grad, own, other, cosine, sine, more, others):
     rows, feats = query_grad.shape
+    width = normed.shape[1]
+    block = 384
+    both_columns = 2 * feats
+
+    def kernel(n_ref, q_ref, own_ref, other_ref, c_ref, s_ref, more_ref, both_ref, out_ref):
+        @pl.when(pl.program_id(0) == 0)
+        def _():
+            pair = turn_pair(own_ref[...] + other_ref[...], c_ref[...], -s_ref[...])
+            both_ref[:, :feats] = q_ref[...]
+            both_ref[:, feats:] = pair.astype(BF16)
+
+        out_ref[:, :both_columns] = mul_tn(n_ref[...], both_ref[...]).astype(BF16)
+        out_ref[:, both_columns:] = more_ref[...]
+
+    total = both_columns + more.shape[1]
+    return call(
+        kernel,
+        width // block,
+        [pl.BlockSpec((rows, block), lambda i: (0, i))]
+        + [whole(rows, feats)] * 3
+        + [whole(rows, feats // 2)] * 2
+        + [tile(block, more.shape[1])],
+        [whole(rows, both_columns), tile(block, total)],
+        [array(BF16, rows, both_columns), array(BF16, width, total)],
+        2 * rows * width * both_columns,
+        (normed, query_grad, own, other, cosine, sine, more),
+        (),
+        others,
+    )
+
+
+def normed_back(place, both, pieces, others):
+    rows, both_columns = both.shape
     width, wide_columns = pieces[0].shape[0] * 4, pieces[0].shape[1]
 
-    def kernel(place_ref, q_ref, own_ref, other_ref, c_ref, s_ref, *refs):
-        both_ref, out_ref, w_ref, sems = refs[5:]
+    def kernel(place_ref, both_ref, *refs):
+        out_ref, w_ref, sems = refs[5:]
 
         @pl.when(pl.program_id(0) == 0)
         def _():
             for copy in load(half_copies(place_ref[2], refs[:5], w_ref), sems):
                 copy.wait()
 
-        pair = turn_pair(own_ref[...] + other_ref[...], c_ref[...], -s_ref[...]).astype(BF16)
-        both_ref[:, :feats] = q_ref[...]
-        both_ref[:, feats:] = pair
-        out_ref[...] = mul_nt(both_ref[...], w_ref[:, : 2 * feats]).astype(BF16)
+        out_ref[...] = mul_nt(both_ref[...], w_ref[:, :both_columns]).astype(BF16)
 
     return call(
         kernel,
         rows // TILE,
-        [SCALARS] + [tile(TILE, feats)] * 3 + [tile(TILE, feats // 2)] * 2 + [ANYWHERE] * 5,
-        [tile(TILE, 2 * feats), tile(TILE, width)],
-        [array(BF16, rows, 2 * feats), array(BF16, rows, width)],
-        4 * rows * feats * width,
-        (place, query_grad, own, other, cosine, sine) + pieces,
+        [SCALARS, tile(TILE, both_columns)] + [ANYWHERE] * 5,
+        [tile(TILE, width)],
+        [array(BF16, rows, width)],
+        2 * rows * both_columns * width,
+        (place, both) + pieces,
         [pltpu.VMEM((width, wide_columns), BF16), pltpu.SemaphoreType.DMA((7,))],
-    )
-
-
-def own_grads(place, own, other, weights, gain):
-    line, rows, columns = own.shape
+        others,
+    )[0]
+
+
+def weight_grad(left, right, block, others):
+    rows, width = left.shape
+    columns = right.shape[1]
+
+    def kernel(left_ref, right_ref, out_ref):
+        out_ref[...] = mul_tn(left_ref[...], right_ref[...]).astype(BF16)
+
+    return call(
+        kernel,
+        width // block,
+        [pl.BlockSpec((rows, block), lambda i: (0, i)), whole(rows, columns)],
+        [tile(block, columns)],
+        [array(BF16, width, columns)],
+        2 * rows * width * columns,
+        (left, right),
+        (),
+        others,
+    )[0]
+
+
+def own_grads(terms, weights, gain):
+    heads, rows, columns = terms.shape
     feats = HEAD_FEATURES
 
-    def kernel(place_ref, own_ref, other_ref, wq, wk, wv, g_ref, dq, dk, dv, gains_ref, first_ref):
-        front = place_ref[1] == 0
+    def kernel(terms_ref, wq, wk, wv, g_ref, dq, dk, dv, gains_ref, first_ref):
         total, first = 0.0, 0.0
-        for step in range(line):
-            plane = (place_ref[0] + (line - step)) % line
-            a, b = own_ref[step].astype(F32), other_ref[step].astype(F32)
-            pair = jnp.where(front, a, b), jnp.where(front, b, a)
-            total += a[:, 2 * feats :] + b[:, 2 * feats :]
-            at = pl.ds(pl.multiple_of(plane * feats, feats), feats)
-            for core, (out, w) in enumerate(((dk, wk), (dv, wv))):
-                value = pair[core][:, feats : 2 * feats]
+        for h in range(heads):
+            term = terms_ref[h].astype(F32)
+            total += term[:, 2 * feats :]
+            pair, w = ((dk, wk), (dv, wv))[h % CORES]
+            group = h // CORES
+            for out, weight, at, value in (
+                (dq, wq, slice(h * feats, (h + 1) * feats), term[:, :feats]),
+                (pair, w, slice(group * feats, (group + 1) * feats), term[:, feats : 2 * feats]),
+            ):
                 out[:, at] = value
-                first += jnp.sum(w[:, at].astype(F32) * value, axis=1, keepdims=True)
-                spot = pl.ds(pl.multiple_of((plane * CORES + core) * feats, feats), feats)
-                value = pair[core][:, :feats]
-                dq[:, spot] = value
-                first += jnp.sum(wq[:, spot].astype(F32) * value, axis=1, keepdims=True)
+                first += jnp.sum(weight[:, at].astype(F32) * value, axis=1, keepdims=True)
         gains_ref[...] = total
         first_ref[...] = first / g_ref[...].astype(F32)
 
@@ -1013,37 +1058,12 @@
     return call(
         kernel,
         1,
-        [SCALARS, whole(*own.shape), whole(*own.shape)] + [whole(*w.shape) for w in weights] + [whole(rows, 1)],
+        [whole(*terms.shape)] + [whole(*w.shape) for w in weights] + [whole(rows, 1)],
         [whole(*s) for s in shapes],
         [array(F32, *s) for s in shapes],
         0,
-        (place, own, other) + weights + (gain,),
-    )
-
-
-def weight_grad(left, right, block, others, more=None):
-    rows, width = left.shape
-    columns = right.shape[1]
-    total = columns + (0 if more is None else more.shape[1])
-
-    def kernel(left_ref, right_ref, *refs):
-        refs[-1][:, :columns] = mul_tn(left_ref[...], right_ref[...]).astype(BF16)
-        if more is not None:
-            refs[-1][:, columns:] = refs[0][...]
-
-    extra = () if more is None else (more,)
-    return call(
-        kernel,
-        width // block,
-        [pl.BlockSpec((rows, block), lambda i: (0, i)), whole(rows, columns)]
-        + [tile(block, v.shape[1]) for v in extra],
-        [tile(block, total)],
-        [array(BF16, width, total)],
-        2 * rows * width * columns,
-        (left, right) + extra,
-        (),
-        others,
-    )[0]
+        (terms,) + weights + (gain,),
+    )
 
 
 def head_body(
@@ -1075,6 +1095,7 @@
     feats = HEAD_FEATURES
     pad = 128
     gather = lambda v: lax.all_gather(v, "ctx", axis=0, tiled=True)
+    to_all = lambda v: lax.all_to_all(v, "ctx", split_axis=0, concat_axis=0, tiled=True)
     scatter = lambda v: lax.psum_scatter(v, "ctx", scatter_dimension=0, tiled=True)
 
     place = jnp.stack([moves.plane, moves.core, moves.seq]).astype(jnp.int32)
@@ -1145,9 +1166,9 @@
     next(out_move)
     next(out_move)
     gate_far, up_far = pin(gate_far), pin(up_far)
+    gate_last, up_last = order.late(near_x, block), order.late(near_y, block)
     low_near, high_near, low_far, high_far = next(out_move)
-    gate_last = moves.across(hold(near_x[:block]), 2)
-    up_last = moves.across(hold(near_y[:block]), 1)
+    gate_last, up_last = moves.across(hold(gate_last), 2), moves.across(hold(up_last), 1)
     out_own = jnp.concatenate(
         [out_two, out_far, low_near, high_near, *(v.reshape(4, *v.shape[2:]) for v in (low_far, high_far))]
     )
@@ -1174,6 +1195,11 @@
     scale_two, unit_two = rms_parts(hold(branch))
     residual = wide(tokens) + unit_two * gain_two
     scale_three, unit_three = rms_parts(residual)
+    later = hold(place)
+    w_out = lax.dynamic_slice_in_dim(
+        w_full.reshape(-1, width), (later[0] * CORES + later[1]) * feats, feats, 0
+    )
+    w_out = pin(w_out)
     unit_two, unit_three, residual = pin(unit_two), pin(unit_three), pin(residual)
 
     upstream = wide(cotangent)
@@ -1183,76 +1209,73 @@
     feed_grad, fourth_term = rms_back(scale_four, unit_four, gain_four, upstream)
     feed_low = pin(narrow(feed_grad))
     grad_all = pin(gather(feed_low), feed_low)
+    shape = (n_seq, block, hidden.shape[1])
     gate_low, up_low, input_part = feed_back(
-        place, grad_all, gate_factor, up_factor, gate_pieces, up_pieces, down_pieces
+        place, grad_all, gate_factor, up_factor, gate_pieces, up_pieces, down_pieces, order.last
     )
     order.mark(input_part)
     feed_input_grad = scatter(input_part)
-    shape = (n_seq, block, gate_low.shape[1])
     down_term = weight_grad(grad_all, hidden, 384, order.last).reshape(shape)
     order.mark(down_term)
-    down_move = moves.scatter_halves(down_term, pin)
+    plain = lambda value, sent=None: pin(value)
+    down_move = moves.scatter_halves(down_term, plain)
     next(down_move)
     gate_term = weight_grad(feed_all, gate_low, 384, order.last).reshape(shape)
     order.mark(gate_term)
-    gate_move = moves.scatter_whole(gate_term, 1, pin)
+    gate_move = moves.scatter_whole(gate_term, 1, plain)
     next(gate_move)
     up_term = weight_grad(feed_all, up_low, 384, order.last).reshape(shape)
     order.mark(up_term)
-    up_move = moves.scatter_whole(up_term, 2, pin)
+    up_move = moves.scatter_whole(up_term, 2, plain)
     next(up_move)
+    next(down_move)
     feed_input_grad = wide(pin(feed_input_grad, input_part))
     middle_grad, third_term = rms_back(scale_three, unit_three, gain_three, feed_input_grad)
     residual_grad = upstream + middle_grad
     branch_grad, second_term = rms_back(scale_two, unit_two, gain_two, residual_grad)
     branch_low = pin(narrow(branch_grad))
+
     branch_all = gather(branch_low)
-
-    mixed_own = pin(mixed_back(branch_low, w_full.reshape(-1, width)))
-    mixed_grad = lax.all_to_all(mixed_own, "ctx", split_axis=0, concat_axis=0, tiled=True)
-    next(down_move)
-    mixed_grad = pin(mixed_grad.reshape(-1, feats))
+    next(gate_move), next(up_move)
+    branch_all = pin(branch_all, branch_low)
     query_grad, pair_own, pair_send = attend_head_back(
-        place, query, key, value, mixed_grad, spot, spots, cosine, sine, order.last
+        place, query, key, value, branch_all, w_out, spot, spots, cosine, sine, order.last
     )
     order.mark(query_grad)
     pair_other = moves.swap(pair_send)
-    pair_other = pin(pair_other)
-    qkv_grad, normed_part = normed_back(
-        place, query_grad, pair_own, pair_other, pair_cosine, pair_sine, columns
-    )
+    pair_other = pin(pair_other, pair_send)
+    down_sum = next(down_move).T
+    terms = jnp.stack([second_term, third_term, fourth_term])
+    terms = narrow(jnp.pad(terms, ((0, pad - 3), (0, 0))).T)
+    qkv_grad, qkv_term = qkv_back(
+        normed, query_grad, pair_own, pair_other, pair_cosine, pair_sine, terms, order.last
+    )
+    order.mark(qkv_term)
+    qkv_move = moves.scatter_halves(qkv_term.reshape(n_seq, width // n_seq, -1), pin)
+    next(qkv_move)
+    normed_part = normed_back(place, qkv_grad, columns, order.last)
     order.mark(normed_part)
     normed_grad = scatter(normed_part)
 
-    terms = jnp.stack([second_term, third_term, fourth_term])
-    terms = narrow(jnp.pad(terms, ((0, pad - 3), (0, 0))).T)
-    qkv_term = weight_grad(normed, qkv_grad, 384, order.last, terms)
-    order.mark(qkv_term)
-    down_sum = next(down_move).T
-    qkv_move = moves.scatter_halves(qkv_term.reshape(n_seq, width // n_seq, -1), pin)
-    next(qkv_move)
-    branch_all = pin(branch_all, branch_low)
     output_term = weight_grad(mixed, branch_all, feats, order.last)
     order.mark(output_term)
     out_term = output_term.reshape(CORES, CORES, out_rows, width).transpose(1, 0, 2, 3)
     out_term = moves.exchange_cores(out_term).reshape(line, out_rows, width)
     next(qkv_move)
-    next(gate_move), next(up_move)
+    gate_sum, up_sum = next(gate_move), next(up_move)
     out_move = moves.scatter_whole(pin(out_term), 2, pin)
     next(out_move)
-    own_term = pin(narrow(next(qkv_move))).reshape(line, CORES, feat_rows, 2 * feats + pad)
-    own_term = pin(moves.exchange_steps(own_term))
-    own_other = moves.swap(lax.dynamic_index_in_dim(own_term, 1 - moves.core, 1, False))
-    own_term = lax.dynamic_index_in_dim(own_term, moves.core, 1, False)
+    own_in = pin(narrow(next(qkv_move))).reshape(n_ctx, feat_rows, 2 * feats + pad)
+    own_term = to_all(own_in)
     next(out_move)
+    grad_output = moves.transpose_chips(pin(narrow(next(out_move))))
+    own_term = pin(own_term, own_in)
     normed_grad = pin(normed_grad)
     scale_one, unit_one = rms_parts(wide(tokens))
     input_grad, _ = rms_back(scale_one, unit_one, gain_one, wide(normed_grad))
     grad_tokens = pin(narrow(residual_grad + input_grad))
-    grad_output = moves.transpose_chips(narrow(next(out_move)))
-    gate_sum, up_sum = next(gate_move), next(up_move)
     grad_query, grad_key, grad_value, grad_gains, grad_first = own_grads(
-        place, own_term, pin(own_other), (w_query, w_key, w_value), first_gain[:, None]
+        own_term, (w_query, w_key, w_value), first_gain[:, None]
     )
     grad_output = wide(pin(grad_output))
     return (

time: 661 us -> 648 us (0.980)
  local copies, waits for them, and re-layouts: 81.3 us -> 67 us
  waiting for transfers between devices: 236 us -> 249 us
    ppermute x45 -> x41, waiting for transfers between devices: 114 us -> 147 us  [_send(): return lax.ppermute(value, ('seq', 'ctx'), pairs)]
    all_to_all x1, waiting for transfers between devices: 22.3 us -> 3.28 us  [head_body(): lax.all_to_all(v, 'ctx', split_axis=0, concat_axis=0, tiled=True)]
    pallas_call x15 -> x14, Pallas kernels: 174 us -> 164 us  [call(): pl.pallas_call(body, grid=(steps,), in_specs=in_specs + [ANYWHERE] * len(...]
    slice x4 -> x3, local copies, waits for them, and re-layouts: 12.7 us -> 5.72 us  [the longest x2 4.41 us: scatter_halves(): low = self.scatter_whole(terms[:, :half], 1, gate, ready)]
    pallas_call x0 -> x2, Pallas kernels: none -> 6.96 us  [copied(): pl.pallas_call(kernel, grid=(4,), in_specs=[part] + [pl.BlockSpec(memory_...]
    ppermute x45 -> x41, starting transfers between devices: 43 us -> 38 us  [_send(): return lax.ppermute(value, ('seq', 'ctx'), pairs)]
    unnamed x138 -> x137, local copies, waits for them, and re-layouts: 36.4 us -> 33.2 us
    another operation x10 -> x9, other arithmetic: 13.5 us -> 10.8 us  [the longest x7 8.04 us: scatter_whole(): sent = ready(jnp.stack([pick(mask), pick(3)]))]
  transfers between devices with their start and end apart: 53 -> 49, of which waited for: 25 -> 24; matrix products, arithmetic and copies ran while one was open for 22% -> 20% of each run, Pallas kernels for 20% -> 20%
where the time goes in v4:
time: 648 us; the launch traced here: 639 us
  waiting for transfers between devices  249 us (38%)
  Pallas kernels  171 us (26%)
  other arithmetic  89.9 us (14%)
  local copies, waits for them, and re-layouts  67 us (10%)
  starting transfers between devices  45.1 us (7%)
  between operations  16.7 us (3%)
    pallas_call x14, Pallas kernels, call(): pl.pallas_call(body, grid=(steps,), in_specs=in_specs + [ANYWHERE] * len(...  164 us
    ppermute x41, waiting for transfers between devices, _send(): return lax.ppermute(value, ('seq', 'ctx'), pairs)  147 us
    all_gather x3, waiting for transfers between devices, head_body(): gather = lambda v: lax.all_gather(v, 'ctx', axis=0, tiled=True)  58 us
    reduce_scatter x3, waiting for transfers between devices, head_body(): lax.psum_scatter(v, 'ctx', scatter_dimension=0, tiled=True)  40.6 us
    ppermute x41, starting transfers between devices, _send(): return lax.ppermute(value, ('seq', 'ctx'), pairs)  38 us
    unnamed x137, local copies, waits for them, and re-layouts  33.2 us
    convert_element_type x11, other arithmetic, narrow(): return value.astype(jnp.bfloat16)  22.2 us
  transfers between devices with their start and end apart: 49, of which 24 were waited for; matrix products, arithmetic and copies ran while one was open for 20% of the time, Pallas kernels for 20%

profile of v4, /device:TPU:3, one launch (start us, length us, event | category | flops | bytes accessed | tf_op | source)
XLA Modules:
  0.0 639.4 jit_solution(12782243883925938148)
XLA Ops:
  12.1 2.3 collective-permute-start.6
  31.8 4.3 collective-permute-done.1
  37.7 7.5 %collective-permute-done.2 = bf16[2,72,640]{2,1,0:T(8,128)(2,1)S(1)} collective-permute-done((bf16[2,72,640]{2,1,0:T(8,128)(2,1)S(1)}, bf16[2,72,640]{2,1,0:T(8,128)(2,1)S(1)}, u32[]{:S(2)}, u32[]{:S(2)}) %collective-permute-start.2) | collective-permute-done | bytes 184352 | tf_op jit(solution)/shard_map/ppermute | solution.py:471
  46.5 2.3 slice_bitcast_fusion.2
  50.6 14.4 %collective-permute-done.8.refs_0_ = bf16[864,1152]{1,0:T(8,128)(2,1)} collective-permute-done((bf16[864,1152]{1,0:T(8,128)(2,1)}, bf16[864,1152]{1,0:T(8,128)(2,1)}, u32[]{:S(2)}, u32[]{:S(2)}) %collective-permute-start.8) | collective-permute-done | bytes 1990688 | tf_op jit(solution)/shard_map/ppermute | solution.py:471
  65.0 1.9 pad_maximum_fusion.18.refs_0_
  66.9 3.6 collective-permute-done.5.refs_0_
  70.5 1.9 pad_maximum_fusion.14.refs_0_
  77.9 3.0 multiply_cosine_fusion
  89.6 3.8 collective-permute-done.9.refs_0_
  96.6 6.8 %all-gather.6.cloned.1.call-done.refs_0_ = bf16[1024,2304]{1,0:T(8,128)(2,1)} async-done(((bf16[128,2304]{1,0:T(8,128)(2,1)}), bf16[1024,2304]{1,0:T(8,128)(2,1)}) %all-gather.6.cloned.1.call-update) | async-done | bytes 4718608 | tf_op jit(solution)/shard_map/all_gather | solution.py:1097
  103.3 9.3 %shard_map.258 = (bf16[1024,2304]{1,0:T(8,128)(2,1)}, bf16[1024,256]{1,0:T(8,128)(2,1)}, bf16[1024,256]{1,0:T(8,128)(2,1)}, f32[8,2304]{1,0:T(8,128)}) custom-call(s32[3]{0:T(128)} %pad_add_fusion.refs_0_, bf16[1024,2304]{1,0:T(8,128)(2,1)} %shard_map.257.refs_1_.refs_4_, bf16[576,640]{1,0:T(8,128)(2,1)} %shard_map.239.refs_1_.refs_2_, ...), custom_call_target="tpu_custom_call" | custom-call | flops 2415919104 | tf_op jit(solution)/shard_map/pallas_call | solution.py:554
  115.5 2.0 constant_dynamic-update-slice_fusion.5
  117.5 2.1 broadcast_select_fusion
  119.5 5.9 shard_map.261.refs_0_
  125.7 2.3 collective-permute-done.12.refs_0_
  128.2 8.2 %collective-permute-done.13.refs_0_ = bf16[2,64,2304]{2,1,0:T(8,128)(2,1)} collective-permute-done((bf16[2,64,2304]{2,1,0:T(8,128)(2,1)}, bf16[2,64,2304]{2,1,0:T(8,128)(2,1)}, u32[]{:S(2)}, u32[]{:S(2)}) %collective-permute-start.13) | collective-permute-done | bytes 589856 | tf_op jit(solution)/shard_map/ppermute | solution.py:471
  136.4 2.4 pad_maximum_fusion.8.refs_0_
  139.2 3.0 collective-permute-done.14.refs_0_
  148.6 3.5 shard_map.283.refs_0_
  152.1 3.5 shard_map.286.refs_0_
  157.4 9.4 %collective-permute-done.15.refs_0_ = bf16[2,2,64,2304]{3,2,1,0:T(8,128)(2,1)} collective-permute-done((bf16[2,2,64,2304]{3,2,1,0:T(8,128)(2,1)}, bf16[2,2,64,2304]{3,2,1,0:T(8,128)(2,1)}, u32[]{:S(2)}, u32[]{:S(2)}) %collective-permute-start.15) | collective-permute-done | bytes 1179680 | tf_op jit(solution)/shard_map/ppermute | solution.py:471
  166.8 2.4 constant_dynamic-update-slice_fusion.1
  170.3 2.4 constant_dynamic-update-slice_fusion.refs_0_
  172.7 2.7 collective-permute-start.19
  176.6 6.6 %collective-permute-done.19.refs_0_ = bf16[16,64,2304]{2,1,0:T(8,128)(2,1)} collective-permute-done((bf16[16,64,2304]{2,1,0:T(8,128)(2,1)}, bf16[16,64,2304]{2,1,0:T(8,128)(2,1)}, u32[]{:S(2)}, u32[]{:S(2)}) %collective-permute-start.19) | collective-permute-done | bytes 4718624 | tf_op jit(solution)/shard_map/ppermute | solution.py:471
  183.2 21.3 %shard_map.282 = (bf16[1024,2304]{1,0:T(8,128)(2,1)}, f32[128,2304]{1,0:T(8,128)}, bf16[16,2,64,2304]{3,2,1,0:T(8,128)(2,1)}) custom-call(s32[3]{0:T(128)} %pad_add_fusion.refs_0_, bf16[8,1024,256]{2,1,0:T(8,128)(2,1)} %shard_map.281.refs_1_, bf16[16,64,2304]{2,1,0:T(8,128)(2,1)} %shard_map.275.refs_1_.refs_0_.refs_2_, ...), custom_call_target="tpu_custom_call" | custom-call | flops 9663676416 | tf_op jit(solution)/shard_map/pallas_call | solution.py:554
  209.2 18.9 %shard_map.289 = (bf16[1024,1152]{1,0:T(8,128)(2,1)}, bf16[1024,1152]{1,0:T(8,128)(2,1)}, bf16[1024,1152]{1,0:T(8,128)(2,1)}) custom-call(s32[3]{0:T(128)} %pad_add_fusion.refs_0_, bf16[1024,2304]{1,0:T(8,128)(2,1)} %get-tuple-element.40.refs_1_.refs_0_, bf16[576,1152]{1,0:T(8,128)(2,1)} %refs_4_.1, ...), custom_call_target="tpu_custom_call" | custom-call | flops 10871635968 | tf_op jit(solution)/shard_map/pallas_call | solution.py:554
  228.1 8.9 %collective-permute-done.22.refs_0_ = bf16[2,288,1152]{2,1,0:T(8,128)(2,1)S(1)} collective-permute-done((bf16[2,288,1152]{2,1,0:T(8,128)(2,1)}, bf16[2,288,1152]{2,1,0:T(8,128)(2,1)S(1)}, u32[]{:S(2)}, u32[]{:S(2)}) %collective-permute-start.22) | collective-permute-done | bytes 1327136 | tf_op jit(solution)/shard_map/ppermute | solution.py:471
  239.1 11.9 %shard_map.294.refs_1_.refs_0_ = bf16[1024,2304]{1,0:T(8,128)(2,1)} custom-call(s32[3]{0:T(128)} %pad_add_fusion.refs_0_, bf16[1024,1152]{1,0:T(8,128)(2,1)} %get-tuple-element.41.refs_1_, bf16[576,1152]{1,0:T(8,128)(2,1)} %bitcast.148, bf16[864,1152]{1,0:T(8,128)(2,1)} %shard_map.242.refs_1_.refs_0_.refs_7_.refs_3_.refs_9_.refs_13_, ...), custom_call_target="tpu_custom_call" | custom-call | flops 5435817984 | tf_op jit(solution)/shard_map/pallas_call | solution.py:554
  253.8 2.4 constant_dynamic-slice_fusion.14.refs_0_
  262.8 40.6 %reduce-scatter.4.cloned.1.call-done.refs_0_ = bf16[128,2304]{1,0:T(8,128)(2,1)} async-done(((bf16[1024,2304]{1,0:T(8,128)(2,1)}), bf16[128,2304]{1,0:T(8,128)(2,1)}) %reduce-scatter.4.cloned.1.call-update) | async-done | bytes 589840 | tf_op jit(solution)/shard_map/reduce_scatter | solution.py:1099
  304.9 2.1 fusion.25
  310.0 51.2 %all-gather.8.cloned.1.call-done.refs_0_ = bf16[1024,2304]{1,0:T(8,128)(2,1)} async-done(((bf16[128,2304]{1,0:T(8,128)(2,1)}), bf16[1024,2304]{1,0:T(8,128)(2,1)}) %all-gather.8.cloned.1.call-update) | async-done | bytes 4718608 | tf_op jit(solution)/shard_map/all_gather | solution.py:1097
  361.2 29.0 %shard_map.306 = (bf16[1024,1152]{1,0:T(8,128)(2,1)}, bf16[1024,1152]{1,0:T(8,128)(2,1)}, bf16[1024,2304]{1,0:T(8,128)(2,1)}) custom-call(s32[3]{0:T(128)} %pad_add_fusion.refs_0_, bf16[1024,2304]{1,0:T(8,128)(2,1)} %shard_map.305.refs_1_.refs_17_.refs_0_, bf16[1024,1152]{1,0:T(8,128)(2,1)} %get-tuple-element.43.refs_2_, ...), custom_call_target="tpu_custom_call" | custom-call | flops 16307453952 | tf_op jit(solution)/shard_map/pallas_call | solution.py:554
  390.3 10.8 %shard_map.307 = bf16[2304,1152]{1,0:T(8,128)(2,1)} custom-call(bf16[1024,2304]{1,0:T(8,128)(2,1)} %shard_map.305.refs_1_.refs_17_.refs_0_, bf16[1024,1152]{1,0:T(8,128)(2,1)} %get-tuple-element.41.refs_1_, bf16[1024,2304]{1,0:T(8,128)(2,1)} %get-tuple-element.45.refs_2_.refs_0_), custom_call_target="tpu_custom_call" | custom-call | flops 5435817984 | tf_op jit(solution)/shard_map/pallas_call | solution.py:554
  401.1 3.0 fusion.49
  407.5 10.9 %shard_map.308 = bf16[2304,1152]{1,0:T(8,128)(2,1)} custom-call(bf16[1024,2304]{1,0:T(8,128)(2,1)} %get-tuple-element.40.refs_1_.refs_0_, bf16[1024,1152]{1,0:T(8,128)(2,1)} %get-tuple-element.47.refs_1_, bf16[4,576,1152]{2,1,0:T(8,128)(2,1)} %bitcast.142), custom_call_target="tpu_custom_call" | custom-call | flops 5435817984 | tf_op jit(solution)/shard_map/pallas_call | solution.py:554
  418.4 10.8 %shard_map.309 = bf16[2304,1152]{1,0:T(8,128)(2,1)} custom-call(bf16[1024,2304]{1,0:T(8,128)(2,1)} %get-tuple-element.40.refs_1_.refs_0_, bf16[1024,1152]{1,0:T(8,128)(2,1)} %get-tuple-element.46.refs_1_, bf16[4,576,1152]{2,1,0:T(8,128)(2,1)} %bitcast.143), custom_call_target="tpu_custom_call" | custom-call | flops 5435817984 | tf_op jit(solution)/shard_map/pallas_call | solution.py:554
  429.2 1.9 constant_dynamic-slice_fusion.9
  438.8 2.3 fusion.29
  441.5 2.3 fusion.30
  445.1 2.1 fusion.23
  452.0 43.3 %collective-permute-done.27.refs_0_ = bf16[2,576,1152]{2,1,0:T(8,128)(2,1)} collective-permute-done((bf16[2,576,1152]{2,1,0:T(8,128)(2,1)}, bf16[2,576,1152]{2,1,0:T(8,128)(2,1)}, u32[]{:S(2)}, u32[]{:S(2)}) %collective-permute-start.27) | collective-permute-done | bytes 2654240 | tf_op jit(solution)/shard_map/ppermute | solution.py:471
  495.3 3.1 fusion.8
  499.4 3.1 fusion.9
  504.8 11.9 %shard_map.319 = (bf16[1024,256]{1,0:T(8,128)(2,1)}, f32[1024,256]{1,0:T(8,128)}, f32[1024,256]{1,0:T(8,128)}) custom-call(s32[3]{0:T(128)} %pad_add_fusion.refs_0_, bf16[1024,256]{1,0:T(8,128)(2,1)} %get-tuple-element.36.refs_0_.refs_1_, bf16[1024,256]{1,0:T(8,128)(2,1)} %get-tuple-element.103.refs_1_.refs_2_, ...), custom_call_target="tpu_custom_call" | custom-call | flops 3892314112 | tf_op jit(solution)/shard_map/pallas_call | solution.py:554
  516.6 3.2 collective-permute-start.28
  519.8 2.6 collective-permute-done.28.refs_0_
  522.5 8.5 %shard_map.324 = (bf16[1024,512]{1,0:T(8,128)(2,1)}, bf16[2304,640]{1,0:T(8,128)(2,1)}) custom-call(bf16[1024,2304]{1,0:T(8,128)(2,1)} %get-tuple-element.48.refs_0_, bf16[1024,256]{1,0:T(8,128)(2,1)} %get-tuple-element.49.refs_1_, f32[1024,256]{1,0:T(8,128)} %get-tuple-element.50.refs_2_, f32[1024,256]{1,0:T(8,128)} %shard_map.321.refs_1_.refs_3_, ...), custom_call_target="tpu_custom_call" | custom-call | flops 2415919104 | tf_op jit(solution)/shard_map/pallas_call | solution.py:554
  531.0 7.7 %shard_map.325.refs_2_ = bf16[1024,2304]{1,0:T(8,128)(2,1)} custom-call(s32[3]{0:T(128)} %pad_add_fusion.refs_0_, bf16[1024,512]{1,0:T(8,128)(2,1)} %get-tuple-element.52.refs_1_, bf16[576,640]{1,0:T(8,128)(2,1)} %shard_map.239.refs_1_.refs_2_, bf16[288,640]{1,0:T(8,128)(2,1)} %shard_map.246.refs_1_.refs_3_, bf16[288,640]{1,0:T(8,128)(2,1)} %shard_map.247.refs_1_.refs_4_, ...), custom_call_target="tpu_custom_call" | custom-call | flops 2415919104 | tf_op jit(solution)/shard_map/pallas_call | solution.py:554
  538.8 5.1 shard_map.326.refs_1_
  558.8 5.9 collective-permute-done.31.refs_0_
  564.6 1.9 fusion.34.refs_0_
  567.3 1.9 fusion.35.refs_0_
  572.9 4.1 bitcast_add_fusion.1
  577.0 4.1 bitcast_add_fusion
  584.8 6.2 all-to-all-start
  593.3 8.2 %collective-permute-done.39.refs_0_ = bf16[64,2304]{1,0:T(8,128)(2,1)} collective-permute-done((bf16[64,2304]{1,0:T(8,128)(2,1)}, bf16[64,2304]{1,0:T(8,128)(2,1)}, u32[]{:S(2)}, u32[]{:S(2)}) %collective-permute-start.39) | collective-permute-done | bytes 294944 | tf_op jit(solution)/shard_map/ppermute | solution.py:471
  601.5 2.0 fusion.31.refs_0_
  603.5 3.3 collective-permute-start.40
  606.8 3.3 all-to-all-done.refs_0_
  610.1 2.4 shard_map.348
  618.5 11.1 %collective-permute-done.40.refs_0_ = bf16[64,2304]{1,0:T(8,128)(2,1)S(1)} collective-permute-done((bf16[64,2304]{1,0:T(8,128)(2,1)}, bf16[64,2304]{1,0:T(8,128)(2,1)S(1)}, u32[]{:S(2)}, u32[]{:S(2)}) %collective-permute-start.40) | collective-permute-done | bytes 294944 | tf_op jit(solution)/shard_map/ppermute | solution.py:471
  (400 shorter events, 132.2 us)
Async XLA Ops:
  7.2 3.0 copy-start.41
  7.2 96.1 %all-gather.6.cloned.1.call-start = ((), (), s32[]{:S(2)}) async-start(), calls=%async_computation.4 | async-start | bytes 5308416 | tf_op jit(solution)/shard_map/all_gather | solution.py:1097
  10.5 3.9 copy-start.38
  11.4 14.2 %collective-permute-start = (bf16[4,72,640]{2,1,0:T(8,128)(2,1)}, bf16[4,72,640]{2,1,0:T(8,128)(2,1)}, u32[]{:S(2)}, u32[]{:S(2)}) collective-permute-start(bf16[4,72,640]{2,1,0:T(8,128)(2,1)} %dynamic-slice_bitcast_fusion.1), channel_id=1, source_target_pairs={{0,1},{1,0},{2,3},{3,2},{4,5},{5,4},{6,7},{7,6},{8,9},{9,8},{10,11... | collective-permute-start | bytes 1105928 | tf_op jit(solution)/shard_map/ppermute | solution.py:471
  12.1 52.9 %collective-permute-start.6 = (bf16[64,2304]{1,0:T(8,128)(2,1)}, bf16[64,2304]{1,0:T(8,128)(2,1)}, u32[]{:S(2)}, u32[]{:S(2)}) collective-permute-start(bf16[64,2304]{1,0:T(8,128)(2,1)} %param.18), channel_id=1, source_target_pairs={{0,4},{1,5},{2,6},{3,7},{4,0},{5,1},{6,2},{7,3},{8,12},{9,13},{10,... | collective-permute-start | bytes 884744 | tf_op jit(solution)/shard_map/ppermute | solution.py:471
  17.6 47.3 %collective-permute-start.7 = (bf16[864,1152]{1,0:T(8,128)(2,1)}, bf16[864,1152]{1,0:T(8,128)(2,1)}, u32[]{:S(2)}, u32[]{:S(2)}) collective-permute-start(bf16[864,1152]{1,0:T(8,128)(2,1)} %pad_maximum_fusion.2), channel_id=1, source_target_pairs={{0,16},{1,17},{2,18},{3,19},{4,20},{5,21},{6,22},{7,23},{8,24},{9,... | collective-permute-start | bytes 5971976 | tf_op jit(solution)/shard_map/ppermute | solution.py:471
  20.3 44.7 %collective-permute-start.8 = (bf16[864,1152]{1,0:T(8,128)(2,1)}, bf16[864,1152]{1,0:T(8,128)(2,1)}, u32[]{:S(2)}, u32[]{:S(2)}) collective-permute-start(bf16[864,1152]{1,0:T(8,128)(2,1)} %pad_maximum_fusion.3), channel_id=1, source_target_pairs={{0,8},{1,9},{2,10},{3,11},{4,12},{5,13},{6,14},{7,15},{8,0},{9,1},... | collective-permute-start | bytes 5971976 | tf_op jit(solution)/shard_map/ppermute | solution.py:471
  28.6 7.4 %collective-permute-start.1 = (bf16[2,72,640]{2,1,0:T(8,128)(2,1)}, bf16[2,72,640]{2,1,0:T(8,128)(2,1)}, u32[]{:S(2)}, u32[]{:S(2)}) collective-permute-start(bf16[2,72,640]{2,1,0:T(8,128)(2,1)} %get-tuple-element.109), channel_id=1, source_target_pairs={{0,2},{1,3},{2,4},{3,5},{4,6},{5,7},{6,0},{7,1},{8,10},{9,11},{10,... | collective-permute-start | bytes 552968 | tf_op jit(solution)/shard_map/ppermute | solution.py:471
  29.9 6.1 copy-start.44
  30.8 14.3 %collective-permute-start.2 = (bf16[2,72,640]{2,1,0:T(8,128)(2,1)S(1)}, bf16[2,72,640]{2,1,0:T(8,128)(2,1)S(1)}, u32[]{:S(2)}, u32[]{:S(2)}) collective-permute-start(bf16[2,72,640]{2,1,0:T(8,128)(2,1)S(1)} %copy-done.45), channel_id=1, source_target_pairs={{0,4},{1,5},{2,6},{3,7},{4,0},{5,1},{6,2},{7,3},{8,12},{9,13},{10,... | collective-permute-start | bytes 552968 | tf_op jit(solution)/shard_map/ppermute | solution.py:471
  36.0 9.8 %collective-permute-start.3 = (bf16[2,72,640]{2,1,0:T(8,128)(2,1)S(1)}, bf16[2,72,640]{2,1,0:T(8,128)(2,1)S(1)}, u32[]{:S(2)}, u32[]{:S(2)}) collective-permute-start(bf16[2,72,640]{2,1,0:T(8,128)(2,1)S(1)} %copy-done.44), channel_id=1, source_target_pairs={{0,6},{1,7},{2,0},{3,1},{4,2},{5,3},{6,4},{7,5},{8,14},{9,15},{10,... | collective-permute-start | bytes 552968 | tf_op jit(solution)/shard_map/ppermute | solution.py:471
  48.8 21.7 %collective-permute-start.5 = (bf16[288,640]{1,0:T(8,128)(2,1)}, bf16[288,640]{1,0:T(8,128)(2,1)}, u32[]{:S(2)}, u32[]{:S(2)}) collective-permute-start(bf16[288,640]{1,0:T(8,128)(2,1)} %get-tuple-element.106.refs_0_), channel_id=1, source_target_pairs={{0,16},{1,17},{2,18},{3,19},{4,20},{5,21},{6,22},{7,23},{8,24},{9,... | collective-permute-start | bytes 1105928 | tf_op jit(solution)/shard_map/ppermute | solution.py:471
  49.2 134.0 %all-gather.12.cloned.1.call-start = ((), (), s32[]{:S(2)}) async-start(), calls=%async_computation.10 | async-start | bytes 4718592 | tf_op jit(solution)/shard_map/all_gather | solution.py:1162
  49.3 23.5 %collective-permute-start.4 = (bf16[288,640]{1,0:T(8,128)(2,1)}, bf16[288,640]{1,0:T(8,128)(2,1)}, u32[]{:S(2)}, u32[]{:S(2)}) collective-permute-start(bf16[288,640]{1,0:T(8,128)(2,1)} %get-tuple-element.107), channel_id=1, source_target_pairs={{0,8},{1,9},{2,10},{3,11},{4,12},{5,13},{6,14},{7,15},{8,0},{9,1},... | collective-permute-start | bytes 1105928 | tf_op jit(solution)/shard_map/ppermute | solution.py:471
  66.9 3.6 copy-start.37
  72.4 17.2 %collective-permute-start.10 = (bf16[2,288,640]{2,1,0:T(8,128)(2,1)}, bf16[2,288,640]{2,1,0:T(8,128)(2,1)}, u32[]{:S(2)}, u32[]{:S(2)}) collective-permute-start(bf16[2,288,640]{2,1,0:T(8,128)(2,1)} %pad_maximum_fusion.14.refs_0_), channel_id=1, source_target_pairs={{0,8},{1,9},{2,10},{3,11},{4,12},{5,13},{6,14},{7,15},{8,0},{9,1},... | collective-permute-start | bytes 2211848 | tf_op jit(solution)/shard_map/ppermute | solution.py:471
  72.7 2.9 copy-start.36
  72.8 5.1 copy-start.62
  76.7 16.7 %collective-permute-start.9 = (bf16[2,288,640]{2,1,0:T(8,128)(2,1)S(1)}, bf16[2,288,640]{2,1,0:T(8,128)(2,1)S(1)}, u32[]{:S(2)}, u32[]{:S(2)}) collective-permute-start(bf16[2,288,640]{2,1,0:T(8,128)(2,1)S(1)} %pad_maximum_fusion.13), channel_id=1, source_target_pairs={{0,16},{1,17},{2,18},{3,19},{4,20},{5,21},{6,22},{7,23},{8,24},{9,... | collective-permute-start | bytes 2211848 | tf_op jit(solution)/shard_map/ppermute | solution.py:471
  94.2 54.3 %collective-permute-start.16 = (bf16[576,1152]{1,0:T(8,128)(2,1)}, bf16[576,1152]{1,0:T(8,128)(2,1)}, u32[]{:S(2)}, u32[]{:S(2)}) collective-permute-start(bf16[576,1152]{1,0:T(8,128)(2,1)} %shard_map.268), channel_id=1, source_target_pairs={{0,8},{1,9},{2,10},{3,11},{4,12},{5,13},{6,14},{7,15},{8,0},{9,1},... | collective-permute-start | bytes 3981320 | tf_op jit(solution)/shard_map/ppermute | solution.py:471
  95.4 53.2 %collective-permute-start.17 = (bf16[576,1152]{1,0:T(8,128)(2,1)}, bf16[576,1152]{1,0:T(8,128)(2,1)}, u32[]{:S(2)}, u32[]{:S(2)}) collective-permute-start(bf16[576,1152]{1,0:T(8,128)(2,1)} %shard_map.269), channel_id=1, source_target_pairs={{0,16},{1,17},{2,18},{3,19},{4,20},{5,21},{6,22},{7,23},{8,24},{9,... | collective-permute-start | bytes 3981320 | tf_op jit(solution)/shard_map/ppermute | solution.py:471
  112.6 4.8 collective-permute-start.11
  113.0 15.0 %collective-permute-start.12 = (bf16[2,64,2304]{2,1,0:T(8,128)(2,1)}, bf16[2,64,2304]{2,1,0:T(8,128)(2,1)}, u32[]{:S(2)}, u32[]{:S(2)}) collective-permute-start(bf16[2,64,2304]{2,1,0:T(8,128)(2,1)} %shard_map.263.refs_0_), channel_id=1, source_target_pairs={{0,2},{1,3},{2,0},{3,1},{4,6},{5,7},{6,4},{7,5},{8,10},{9,11},{10,... | collective-permute-start | bytes 1769480 | tf_op jit(solution)/shard_map/ppermute | solution.py:471
  113.0 23.4 %collective-permute-start.13 = (bf16[2,64,2304]{2,1,0:T(8,128)(2,1)}, bf16[2,64,2304]{2,1,0:T(8,128)(2,1)}, u32[]{:S(2)}, u32[]{:S(2)}) collective-permute-start(bf16[2,64,2304]{2,1,0:T(8,128)(2,1)} %shard_map.263.refs_0_), channel_id=1, source_target_pairs={{0,16},{1,17},{2,18},{3,19},{4,20},{5,21},{6,22},{7,23},{8,24},{9,... | collective-permute-start | bytes 1769480 | tf_op jit(solution)/shard_map/ppermute | solution.py:471
  125.5 178.0 %reduce-scatter.4.cloned.1.call-start = ((), (), s32[]{:S(2)}) async-start(), calls=%async_computation.5 | async-start | bytes 5308416 | tf_op jit(solution)/shard_map/reduce_scatter | solution.py:1099
  128.0 14.1 %collective-permute-start.14 = (bf16[2,64,2304]{2,1,0:T(8,128)(2,1)}, bf16[2,64,2304]{2,1,0:T(8,128)(2,1)}, u32[]{:S(2)}, u32[]{:S(2)}) collective-permute-start(bf16[2,64,2304]{2,1,0:T(8,128)(2,1)} %shard_map.265.refs_1_), channel_id=1, source_target_pairs={{0,8},{1,9},{2,10},{3,11},{4,12},{5,13},{6,14},{7,15},{8,0},{9,1},... | collective-permute-start | bytes 1769480 | tf_op jit(solution)/shard_map/ppermute | solution.py:471
  138.8 28.0 %collective-permute-start.15 = (bf16[2,2,64,2304]{3,2,1,0:T(8,128)(2,1)}, bf16[2,2,64,2304]{3,2,1,0:T(8,128)(2,1)}, u32[]{:S(2)}, u32[]{:S(2)}) collective-permute-start(bf16[2,2,64,2304]{3,2,1,0:T(8,128)(2,1)} %pad_maximum_fusion.8.refs_0_), channel_id=1, source_target_pairs={{0,8},{1,9},{2,10},{3,11},{4,12},{5,13},{6,14},{7,15},{8,0},{9,1},... | collective-permute-start | bytes 3538952 | tf_op jit(solution)/shard_map/ppermute | solution.py:471
  143.5 25.8 %collective-permute-start.18 = (bf16[2,2,64,2304]{3,2,1,0:T(8,128)(2,1)S(1)}, bf16[2,2,64,2304]{3,2,1,0:T(8,128)(2,1)S(1)}, u32[]{:S(2)}, u32[]{:S(2)}) collective-permute-start(bf16[2,2,64,2304]{3,2,1,0:T(8,128)(2,1)S(1)} %pad_maximum_fusion.9), channel_id=1, source_target_pairs={{0,16},{1,17},{2,18},{3,19},{4,20},{5,21},{6,22},{7,23},{8,24},{9,... | collective-permute-start | bytes 3538952 | tf_op jit(solution)/shard_map/ppermute | solution.py:471
  172.7 10.6 %collective-permute-start.19 = (bf16[16,64,2304]{2,1,0:T(8,128)(2,1)}, bf16[16,64,2304]{2,1,0:T(8,128)(2,1)}, u32[]{:S(2)}, u32[]{:S(2)}) collective-permute-start(bf16[16,64,2304]{2,1,0:T(8,128)(2,1)} %shard_map.275.refs_1_.refs_0_.refs_2_), channel_id=1, source_target_pairs={{0,1},{1,0},{2,3},{3,2},{4,5},{5,4},{6,7},{7,6},{8,9},{9,8},{10,11... | collective-permute-start | bytes 14155784 | tf_op jit(solution)/shard_map/ppermute | solution.py:471
  175.3 31.1 %collective-permute-start.20 = (bf16[576,1152]{1,0:T(8,128)(2,1)}, bf16[576,1152]{1,0:T(8,128)(2,1)}, u32[]{:S(2)}, u32[]{:S(2)}) collective-permute-start(bf16[576,1152]{1,0:T(8,128)(2,1)} %shard_map.284), channel_id=1, source_target_pairs={{0,16},{1,17},{2,18},{3,19},{4,20},{5,21},{6,22},{7,23},{8,24},{9,... | collective-permute-start | bytes 3981320 | tf_op jit(solution)/shard_map/ppermute | solution.py:471
  176.5 30.8 %collective-permute-start.21 = (bf16[576,1152]{1,0:T(8,128)(2,1)}, bf16[576,1152]{1,0:T(8,128)(2,1)}, u32[]{:S(2)}, u32[]{:S(2)}) collective-permute-start(bf16[576,1152]{1,0:T(8,128)(2,1)} %shard_map.287), channel_id=1, source_target_pairs={{0,8},{1,9},{2,10},{3,11},{4,12},{5,13},{6,14},{7,15},{8,0},{9,1},... | collective-permute-start | bytes 3981320 | tf_op jit(solution)/shard_map/ppermute | solution.py:471
  207.3 29.7 %collective-permute-start.22 = (bf16[2,288,1152]{2,1,0:T(8,128)(2,1)}, bf16[2,288,1152]{2,1,0:T(8,128)(2,1)S(1)}, u32[]{:S(2)}, u32[]{:S(2)}) collective-permute-start(bf16[2,288,1152]{2,1,0:T(8,128)(2,1)} %shard_map.290), channel_id=1, source_target_pairs={{0,8},{1,9},{2,10},{3,11},{4,12},{5,13},{6,14},{7,15},{8,0},{9,1},... | collective-permute-start | bytes 3981320 | tf_op jit(solution)/shard_map/ppermute | solution.py:471
  207.4 30.7 %collective-permute-start.23 = (bf16[2,288,1152]{2,1,0:T(8,128)(2,1)}, bf16[2,288,1152]{2,1,0:T(8,128)(2,1)S(1)}, u32[]{:S(2)}, u32[]{:S(2)}) collective-permute-start(bf16[2,288,1152]{2,1,0:T(8,128)(2,1)} %shard_map.292), channel_id=1, source_target_pairs={{0,16},{1,17},{2,18},{3,19},{4,20},{5,21},{6,22},{7,23},{8,24},{9,... | collective-permute-start | bytes 3981320 | tf_op jit(solution)/shard_map/ppermute | solution.py:471
  251.1 110.2 %all-gather.8.cloned.1.call-start = ((), (), s32[]{:S(2)}) async-start(), calls=%async_computation.6 | async-start | bytes 5308416 | tf_op jit(solution)/shard_map/all_gather | solution.py:1097
  262.8 42.1 %copy-start.27 = (bf16[128,2304]{1,0:T(8,128)(2,1)S(1)}, bf16[128,2304]{1,0:T(8,128)(2,1)}, u32[]{:S(2)}) copy-start(bf16[128,2304]{1,0:T(8,128)(2,1)} %param.27) | copy-start | bytes 1769476
  262.8 42.1 %copy-start.47 = (f32[2304]{0:T(1024)S(1)}, f32[2304]{0:T(1024)}, u32[]{:S(2)}) copy-start(f32[2304]{0:T(1024)} %get-tuple-element.68) | copy-start | bytes 27652
  303.4 3.5 copy-start.1
  303.4 3.5 copy-start.7
  308.4 136.4 %reduce-scatter.6.cloned.1.call-start = ((), (), s32[]{:S(2)}) async-start(), calls=%async_computation.7 | async-start | bytes 5308416 | tf_op jit(solution)/shard_map/reduce_scatter | solution.py:1099
  390.2 114.6 %all-gather.10.cloned.1.call-start = ((), (), s32[]{:S(2)}) async-start(), calls=%async_computation.8 | async-start | bytes 5308416 | tf_op jit(solution)/shard_map/all_gather | solution.py:1097
  405.7 32.0 %collective-permute-start.24 = (bf16[2,288,1152]{2,1,0:T(8,128)(2,1)}, bf16[2,288,1152]{2,1,0:T(8,128)(2,1)S(1)}, u32[]{:S(2)}, u32[]{:S(2)}) collective-permute-start(bf16[2,288,1152]{2,1,0:T(8,128)(2,1)} %pad_maximum_fusion.6), channel_id=1, source_target_pairs={{0,16},{1,17},{2,18},{3,19},{4,20},{5,21},{6,22},{7,23},{8,24},{9,... | collective-permute-start | bytes 3981320 | tf_op jit(solution)/shard_map/ppermute | solution.py:471
  407.2 30.6 %collective-permute-start.25 = (bf16[2,288,1152]{2,1,0:T(8,128)(2,1)S(1)}, bf16[2,288,1152]{2,1,0:T(8,128)(2,1)}, u32[]{:S(2)}, u32[]{:S(2)}) collective-permute-start(bf16[2,288,1152]{2,1,0:T(8,128)(2,1)S(1)} %pad_maximum_fusion.7), channel_id=1, source_target_pairs={{0,8},{1,9},{2,10},{3,11},{4,12},{5,13},{6,14},{7,15},{8,0},{9,1},... | collective-permute-start | bytes 3981320 | tf_op jit(solution)/shard_map/ppermute | solution.py:471
  431.1 3.5 copy-start.29
  432.9 62.4 %collective-permute-start.26 = (bf16[2,576,1152]{2,1,0:T(8,128)(2,1)}, bf16[2,576,1152]{2,1,0:T(8,128)(2,1)}, u32[]{:S(2)}, u32[]{:S(2)}) collective-permute-start(bf16[2,576,1152]{2,1,0:T(8,128)(2,1)} %pad_maximum_fusion), channel_id=1, source_target_pairs={{0,16},{1,17},{2,18},{3,19},{4,20},{5,21},{6,22},{7,23},{8,24},{9,... | collective-permute-start | bytes 7962632 | tf_op jit(solution)/shard_map/ppermute | solution.py:471
  436.6 58.6 %collective-permute-start.27 = (bf16[2,576,1152]{2,1,0:T(8,128)(2,1)}, bf16[2,576,1152]{2,1,0:T(8,128)(2,1)}, u32[]{:S(2)}, u32[]{:S(2)}) collective-permute-start(bf16[2,576,1152]{2,1,0:T(8,128)(2,1)} %pad_maximum_fusion.1), channel_id=1, source_target_pairs={{0,8},{1,9},{2,10},{3,11},{4,12},{5,13},{6,14},{7,15},{8,0},{9,1},... | collective-permute-start | bytes 7962632 | tf_op jit(solution)/shard_map/ppermute | solution.py:471
  441.1 81.4 %collective-permute-start.29 = (bf16[288,1152]{1,0:T(8,128)(2,1)}, bf16[288,1152]{1,0:T(8,128)(2,1)}, u32[]{:S(2)}, u32[]{:S(2)}) collective-permute-start(bf16[288,1152]{1,0:T(8,128)(2,1)} %fusion.29), channel_id=1, source_target_pairs={{0,8},{1,9},{2,10},{3,11},{4,12},{5,13},{6,14},{7,15},{8,0},{9,1},... | collective-permute-start | bytes 1990664 | tf_op jit(solution)/shard_map/ppermute | solution.py:471
  443.8 78.7 %collective-permute-start.30 = (bf16[288,1152]{1,0:T(8,128)(2,1)}, bf16[288,1152]{1,0:T(8,128)(2,1)}, u32[]{:S(2)}, u32[]{:S(2)}) collective-permute-start(bf16[288,1152]{1,0:T(8,128)(2,1)} %fusion.30), channel_id=1, source_target_pairs={{0,16},{1,17},{2,18},{3,19},{4,20},{5,21},{6,22},{7,23},{8,24},{9,... | collective-permute-start | bytes 1990664 | tf_op jit(solution)/shard_map/ppermute | solution.py:471
  450.6 165.1 %reduce-scatter.8.cloned.1.call-start = ((), (), s32[]{:S(2)}) async-start(), calls=%async_computation.9 | async-start | bytes 5308416 | tf_op jit(solution)/shard_map/reduce_scatter | solution.py:1099
  498.4 71.8 %collective-permute-start.34 = (bf16[576,1152]{1,0:T(8,128)(2,1)}, bf16[576,1152]{1,0:T(8,128)(2,1)}, u32[]{:S(2)}, u32[]{:S(2)}) collective-permute-start(bf16[576,1152]{1,0:T(8,128)(2,1)} %fusion.8), channel_id=1, source_target_pairs={{0,8},{1,9},{2,10},{3,11},{4,12},{5,13},{6,14},{7,15},{8,0},{9,1},... | collective-permute-start | bytes 3981320 | tf_op jit(solution)/shard_map/ppermute | solution.py:471
  502.4 67.8 %collective-permute-start.35 = (bf16[576,1152]{1,0:T(8,128)(2,1)}, bf16[576,1152]{1,0:T(8,128)(2,1)}, u32[]{:S(2)}, u32[]{:S(2)}) collective-permute-start(bf16[576,1152]{1,0:T(8,128)(2,1)} %fusion.9), channel_id=1, source_target_pairs={{0,16},{1,17},{2,18},{3,19},{4,20},{5,21},{6,22},{7,23},{8,24},{9,... | collective-permute-start | bytes 3981320 | tf_op jit(solution)/shard_map/ppermute | solution.py:471
  516.6 5.8 collective-permute-start.28
  538.8 5.1 copy-start.10
  546.6 18.0 %collective-permute-start.31 = (bf16[2,288,640]{2,1,0:T(8,128)(2,1)}, bf16[2,288,640]{2,1,0:T(8,128)(2,1)}, u32[]{:S(2)}, u32[]{:S(2)}) collective-permute-start(bf16[2,288,640]{2,1,0:T(8,128)(2,1)} %pad_maximum_fusion.15.refs_0_), channel_id=1, source_target_pairs={{0,8},{1,9},{2,10},{3,11},{4,12},{5,13},{6,14},{7,15},{8,0},{9,1},... | collective-permute-start | bytes 2211848 | tf_op jit(solution)/shard_map/ppermute | solution.py:471
  549.4 18.0 %collective-permute-start.36 = (bf16[2,288,640]{2,1,0:T(8,128)(2,1)}, bf16[2,288,640]{2,1,0:T(8,128)(2,1)}, u32[]{:S(2)}, u32[]{:S(2)}) collective-permute-start(bf16[2,288,640]{2,1,0:T(8,128)(2,1)} %pad_maximum_fusion.16.refs_0_), channel_id=1, source_target_pairs={{0,16},{1,17},{2,18},{3,19},{4,20},{5,21},{6,22},{7,23},{8,24},{9,... | collective-permute-start | bytes 2211848 | tf_op jit(solution)/shard_map/ppermute | solution.py:471
  551.4 6.1 collective-permute-start.33
  566.6 14.5 %collective-permute-start.32 = (bf16[288,640]{1,0:T(8,128)(2,1)}, bf16[288,640]{1,0:T(8,128)(2,1)}, u32[]{:S(2)}, u32[]{:S(2)}) collective-permute-start(bf16[288,640]{1,0:T(8,128)(2,1)} %fusion.34.refs_0_), channel_id=1, source_target_pairs={{0,16},{1,17},{2,18},{3,19},{4,20},{5,21},{6,22},{7,23},{8,24},{9,... | collective-permute-start | bytes 1105928 | tf_op jit(solution)/shard_map/ppermute | solution.py:471
  569.3 13.2 %collective-permute-start.37 = (bf16[288,640]{1,0:T(8,128)(2,1)}, bf16[288,640]{1,0:T(8,128)(2,1)}, u32[]{:S(2)}, u32[]{:S(2)}) collective-permute-start(bf16[288,640]{1,0:T(8,128)(2,1)} %fusion.35.refs_0_), channel_id=1, source_target_pairs={{0,8},{1,9},{2,10},{3,11},{4,12},{5,13},{6,14},{7,15},{8,0},{9,1},... | collective-permute-start | bytes 1105928 | tf_op jit(solution)/shard_map/ppermute | solution.py:471
  572.2 18.7 %collective-permute-start.38 = (bf16[2,64,2304]{2,1,0:T(8,128)(2,1)}, bf16[2,64,2304]{2,1,0:T(8,128)(2,1)}, u32[]{:S(2)}, u32[]{:S(2)}) collective-permute-start(bf16[2,64,2304]{2,1,0:T(8,128)(2,1)} %pad_maximum_fusion.19.refs_0_), channel_id=1, source_target_pairs={{0,16},{1,17},{2,18},{3,19},{4,20},{5,21},{6,22},{7,23},{8,24},{9,... | collective-permute-start | bytes 1769480 | tf_op jit(solution)/shard_map/ppermute | solution.py:471
  584.8 25.3 %all-to-all-start = ((bf16[8,72,640]{2,1,0:T(8,128)(2,1)}), bf16[8,72,640]{2,1,0:T(8,128)(2,1)}, u32[]{:S(2)}, u32[]{:S(2)}) async-start(bf16[8,72,640]{2,1,0:T(8,128)(2,1)} %bitcast.137), calls=%async_computation.3 | async-start | bytes 1474560 | tf_op jit(solution)/shard_map/all_to_all | solution.py:1098
  592.8 8.8 %collective-permute-start.39 = (bf16[64,2304]{1,0:T(8,128)(2,1)}, bf16[64,2304]{1,0:T(8,128)(2,1)}, u32[]{:S(2)}, u32[]{:S(2)}) collective-permute-start(bf16[64,2304]{1,0:T(8,128)(2,1)} %fusion.38.refs_0_), channel_id=1, source_target_pairs={{0,8},{1,9},{2,10},{3,11},{4,12},{5,13},{6,14},{7,15},{8,0},{9,1},... | collective-permute-start | bytes 884744 | tf_op jit(solution)/shard_map/ppermute | solution.py:471
  603.5 26.1 %collective-permute-start.40 = (bf16[64,2304]{1,0:T(8,128)(2,1)}, bf16[64,2304]{1,0:T(8,128)(2,1)S(1)}, u32[]{:S(2)}, u32[]{:S(2)}) collective-permute-start(bf16[64,2304]{1,0:T(8,128)(2,1)} %shard_map.343.refs_1_), channel_id=1, source_target_pairs={{0,0},{1,1},{2,8},{3,9},{4,16},{5,17},{6,24},{7,25},{8,2},{9,3},{1... | collective-permute-start | bytes 884744 | tf_op jit(solution)/shard_map/ppermute | solution.py:471
  612.5 3.1 copy-start.19
  612.5 3.1 copy-start.46
  612.5 3.1 copy-start.58
  (48 other events, 71.4 us)
Sparse Core Ops, SparseCore 0:
  49.4 53.9 all-gather.5
  125.6 46.9 all-gather.11
  251.2 52.1 reduce-scatter.3
  308.6 52.6 all-gather.7
  390.3 51.2 reduce-scatter.5
  450.7 51.4 all-gather.9
  538.9 50.7 reduce-scatter.7

commit v5 on v4

--- a/solution.py
+++ b/solution.py
@@ -1132,6 +1132,8 @@
     near_x, near_y = pin(near_x), pin(near_y)
     out_two = pin(jnp.stack([w_output, pin(out_near)]))
     next(columns_move)
+    gate_far = moves.across(hold(w_gate), 2)
+    up_far = moves.across(hold(w_up), 1)
 
     block_size = rows // 2
     offsets = jnp.arange(block_size, dtype=jnp.int32)
@@ -1145,11 +1147,9 @@
     tables = (cosine, sine, pair_cosine, pair_sine)
 
     columns = (own_columns,) + next(columns_move)
-    gate_far = moves.across(hold(w_gate), 2)
-    up_far = moves.across(hold(w_up), 1)
-    tokens_all = pin(tokens_all, tokens_in)
     out_two = hold(out_two)
     out_far = moves.plane_swap(out_two, 1)
+    tokens_all = pin(tokens_all, tokens_in)
 
     normed, query, pair, gains = project_rows(place, tokens_all, columns, feats, tables)
     gain_one, gain_two, gain_three, gain_four = (gains[i : i + 1] for i in range(4))
@@ -1158,10 +1158,10 @@
     pair_other = pin(pair_other, pair)
     key = jnp.where(core_zero, pair, pair_other)
     value = jnp.where(core_zero, pair_other, pair)
+    out_far = pin(out_far, out_two)
     mixed = pin(attend_head(query, key, value, spot, spots, order.last))
     mixed_all = lax.all_gather(mixed, "ctx", axis=0)
 
-    out_far = pin(out_far, out_two)
     out_move = moves.gather_halves(out_two, out_far, pin)
     next(out_move)
     next(out_move)
@@ -1269,11 +1269,11 @@
     own_term = to_all(own_in)
     next(out_move)
     grad_output = moves.transpose_chips(pin(narrow(next(out_move))))
-    own_term = pin(own_term, own_in)
     normed_grad = pin(normed_grad)
     scale_one, unit_one = rms_parts(wide(tokens))
     input_grad, _ = rms_back(scale_one, unit_one, gain_one, wide(normed_grad))
     grad_tokens = pin(narrow(residual_grad + input_grad))
+    own_term = pin(own_term, own_in)
     grad_query, grad_key, grad_value, grad_gains, grad_first = own_grads(
         own_term, (w_query, w_key, w_value), first_gain[:, None]
     )

time: 648 us -> 647 us (level)
  waiting for transfers between devices: 249 us -> 242 us
  starting transfers between devices: 45.1 us -> 51.9 us
    ppermute x41, starting transfers between devices: 38 us -> 44.8 us  [_send(): return lax.ppermute(value, ('seq', 'ctx'), pairs)]
    unnamed x137 -> x139, local copies, waits for them, and re-layouts: 33.2 us -> 33.6 us
  transfers between devices with their start and end apart: 49 -> 49, of which waited for: 24 -> 21; matrix products, arithmetic and copies ran while one was open for 20% -> 20% of each run, Pallas kernels for 20% -> 20%
where the time goes in v5:
time: 647 us; the launch traced here: 638 us
  waiting for transfers between devices  242 us (37%)
  Pallas kernels  171 us (26%)
  other arithmetic  89.6 us (14%)
  local copies, waits for them, and re-layouts  66.4 us (10%)
  starting transfers between devices  51.9 us (8%)
  between operations  16.7 us (3%)
    pallas_call x14, Pallas kernels, call(): pl.pallas_call(body, grid=(steps,), in_specs=in_specs + [ANYWHERE] * len(...  164 us
    ppermute x41, waiting for transfers between devices, _send(): return lax.ppermute(value, ('seq', 'ctx'), pairs)  147 us
    all_gather x3, waiting for transfers between devices, head_body(): gather = lambda v: lax.all_gather(v, 'ctx', axis=0, tiled=True)  53.7 us
    ppermute x41, starting transfers between devices, _send(): return lax.ppermute(value, ('seq', 'ctx'), pairs)  44.8 us
    reduce_scatter x3, waiting for transfers between devices, head_body(): lax.psum_scatter(v, 'ctx', scatter_dimension=0, tiled=True)  41.4 us
    unnamed x139, local copies, waits for them, and re-layouts  33.6 us
    convert_element_type x11, other arithmetic, narrow(): return value.astype(jnp.bfloat16)  22.2 us
  transfers between devices with their start and end apart: 49, of which 21 were waited for; matrix products, arithmetic and copies ran while one was open for 20% of the time, Pallas kernels for 20%

profile of v5, /device:TPU:3, one launch (start us, length us, event | category | flops | bytes accessed | tf_op | source)
XLA Modules:
  0.0 638.5 jit_solution(18092995686571812004)
XLA Ops:
  12.1 2.3 collective-permute-start.6
  31.8 4.3 collective-permute-done.1
  37.7 7.5 %collective-permute-done.2 = bf16[2,72,640]{2,1,0:T(8,128)(2,1)S(1)} collective-permute-done((bf16[2,72,640]{2,1,0:T(8,128)(2,1)S(1)}, bf16[2,72,640]{2,1,0:T(8,128)(2,1)S(1)}, u32[]{:S(2)}, u32[]{:S(2)}) %collective-permute-start.2) | collective-permute-done | bytes 184352 | tf_op jit(solution)/shard_map/ppermute | solution.py:471
  46.5 2.3 slice_bitcast_fusion.2
  50.6 14.4 %collective-permute-done.8.refs_0_ = bf16[864,1152]{1,0:T(8,128)(2,1)} collective-permute-done((bf16[864,1152]{1,0:T(8,128)(2,1)}, bf16[864,1152]{1,0:T(8,128)(2,1)}, u32[]{:S(2)}, u32[]{:S(2)}) %collective-permute-start.8) | collective-permute-done | bytes 1990688 | tf_op jit(solution)/shard_map/ppermute | solution.py:471
  65.0 1.9 pad_maximum_fusion.18.refs_0_
  66.9 3.6 collective-permute-done.5.refs_0_
  70.5 1.9 pad_maximum_fusion.14.refs_0_
  79.1 3.0 multiply_cosine_fusion
  89.8 4.8 collective-permute-done.9.refs_0_
  97.9 2.0 constant_dynamic-update-slice_fusion.5
  99.8 2.5 all-gather.6.cloned.1.call-done.refs_0_
  102.3 9.2 %shard_map.258 = (bf16[1024,2304]{1,0:T(8,128)(2,1)}, bf16[1024,256]{1,0:T(8,128)(2,1)}, bf16[1024,256]{1,0:T(8,128)(2,1)}, f32[8,2304]{1,0:T(8,128)}) custom-call(s32[3]{0:T(128)} %pad_add_fusion.refs_0_, bf16[1024,2304]{1,0:T(8,128)(2,1)} %shard_map.257.refs_1_.refs_4_, bf16[576,640]{1,0:T(8,128)(2,1)} %shard_map.239.refs_1_.refs_2_, ...), custom_call_target="tpu_custom_call" | custom-call | flops 2415919104 | tf_op jit(solution)/shard_map/pallas_call | solution.py:554
  111.5 2.3 collective-permute-start.11
  117.3 2.1 broadcast_select_fusion
  119.3 5.9 shard_map.264.refs_0_
  125.5 10.2 %collective-permute-done.13.refs_0_ = bf16[2,64,2304]{2,1,0:T(8,128)(2,1)} collective-permute-done((bf16[2,64,2304]{2,1,0:T(8,128)(2,1)}, bf16[2,64,2304]{2,1,0:T(8,128)(2,1)}, u32[]{:S(2)}, u32[]{:S(2)}) %collective-permute-start.13) | collective-permute-done | bytes 589856 | tf_op jit(solution)/shard_map/ppermute | solution.py:471
  135.7 2.4 pad_maximum_fusion.8.refs_0_
  143.7 1.9 constant_dynamic-update-slice_fusion.3
  145.6 3.5 shard_map.283.refs_0_
  149.1 3.5 shard_map.286.refs_0_
  152.6 1.9 constant_dynamic-update-slice_fusion.2
  154.6 8.9 %collective-permute-done.15.refs_0_ = bf16[2,2,64,2304]{3,2,1,0:T(8,128)(2,1)} collective-permute-done((bf16[2,2,64,2304]{3,2,1,0:T(8,128)(2,1)}, bf16[2,2,64,2304]{3,2,1,0:T(8,128)(2,1)}, u32[]{:S(2)}, u32[]{:S(2)}) %collective-permute-start.15) | collective-permute-done | bytes 1179680 | tf_op jit(solution)/shard_map/ppermute | solution.py:471
  163.5 2.4 constant_dynamic-update-slice_fusion.1
  166.9 2.4 constant_dynamic-update-slice_fusion.refs_0_
  169.3 3.3 collective-permute-start.19
  174.9 5.6 collective-permute-done.19.refs_0_
  180.5 21.3 %shard_map.282 = (bf16[1024,2304]{1,0:T(8,128)(2,1)}, f32[128,2304]{1,0:T(8,128)}, bf16[16,2,64,2304]{3,2,1,0:T(8,128)(2,1)}) custom-call(s32[3]{0:T(128)} %pad_add_fusion.refs_0_, bf16[8,1024,256]{2,1,0:T(8,128)(2,1)} %shard_map.281.refs_1_, bf16[16,64,2304]{2,1,0:T(8,128)(2,1)} %shard_map.275.refs_1_.refs_0_.refs_2_, ...), custom_call_target="tpu_custom_call" | custom-call | flops 9663676416 | tf_op jit(solution)/shard_map/pallas_call | solution.py:554
  207.3 18.9 %shard_map.289 = (bf16[1024,1152]{1,0:T(8,128)(2,1)}, bf16[1024,1152]{1,0:T(8,128)(2,1)}, bf16[1024,1152]{1,0:T(8,128)(2,1)}) custom-call(s32[3]{0:T(128)} %pad_add_fusion.refs_0_, bf16[1024,2304]{1,0:T(8,128)(2,1)} %get-tuple-element.40.refs_1_.refs_0_, bf16[576,1152]{1,0:T(8,128)(2,1)} %refs_4_.1, ...), custom_call_target="tpu_custom_call" | custom-call | flops 10871635968 | tf_op jit(solution)/shard_map/pallas_call | solution.py:554
  226.2 8.0 %collective-permute-done.22.refs_0_ = bf16[2,288,1152]{2,1,0:T(8,128)(2,1)S(1)} collective-permute-done((bf16[2,288,1152]{2,1,0:T(8,128)(2,1)}, bf16[2,288,1152]{2,1,0:T(8,128)(2,1)S(1)}, u32[]{:S(2)}, u32[]{:S(2)}) %collective-permute-start.22) | collective-permute-done | bytes 1327136 | tf_op jit(solution)/shard_map/ppermute | solution.py:471
  236.3 11.9 %shard_map.294.refs_1_.refs_0_ = bf16[1024,2304]{1,0:T(8,128)(2,1)} custom-call(s32[3]{0:T(128)} %pad_add_fusion.refs_0_, bf16[1024,1152]{1,0:T(8,128)(2,1)} %get-tuple-element.41.refs_1_, bf16[576,1152]{1,0:T(8,128)(2,1)} %bitcast.148, bf16[864,1152]{1,0:T(8,128)(2,1)} %shard_map.242.refs_1_.refs_0_.refs_7_.refs_3_.refs_9_.refs_13_, ...), custom_call_target="tpu_custom_call" | custom-call | flops 5435817984 | tf_op jit(solution)/shard_map/pallas_call | solution.py:554
  250.9 2.4 constant_dynamic-slice_fusion.14.refs_0_
  259.8 41.4 %reduce-scatter.4.cloned.1.call-done.refs_0_ = bf16[128,2304]{1,0:T(8,128)(2,1)} async-done(((bf16[1024,2304]{1,0:T(8,128)(2,1)}), bf16[128,2304]{1,0:T(8,128)(2,1)}) %reduce-scatter.4.cloned.1.call-update) | async-done | bytes 589840 | tf_op jit(solution)/shard_map/reduce_scatter | solution.py:1099
  302.6 2.1 fusion.25
  307.7 51.2 %all-gather.8.cloned.1.call-done.refs_0_ = bf16[1024,2304]{1,0:T(8,128)(2,1)} async-done(((bf16[128,2304]{1,0:T(8,128)(2,1)}), bf16[1024,2304]{1,0:T(8,128)(2,1)}) %all-gather.8.cloned.1.call-update) | async-done | bytes 4718608 | tf_op jit(solution)/shard_map/all_gather | solution.py:1097
  359.0 29.0 %shard_map.306 = (bf16[1024,1152]{1,0:T(8,128)(2,1)}, bf16[1024,1152]{1,0:T(8,128)(2,1)}, bf16[1024,2304]{1,0:T(8,128)(2,1)}) custom-call(s32[3]{0:T(128)} %pad_add_fusion.refs_0_, bf16[1024,2304]{1,0:T(8,128)(2,1)} %shard_map.305.refs_1_.refs_17_.refs_0_, bf16[1024,1152]{1,0:T(8,128)(2,1)} %get-tuple-element.43.refs_2_, ...), custom_call_target="tpu_custom_call" | custom-call | flops 16307453952 | tf_op jit(solution)/shard_map/pallas_call | solution.py:554
  388.0 10.8 %shard_map.307 = bf16[2304,1152]{1,0:T(8,128)(2,1)} custom-call(bf16[1024,2304]{1,0:T(8,128)(2,1)} %shard_map.305.refs_1_.refs_17_.refs_0_, bf16[1024,1152]{1,0:T(8,128)(2,1)} %get-tuple-element.41.refs_1_, bf16[1024,2304]{1,0:T(8,128)(2,1)} %get-tuple-element.45.refs_2_.refs_0_), custom_call_target="tpu_custom_call" | custom-call | flops 5435817984 | tf_op jit(solution)/shard_map/pallas_call | solution.py:554
  398.8 3.0 fusion.49
  405.3 10.9 %shard_map.308 = bf16[2304,1152]{1,0:T(8,128)(2,1)} custom-call(bf16[1024,2304]{1,0:T(8,128)(2,1)} %get-tuple-element.40.refs_1_.refs_0_, bf16[1024,1152]{1,0:T(8,128)(2,1)} %get-tuple-element.47.refs_1_, bf16[4,576,1152]{2,1,0:T(8,128)(2,1)} %bitcast.142), custom_call_target="tpu_custom_call" | custom-call | flops 5435817984 | tf_op jit(solution)/shard_map/pallas_call | solution.py:554
  416.1 10.8 %shard_map.309 = bf16[2304,1152]{1,0:T(8,128)(2,1)} custom-call(bf16[1024,2304]{1,0:T(8,128)(2,1)} %get-tuple-element.40.refs_1_.refs_0_, bf16[1024,1152]{1,0:T(8,128)(2,1)} %get-tuple-element.46.refs_1_, bf16[4,576,1152]{2,1,0:T(8,128)(2,1)} %bitcast.143), custom_call_target="tpu_custom_call" | custom-call | flops 5435817984 | tf_op jit(solution)/shard_map/pallas_call | solution.py:554
  426.9 1.9 constant_dynamic-slice_fusion.9
  436.6 2.3 fusion.29
  439.2 2.3 fusion.30
  442.8 2.1 fusion.23
  449.7 43.3 %collective-permute-done.27.refs_0_ = bf16[2,576,1152]{2,1,0:T(8,128)(2,1)} collective-permute-done((bf16[2,576,1152]{2,1,0:T(8,128)(2,1)}, bf16[2,576,1152]{2,1,0:T(8,128)(2,1)}, u32[]{:S(2)}, u32[]{:S(2)}) %collective-permute-start.27) | collective-permute-done | bytes 2654240 | tf_op jit(solution)/shard_map/ppermute | solution.py:471
  493.0 3.1 fusion.8
  497.1 3.1 fusion.9
  502.5 11.9 %shard_map.319 = (bf16[1024,256]{1,0:T(8,128)(2,1)}, f32[1024,256]{1,0:T(8,128)}, f32[1024,256]{1,0:T(8,128)}) custom-call(s32[3]{0:T(128)} %pad_add_fusion.refs_0_, bf16[1024,256]{1,0:T(8,128)(2,1)} %get-tuple-element.36.refs_0_.refs_1_, bf16[1024,256]{1,0:T(8,128)(2,1)} %get-tuple-element.103.refs_1_.refs_2_, ...), custom_call_target="tpu_custom_call" | custom-call | flops 3892314112 | tf_op jit(solution)/shard_map/pallas_call | solution.py:554
  514.4 3.2 collective-permute-start.28
  517.6 2.6 collective-permute-done.28.refs_0_
  520.2 8.5 %shard_map.324 = (bf16[1024,512]{1,0:T(8,128)(2,1)}, bf16[2304,640]{1,0:T(8,128)(2,1)}) custom-call(bf16[1024,2304]{1,0:T(8,128)(2,1)} %get-tuple-element.48.refs_0_, bf16[1024,256]{1,0:T(8,128)(2,1)} %get-tuple-element.49.refs_1_, f32[1024,256]{1,0:T(8,128)} %get-tuple-element.50.refs_2_, f32[1024,256]{1,0:T(8,128)} %shard_map.321.refs_1_.refs_3_, ...), custom_call_target="tpu_custom_call" | custom-call | flops 2415919104 | tf_op jit(solution)/shard_map/pallas_call | solution.py:554
  528.7 7.7 %shard_map.325.refs_2_ = bf16[1024,2304]{1,0:T(8,128)(2,1)} custom-call(s32[3]{0:T(128)} %pad_add_fusion.refs_0_, bf16[1024,512]{1,0:T(8,128)(2,1)} %get-tuple-element.52.refs_1_, bf16[576,640]{1,0:T(8,128)(2,1)} %shard_map.239.refs_1_.refs_2_, bf16[288,640]{1,0:T(8,128)(2,1)} %shard_map.246.refs_1_.refs_3_, bf16[288,640]{1,0:T(8,128)(2,1)} %shard_map.247.refs_1_.refs_4_, ...), custom_call_target="tpu_custom_call" | custom-call | flops 2415919104 | tf_op jit(solution)/shard_map/pallas_call | solution.py:554
  536.5 5.1 shard_map.326.refs_1_
  556.5 5.8 collective-permute-done.35.refs_0_
  562.4 1.9 fusion.34.refs_0_
  565.0 1.9 fusion.35.refs_0_
  570.6 4.1 bitcast_add_fusion.1
  574.7 4.1 bitcast_add_fusion
  582.5 6.2 all-to-all-start
  591.0 8.3 %collective-permute-done.39.refs_0_ = bf16[64,2304]{1,0:T(8,128)(2,1)} collective-permute-done((bf16[64,2304]{1,0:T(8,128)(2,1)}, bf16[64,2304]{1,0:T(8,128)(2,1)}, u32[]{:S(2)}, u32[]{:S(2)}) %collective-permute-start.39) | collective-permute-done | bytes 294944 | tf_op jit(solution)/shard_map/ppermute | solution.py:471
  599.3 2.0 fusion.31.refs_0_
  601.3 3.4 collective-permute-start.40
  607.8 2.4 shard_map.348
  610.3 17.0 %collective-permute-done.40.refs_0_ = bf16[64,2304]{1,0:T(8,128)(2,1)S(1)} collective-permute-done((bf16[64,2304]{1,0:T(8,128)(2,1)}, bf16[64,2304]{1,0:T(8,128)(2,1)S(1)}, u32[]{:S(2)}, u32[]{:S(2)}) %collective-permute-start.40) | collective-permute-done | bytes 294944 | tf_op jit(solution)/shard_map/ppermute | solution.py:471
  (403 shorter events, 130.2 us)
Async XLA Ops:
  7.2 95.1 %all-gather.6.cloned.1.call-start = ((), (), s32[]{:S(2)}) async-start(), calls=%async_computation.4 | async-start | bytes 5308416 | tf_op jit(solution)/shard_map/all_gather | solution.py:1097
  10.5 3.9 copy-start.37
  11.4 14.2 %collective-permute-start = (bf16[4,72,640]{2,1,0:T(8,128)(2,1)}, bf16[4,72,640]{2,1,0:T(8,128)(2,1)}, u32[]{:S(2)}, u32[]{:S(2)}) collective-permute-start(bf16[4,72,640]{2,1,0:T(8,128)(2,1)} %dynamic-slice_bitcast_fusion.1), channel_id=1, source_target_pairs={{0,1},{1,0},{2,3},{3,2},{4,5},{5,4},{6,7},{7,6},{8,9},{9,8},{10,11... | collective-permute-start | bytes 1105928 | tf_op jit(solution)/shard_map/ppermute | solution.py:471
  12.1 52.9 %collective-permute-start.6 = (bf16[64,2304]{1,0:T(8,128)(2,1)}, bf16[64,2304]{1,0:T(8,128)(2,1)}, u32[]{:S(2)}, u32[]{:S(2)}) collective-permute-start(bf16[64,2304]{1,0:T(8,128)(2,1)} %param.18), channel_id=1, source_target_pairs={{0,4},{1,5},{2,6},{3,7},{4,0},{5,1},{6,2},{7,3},{8,12},{9,13},{10,... | collective-permute-start | bytes 884744 | tf_op jit(solution)/shard_map/ppermute | solution.py:471
  17.6 47.3 %collective-permute-start.7 = (bf16[864,1152]{1,0:T(8,128)(2,1)}, bf16[864,1152]{1,0:T(8,128)(2,1)}, u32[]{:S(2)}, u32[]{:S(2)}) collective-permute-start(bf16[864,1152]{1,0:T(8,128)(2,1)} %pad_maximum_fusion.2), channel_id=1, source_target_pairs={{0,16},{1,17},{2,18},{3,19},{4,20},{5,21},{6,22},{7,23},{8,24},{9,... | collective-permute-start | bytes 5971976 | tf_op jit(solution)/shard_map/ppermute | solution.py:471
  20.3 44.7 %collective-permute-start.8 = (bf16[864,1152]{1,0:T(8,128)(2,1)}, bf16[864,1152]{1,0:T(8,128)(2,1)}, u32[]{:S(2)}, u32[]{:S(2)}) collective-permute-start(bf16[864,1152]{1,0:T(8,128)(2,1)} %pad_maximum_fusion.3), channel_id=1, source_target_pairs={{0,8},{1,9},{2,10},{3,11},{4,12},{5,13},{6,14},{7,15},{8,0},{9,1},... | collective-permute-start | bytes 5971976 | tf_op jit(solution)/shard_map/ppermute | solution.py:471
  28.6 7.4 %collective-permute-start.1 = (bf16[2,72,640]{2,1,0:T(8,128)(2,1)}, bf16[2,72,640]{2,1,0:T(8,128)(2,1)}, u32[]{:S(2)}, u32[]{:S(2)}) collective-permute-start(bf16[2,72,640]{2,1,0:T(8,128)(2,1)} %get-tuple-element.109), channel_id=1, source_target_pairs={{0,2},{1,3},{2,4},{3,5},{4,6},{5,7},{6,0},{7,1},{8,10},{9,11},{10,... | collective-permute-start | bytes 552968 | tf_op jit(solution)/shard_map/ppermute | solution.py:471
  29.9 6.1 copy-start.44
  30.8 14.3 %collective-permute-start.2 = (bf16[2,72,640]{2,1,0:T(8,128)(2,1)S(1)}, bf16[2,72,640]{2,1,0:T(8,128)(2,1)S(1)}, u32[]{:S(2)}, u32[]{:S(2)}) collective-permute-start(bf16[2,72,640]{2,1,0:T(8,128)(2,1)S(1)} %copy-done.45), channel_id=1, source_target_pairs={{0,4},{1,5},{2,6},{3,7},{4,0},{5,1},{6,2},{7,3},{8,12},{9,13},{10,... | collective-permute-start | bytes 552968 | tf_op jit(solution)/shard_map/ppermute | solution.py:471
  36.0 9.8 %collective-permute-start.3 = (bf16[2,72,640]{2,1,0:T(8,128)(2,1)S(1)}, bf16[2,72,640]{2,1,0:T(8,128)(2,1)S(1)}, u32[]{:S(2)}, u32[]{:S(2)}) collective-permute-start(bf16[2,72,640]{2,1,0:T(8,128)(2,1)S(1)} %copy-done.44), channel_id=1, source_target_pairs={{0,6},{1,7},{2,0},{3,1},{4,2},{5,3},{6,4},{7,5},{8,14},{9,15},{10,... | collective-permute-start | bytes 552968 | tf_op jit(solution)/shard_map/ppermute | solution.py:471
  48.8 21.7 %collective-permute-start.5 = (bf16[288,640]{1,0:T(8,128)(2,1)}, bf16[288,640]{1,0:T(8,128)(2,1)}, u32[]{:S(2)}, u32[]{:S(2)}) collective-permute-start(bf16[288,640]{1,0:T(8,128)(2,1)} %get-tuple-element.106.refs_0_), channel_id=1, source_target_pairs={{0,16},{1,17},{2,18},{3,19},{4,20},{5,21},{6,22},{7,23},{8,24},{9,... | collective-permute-start | bytes 1105928 | tf_op jit(solution)/shard_map/ppermute | solution.py:471
  49.2 131.2 %all-gather.12.cloned.1.call-start = ((), (), s32[]{:S(2)}) async-start(), calls=%async_computation.10 | async-start | bytes 4718592 | tf_op jit(solution)/shard_map/all_gather | solution.py:1163
  49.3 23.5 %collective-permute-start.4 = (bf16[288,640]{1,0:T(8,128)(2,1)}, bf16[288,640]{1,0:T(8,128)(2,1)}, u32[]{:S(2)}, u32[]{:S(2)}) collective-permute-start(bf16[288,640]{1,0:T(8,128)(2,1)} %get-tuple-element.107), channel_id=1, source_target_pairs={{0,8},{1,9},{2,10},{3,11},{4,12},{5,13},{6,14},{7,15},{8,0},{9,1},... | collective-permute-start | bytes 1105928 | tf_op jit(solution)/shard_map/ppermute | solution.py:471
  66.9 3.6 copy-start.36
  72.4 17.4 %collective-permute-start.10 = (bf16[2,288,640]{2,1,0:T(8,128)(2,1)}, bf16[2,288,640]{2,1,0:T(8,128)(2,1)}, u32[]{:S(2)}, u32[]{:S(2)}) collective-permute-start(bf16[2,288,640]{2,1,0:T(8,128)(2,1)} %pad_maximum_fusion.14.refs_0_), channel_id=1, source_target_pairs={{0,8},{1,9},{2,10},{3,11},{4,12},{5,13},{6,14},{7,15},{8,0},{9,1},... | collective-permute-start | bytes 2211848 | tf_op jit(solution)/shard_map/ppermute | solution.py:471
  72.8 3.9 copy-start.35
  77.9 16.7 %collective-permute-start.9 = (bf16[2,288,640]{2,1,0:T(8,128)(2,1)S(1)}, bf16[2,288,640]{2,1,0:T(8,128)(2,1)S(1)}, u32[]{:S(2)}, u32[]{:S(2)}) collective-permute-start(bf16[2,288,640]{2,1,0:T(8,128)(2,1)S(1)} %pad_maximum_fusion.13), channel_id=1, source_target_pairs={{0,16},{1,17},{2,18},{3,19},{4,20},{5,21},{6,22},{7,23},{8,24},{9,... | collective-permute-start | bytes 2211848 | tf_op jit(solution)/shard_map/ppermute | solution.py:471
  83.8 61.8 %collective-permute-start.16 = (bf16[576,1152]{1,0:T(8,128)(2,1)}, bf16[576,1152]{1,0:T(8,128)(2,1)}, u32[]{:S(2)}, u32[]{:S(2)}) collective-permute-start(bf16[576,1152]{1,0:T(8,128)(2,1)} %shard_map.268), channel_id=1, source_target_pairs={{0,8},{1,9},{2,10},{3,11},{4,12},{5,13},{6,14},{7,15},{8,0},{9,1},... | collective-permute-start | bytes 3981320 | tf_op jit(solution)/shard_map/ppermute | solution.py:471
  85.0 60.6 %collective-permute-start.17 = (bf16[576,1152]{1,0:T(8,128)(2,1)}, bf16[576,1152]{1,0:T(8,128)(2,1)}, u32[]{:S(2)}, u32[]{:S(2)}) collective-permute-start(bf16[576,1152]{1,0:T(8,128)(2,1)} %shard_map.269), channel_id=1, source_target_pairs={{0,16},{1,17},{2,18},{3,19},{4,20},{5,21},{6,22},{7,23},{8,24},{9,... | collective-permute-start | bytes 3981320 | tf_op jit(solution)/shard_map/ppermute | solution.py:471
  95.4 20.5 %collective-permute-start.12 = (bf16[2,64,2304]{2,1,0:T(8,128)(2,1)}, bf16[2,64,2304]{2,1,0:T(8,128)(2,1)}, u32[]{:S(2)}, u32[]{:S(2)}) collective-permute-start(bf16[2,64,2304]{2,1,0:T(8,128)(2,1)} %shard_map.261.refs_0_), channel_id=1, source_target_pairs={{0,2},{1,3},{2,0},{3,1},{4,6},{5,7},{6,4},{7,5},{8,10},{9,11},{10,... | collective-permute-start | bytes 1769480 | tf_op jit(solution)/shard_map/ppermute | solution.py:471
  96.7 38.9 %collective-permute-start.13 = (bf16[2,64,2304]{2,1,0:T(8,128)(2,1)}, bf16[2,64,2304]{2,1,0:T(8,128)(2,1)}, u32[]{:S(2)}, u32[]{:S(2)}) collective-permute-start(bf16[2,64,2304]{2,1,0:T(8,128)(2,1)} %shard_map.261.refs_0_), channel_id=1, source_target_pairs={{0,16},{1,17},{2,18},{3,19},{4,20},{5,21},{6,22},{7,23},{8,24},{9,... | collective-permute-start | bytes 1769480 | tf_op jit(solution)/shard_map/ppermute | solution.py:471
  111.5 4.4 collective-permute-start.11
  115.9 23.2 %collective-permute-start.14 = (bf16[2,64,2304]{2,1,0:T(8,128)(2,1)}, bf16[2,64,2304]{2,1,0:T(8,128)(2,1)}, u32[]{:S(2)}, u32[]{:S(2)}) collective-permute-start(bf16[2,64,2304]{2,1,0:T(8,128)(2,1)} %shard_map.263.refs_5_.refs_1_), channel_id=1, source_target_pairs={{0,8},{1,9},{2,10},{3,11},{4,12},{5,13},{6,14},{7,15},{8,0},{9,1},... | collective-permute-start | bytes 1769480 | tf_op jit(solution)/shard_map/ppermute | solution.py:471
  125.3 175.9 %reduce-scatter.4.cloned.1.call-start = ((), (), s32[]{:S(2)}) async-start(), calls=%async_computation.5 | async-start | bytes 5308416 | tf_op jit(solution)/shard_map/reduce_scatter | solution.py:1099
  138.0 25.4 %collective-permute-start.15 = (bf16[2,2,64,2304]{3,2,1,0:T(8,128)(2,1)}, bf16[2,2,64,2304]{3,2,1,0:T(8,128)(2,1)}, u32[]{:S(2)}, u32[]{:S(2)}) collective-permute-start(bf16[2,2,64,2304]{3,2,1,0:T(8,128)(2,1)} %pad_maximum_fusion.8.refs_0_), channel_id=1, source_target_pairs={{0,8},{1,9},{2,10},{3,11},{4,12},{5,13},{6,14},{7,15},{8,0},{9,1},... | collective-permute-start | bytes 3538952 | tf_op jit(solution)/shard_map/ppermute | solution.py:471
  140.5 25.4 %collective-permute-start.18 = (bf16[2,2,64,2304]{3,2,1,0:T(8,128)(2,1)S(1)}, bf16[2,2,64,2304]{3,2,1,0:T(8,128)(2,1)S(1)}, u32[]{:S(2)}, u32[]{:S(2)}) collective-permute-start(bf16[2,2,64,2304]{3,2,1,0:T(8,128)(2,1)S(1)} %pad_maximum_fusion.9), channel_id=1, source_target_pairs={{0,16},{1,17},{2,18},{3,19},{4,20},{5,21},{6,22},{7,23},{8,24},{9,... | collective-permute-start | bytes 3538952 | tf_op jit(solution)/shard_map/ppermute | solution.py:471
  169.3 11.2 %collective-permute-start.19 = (bf16[16,64,2304]{2,1,0:T(8,128)(2,1)}, bf16[16,64,2304]{2,1,0:T(8,128)(2,1)}, u32[]{:S(2)}, u32[]{:S(2)}) collective-permute-start(bf16[16,64,2304]{2,1,0:T(8,128)(2,1)} %shard_map.275.refs_1_.refs_0_.refs_2_), channel_id=1, source_target_pairs={{0,1},{1,0},{2,3},{3,2},{4,5},{5,4},{6,7},{7,6},{8,9},{9,8},{10,11... | collective-permute-start | bytes 14155784 | tf_op jit(solution)/shard_map/ppermute | solution.py:471
  172.6 31.1 %collective-permute-start.20 = (bf16[576,1152]{1,0:T(8,128)(2,1)}, bf16[576,1152]{1,0:T(8,128)(2,1)}, u32[]{:S(2)}, u32[]{:S(2)}) collective-permute-start(bf16[576,1152]{1,0:T(8,128)(2,1)} %shard_map.284), channel_id=1, source_target_pairs={{0,16},{1,17},{2,18},{3,19},{4,20},{5,21},{6,22},{7,23},{8,24},{9,... | collective-permute-start | bytes 3981320 | tf_op jit(solution)/shard_map/ppermute | solution.py:471
  173.7 30.8 %collective-permute-start.21 = (bf16[576,1152]{1,0:T(8,128)(2,1)}, bf16[576,1152]{1,0:T(8,128)(2,1)}, u32[]{:S(2)}, u32[]{:S(2)}) collective-permute-start(bf16[576,1152]{1,0:T(8,128)(2,1)} %shard_map.287), channel_id=1, source_target_pairs={{0,8},{1,9},{2,10},{3,11},{4,12},{5,13},{6,14},{7,15},{8,0},{9,1},... | collective-permute-start | bytes 3981320 | tf_op jit(solution)/shard_map/ppermute | solution.py:471
  204.5 29.7 %collective-permute-start.22 = (bf16[2,288,1152]{2,1,0:T(8,128)(2,1)}, bf16[2,288,1152]{2,1,0:T(8,128)(2,1)S(1)}, u32[]{:S(2)}, u32[]{:S(2)}) collective-permute-start(bf16[2,288,1152]{2,1,0:T(8,128)(2,1)} %shard_map.290), channel_id=1, source_target_pairs={{0,8},{1,9},{2,10},{3,11},{4,12},{5,13},{6,14},{7,15},{8,0},{9,1},... | collective-permute-start | bytes 3981320 | tf_op jit(solution)/shard_map/ppermute | solution.py:471
  205.7 29.6 %collective-permute-start.23 = (bf16[2,288,1152]{2,1,0:T(8,128)(2,1)}, bf16[2,288,1152]{2,1,0:T(8,128)(2,1)S(1)}, u32[]{:S(2)}, u32[]{:S(2)}) collective-permute-start(bf16[2,288,1152]{2,1,0:T(8,128)(2,1)} %shard_map.292), channel_id=1, source_target_pairs={{0,16},{1,17},{2,18},{3,19},{4,20},{5,21},{6,22},{7,23},{8,24},{9,... | collective-permute-start | bytes 3981320 | tf_op jit(solution)/shard_map/ppermute | solution.py:471
  248.2 110.7 %all-gather.8.cloned.1.call-start = ((), (), s32[]{:S(2)}) async-start(), calls=%async_computation.6 | async-start | bytes 5308416 | tf_op jit(solution)/shard_map/all_gather | solution.py:1097
  259.8 42.8 %copy-start.26 = (bf16[128,2304]{1,0:T(8,128)(2,1)S(1)}, bf16[128,2304]{1,0:T(8,128)(2,1)}, u32[]{:S(2)}) copy-start(bf16[128,2304]{1,0:T(8,128)(2,1)} %param.27) | copy-start | bytes 1769476
  259.8 42.8 %copy-start.47 = (f32[2304]{0:T(1024)S(1)}, f32[2304]{0:T(1024)}, u32[]{:S(2)}) copy-start(f32[2304]{0:T(1024)} %get-tuple-element.68) | copy-start | bytes 27652
  301.2 3.5 copy-start.1
  301.2 3.5 copy-start.7
  306.2 136.3 %reduce-scatter.6.cloned.1.call-start = ((), (), s32[]{:S(2)}) async-start(), calls=%async_computation.7 | async-start | bytes 5308416 | tf_op jit(solution)/shard_map/reduce_scatter | solution.py:1099
  387.9 114.6 %all-gather.10.cloned.1.call-start = ((), (), s32[]{:S(2)}) async-start(), calls=%async_computation.8 | async-start | bytes 5308416 | tf_op jit(solution)/shard_map/all_gather | solution.py:1097
  403.5 32.0 %collective-permute-start.24 = (bf16[2,288,1152]{2,1,0:T(8,128)(2,1)}, bf16[2,288,1152]{2,1,0:T(8,128)(2,1)S(1)}, u32[]{:S(2)}, u32[]{:S(2)}) collective-permute-start(bf16[2,288,1152]{2,1,0:T(8,128)(2,1)} %pad_maximum_fusion.6), channel_id=1, source_target_pairs={{0,16},{1,17},{2,18},{3,19},{4,20},{5,21},{6,22},{7,23},{8,24},{9,... | collective-permute-start | bytes 3981320 | tf_op jit(solution)/shard_map/ppermute | solution.py:471
  404.9 30.6 %collective-permute-start.25 = (bf16[2,288,1152]{2,1,0:T(8,128)(2,1)S(1)}, bf16[2,288,1152]{2,1,0:T(8,128)(2,1)}, u32[]{:S(2)}, u32[]{:S(2)}) collective-permute-start(bf16[2,288,1152]{2,1,0:T(8,128)(2,1)S(1)} %pad_maximum_fusion.7), channel_id=1, source_target_pairs={{0,8},{1,9},{2,10},{3,11},{4,12},{5,13},{6,14},{7,15},{8,0},{9,1},... | collective-permute-start | bytes 3981320 | tf_op jit(solution)/shard_map/ppermute | solution.py:471
  428.9 3.5 copy-start.28
  430.6 62.4 %collective-permute-start.26 = (bf16[2,576,1152]{2,1,0:T(8,128)(2,1)}, bf16[2,576,1152]{2,1,0:T(8,128)(2,1)}, u32[]{:S(2)}, u32[]{:S(2)}) collective-permute-start(bf16[2,576,1152]{2,1,0:T(8,128)(2,1)} %pad_maximum_fusion), channel_id=1, source_target_pairs={{0,16},{1,17},{2,18},{3,19},{4,20},{5,21},{6,22},{7,23},{8,24},{9,... | collective-permute-start | bytes 7962632 | tf_op jit(solution)/shard_map/ppermute | solution.py:471
  434.4 58.7 %collective-permute-start.27 = (bf16[2,576,1152]{2,1,0:T(8,128)(2,1)}, bf16[2,576,1152]{2,1,0:T(8,128)(2,1)}, u32[]{:S(2)}, u32[]{:S(2)}) collective-permute-start(bf16[2,576,1152]{2,1,0:T(8,128)(2,1)} %pad_maximum_fusion.1), channel_id=1, source_target_pairs={{0,8},{1,9},{2,10},{3,11},{4,12},{5,13},{6,14},{7,15},{8,0},{9,1},... | collective-permute-start | bytes 7962632 | tf_op jit(solution)/shard_map/ppermute | solution.py:471
  438.9 81.3 %collective-permute-start.29 = (bf16[288,1152]{1,0:T(8,128)(2,1)}, bf16[288,1152]{1,0:T(8,128)(2,1)}, u32[]{:S(2)}, u32[]{:S(2)}) collective-permute-start(bf16[288,1152]{1,0:T(8,128)(2,1)} %fusion.29), channel_id=1, source_target_pairs={{0,8},{1,9},{2,10},{3,11},{4,12},{5,13},{6,14},{7,15},{8,0},{9,1},... | collective-permute-start | bytes 1990664 | tf_op jit(solution)/shard_map/ppermute | solution.py:471
  441.5 78.7 %collective-permute-start.30 = (bf16[288,1152]{1,0:T(8,128)(2,1)}, bf16[288,1152]{1,0:T(8,128)(2,1)}, u32[]{:S(2)}, u32[]{:S(2)}) collective-permute-start(bf16[288,1152]{1,0:T(8,128)(2,1)} %fusion.30), channel_id=1, source_target_pairs={{0,16},{1,17},{2,18},{3,19},{4,20},{5,21},{6,22},{7,23},{8,24},{9,... | collective-permute-start | bytes 1990664 | tf_op jit(solution)/shard_map/ppermute | solution.py:471
  448.3 156.4 %reduce-scatter.8.cloned.1.call-start = ((), (), s32[]{:S(2)}) async-start(), calls=%async_computation.9 | async-start | bytes 5308416 | tf_op jit(solution)/shard_map/reduce_scatter | solution.py:1099
  496.1 71.8 %collective-permute-start.32 = (bf16[576,1152]{1,0:T(8,128)(2,1)}, bf16[576,1152]{1,0:T(8,128)(2,1)}, u32[]{:S(2)}, u32[]{:S(2)}) collective-permute-start(bf16[576,1152]{1,0:T(8,128)(2,1)} %fusion.8), channel_id=1, source_target_pairs={{0,8},{1,9},{2,10},{3,11},{4,12},{5,13},{6,14},{7,15},{8,0},{9,1},... | collective-permute-start | bytes 3981320 | tf_op jit(solution)/shard_map/ppermute | solution.py:471
  500.2 67.7 %collective-permute-start.33 = (bf16[576,1152]{1,0:T(8,128)(2,1)}, bf16[576,1152]{1,0:T(8,128)(2,1)}, u32[]{:S(2)}, u32[]{:S(2)}) collective-permute-start(bf16[576,1152]{1,0:T(8,128)(2,1)} %fusion.9), channel_id=1, source_target_pairs={{0,16},{1,17},{2,18},{3,19},{4,20},{5,21},{6,22},{7,23},{8,24},{9,... | collective-permute-start | bytes 3981320 | tf_op jit(solution)/shard_map/ppermute | solution.py:471
  514.4 5.8 collective-permute-start.28
  536.5 5.1 copy-start.9
  544.4 18.0 %collective-permute-start.35 = (bf16[2,288,640]{2,1,0:T(8,128)(2,1)}, bf16[2,288,640]{2,1,0:T(8,128)(2,1)}, u32[]{:S(2)}, u32[]{:S(2)}) collective-permute-start(bf16[2,288,640]{2,1,0:T(8,128)(2,1)} %pad_maximum_fusion.16.refs_0_), channel_id=1, source_target_pairs={{0,8},{1,9},{2,10},{3,11},{4,12},{5,13},{6,14},{7,15},{8,0},{9,1},... | collective-permute-start | bytes 2211848 | tf_op jit(solution)/shard_map/ppermute | solution.py:471
  547.1 17.9 %collective-permute-start.34 = (bf16[2,288,640]{2,1,0:T(8,128)(2,1)}, bf16[2,288,640]{2,1,0:T(8,128)(2,1)}, u32[]{:S(2)}, u32[]{:S(2)}) collective-permute-start(bf16[2,288,640]{2,1,0:T(8,128)(2,1)} %pad_maximum_fusion.15.refs_0_), channel_id=1, source_target_pairs={{0,16},{1,17},{2,18},{3,19},{4,20},{5,21},{6,22},{7,23},{8,24},{9,... | collective-permute-start | bytes 2211848 | tf_op jit(solution)/shard_map/ppermute | solution.py:471
  549.1 6.1 collective-permute-start.31
  564.3 14.5 %collective-permute-start.37 = (bf16[288,640]{1,0:T(8,128)(2,1)}, bf16[288,640]{1,0:T(8,128)(2,1)}, u32[]{:S(2)}, u32[]{:S(2)}) collective-permute-start(bf16[288,640]{1,0:T(8,128)(2,1)} %fusion.34.refs_0_), channel_id=1, source_target_pairs={{0,16},{1,17},{2,18},{3,19},{4,20},{5,21},{6,22},{7,23},{8,24},{9,... | collective-permute-start | bytes 1105928 | tf_op jit(solution)/shard_map/ppermute | solution.py:471
  567.0 13.2 %collective-permute-start.38 = (bf16[288,640]{1,0:T(8,128)(2,1)}, bf16[288,640]{1,0:T(8,128)(2,1)}, u32[]{:S(2)}, u32[]{:S(2)}) collective-permute-start(bf16[288,640]{1,0:T(8,128)(2,1)} %fusion.35.refs_0_), channel_id=1, source_target_pairs={{0,8},{1,9},{2,10},{3,11},{4,12},{5,13},{6,14},{7,15},{8,0},{9,1},... | collective-permute-start | bytes 1105928 | tf_op jit(solution)/shard_map/ppermute | solution.py:471
  569.9 18.7 %collective-permute-start.36 = (bf16[2,64,2304]{2,1,0:T(8,128)(2,1)}, bf16[2,64,2304]{2,1,0:T(8,128)(2,1)}, u32[]{:S(2)}, u32[]{:S(2)}) collective-permute-start(bf16[2,64,2304]{2,1,0:T(8,128)(2,1)} %pad_maximum_fusion.19.refs_0_), channel_id=1, source_target_pairs={{0,16},{1,17},{2,18},{3,19},{4,20},{5,21},{6,22},{7,23},{8,24},{9,... | collective-permute-start | bytes 1769480 | tf_op jit(solution)/shard_map/ppermute | solution.py:471
  582.5 25.4 %all-to-all-start = ((bf16[8,72,640]{2,1,0:T(8,128)(2,1)}), bf16[8,72,640]{2,1,0:T(8,128)(2,1)}, u32[]{:S(2)}, u32[]{:S(2)}) async-start(bf16[8,72,640]{2,1,0:T(8,128)(2,1)} %bitcast.137), calls=%async_computation.3 | async-start | bytes 1474560 | tf_op jit(solution)/shard_map/all_to_all | solution.py:1098
  590.5 8.8 %collective-permute-start.39 = (bf16[64,2304]{1,0:T(8,128)(2,1)}, bf16[64,2304]{1,0:T(8,128)(2,1)}, u32[]{:S(2)}, u32[]{:S(2)}) collective-permute-start(bf16[64,2304]{1,0:T(8,128)(2,1)} %fusion.38.refs_0_), channel_id=1, source_target_pairs={{0,8},{1,9},{2,10},{3,11},{4,12},{5,13},{6,14},{7,15},{8,0},{9,1},... | collective-permute-start | bytes 884744 | tf_op jit(solution)/shard_map/ppermute | solution.py:471
  601.2 3.5 copy-start.46
  601.2 3.5 copy-start.59
  601.2 5.0 copy-start.14
  601.3 26.0 %collective-permute-start.40 = (bf16[64,2304]{1,0:T(8,128)(2,1)}, bf16[64,2304]{1,0:T(8,128)(2,1)S(1)}, u32[]{:S(2)}, u32[]{:S(2)}) collective-permute-start(bf16[64,2304]{1,0:T(8,128)(2,1)} %shard_map.343.refs_1_), channel_id=1, source_target_pairs={{0,0},{1,1},{2,8},{3,9},{4,16},{5,17},{6,24},{7,25},{8,2},{9,3},{1... | collective-permute-start | bytes 884744 | tf_op jit(solution)/shard_map/ppermute | solution.py:471
  610.3 19.6 %copy-start.41 = (f32[72,128]{1,0:T(8,128)S(1)}, f32[72,128]{1,0:T(8,128)}, u32[]{:S(2)}) copy-start(f32[72,128]{1,0:T(8,128)} %get-tuple-element.58) | copy-start | bytes 110596
  610.3 20.3 %copy-start.49 = (f32[72,1]{1,0:T(8,128)S(1)}, f32[72,1]{1,0:T(8,128)}, u32[]{:S(2)}) copy-start(f32[72,1]{1,0:T(8,128)} %get-tuple-element.57) | copy-start | bytes 868
  (49 other events, 79.2 us)
Sparse Core Ops, SparseCore 0:
  49.4 52.8 all-gather.5
  125.4 47.9 all-gather.11
  248.4 52.7 reduce-scatter.3
  306.3 52.6 all-gather.7
  388.1 51.2 reduce-scatter.5
  448.4 51.4 all-gather.9
  536.6 50.7 reduce-scatter.7
